TPU v7x, 32 devices: a whole 2x2x4 slice. The times are simulated.
32 devices in a mesh: tm: 2 (over x), space: 16 (over z, y, core).
Axes of the slice: x: 2, y: 2, z: 4, core: 2. Of those that a mesh axis runs over, the one named last changes fastest.
Arguments:
- eof_basis: bfloat16 [131072, 256], P('space'), may hold values from -0.015625 to 0.015625
- snapshots: bfloat16 [131072, 128], P('space', 'tm'), may hold values from -6 to 6
- inverse_energy: float32 [256], replicated, may hold values from 0.044194173 to 0.44194174
- eigen_vectors: bfloat16 [256, 512], replicated, may hold values from -0.375 to 0.375
Outputs:
- reduced_operator: float32 [256, 256], replicated
- rebuilt_modes: bfloat16 [512, 131072], P('tm', 'space')
All inputs are finite; a program needn't handle non-finite values.
Results may differ from a plain program's by a relative error of at most 0.0049.
Values may be sent and summed in bfloat16 or wider, within the bound.
No kernel may reach another device: no remote copies, remote signals or barrier semaphores. Data moves between devices by JAX's collectives and lax.ppermute only.
A program may use at most 64 MiB of HBM per device.

v0:
```python
import jax
import jax.numpy as jnp
from jax import lax
from jax.sharding import PartitionSpec as P


def passed_along(block, axis, distance):
    devices = range(lax.axis_size(axis))
    route = [(i - distance, i) for i in devices if i - distance in devices]
    return lax.ppermute(block, axis, route)


def per_device(eof_basis, snapshots, inverse_energy, eigen_vectors):
    partial_value = lax.dot_general(
        eof_basis, snapshots, (((0,), (0,)), ((), ())), preferred_element_type=jnp.float32
    )
    coeffs = lax.psum(partial_value, "space")
    previous = passed_along(coeffs[:, -1:], "tm", 1)
    lagged = jnp.concatenate([previous, coeffs[:, :-1]], axis=1)
    scaled = lagged * inverse_energy[:, None]
    local_part = jnp.dot(coeffs, scaled.T, precision=lax.Precision.HIGHEST)
    reduced_operator = lax.psum(local_part, "tm")
    hour_weights = jnp.dot(
        scaled.T, eigen_vectors.astype(jnp.float32), precision=lax.Precision.HIGHEST
    ).astype(jnp.bfloat16)
    mode_rows = hour_weights.shape[1] // lax.axis_size("tm")
    all_weights = lax.all_gather(hour_weights, "tm", axis=0, tiled=True)
    mine = lax.dynamic_slice_in_dim(all_weights, lax.axis_index("tm") * mode_rows, mode_rows, 1)
    rebuilt = lax.dot_general(
        mine,
        lax.all_gather(snapshots, "tm", axis=1, tiled=True),
        (((0,), (1,)), ((), ())),
        preferred_element_type=jnp.float32,
    )
    return (reduced_operator, rebuilt.astype(jnp.bfloat16))


def solution(mesh):
    in_specs = (P("space", None), P("space", "tm"), P(), P())
    out_specs = (P(), P("tm", "space"))
    return jax.shard_map(
        per_device, mesh=mesh, in_specs=in_specs, out_specs=out_specs, check_vma=False
    )
```

profile of v0, /device:TPU:0, one launch (start us, length us, event | category | flops | bytes accessed | tf_op | source)
XLA Modules:
  0.0 148.0 jit_solution(3100853406295683494)
XLA Ops:
  8.0 0.0 copy-start
  8.0 0.0 copy-start.1
  8.0 0.0 all-reduce.3.cloned.1.call-start
  8.1 4.0 %fusion.7 = f32[256,64]{0,1:T(8,128)} fusion(bf16[8192,64]{0,1:T(8,128)(2,1)} %param.5, bf16[8192,256]{1,0:T(8,128)(2,1)} %param.4), kind=kOutput, calls=%fused_computation.10 | convolution fusion | flops 268435456 | bytes 5308416 | tf_op jit(solution)/shard_map/dot_general | solution.py:14
  12.0 0.0 all-reduce.3.cloned.1.call-update
  12.1 0.0 all-gather.2.cloned.1.call-start
  12.1 0.5 all-gather.2.cloned.1.call-update
  12.6 0.0 all-reduce.5.cloned.1.call-start
  12.7 87.4 %all-reduce.3.cloned.1.call-done = f32[256,64]{0,1:T(8,128)} async-done(((f32[256,64]{0,1:T(8,128)}), f32[256,64]{0,1:T(8,128)}) %all-reduce.3.cloned.1.call-update) | async-done | bytes 65552 | tf_op jit(solution)/shard_map/psum | solution.py:17
  100.1 0.7 slice.8
  100.8 3.4 %collective-permute-start = (f32[256,1]{0,1:T(1,128)S(1)}, f32[256,1]{0,1:T(1,128)S(1)}, u32[]{:S(2)}, u32[]{:S(2)}) collective-permute-start(f32[256,1]{0,1:T(1,128)S(1)} %slice.8), channel_id=1, source_target_pairs={{0,16},{1,17},{2,18},{3,19},{4,20},{5,21},{6,22},{7,23},{8,24},{9,... | collective-permute-start | bytes 3080 | tf_op jit(solution)/shard_map/ppermute | solution.py:10
  104.2 1.3 collective-permute-done
  105.5 0.0 copy-done
  105.5 0.0 copy-done.1
  105.5 1.1 convolution_convert_fusion.1
  106.6 5.2 %all_gather.6 = bf16[128,512]{1,0:T(8,128)(2,1)S(1)} all-gather(bf16[64,512]{1,0:T(8,128)(2,1)S(1)} %convolution_convert_fusion.1), channel_id=1, replica_groups=mesh['tm'=2,'space'=16] {'tm'}, dimensions={0}, use_global_device_ids=true | all-gather | bytes 196608 | tf_op jit(solution)/shard_map/all_gather | solution.py:27
  111.7 2.0 %fusion.1 = f32[256,256]{1,0:T(8,128)} fusion(f32[256,64]{0,1:T(8,128)} %all-reduce.3.cloned.1.call-done, f32[256,63]{0,1:T(8,128)} %bitcast.7, f32[256,1]{0,1:T(1,128)S(1)} %collective-permute-done, f32[256]{0:T(256)S(1)} %copy-done.1), kind=kOutput, calls=%fused_computation.4 | convolution fusion | flops 50364416 | bytes 394240 | tf_op jit(solution)/shard_map/dot_general | solution.py:21
  113.8 0.0 all-reduce.5.cloned.1.call-update
  113.8 0.0 all-gather.2.cloned.1.call-done
  113.8 4.9 %convolution_convert_fusion = bf16[256,8192]{1,0:T(8,128)(2,1)} fusion(bf16[8192,128]{0,1:T(8,128)(2,1)} %all-gather.2.cloned.1.call-done, bf16[128,512]{1,0:T(8,128)(2,1)S(1)} %all_gather.6, s32[]{:T(128)S(6)} %select_n.3), kind=kOutput, calls=%fused_computation | convolution fusion | flops 538968064 | bytes 6356996 | tf_op jit(solution)/shard_map/dot_general | solution.py:29
  118.7 20.2 %all-reduce.5.cloned.1.call-done = f32[256,256]{1,0:T(8,128)} async-done(((f32[256,256]{1,0:T(8,128)}), f32[256,256]{1,0:T(8,128)}) %all-reduce.5.cloned.1.call-update) | async-done | bytes 262160 | tf_op jit(solution)/shard_map/psum | solution.py:22
  138.9 1.7 %copy.8 = f32[256,256]{1,0:T(8,128)} copy(f32[256,256]{1,0:T(8,128)} %all-reduce.5.cloned.1.call-done) | data formatting | bytes 524288
Async XLA Ops:
  8.0 97.5 %copy-start = (bf16[256,512]{1,0:T(8,128)(2,1)S(1)}, bf16[256,512]{1,0:T(8,128)(2,1)}, u32[]{:S(2)}) copy-start(bf16[256,512]{1,0:T(8,128)(2,1)} %param.7) | copy-start | bytes 786436
  8.0 97.4 %copy-start.1 = (f32[256]{0:T(256)S(1)}, f32[256]{0:T(256)}, u32[]{:S(2)}) copy-start(f32[256]{0:T(256)} %param.6) | copy-start | bytes 3076
  8.0 92.1 %all-reduce.3.cloned.1.call-start = ((), (), s32[]{:S(2)}) async-start(), calls=%async_computation | async-start | bytes 131072 | tf_op jit(solution)/shard_map/psum | solution.py:17
  12.1 101.8 %all-gather.2.cloned.1.call-start = ((), (), s32[]{:S(2)}) async-start(), calls=%async_computation.2 | async-start | bytes 3145728 | tf_op jit(solution)/shard_map/all_gather | solution.py:31
  12.6 126.3 %all-reduce.5.cloned.1.call-start = ((), (), s32[]{:S(2)}) async-start(), calls=%async_computation.1 | async-start | bytes 524288 | tf_op jit(solution)/shard_map/psum | solution.py:22
  100.8 4.7 %collective-permute-start = (f32[256,1]{0,1:T(1,128)S(1)}, f32[256,1]{0,1:T(1,128)S(1)}, u32[]{:S(2)}, u32[]{:S(2)}) collective-permute-start(f32[256,1]{0,1:T(1,128)S(1)} %slice.8), channel_id=1, source_target_pairs={{0,16},{1,17},{2,18},{3,19},{4,20},{5,21},{6,22},{7,23},{8,24},{9,... | collective-permute-start | bytes 3080 | tf_op jit(solution)/shard_map/ppermute | solution.py:10
Sparse Core Ops, SparseCore 0:
  12.9 87.1 all-reduce.2
Sparse Core Ops, SparseCore 1:
  14.1 35.7 all-gather.1
  113.9 25.0 all-reduce.4
where the time goes:
time: 148 us
  waiting for transfers between devices  109 us (74%)
  between operations  15.5 us (10%)
  matrix products  12 us (8%)
  blocking collectives  5.16 us (3%)
  starting transfers between devices  3.48 us (2%)
  local copies, waits for them, and re-layouts  2.38 us (2%)
    psum x1, waiting for transfers between devices, per_device(): coeffs = lax.psum(partial_value, 'space')  87.4 us
    psum x1, waiting for transfers between devices, per_device(): reduced_operator = lax.psum(local_part, 'tm')  20.2 us
    all_gather x1, blocking collectives, per_device(): all_weights = lax.all_gather(hour_weights, 'tm', axis=0, tiled=True)  5.16 us
    dot_general x1, matrix products, per_device(): lax.dot_general(mine, lax.all_gather(snapshots, 'tm', axis=1, tiled=True)...  4.89 us
    dot_general x1, matrix products, per_device(): lax.dot_general(eof_basis, snapshots, (((0,), (0,)), ((), ())), preferred...  3.96 us
    ppermute x1, starting transfers between devices, passed_along(): return lax.ppermute(block, axis, route)  3.36 us
  transfers between devices with their start and end apart: 4, of which 3 were waited for; matrix products, arithmetic and copies ran while one was open for 6% of the time, Pallas kernels for 0%

commit v1 on v0

v1 whole, which is shorter than its diff:
```python
import jax
import jax.numpy as jnp
from jax import lax
from jax.sharding import PartitionSpec as P


def per_device(eof_basis, snapshots, inverse_energy, eigen_vectors):
    tm, space = lax.axis_size("tm"), lax.axis_size("space")
    me = lax.axis_index("tm")
    hours, rank = snapshots.shape[1], eof_basis.shape[1]

    held = [snapshots]
    for k in range(1, tm):
        route = [((i + k) % tm, i) for i in range(tm)]
        held.append(lax.ppermute(snapshots, "tm", route))

    partial_sum = lax.dot_general(
        snapshots, eof_basis, (((0,), (0,)), ((), ())), preferred_element_type=jnp.float32
    )
    pieces = (
        partial_sum.reshape(hours // 8, 8, rank // 128, 128)
        .transpose(0, 2, 1, 3)
        .reshape(space, -1, 128)
    )
    shares = lax.all_to_all(pieces, "space", 0, 0, tiled=True)
    mine = jnp.sum(shares, axis=0)
    every = lax.all_gather(mine, ("tm", "space"), axis=0)
    coeffs = (
        every.reshape(tm * hours // 8, rank // 128, 8, 128)
        .transpose(0, 2, 1, 3)
        .reshape(tm * hours, rank)
    )
    lagged = jnp.concatenate([jnp.zeros((1, rank), jnp.float32), coeffs[:-1]], axis=0)
    scaled = lagged * inverse_energy[None, :]
    reduced_operator = lax.dot_general(
        coeffs, scaled, (((0,), (0,)), ((), ())), precision=lax.Precision.HIGHEST
    )
    rows = eigen_vectors.shape[1] // tm
    vectors = lax.dynamic_slice_in_dim(eigen_vectors, me * rows, rows, 1)
    weights = jnp.dot(
        scaled, vectors.astype(jnp.float32), precision=lax.Precision.HIGHEST
    ).astype(jnp.bfloat16)
    rebuilt = 0.0
    for k in range(tm):
        part = lax.dynamic_slice_in_dim(weights, ((me + k) % tm) * hours, hours, 0)
        rebuilt = rebuilt + lax.dot_general(
            part, held[k], (((0,), (1,)), ((), ())), preferred_element_type=jnp.float32
        )
    return (reduced_operator, rebuilt.astype(jnp.bfloat16))


def solution(mesh):
    in_specs = (P("space", None), P("space", "tm"), P(), P())
    out_specs = (P(), P("tm", "space"))
    return jax.shard_map(
        per_device, mesh=mesh, in_specs=in_specs, out_specs=out_specs, check_vma=False
    )
```

time: 148 us -> 63.7 us (0.43)
  waiting for transfers between devices: 109 us -> 5.32 us
  blocking collectives: 5.16 us -> 38.5 us
  between operations: 15.5 us -> 0.69 us
  starting transfers between devices: 3.48 us -> 8.94 us
  local copies, waits for them, and re-layouts: 2.38 us -> 0.02 us
  matrix products: 12 us -> 9.99 us
    psum x2 -> x0, waiting for transfers between devices: 108 us -> none  [the longest x1 87.4 us: per_device(): coeffs = lax.psum(partial_value, 'space')]
    all_gather x1, blocking collectives: 5.16 us -> 38.5 us  [per_device(): every = lax.all_gather(mine, ('tm', 'space'), axis=0)]
    all_to_all x0 -> x1, starting transfers between devices: none -> 7.38 us  [per_device(): shares = lax.all_to_all(pieces, 'space', 0, 0, tiled=True)]
    all_to_all x0 -> x1, waiting for transfers between devices: none -> 5.32 us  [per_device(): shares = lax.all_to_all(pieces, 'space', 0, 0, tiled=True)]
    dot_general x4 -> x5, matrix products: 12 us -> 9.99 us  [the longest x2 4.6 us: per_device(): lax.dot_general(part, held[k], (((0,), (1,)), ((), ())), preferred_elemen...]
    ppermute x1, starting transfers between devices: 3.36 us -> 1.57 us  [per_device(): held.append(lax.ppermute(snapshots, 'tm', route))]
    unnamed x5 -> x6, local copies, waits for them, and re-layouts: 1.68 us -> 0.02 us
  transfers between devices with their start and end apart: 4 -> 2, of which waited for: 3 -> 1; matrix products, arithmetic and copies ran while one was open for 6% -> 4% of each run, Pallas kernels for 0% -> 0%
where the time goes in v1:
time: 63.7 us; the launch traced here: 63.5 us
  blocking collectives  38.5 us (60%)
  matrix products  9.99 us (16%)
  starting transfers between devices  8.94 us (14%)
  waiting for transfers between devices  5.32 us (8%)
  between operations  0.69 us (1%)
    all_gather x1, blocking collectives, per_device(): every = lax.all_gather(mine, ('tm', 'space'), axis=0)  38.5 us
    all_to_all x1, starting transfers between devices, per_device(): shares = lax.all_to_all(pieces, 'space', 0, 0, tiled=True)  7.38 us
    all_to_all x1, waiting for transfers between devices, per_device(): shares = lax.all_to_all(pieces, 'space', 0, 0, tiled=True)  5.32 us
    dot_general x2, matrix products, per_device(): lax.dot_general(part, held[k], (((0,), (1,)), ((), ())), preferred_elemen...  4.6 us
    dot_general x1, matrix products, per_device(): lax.dot_general(snapshots, eof_basis, (((0,), (0,)), ((), ())), preferred...  4.04 us
    ppermute x1, starting transfers between devices, per_device(): held.append(lax.ppermute(snapshots, 'tm', route))  1.57 us
  transfers between devices with their start and end apart: 2, of which 1 were waited for; matrix products, arithmetic and copies ran while one was open for 4% of the time, Pallas kernels for 0%

profile of v1, /device:TPU:0, one launch (start us, length us, event | category | flops | bytes accessed | tf_op | source)
XLA Modules:
  0.0 63.5 jit_solution(18350828961311512009)
XLA Ops:
  0.6 0.0 copy-start
  0.6 0.0 copy-start.1
  0.7 0.0 copy-start.2
  0.7 4.0 %fusion.13 = f32[64,256]{1,0:T(8,128)} fusion(bf16[8192,64]{0,1:T(8,128)(2,1)} %param.5, bf16[8192,256]{1,0:T(8,128)(2,1)} %param.4), kind=kOutput, calls=%fused_computation.16 | convolution fusion | flops 268435456 | bytes 5308416 | tf_op jit(solution)/shard_map/dot_general | solution.py:17
  4.7 7.4 %all-to-all-start = ((f32[16,8,128]{2,1,0:T(8,128)}), f32[16,8,128]{2,1,0:T(8,128)S(1)}, u32[]{:S(2)}, u32[]{:S(2)}) async-start(f32[16,8,128]{2,1,0:T(8,128)} %bitcast.2), calls=%async_computation | async-start | bytes 131072 | tf_op jit(solution)/shard_map/all_to_all | solution.py:25
  12.1 0.0 copy-done.1
  12.1 1.6 %collective-permute-start = (bf16[8192,64]{0,1:T(8,128)(2,1)S(1)}, bf16[8192,64]{0,1:T(8,128)(2,1)S(1)}, u32[]{:S(2)}, u32[]{:S(2)}) collective-permute-start(bf16[8192,64]{0,1:T(8,128)(2,1)S(1)} %copy-done.1), channel_id=1, source_target_pairs={{16,0},{0,16},{17,1},{1,17},{18,2},{2,18},{19,3},{3,19},{20,4},{4,... | collective-permute-start | bytes 3145736 | tf_op jit(solution)/shard_map/ppermute | solution.py:15
  13.7 5.3 %all-to-all-done = f32[16,8,128]{2,1,0:T(8,128)S(1)} async-done(((f32[16,8,128]{2,1,0:T(8,128)}), f32[16,8,128]{2,1,0:T(8,128)S(1)}, u32[]{:S(2)}, u32[]{:S(2)}) %all-to-all-start) | async-done | bytes 65568 | tf_op jit(solution)/shard_map/all_to_all | solution.py:25
  19.0 38.5 %all-gather = f32[256,128]{1,0:T(8,128)S(1)} all-gather(f32[8,128]{1,0:T(8,128)S(1)} %reduce_sum.9), channel_id=2, replica_groups=mesh['tm'=2,'space'=16] {'tm','space'}, dimensions={0}, use_global_device_ids=true | all-gather | bytes 135168 | tf_op jit(solution)/shard_map/all_gather | solution.py:27
  57.5 0.0 copy-done
  57.5 0.0 copy-done.2
  57.5 0.2 convolution_convert_fusion
  57.8 1.1 %fusion.2 = f32[256,256]{1,0:T(8,128)} fusion(f32[128,256]{1,0:T(8,128)S(1)} %bitcast.17, f32[127,256]{1,0:T(8,128)S(1)} %bitcast.18, f32[256]{0:T(256)S(1)} %copy-done.2), kind=kOutput, calls=%fused_computation.5 | convolution fusion | flops 100696064 | bytes 524288 | tf_op jit(solution)/shard_map/dot_general | solution.py:35
  58.9 1.3 %fusion.6 = f32[256,8192]{1,0:T(8,128)S(1)} fusion(bf16[8192,64]{0,1:T(8,128)(2,1)S(1)} %copy-done.1, bf16[128,256]{1,0:T(8,128)(2,1)S(1)} %convolution_convert_fusion, s32[]{:T(128)S(6)} %select_n.22), kind=kOutput, calls=%fused_computation.9 | convolution fusion | flops 268435456 | bytes 9469956 | tf_op jit(solution)/shard_map/dot_general | solution.py:46
  60.2 0.0 collective-permute-done
  60.2 3.3 %fusion = bf16[256,8192]{1,0:T(8,128)(2,1)} fusion(f32[256,8192]{1,0:T(8,128)S(1)} %fusion.6, bf16[8192,64]{0,1:T(8,128)(2,1)S(1)} %collective-permute-done, bf16[128,256]{1,0:T(8,128)(2,1)S(1)} %convolution_convert_fusion, s32[]{:T(128)S(6)} %select_n.24), kind=kOutput, calls=%fused_computation.1 | convolution fusion | flops 272629760 | bytes 13664260 | tf_op jit(solution)/shard_map/dot_general | solution.py:46
  (1 shorter events, 0.0 us)
Async XLA Ops:
  0.6 56.9 %copy-start = (bf16[256,512]{1,0:T(8,128)(2,1)S(1)}, bf16[256,512]{1,0:T(8,128)(2,1)}, u32[]{:S(2)}) copy-start(bf16[256,512]{1,0:T(8,128)(2,1)} %param.7) | copy-start | bytes 786436
  0.6 11.4 %copy-start.1 = (bf16[8192,64]{0,1:T(8,128)(2,1)S(1)}, bf16[8192,64]{0,1:T(8,128)(2,1)}, u32[]{:S(2)}) copy-start(bf16[8192,64]{0,1:T(8,128)(2,1)} %param.5) | copy-start | bytes 3145732
  0.7 56.9 %copy-start.2 = (f32[256]{0:T(256)S(1)}, f32[256]{0:T(256)}, u32[]{:S(2)}) copy-start(f32[256]{0:T(256)} %param.6) | copy-start | bytes 3076
  4.7 14.3 %all-to-all-start = ((f32[16,8,128]{2,1,0:T(8,128)}), f32[16,8,128]{2,1,0:T(8,128)S(1)}, u32[]{:S(2)}, u32[]{:S(2)}) async-start(f32[16,8,128]{2,1,0:T(8,128)} %bitcast.2), calls=%async_computation | async-start | bytes 131072 | tf_op jit(solution)/shard_map/all_to_all | solution.py:25
  12.1 48.1 %collective-permute-start = (bf16[8192,64]{0,1:T(8,128)(2,1)S(1)}, bf16[8192,64]{0,1:T(8,128)(2,1)S(1)}, u32[]{:S(2)}, u32[]{:S(2)}) collective-permute-start(bf16[8192,64]{0,1:T(8,128)(2,1)S(1)} %copy-done.1), channel_id=1, source_target_pairs={{16,0},{0,16},{17,1},{1,17},{18,2},{2,18},{19,3},{3,19},{20,4},{4,... | collective-permute-start | bytes 3145736 | tf_op jit(solution)/shard_map/ppermute | solution.py:15

commit v2 on v1

v2 whole, which is shorter than its diff:
```python
import jax
import jax.numpy as jnp
import numpy as np
from jax import lax
from jax.sharding import Mesh, PartitionSpec as P


def sent_to_all(block, axes):
    count = lax.axis_size(axes)
    copies = jnp.broadcast_to(block[None], (count,) + block.shape)
    return lax.all_to_all(copies, axes, 0, 0, tiled=True)


def per_device(eof_basis, snapshots, inverse_energy, eigen_vectors):
    tm, inner = lax.axis_size("tm"), lax.axis_size("inner")
    me = lax.axis_index("tm")
    hours, rank = snapshots.shape[1], eof_basis.shape[1]

    held = [snapshots]
    for k in range(1, tm):
        route = [((i + k) % tm, i) for i in range(tm)]
        held.append(lax.ppermute(snapshots, "tm", route))

    partial_sum = lax.dot_general(
        snapshots, eof_basis, (((0,), (0,)), ((), ())), preferred_element_type=jnp.float32
    )
    pieces = partial_sum.reshape(inner, hours // inner, rank)
    mine = jnp.sum(lax.all_to_all(pieces, "inner", 0, 0, tiled=True), axis=0)
    mine = jnp.sum(sent_to_all(mine, "outer"), axis=0)
    coeffs = sent_to_all(mine, ("tm", "inner")).reshape(tm * hours, rank)

    lagged = jnp.concatenate([jnp.zeros((1, rank), jnp.float32), coeffs[:-1]], axis=0)
    scaled = lagged * inverse_energy[None, :]
    reduced_operator = lax.dot_general(
        coeffs, scaled, (((0,), (0,)), ((), ())), precision=lax.Precision.HIGHEST
    )
    rows = eigen_vectors.shape[1] // tm
    vectors = lax.dynamic_slice_in_dim(eigen_vectors, me * rows, rows, 1)
    weights = jnp.dot(
        scaled, vectors.astype(jnp.float32), precision=lax.Precision.HIGHEST
    ).astype(jnp.bfloat16)
    rebuilt = 0.0
    for k in range(tm):
        part = lax.dynamic_slice_in_dim(weights, ((me + k) % tm) * hours, hours, 0)
        rebuilt = rebuilt + lax.dot_general(
            part, held[k], (((0,), (1,)), ((), ())), preferred_element_type=jnp.float32
        )
    return (reduced_operator, rebuilt.astype(jnp.bfloat16))


def solution(mesh):
    tm, space = mesh.shape["tm"], mesh.shape["space"]
    inner = 1
    while inner * inner < space and space % (2 * inner) == 0:
        inner *= 2
    split = Mesh(mesh.devices.reshape(tm, space // inner, inner), ("tm", "outer", "inner"))
    cells = ("outer", "inner")
    in_specs = (P(cells, None), P(cells, "tm"), P(), P())
    out_specs = (P(), P("tm", cells))
    return jax.shard_map(
        per_device, mesh=split, in_specs=in_specs, out_specs=out_specs, check_vma=False
    )
```

time: 63.7 us -> 50 us (0.78)
  blocking collectives: 38.5 us -> 8.16 us
  waiting for transfers between devices: 5.32 us -> 20.3 us
  local copies, waits for them, and re-layouts: 0.02 us -> 1.32 us
  starting transfers between devices: 8.94 us -> 9.73 us
    all_gather x1 -> x0, blocking collectives: 38.5 us -> none  [per_device(): every = lax.all_gather(mine, ('tm', 'space'), axis=0)]
    all_to_all x1 -> x2, waiting for transfers between devices: 5.32 us -> 20.3 us  [sent_to_all(): return lax.all_to_all(copies, axes, 0, 0, tiled=True)]
    all_to_all x0 -> x1, blocking collectives: none -> 8.16 us  [per_device(): mine = jnp.sum(lax.all_to_all(pieces, 'inner', 0, 0, tiled=True), axis=0)]
    broadcast_in_dim x0 -> x2, local copies, waits for them, and re-layouts: none -> 1.3 us  [sent_to_all(): copies = jnp.broadcast_to(block[None], (count,) + block.shape)]
    all_to_all x1 -> x2, starting transfers between devices: 7.38 us -> 8.24 us  [sent_to_all(): return lax.all_to_all(copies, axes, 0, 0, tiled=True)]
  transfers between devices with their start and end apart: 2 -> 3, of which waited for: 1 -> 2; matrix products, arithmetic and copies ran while one was open for 4% -> 7% of each run, Pallas kernels for 0% -> 0%
where the time goes in v2:
time: 50 us; the launch traced here: 49.6 us
  waiting for transfers between devices  20.3 us (41%)
  starting transfers between devices  9.73 us (19%)
  matrix products  9.36 us (19%)
  blocking collectives  8.16 us (16%)
  local copies, waits for them, and re-layouts  1.32 us (3%)
  between operations  0.72 us (1%)
    all_to_all x2, waiting for transfers between devices, sent_to_all(): return lax.all_to_all(copies, axes, 0, 0, tiled=True)  20.3 us
    all_to_all x2, starting transfers between devices, sent_to_all(): return lax.all_to_all(copies, axes, 0, 0, tiled=True)  8.24 us
    all_to_all x1, blocking collectives, per_device(): mine = jnp.sum(lax.all_to_all(pieces, 'inner', 0, 0, tiled=True), axis=0)  8.16 us
    dot_general x2, matrix products, per_device(): lax.dot_general(part, held[k], (((0,), (1,)), ((), ())), preferred_elemen...  4.6 us
    dot_general x1, matrix products, per_device(): lax.dot_general(snapshots, eof_basis, (((0,), (0,)), ((), ())), preferred...  3.41 us
    ppermute x1, starting transfers between devices, per_device(): held.append(lax.ppermute(snapshots, 'tm', route))  1.49 us
    broadcast_in_dim x2, local copies, waits for them, and re-layouts, sent_to_all(): copies = jnp.broadcast_to(block[None], (count,) + block.shape)  1.3 us
    dot_general x1, matrix products, per_device(): lax.dot_general(coeffs, scaled, (((0,), (0,)), ((), ())), precision=lax.P...  1.12 us
  transfers between devices with their start and end apart: 3, of which 2 were waited for; matrix products, arithmetic and copies ran while one was open for 7% of the time, Pallas kernels for 0%

profile of v2, /device:TPU:0, one launch (start us, length us, event | category | flops | bytes accessed | tf_op | source)
XLA Modules:
  0.0 49.6 jit_solution(15197074162604017554)
XLA Ops:
  0.6 0.0 copy-start
  0.6 0.0 copy-start.1
  0.7 0.0 copy-start.2
  0.7 3.4 %fusion.13 = f32[64,256]{1,0:T(8,128)S(1)} fusion(bf16[8192,64]{0,1:T(8,128)(2,1)} %param.5, bf16[8192,256]{1,0:T(8,128)(2,1)} %param.4), kind=kOutput, calls=%fused_computation.16 | convolution fusion | flops 268435456 | bytes 5308416 | tf_op jit(solution)/shard_map/dot_general | solution.py:24
  4.1 8.2 %all_to_all.15 = f32[4,16,256]{2,1,0:T(8,128)S(1)} all-to-all(f32[4,16,256]{2,1,0:T(8,128)S(1)} %bitcast.11), channel_id=1, replica_groups=mesh['tm'=2,'outer'=4,'inner'=4] {'inner'}, dimensions={0} | all-to-all | bytes 131072 | tf_op jit(solution)/shard_map/all_to_all | solution.py:28
  12.2 0.6 %broadcast_in_dim.4 = f32[4,16,256]{2,1,0:T(8,128)} broadcast(f32[16,256]{1,0:T(8,128)S(1)} %reduce_sum.18), dimensions={1,2} | broadcast | bytes 81920 | tf_op jit(solution)/shard_map/broadcast_in_dim | solution.py:10
  12.9 4.9 %all-to-all-start.1 = ((f32[4,16,256]{2,1,0:T(8,128)}), f32[4,16,256]{2,1,0:T(8,128)S(1)}, u32[]{:S(2)}, u32[]{:S(2)}) async-start(f32[4,16,256]{2,1,0:T(8,128)} %broadcast_in_dim.4), calls=%async_computation.1 | async-start | bytes 131072 | tf_op jit(solution)/shard_map/all_to_all | solution.py:11
  17.7 0.0 copy-done.1
  17.8 1.5 %collective-permute-start = (bf16[8192,64]{0,1:T(8,128)(2,1)S(1)}, bf16[8192,64]{0,1:T(8,128)(2,1)S(1)}, u32[]{:S(2)}, u32[]{:S(2)}) collective-permute-start(bf16[8192,64]{0,1:T(8,128)(2,1)S(1)} %copy-done.1), channel_id=1, source_target_pairs={{16,0},{0,16},{17,1},{1,17},{18,2},{2,18},{19,3},{3,19},{20,4},{4,... | collective-permute-start | bytes 3145736 | tf_op jit(solution)/shard_map/ppermute | solution.py:22
  19.2 4.2 %all-to-all-done.1 = f32[4,16,256]{2,1,0:T(8,128)S(1)} async-done(((f32[4,16,256]{2,1,0:T(8,128)}), f32[4,16,256]{2,1,0:T(8,128)S(1)}, u32[]{:S(2)}, u32[]{:S(2)}) %all-to-all-start.1) | async-done | bytes 65568 | tf_op jit(solution)/shard_map/all_to_all | solution.py:11
  23.5 0.7 %broadcast_in_dim.5 = f32[8,16,256]{2,1,0:T(8,128)} broadcast(f32[16,256]{1,0:T(8,128)S(1)} %reduce_sum.19), dimensions={1,2} | broadcast | bytes 147456 | tf_op jit(solution)/shard_map/broadcast_in_dim | solution.py:10
  24.2 3.4 %all-to-all-start.2 = ((f32[8,16,256]{2,1,0:T(8,128)}), f32[8,16,256]{2,1,0:T(8,128)S(1)}, u32[]{:S(2)}, u32[]{:S(2)}) async-start(f32[8,16,256]{2,1,0:T(8,128)} %broadcast_in_dim.5), calls=%async_computation.2 | async-start | bytes 262144 | tf_op jit(solution)/shard_map/all_to_all | solution.py:11
  27.6 16.0 %all-to-all-done.2 = f32[8,16,256]{2,1,0:T(8,128)S(1)} async-done(((f32[8,16,256]{2,1,0:T(8,128)}), f32[8,16,256]{2,1,0:T(8,128)S(1)}, u32[]{:S(2)}, u32[]{:S(2)}) %all-to-all-start.2) | async-done | bytes 131104 | tf_op jit(solution)/shard_map/all_to_all | solution.py:11
  43.6 0.0 copy-done
  43.6 0.0 copy-done.2
  43.6 0.2 convolution_convert_fusion
  43.8 1.1 %fusion.2 = f32[256,256]{1,0:T(8,128)} fusion(f32[128,256]{1,0:T(8,128)S(1)} %bitcast.9, f32[127,256]{1,0:T(8,128)S(1)} %bitcast.10, f32[256]{0:T(256)S(1)} %copy-done.2), kind=kOutput, calls=%fused_computation.5 | convolution fusion | flops 100696064 | bytes 524288 | tf_op jit(solution)/shard_map/dot_general | solution.py:34
  45.0 1.3 %fusion.6 = f32[256,8192]{1,0:T(8,128)S(1)} fusion(bf16[8192,64]{0,1:T(8,128)(2,1)S(1)} %copy-done.1, bf16[128,256]{1,0:T(8,128)(2,1)S(1)} %convolution_convert_fusion, s32[]{:T(128)S(6)} %select_n.22), kind=kOutput, calls=%fused_computation.9 | convolution fusion | flops 268435456 | bytes 9469956 | tf_op jit(solution)/shard_map/dot_general | solution.py:45
  46.2 0.0 collective-permute-done
  46.2 3.3 %fusion = bf16[256,8192]{1,0:T(8,128)(2,1)} fusion(f32[256,8192]{1,0:T(8,128)S(1)} %fusion.6, bf16[8192,64]{0,1:T(8,128)(2,1)S(1)} %collective-permute-done, bf16[128,256]{1,0:T(8,128)(2,1)S(1)} %convolution_convert_fusion, s32[]{:T(128)S(6)} %select_n.24), kind=kOutput, calls=%fused_computation.1 | convolution fusion | flops 272629760 | bytes 13664260 | tf_op jit(solution)/shard_map/dot_general | solution.py:45
  (2 shorter events, 0.0 us)
Async XLA Ops:
  0.6 43.0 %copy-start = (bf16[256,512]{1,0:T(8,128)(2,1)S(1)}, bf16[256,512]{1,0:T(8,128)(2,1)}, u32[]{:S(2)}) copy-start(bf16[256,512]{1,0:T(8,128)(2,1)} %param.7) | copy-start | bytes 786436
  0.6 17.1 %copy-start.1 = (bf16[8192,64]{0,1:T(8,128)(2,1)S(1)}, bf16[8192,64]{0,1:T(8,128)(2,1)}, u32[]{:S(2)}) copy-start(bf16[8192,64]{0,1:T(8,128)(2,1)} %param.5) | copy-start | bytes 3145732
  0.7 42.9 %copy-start.2 = (f32[256]{0:T(256)S(1)}, f32[256]{0:T(256)}, u32[]{:S(2)}) copy-start(f32[256]{0:T(256)} %param.6) | copy-start | bytes 3076
  12.9 10.6 %all-to-all-start.1 = ((f32[4,16,256]{2,1,0:T(8,128)}), f32[4,16,256]{2,1,0:T(8,128)S(1)}, u32[]{:S(2)}, u32[]{:S(2)}) async-start(f32[4,16,256]{2,1,0:T(8,128)} %broadcast_in_dim.4), calls=%async_computation.1 | async-start | bytes 131072 | tf_op jit(solution)/shard_map/all_to_all | solution.py:11
  17.8 28.5 %collective-permute-start = (bf16[8192,64]{0,1:T(8,128)(2,1)S(1)}, bf16[8192,64]{0,1:T(8,128)(2,1)S(1)}, u32[]{:S(2)}, u32[]{:S(2)}) collective-permute-start(bf16[8192,64]{0,1:T(8,128)(2,1)S(1)} %copy-done.1), channel_id=1, source_target_pairs={{16,0},{0,16},{17,1},{1,17},{18,2},{2,18},{19,3},{3,19},{20,4},{4,... | collective-permute-start | bytes 3145736 | tf_op jit(solution)/shard_map/ppermute | solution.py:22
  24.2 19.4 %all-to-all-start.2 = ((f32[8,16,256]{2,1,0:T(8,128)}), f32[8,16,256]{2,1,0:T(8,128)S(1)}, u32[]{:S(2)}, u32[]{:S(2)}) async-start(f32[8,16,256]{2,1,0:T(8,128)} %broadcast_in_dim.5), calls=%async_computation.2 | async-start | bytes 262144 | tf_op jit(solution)/shard_map/all_to_all | solution.py:11

commit v3 on v2

--- a/solution.py
+++ b/solution.py
@@ -3,12 +3,6 @@
 import numpy as np
 from jax import lax
 from jax.sharding import Mesh, PartitionSpec as P
-
-
-def sent_to_all(block, axes):
-    count = lax.axis_size(axes)
-    copies = jnp.broadcast_to(block[None], (count,) + block.shape)
-    return lax.all_to_all(copies, axes, 0, 0, tiled=True)
 
 
 def per_device(eof_basis, snapshots, inverse_energy, eigen_vectors):
@@ -26,8 +20,8 @@
     )
     pieces = partial_sum.reshape(inner, hours // inner, rank)
     mine = jnp.sum(lax.all_to_all(pieces, "inner", 0, 0, tiled=True), axis=0)
-    mine = jnp.sum(sent_to_all(mine, "outer"), axis=0)
-    coeffs = sent_to_all(mine, ("tm", "inner")).reshape(tm * hours, rank)
+    mine = jnp.sum(lax.all_gather(mine, "outer", axis=0), axis=0)
+    coeffs = lax.all_gather(mine, ("tm", "inner"), axis=0).reshape(tm * hours, rank)
 
     lagged = jnp.concatenate([jnp.zeros((1, rank), jnp.float32), coeffs[:-1]], axis=0)
     scaled = lagged * inverse_energy[None, :]

time: 50 us -> 43 us (0.86)
  waiting for transfers between devices: 20.3 us -> 4.06 us
  blocking collectives: 8.16 us -> 21.7 us
  starting transfers between devices: 9.73 us -> 6.29 us
  local copies, waits for them, and re-layouts: 1.32 us -> 0.02 us
  matrix products: 9.36 us -> 9.91 us
    all_gather x0 -> x2, blocking collectives: none -> 21.7 us  [the longest x1 13.4 us: per_device(): mine = jnp.sum(lax.all_gather(mine, 'outer', axis=0), axis=0)]
    all_to_all x2 -> x1, waiting for transfers between devices: 20.3 us -> 4.06 us  [per_device(): mine = jnp.sum(lax.all_to_all(pieces, 'inner', 0, 0, tiled=True), axis=0)]
    all_to_all x1 -> x0, blocking collectives: 8.16 us -> none  [per_device(): mine = jnp.sum(lax.all_to_all(pieces, 'inner', 0, 0, tiled=True), axis=0)]
    all_to_all x2 -> x1, starting transfers between devices: 8.24 us -> 3.28 us  [per_device(): mine = jnp.sum(lax.all_to_all(pieces, 'inner', 0, 0, tiled=True), axis=0)]
    ppermute x1, starting transfers between devices: 1.49 us -> 3 us  [per_device(): held.append(lax.ppermute(snapshots, 'tm', route))]
    broadcast_in_dim x2 -> x0, local copies, waits for them, and re-layouts: 1.3 us -> none  [sent_to_all(): copies = jnp.broadcast_to(block[None], (count,) + block.shape)]
    dot_general x1, matrix products: 3.41 us -> 3.94 us  [per_device(): lax.dot_general(snapshots, eof_basis, (((0,), (0,)), ((), ())), preferred...]
  transfers between devices with their start and end apart: 3 -> 2, of which waited for: 2 -> 1; matrix products, arithmetic and copies ran while one was open for 7% -> 15% of each run, Pallas kernels for 0% -> 0%
where the time goes in v3:
time: 43 us; the launch traced here: 42.7 us
  blocking collectives  21.7 us (50%)
  matrix products  9.91 us (23%)
  starting transfers between devices  6.29 us (15%)
  waiting for transfers between devices  4.06 us (9%)
  between operations  0.72 us (2%)
    all_gather x1, blocking collectives, per_device(): mine = jnp.sum(lax.all_gather(mine, 'outer', axis=0), axis=0)  13.4 us
    all_gather x1, blocking collectives, per_device(): lax.all_gather(mine, ('tm', 'inner'), axis=0).reshape(tm * hours, rank)  8.24 us
    dot_general x2, matrix products, per_device(): lax.dot_general(part, held[k], (((0,), (1,)), ((), ())), preferred_elemen...  4.61 us
    all_to_all x1, waiting for transfers between devices, per_device(): mine = jnp.sum(lax.all_to_all(pieces, 'inner', 0, 0, tiled=True), axis=0)  4.06 us
    dot_general x1, matrix products, per_device(): lax.dot_general(snapshots, eof_basis, (((0,), (0,)), ((), ())), preferred...  3.94 us
    all_to_all x1, starting transfers between devices, per_device(): mine = jnp.sum(lax.all_to_all(pieces, 'inner', 0, 0, tiled=True), axis=0)  3.28 us
    ppermute x1, starting transfers between devices, per_device(): held.append(lax.ppermute(snapshots, 'tm', route))  3 us
    dot_general x1, matrix products, per_device(): lax.dot_general(coeffs, scaled, (((0,), (0,)), ((), ())), precision=lax.P...  1.12 us
  transfers between devices with their start and end apart: 2, of which 1 were waited for; matrix products, arithmetic and copies ran while one was open for 15% of the time, Pallas kernels for 0%

profile of v3, /device:TPU:0, one launch (start us, length us, event | category | flops | bytes accessed | tf_op | source)
XLA Modules:
  0.0 42.7 jit_solution(4486773951350650558)
XLA Ops:
  0.6 0.0 copy-start
  0.6 0.0 copy-start.1
  0.7 0.0 copy-start.2
  0.7 3.0 %collective-permute-start = (bf16[8192,64]{0,1:T(8,128)(2,1)}, bf16[8192,64]{0,1:T(8,128)(2,1)S(1)}, u32[]{:S(2)}, u32[]{:S(2)}) collective-permute-start(bf16[8192,64]{0,1:T(8,128)(2,1)} %param.5), channel_id=1, source_target_pairs={{16,0},{0,16},{17,1},{1,17},{18,2},{2,18},{19,3},{3,19},{20,4},{4,... | collective-permute-start | bytes 3145736 | tf_op jit(solution)/shard_map/ppermute | solution.py:16
  3.7 3.9 %fusion.13 = f32[64,256]{1,0:T(8,128)} fusion(bf16[8192,64]{0,1:T(8,128)(2,1)} %param.5, bf16[8192,256]{1,0:T(8,128)(2,1)} %param.4), kind=kOutput, calls=%fused_computation.16 | convolution fusion | flops 268435456 | bytes 5308416 | tf_op jit(solution)/shard_map/dot_general | solution.py:18
  7.6 3.3 %all-to-all-start = ((f32[4,16,256]{2,1,0:T(8,128)}), f32[4,16,256]{2,1,0:T(8,128)S(1)}, u32[]{:S(2)}, u32[]{:S(2)}) async-start(f32[4,16,256]{2,1,0:T(8,128)} %bitcast), calls=%async_computation | async-start | bytes 131072 | tf_op jit(solution)/shard_map/all_to_all | solution.py:22
  10.9 4.1 %all-to-all-done = f32[4,16,256]{2,1,0:T(8,128)S(1)} async-done(((f32[4,16,256]{2,1,0:T(8,128)}), f32[4,16,256]{2,1,0:T(8,128)S(1)}, u32[]{:S(2)}, u32[]{:S(2)}) %all-to-all-start) | async-done | bytes 65568 | tf_op jit(solution)/shard_map/all_to_all | solution.py:22
  15.0 13.4 %all-gather = f32[64,256]{1,0:T(8,128)S(1)} all-gather(f32[16,256]{1,0:T(8,128)S(1)} %reduce_sum.18), channel_id=2, replica_groups=mesh['tm'=2,'outer'=4,'inner'=4] {'outer'}, dimensions={0}, use_global_device_ids=true | all-gather | bytes 81920 | tf_op jit(solution)/shard_map/all_gather | solution.py:23
  28.4 8.2 %all-gather.1 = f32[128,256]{1,0:T(8,128)S(1)} all-gather(f32[16,256]{1,0:T(8,128)S(1)} %reduce_sum.19), channel_id=3, replica_groups=mesh['tm'=2,'outer'=4,'inner'=4] {'tm','inner'}, dimensions={0}, use_global_device_ids=true | all-gather | bytes 147456 | tf_op jit(solution)/shard_map/all_gather | solution.py:24
  36.7 0.0 copy-done
  36.7 0.0 copy-done.2
  36.7 0.2 convolution_convert_fusion
  36.9 1.1 %fusion.2 = f32[256,256]{1,0:T(8,128)} fusion(f32[128,256]{1,0:T(8,128)S(1)} %all-gather.1, f32[127,256]{1,0:T(8,128)S(1)} %bitcast.9, f32[256]{0:T(256)S(1)} %copy-done.2), kind=kOutput, calls=%fused_computation.5 | convolution fusion | flops 100696064 | bytes 524288 | tf_op jit(solution)/shard_map/dot_general | solution.py:28
  38.0 0.0 copy-done.1
  38.0 1.3 %fusion.6 = f32[256,8192]{1,0:T(8,128)S(1)} fusion(bf16[8192,64]{0,1:T(8,128)(2,1)S(1)} %copy-done.1, bf16[128,256]{1,0:T(8,128)(2,1)S(1)} %convolution_convert_fusion, s32[]{:T(128)S(6)} %select_n.22), kind=kOutput, calls=%fused_computation.9 | convolution fusion | flops 268435456 | bytes 9469956 | tf_op jit(solution)/shard_map/dot_general | solution.py:39
  39.3 0.0 collective-permute-done
  39.3 3.3 %fusion = bf16[256,8192]{1,0:T(8,128)(2,1)} fusion(f32[256,8192]{1,0:T(8,128)S(1)} %fusion.6, bf16[8192,64]{0,1:T(8,128)(2,1)S(1)} %collective-permute-done, bf16[128,256]{1,0:T(8,128)(2,1)S(1)} %convolution_convert_fusion, s32[]{:T(128)S(6)} %select_n.24), kind=kOutput, calls=%fused_computation.1 | convolution fusion | flops 272629760 | bytes 13664260 | tf_op jit(solution)/shard_map/dot_general | solution.py:39
  (2 shorter events, 0.0 us)
Async XLA Ops:
  0.6 36.0 %copy-start = (bf16[256,512]{1,0:T(8,128)(2,1)S(1)}, bf16[256,512]{1,0:T(8,128)(2,1)}, u32[]{:S(2)}) copy-start(bf16[256,512]{1,0:T(8,128)(2,1)} %param.7) | copy-start | bytes 786436
  0.6 37.4 %copy-start.1 = (bf16[8192,64]{0,1:T(8,128)(2,1)S(1)}, bf16[8192,64]{0,1:T(8,128)(2,1)}, u32[]{:S(2)}) copy-start(bf16[8192,64]{0,1:T(8,128)(2,1)} %param.5) | copy-start | bytes 3145732
  0.7 36.0 %copy-start.2 = (f32[256]{0:T(256)S(1)}, f32[256]{0:T(256)}, u32[]{:S(2)}) copy-start(f32[256]{0:T(256)} %param.6) | copy-start | bytes 3076
  0.7 38.7 %collective-permute-start = (bf16[8192,64]{0,1:T(8,128)(2,1)}, bf16[8192,64]{0,1:T(8,128)(2,1)S(1)}, u32[]{:S(2)}, u32[]{:S(2)}) collective-permute-start(bf16[8192,64]{0,1:T(8,128)(2,1)} %param.5), channel_id=1, source_target_pairs={{16,0},{0,16},{17,1},{1,17},{18,2},{2,18},{19,3},{3,19},{20,4},{4,... | collective-permute-start | bytes 3145736 | tf_op jit(solution)/shard_map/ppermute | solution.py:16
  7.6 7.4 %all-to-all-start = ((f32[4,16,256]{2,1,0:T(8,128)}), f32[4,16,256]{2,1,0:T(8,128)S(1)}, u32[]{:S(2)}, u32[]{:S(2)}) async-start(f32[4,16,256]{2,1,0:T(8,128)} %bitcast), calls=%async_computation | async-start | bytes 131072 | tf_op jit(solution)/shard_map/all_to_all | solution.py:22

commit v4 on v3

v4 whole, which is shorter than its diff:
```python
import functools

import jax
import jax.numpy as jnp
from jax import lax
from jax.experimental import pallas as pl
from jax.experimental.pallas import tpu as pltpu
from jax.sharding import Mesh, PartitionSpec as P

ROWS = (((1,), (0,)), ((), ()))
FIRST = (((0,), (0,)), ((), ()))
LAST = (((1,), (1,)), ((), ()))
FREE = pl.CostEstimate(flops=0, bytes_accessed=0, transcendentals=0)


def in_parts(value):
    high = value.astype(jnp.bfloat16)
    return high, (value - high.astype(jnp.float32)).astype(jnp.bfloat16)


def product(left, right, dims):
    return lax.dot_general(left, right, dims, preferred_element_type=jnp.float32)


def project_kernel(tiles, snapshots, basis, out, fields, patterns, arrived):
    cells = snapshots.shape[1]
    tile = cells // tiles
    copies = []
    for i in range(tiles):
        span = pl.ds(i * tile, tile)
        copies.append(
            (
                pltpu.make_async_copy(snapshots.at[:, span], fields.at[:, span], arrived.at[0, i]),
                pltpu.make_async_copy(basis.at[span], patterns.at[span], arrived.at[1, i]),
            )
        )
    for pair in copies:
        for copy in pair:
            copy.start()
    total = jnp.zeros(out.shape, jnp.float32)
    for i, pair in enumerate(copies):
        for copy in pair:
            copy.wait()
        span = pl.ds(i * tile, tile)
        total += product(fields[:, span], patterns[span], ROWS)
    out[...] = total


def project(snapshots, basis, tiles):
    hours = snapshots.shape[0]
    rank = basis.shape[1]
    return pl.pallas_call(
        functools.partial(project_kernel, tiles),
        out_shape=jax.ShapeDtypeStruct((hours, rank), jnp.float32),
        in_specs=[pl.BlockSpec(memory_space=pl.ANY)] * 2,
        out_specs=pl.BlockSpec(memory_space=pltpu.VMEM),
        scratch_shapes=[
            pltpu.VMEM(snapshots.shape, snapshots.dtype),
            pltpu.VMEM(basis.shape, basis.dtype),
            pltpu.SemaphoreType.DMA((2, tiles)),
        ],
        compiler_params=pltpu.CompilerParams(vmem_limit_bytes=59 * 2**20),
        cost_estimate=FREE,
        name="project",
    )(snapshots, basis)


def rebuild_kernel(tiles, me, energy, coeffs, vectors, *refs):
    count = len(refs) - 9
    held, refs = refs[:count], refs[count:]
    operator, modes, fields, known, turned, scaled, made, arrived, sent = refs
    hours, cells = held[0].shape
    tile = cells // tiles
    inputs = [
        pltpu.make_async_copy(coeffs, known, arrived.at[count]),
        pltpu.make_async_copy(vectors, turned, arrived.at[count + 1]),
    ]
    blocks = [
        pltpu.make_async_copy(block, fields.at[pl.ds(k * hours, hours)], arrived.at[k])
        for k, block in enumerate(held)
    ]
    for copy in inputs + blocks:
        copy.start()
    for copy in inputs:
        copy.wait()
    every = known[...]
    hour = lax.broadcasted_iota(jnp.int32, every.shape, 0)
    scaled[...] = jnp.where(hour == 0, 0.0, pltpu.roll(every, 1, 0)) * energy[...]
    first = [pl.multiple_of(lax.rem(me[0] + k, count) * hours, hours) for k in range(count)]
    ordered = jnp.concatenate([scaled[pl.ds(at, hours)] for at in first], axis=0)
    high, low = in_parts(ordered)
    weights = (product(turned[...], high, LAST) + product(turned[...], low, LAST)).astype(
        jnp.bfloat16
    )
    for copy in blocks:
        copy.wait()
    outgoing = []
    for i in range(tiles):
        span = pl.ds(i * tile, tile)
        made[:, span] = product(weights, fields[:, span], ROWS).astype(made.dtype)
        copy = pltpu.make_async_copy(made.at[:, span], modes.at[:, span], sent.at[i])
        copy.start()
        outgoing.append(copy)
    high, low = in_parts(every)
    s_high, s_low = in_parts(scaled[...])
    operator[...] = (
        product(high, s_high, FIRST) + product(high, s_low, FIRST) + product(low, s_high, FIRST)
    )
    for copy in outgoing:
        copy.wait()


def rebuild(me, energy, coeffs, vectors, held, tiles):
    cells = held[0].shape[1]
    total, rank = coeffs.shape
    modes = vectors.shape[0]
    anywhere = pl.BlockSpec(memory_space=pl.ANY)
    return pl.pallas_call(
        functools.partial(rebuild_kernel, tiles),
        out_shape=(
            jax.ShapeDtypeStruct((rank, rank), jnp.float32),
            jax.ShapeDtypeStruct((modes, cells), jnp.bfloat16),
        ),
        in_specs=[
            pl.BlockSpec(memory_space=pltpu.SMEM),
            pl.BlockSpec(memory_space=pltpu.VMEM),
        ]
        + [anywhere] * (2 + len(held)),
        out_specs=(pl.BlockSpec(memory_space=pltpu.VMEM), anywhere),
        scratch_shapes=[
            pltpu.VMEM((total, cells), held[0].dtype),
            pltpu.VMEM(coeffs.shape, coeffs.dtype),
            pltpu.VMEM(vectors.shape, vectors.dtype),
            pltpu.VMEM(coeffs.shape, jnp.float32),
            pltpu.VMEM((modes, cells), jnp.bfloat16),
            pltpu.SemaphoreType.DMA((len(held) + 2,)),
            pltpu.SemaphoreType.DMA((tiles,)),
        ],
        compiler_params=pltpu.CompilerParams(vmem_limit_bytes=40 * 2**20),
        cost_estimate=FREE,
        name="rebuild",
    )(me[None], energy[None, :], coeffs, vectors, *held)


def swapped(value, axis, bit):
    route = [(i ^ bit, i) for i in range(lax.axis_size(axis))]
    return lax.ppermute(value, axis, route)


def per_device(eof_basis, snapshots, inverse_energy, eigen_vectors):
    tm, outer, inner = (lax.axis_size(a) for a in ("tm", "outer", "inner"))
    me = lax.axis_index("tm")
    fields = snapshots.T
    hours, rank = fields.shape[0], eof_basis.shape[1]

    held = [fields]
    for k in range(1, tm):
        route = [((i + k) % tm, i) for i in range(tm)]
        held.append(lax.ppermute(fields, "tm", route))

    pieces = project(fields, eof_basis, 8).reshape(inner, hours // inner, rank)
    mine = jnp.sum(lax.all_to_all(pieces, "inner", 0, 0, tiled=True), axis=0)
    bit = 1
    while bit < outer:
        mine = mine + swapped(mine, "outer", bit)
        bit *= 2
    coeffs = lax.all_gather(mine, ("tm", "inner"), axis=0).reshape(tm * hours, rank)

    rows = eigen_vectors.shape[1] // tm
    vectors = lax.dynamic_slice_in_dim(eigen_vectors, me * rows, rows, 1)
    return rebuild(me, inverse_energy, coeffs, vectors.T, held, 8)


def solution(mesh):
    tm, space = mesh.shape["tm"], mesh.shape["space"]
    inner = 1
    while inner * inner < space and space % (2 * inner) == 0:
        inner *= 2
    split = Mesh(mesh.devices.reshape(tm, space // inner, inner), ("tm", "outer", "inner"))
    cells = ("outer", "inner")
    in_specs = (P(cells, None), P(cells, "tm"), P(), P())
    out_specs = (P(), P("tm", cells))
    return jax.shard_map(
        per_device, mesh=split, in_specs=in_specs, out_specs=out_specs, check_vma=False
    )
```

time: 43 us -> 35.9 us (0.83)
  matrix products: 9.91 us -> 0 us
  Pallas kernels: 0 us -> 7.52 us
  blocking collectives: 21.7 us -> 16 us
  starting transfers between devices: 6.29 us -> 7.24 us
    all_gather x1 -> x0, blocking collectives: 13.4 us -> none  [per_device(): mine = jnp.sum(lax.all_gather(mine, 'outer', axis=0), axis=0)]
    dot_general x5 -> x0, matrix products: 9.91 us -> none  [the longest x2 4.61 us: per_device(): lax.dot_general(part, held[k], (((0,), (1,)), ((), ())), preferred_elemen...]
    pallas_call x0 -> x2, Pallas kernels: none -> 7.52 us  [the longest x1 3.93 us: rebuild(): pl.pallas_call(functools.partial(rebuild_kernel, tiles), out_shape=(jax.S...]
    all_to_all x0 -> x1, blocking collectives: none -> 7.38 us  [per_device(): mine = jnp.sum(lax.all_to_all(pieces, 'inner', 0, 0, tiled=True), axis=0)]
    ppermute x1 -> x3, starting transfers between devices: 3 us -> 7.24 us  [the longest x2 4.23 us: swapped(): return lax.ppermute(value, axis, route)]
    ppermute x1 -> x3, waiting for transfers between devices: 0.01 us -> 4.09 us  [the longest x2 4.09 us: swapped(): return lax.ppermute(value, axis, route)]
    all_to_all x1 -> x0, waiting for transfers between devices: 4.06 us -> none  [per_device(): mine = jnp.sum(lax.all_to_all(pieces, 'inner', 0, 0, tiled=True), axis=0)]
    all_to_all x1 -> x0, starting transfers between devices: 3.28 us -> none  [per_device(): mine = jnp.sum(lax.all_to_all(pieces, 'inner', 0, 0, tiled=True), axis=0)]
  transfers between devices with their start and end apart: 2 -> 3, of which waited for: 1 -> 2; matrix products, arithmetic and copies ran while one was open for 15% -> 0% of each run, Pallas kernels for 0% -> 10%
where the time goes in v4:
time: 35.9 us; the launch traced here: 35.6 us
  blocking collectives  16 us (45%)
  Pallas kernels  7.52 us (21%)
  starting transfers between devices  7.24 us (20%)
  waiting for transfers between devices  4.09 us (11%)
  between operations  0.68 us (2%)
    all_gather x1, blocking collectives, per_device(): lax.all_gather(mine, ('tm', 'inner'), axis=0).reshape(tm * hours, rank)  8.57 us
    all_to_all x1, blocking collectives, per_device(): mine = jnp.sum(lax.all_to_all(pieces, 'inner', 0, 0, tiled=True), axis=0)  7.38 us
    ppermute x2, starting transfers between devices, swapped(): return lax.ppermute(value, axis, route)  4.23 us
    ppermute x2, waiting for transfers between devices, swapped(): return lax.ppermute(value, axis, route)  4.09 us
    pallas_call x1, Pallas kernels, rebuild(): pl.pallas_call(functools.partial(rebuild_kernel, tiles), out_shape=(jax.S...  3.93 us
    pallas_call x1, Pallas kernels, project(): pl.pallas_call(functools.partial(project_kernel, tiles), out_shape=jax.Sh...  3.59 us
    ppermute x1, starting transfers between devices, per_device(): held.append(lax.ppermute(fields, 'tm', route))  3 us
  transfers between devices with their start and end apart: 3, of which 2 were waited for; matrix products, arithmetic and copies ran while one was open for 0% of the time, Pallas kernels for 10%

profile of v4, /device:TPU:0, one launch (start us, length us, event | category | flops | bytes accessed | tf_op | source)
XLA Modules:
  0.0 35.6 jit_solution(10679567300411873584)
XLA Ops:
  0.6 0.0 copy-start
  0.6 0.0 copy-start.1
  0.7 0.0 copy-start.2
  0.7 3.0 %collective-permute-start.2 = (bf16[64,8192]{1,0:T(8,128)(2,1)}, bf16[64,8192]{1,0:T(8,128)(2,1)S(1)}, u32[]{:S(2)}, u32[]{:S(2)}) collective-permute-start(bf16[64,8192]{1,0:T(8,128)(2,1)} %bitcast.5), channel_id=1, source_target_pairs={{16,0},{0,16},{17,1},{1,17},{18,2},{2,18},{19,3},{3,19},{20,4},{4,... | collective-permute-start | bytes 3145736 | tf_op jit(solution)/shard_map/ppermute | solution.py:159
  3.7 3.6 %project.1 = f32[64,256]{1,0:T(8,128)} custom-call(bf16[64,8192]{1,0:T(8,128)(2,1)} %bitcast.6, bf16[8192,256]{1,0:T(8,128)(2,1)} %basis.1), custom_call_target="tpu_custom_call" | custom-call | tf_op jit(solution)/shard_map/project/pallas_call | solution.py:52
  7.3 7.4 %all_to_all.5 = f32[4,16,256]{2,1,0:T(8,128)S(1)} all-to-all(f32[4,16,256]{2,1,0:T(8,128)} %bitcast.10), channel_id=1, replica_groups=mesh['tm'=2,'outer'=4,'inner'=4] {'inner'}, dimensions={0} | all-to-all | bytes 131072 | tf_op jit(solution)/shard_map/all_to_all | solution.py:162
  14.7 1.6 %collective-permute-start = (f32[16,256]{1,0:T(8,128)S(1)}, f32[16,256]{1,0:T(8,128)S(1)}, u32[]{:S(2)}, u32[]{:S(2)}) collective-permute-start(f32[16,256]{1,0:T(8,128)S(1)} %reduce_sum.9), channel_id=1, source_target_pairs={{4,0},{0,4},{12,8},{8,12},{5,1},{1,5},{13,9},{9,13},{6,2},{2,6},{1... | collective-permute-start | bytes 49160 | tf_op jit(solution)/shard_map/ppermute | solution.py:147
  16.3 2.2 %collective-permute-done = f32[16,256]{1,0:T(8,128)S(1)} collective-permute-done((f32[16,256]{1,0:T(8,128)S(1)}, f32[16,256]{1,0:T(8,128)S(1)}, u32[]{:S(2)}, u32[]{:S(2)}) %collective-permute-start) | collective-permute-done | bytes 16416 | tf_op jit(solution)/shard_map/ppermute | solution.py:147
  18.5 2.6 %collective-permute-start.1 = (f32[16,256]{1,0:T(8,128)S(1)}, f32[16,256]{1,0:T(8,128)S(1)}, u32[]{:S(2)}, u32[]{:S(2)}) collective-permute-start(f32[16,256]{1,0:T(8,128)S(1)} %add.9), channel_id=1, source_target_pairs={{8,0},{12,4},{0,8},{4,12},{9,1},{13,5},{1,9},{5,13},{10,2},{14,6},... | collective-permute-start | bytes 49160 | tf_op jit(solution)/shard_map/ppermute | solution.py:147
  21.1 0.0 copy-done
  21.1 0.1 copy.7
  21.2 1.9 %collective-permute-done.1 = f32[16,256]{1,0:T(8,128)S(1)} collective-permute-done((f32[16,256]{1,0:T(8,128)S(1)}, f32[16,256]{1,0:T(8,128)S(1)}, u32[]{:S(2)}, u32[]{:S(2)}) %collective-permute-start.1) | collective-permute-done | bytes 16416 | tf_op jit(solution)/shard_map/ppermute | solution.py:147
  23.1 8.6 %all-gather.coeffs = f32[128,256]{1,0:T(8,128)S(1)} all-gather(f32[16,256]{1,0:T(8,128)S(1)} %add.10), channel_id=2, replica_groups=mesh['tm'=2,'outer'=4,'inner'=4] {'tm','inner'}, dimensions={0}, use_global_device_ids=true | all-gather | bytes 147456 | tf_op jit(solution)/shard_map/all_gather | solution.py:167
  31.7 0.0 collective-permute-done.2.refs_1_
  31.7 0.0 copy-done.1
  31.7 0.0 copy-done.2
  31.7 3.9 %rebuild.1 = (f32[256,256]{1,0:T(8,128)}, bf16[256,8192]{1,0:T(8,128)(2,1)}) custom-call(s32[1]{0:T(128)} %bitcast.me, f32[1,256]{1,0:T(1,128)S(1)} %bitcast.9, f32[128,256]{1,0:T(8,128)S(1)} %all-gather.coeffs, bf16[256,256]{1,0:T(8,128)(2,1)S(1)} %bitcast.8, bf16[64,8192]{1,0:T(8,128)(2,1)S(1)} %bitcast.7, bf16[64,8192]{1,0:T(8,128)(2,1)S(1)} %collective-permute-done.2.refs_1_), custom_call_target="tpu_custom_call" | custom-call | tf_op jit(solution)/shard_map/rebuild/pallas_call | solution.py:118
  (4 shorter events, 0.0 us)
Async XLA Ops:
  0.6 20.4 %copy-start = (bf16[256,512]{1,0:T(8,128)(2,1)S(1)}, bf16[256,512]{1,0:T(8,128)(2,1)}, u32[]{:S(2)}) copy-start(bf16[256,512]{1,0:T(8,128)(2,1)} %param.7) | copy-start | bytes 786436
  0.6 31.0 %copy-start.1 = (bf16[8192,64]{0,1:T(8,128)(2,1)S(1)}, bf16[8192,64]{0,1:T(8,128)(2,1)}, u32[]{:S(2)}) copy-start(bf16[8192,64]{0,1:T(8,128)(2,1)} %param.5) | copy-start | bytes 3145732
  0.7 31.0 %copy-start.2 = (f32[256]{0:T(256)S(1)}, f32[256]{0:T(256)}, u32[]{:S(2)}) copy-start(f32[256]{0:T(256)} %param.6) | copy-start | bytes 3076
  0.7 31.0 %collective-permute-start.2 = (bf16[64,8192]{1,0:T(8,128)(2,1)}, bf16[64,8192]{1,0:T(8,128)(2,1)S(1)}, u32[]{:S(2)}, u32[]{:S(2)}) collective-permute-start(bf16[64,8192]{1,0:T(8,128)(2,1)} %bitcast.5), channel_id=1, source_target_pairs={{16,0},{0,16},{17,1},{1,17},{18,2},{2,18},{19,3},{3,19},{20,4},{4,... | collective-permute-start | bytes 3145736 | tf_op jit(solution)/shard_map/ppermute | solution.py:159
  14.7 3.8 %collective-permute-start = (f32[16,256]{1,0:T(8,128)S(1)}, f32[16,256]{1,0:T(8,128)S(1)}, u32[]{:S(2)}, u32[]{:S(2)}) collective-permute-start(f32[16,256]{1,0:T(8,128)S(1)} %reduce_sum.9), channel_id=1, source_target_pairs={{4,0},{0,4},{12,8},{8,12},{5,1},{1,5},{13,9},{9,13},{6,2},{2,6},{1... | collective-permute-start | bytes 49160 | tf_op jit(solution)/shard_map/ppermute | solution.py:147
  18.5 4.6 %collective-permute-start.1 = (f32[16,256]{1,0:T(8,128)S(1)}, f32[16,256]{1,0:T(8,128)S(1)}, u32[]{:S(2)}, u32[]{:S(2)}) collective-permute-start(f32[16,256]{1,0:T(8,128)S(1)} %add.9), channel_id=1, source_target_pairs={{8,0},{12,4},{0,8},{4,12},{9,1},{13,5},{1,9},{5,13},{10,2},{14,6},... | collective-permute-start | bytes 49160 | tf_op jit(solution)/shard_map/ppermute | solution.py:147

commit v5 on v4

--- a/solution.py
+++ b/solution.py
@@ -10,6 +10,7 @@
 ROWS = (((1,), (0,)), ((), ()))
 FIRST = (((0,), (0,)), ((), ()))
 LAST = (((1,), (1,)), ((), ()))
+AHEAD = 4
 FREE = pl.CostEstimate(flops=0, bytes_accessed=0, transcendentals=0)
 
 
@@ -34,13 +35,16 @@
                 pltpu.make_async_copy(basis.at[span], patterns.at[span], arrived.at[1, i]),
             )
         )
-    for pair in copies:
+    for pair in copies[:AHEAD]:
         for copy in pair:
             copy.start()
     total = jnp.zeros(out.shape, jnp.float32)
     for i, pair in enumerate(copies):
         for copy in pair:
             copy.wait()
+        for pair in copies[i + AHEAD : i + AHEAD + 1]:
+            for copy in pair:
+                copy.start()
         span = pl.ds(i * tile, tile)
         total += product(fields[:, span], patterns[span], ROWS)
     out[...] = total
@@ -158,12 +162,12 @@
         route = [((i + k) % tm, i) for i in range(tm)]
         held.append(lax.ppermute(fields, "tm", route))
 
-    pieces = project(fields, eof_basis, 8).reshape(inner, hours // inner, rank)
-    mine = jnp.sum(lax.all_to_all(pieces, "inner", 0, 0, tiled=True), axis=0)
-    bit = 1
-    while bit < outer:
-        mine = mine + swapped(mine, "outer", bit)
-        bit *= 2
+    halves = project(fields, eof_basis, 8).reshape(inner, hours // inner, rank)
+    core = lax.axis_index("inner")
+    given = lax.dynamic_index_in_dim(halves, 1 - core, 0, keepdims=False)
+    kept = lax.dynamic_index_in_dim(halves, core, 0, keepdims=False)
+    mine = kept + swapped(given, "inner", 1)
+    mine = lax.psum(mine, "outer")
     coeffs = lax.all_gather(mine, ("tm", "inner"), axis=0).reshape(tm * hours, rank)
 
     rows = eigen_vectors.shape[1] // tm
@@ -173,9 +177,7 @@
 
 def solution(mesh):
     tm, space = mesh.shape["tm"], mesh.shape["space"]
-    inner = 1
-    while inner * inner < space and space % (2 * inner) == 0:
-        inner *= 2
+    inner = 2
     split = Mesh(mesh.devices.reshape(tm, space // inner, inner), ("tm", "outer", "inner"))
     cells = ("outer", "inner")
     in_specs = (P(cells, None), P(cells, "tm"), P(), P())

time: 35.9 us -> 57.5 us (1.60)
  blocking collectives: 16 us -> 42.8 us
  starting transfers between devices: 7.24 us -> 3.01 us
  waiting for transfers between devices: 4.09 us -> 1.08 us
  local copies, waits for them, and re-layouts: 0.13 us -> 0.89 us
  other arithmetic: 0.02 us -> 0.76 us
    psum x0 -> x1, blocking collectives: none -> 37.4 us  [per_device(): mine = lax.psum(mine, 'outer')]
    all_to_all x1 -> x0, blocking collectives: 7.38 us -> none  [per_device(): mine = jnp.sum(lax.all_to_all(pieces, 'inner', 0, 0, tiled=True), axis=0)]
    ppermute x2 -> x1, starting transfers between devices: 4.23 us -> 0.01 us  [swapped(): return lax.ppermute(value, axis, route)]
    all_gather x1, blocking collectives: 8.57 us -> 5.41 us  [per_device(): lax.all_gather(mine, ('tm', 'inner'), axis=0).reshape(tm * hours, rank)]
    ppermute x2 -> x1, waiting for transfers between devices: 4.09 us -> 1.08 us  [swapped(): return lax.ppermute(value, axis, route)]
    squeeze x0 -> x1, local copies, waits for them, and re-layouts: none -> 0.77 us  [per_device(): given = lax.dynamic_index_in_dim(halves, 1 - core, 0, keepdims=False)]
    all_gather x0 -> x1, other arithmetic: none -> 0.76 us  [per_device(): lax.all_gather(mine, ('tm', 'inner'), axis=0).reshape(tm * hours, rank)]
  transfers between devices with their start and end apart: 3 -> 2, of which waited for: 2 -> 1; matrix products, arithmetic and copies ran while one was open for 0% -> 3% of each run, Pallas kernels for 10% -> 7%
where the time goes in v5:
time: 57.5 us; the launch traced here: 57.2 us
  blocking collectives  42.8 us (74%)
  Pallas kernels  7.97 us (14%)
  starting transfers between devices  3.01 us (5%)
  waiting for transfers between devices  1.08 us (2%)
  local copies, waits for them, and re-layouts  0.89 us (2%)
  other arithmetic  0.76 us (1%)
  between operations  0.68 us (1%)
    psum x1, blocking collectives, per_device(): mine = lax.psum(mine, 'outer')  37.4 us
    all_gather x1, blocking collectives, per_device(): lax.all_gather(mine, ('tm', 'inner'), axis=0).reshape(tm * hours, rank)  5.41 us
    pallas_call x1, Pallas kernels, project(): pl.pallas_call(functools.partial(project_kernel, tiles), out_shape=jax.Sh...  4.05 us
    pallas_call x1, Pallas kernels, rebuild(): pl.pallas_call(functools.partial(rebuild_kernel, tiles), out_shape=(jax.S...  3.92 us
    ppermute x1, starting transfers between devices, per_device(): held.append(lax.ppermute(fields, 'tm', route))  3 us
  transfers between devices with their start and end apart: 2, of which 1 were waited for; matrix products, arithmetic and copies ran while one was open for 3% of the time, Pallas kernels for 7%

profile of v5, /device:TPU:0, one launch (start us, length us, event | category | flops | bytes accessed | tf_op | source)
XLA Modules:
  0.0 57.2 jit_solution(4553978858738920089)
XLA Ops:
  0.6 0.0 copy-start
  0.6 0.0 copy-start.1
  0.7 0.0 copy-start.2
  0.7 3.0 %collective-permute-start.1 = (bf16[64,8192]{1,0:T(8,128)(2,1)}, bf16[64,8192]{1,0:T(8,128)(2,1)S(1)}, u32[]{:S(2)}, u32[]{:S(2)}) collective-permute-start(bf16[64,8192]{1,0:T(8,128)(2,1)} %bitcast.14), channel_id=1, source_target_pairs={{16,0},{0,16},{17,1},{1,17},{18,2},{2,18},{19,3},{3,19},{20,4},{4,... | collective-permute-start | bytes 3145736 | tf_op jit(solution)/shard_map/ppermute | solution.py:163
  3.7 4.0 %project.1 = f32[64,256]{1,0:T(8,128)} custom-call(bf16[64,8192]{1,0:T(8,128)(2,1)} %bitcast.15, bf16[8192,256]{1,0:T(8,128)(2,1)} %basis.1), custom_call_target="tpu_custom_call" | custom-call | tf_op jit(solution)/shard_map/project/pallas_call | solution.py:56
  7.7 0.8 %dynamic-slice_bitcast_fusion = f32[32,256]{1,0:T(8,128)S(1)} fusion(f32[2,32,256]{2,1,0:T(8,128)} %bitcast.20, s32[]{:T(128)S(6)} %select_n.11), kind=kLoop, calls=%fused_computation.2 | loop fusion | bytes 65540 | tf_op jit(solution)/shard_map/jit(dynamic_index_in_dim)/squeeze | solution.py:167
  8.5 0.0 collective-permute-start
  8.5 0.0 copy-done
  8.5 0.1 copy.8
  8.6 1.1 %collective-permute-done = f32[32,256]{1,0:T(8,128)S(1)} collective-permute-done((f32[32,256]{1,0:T(8,128)S(1)}, f32[32,256]{1,0:T(8,128)S(1)}, u32[]{:S(2)}, u32[]{:S(2)}) %collective-permute-start) | collective-permute-done | bytes 32800 | tf_op jit(solution)/shard_map/ppermute | solution.py:151
  9.7 0.8 %fusion = f32[1,32,256]{2,1,0:T(8,128)S(1)} fusion(f32[32,256]{1,0:T(8,128)S(1)} %collective-permute-done, f32[2,32,256]{2,1,0:T(8,128)} %bitcast.21, s32[]{:T(128)S(6)} %select_n.10), kind=kLoop, calls=%fused_computation.1 | loop fusion | flops 8192 | bytes 98308 | tf_op jit(solution)/shard_map/all_gather | solution.py:171
  10.5 37.4 %psum.7 = f32[1,32,256]{2,1,0:T(8,128)S(1)} all-reduce(f32[1,32,256]{2,1,0:T(8,128)S(1)} %fusion), channel_id=1, replica_groups=mesh['tm'=2,'outer'=8,'inner'=2] {'outer'}, use_global_device_ids=true, to_apply=%region_0.1 | all-reduce | flops 8192 | bytes 65536 | tf_op jit(solution)/shard_map/psum | solution.py:170
  47.9 5.4 %all_gather.7 = f32[4,32,256]{2,1,0:T(8,128)S(1)} all-gather(f32[1,32,256]{2,1,0:T(8,128)S(1)} %psum.7), channel_id=1, replica_groups=mesh['tm'=2,'outer'=8,'inner'=2] {'tm','inner'}, dimensions={0}, use_global_device_ids=true | all-gather | bytes 163840 | tf_op jit(solution)/shard_map/all_gather | solution.py:171
  53.3 0.0 collective-permute-done.1.refs_1_
  53.3 0.0 copy-done.1
  53.3 0.0 copy-done.2
  53.3 3.9 %rebuild.1 = (f32[256,256]{1,0:T(8,128)}, bf16[256,8192]{1,0:T(8,128)(2,1)}) custom-call(s32[1]{0:T(128)} %bitcast.me, f32[1,256]{1,0:T(1,128)S(1)} %bitcast.19, f32[128,256]{1,0:T(8,128)S(1)} %bitcast.17, bf16[256,256]{1,0:T(8,128)(2,1)S(1)} %bitcast.18, bf16[64,8192]{1,0:T(8,128)(2,1)S(1)} %bitcast.16, bf16[64,8192]{1,0:T(8,128)(2,1)S(1)} %collective-permute-done.1.refs_1_), custom_call_target="tpu_custom_call" | custom-call | tf_op jit(solution)/shard_map/rebuild/pallas_call | solution.py:122
  (1 shorter events, 0.0 us)
Async XLA Ops:
  0.6 7.9 %copy-start = (bf16[256,512]{1,0:T(8,128)(2,1)S(1)}, bf16[256,512]{1,0:T(8,128)(2,1)}, u32[]{:S(2)}) copy-start(bf16[256,512]{1,0:T(8,128)(2,1)} %param.7) | copy-start | bytes 786436
  0.6 52.6 %copy-start.1 = (bf16[8192,64]{0,1:T(8,128)(2,1)S(1)}, bf16[8192,64]{0,1:T(8,128)(2,1)}, u32[]{:S(2)}) copy-start(bf16[8192,64]{0,1:T(8,128)(2,1)} %param.5) | copy-start | bytes 3145732
  0.7 52.6 %copy-start.2 = (f32[256]{0:T(256)S(1)}, f32[256]{0:T(256)}, u32[]{:S(2)}) copy-start(f32[256]{0:T(256)} %param.6) | copy-start | bytes 3076
  0.7 52.6 %collective-permute-start.1 = (bf16[64,8192]{1,0:T(8,128)(2,1)}, bf16[64,8192]{1,0:T(8,128)(2,1)S(1)}, u32[]{:S(2)}, u32[]{:S(2)}) collective-permute-start(bf16[64,8192]{1,0:T(8,128)(2,1)} %bitcast.14), channel_id=1, source_target_pairs={{16,0},{0,16},{17,1},{1,17},{18,2},{2,18},{19,3},{3,19},{20,4},{4,... | collective-permute-start | bytes 3145736 | tf_op jit(solution)/shard_map/ppermute | solution.py:163
  8.5 1.2 %collective-permute-start = (f32[32,256]{1,0:T(8,128)S(1)}, f32[32,256]{1,0:T(8,128)S(1)}, u32[]{:S(2)}, u32[]{:S(2)}) collective-permute-start(f32[32,256]{1,0:T(8,128)S(1)} %dynamic-slice_bitcast_fusion), channel_id=1, source_target_pairs={{1,0},{0,1},{3,2},{2,3},{5,4},{4,5},{7,6},{6,7},{9,8},{8,9},{11,10... | collective-permute-start | bytes 98312 | tf_op jit(solution)/shard_map/ppermute | solution.py:151

commit v6 on v4

v6 whole, which is shorter than its diff:
```python
import functools

import jax
import jax.numpy as jnp
from jax import lax
from jax.experimental import pallas as pl
from jax.experimental.pallas import tpu as pltpu
from jax.sharding import Mesh, PartitionSpec as P

ROWS = (((1,), (0,)), ((), ()))
FIRST = (((0,), (0,)), ((), ()))
LAST = (((1,), (1,)), ((), ()))
FREE = pl.CostEstimate(flops=0, bytes_accessed=0, transcendentals=0)


def in_parts(value):
    high = value.astype(jnp.bfloat16)
    return high, (value - high.astype(jnp.float32)).astype(jnp.bfloat16)


def product(left, right, dims):
    return lax.dot_general(left, right, dims, preferred_element_type=jnp.float32)


def project_kernel(tiles, core, snapshots, basis, kept, given, fields, patterns, halves, arrived):
    cells = snapshots.shape[1]
    tile = cells // tiles
    copies = []
    for i in range(tiles):
        span = pl.ds(i * tile, tile)
        copies.append(
            (
                pltpu.make_async_copy(snapshots.at[:, span], fields.at[:, span], arrived.at[0, i]),
                pltpu.make_async_copy(basis.at[span], patterns.at[span], arrived.at[1, i]),
            )
        )
    for pair in copies:
        for copy in pair:
            copy.start()
    total = jnp.zeros((fields.shape[0], patterns.shape[1]), jnp.float32)
    for i, pair in enumerate(copies):
        for copy in pair:
            copy.wait()
        span = pl.ds(i * tile, tile)
        total += product(fields[:, span], patterns[span], ROWS)
    half = kept.shape[0]
    halves[0] = total[:half]
    halves[1] = total[half:]
    kept[...] = halves[core[0]]
    given[...] = halves[1 - core[0]]


def project(core, snapshots, basis, tiles):
    hours = snapshots.shape[0]
    rank = basis.shape[1]
    half = jax.ShapeDtypeStruct((hours // 2, rank), jnp.float32)
    return pl.pallas_call(
        functools.partial(project_kernel, tiles),
        out_shape=(half, half),
        in_specs=[pl.BlockSpec(memory_space=pltpu.SMEM)]
        + [pl.BlockSpec(memory_space=pl.ANY)] * 2,
        out_specs=(pl.BlockSpec(memory_space=pltpu.VMEM),) * 2,
        scratch_shapes=[
            pltpu.VMEM(snapshots.shape, snapshots.dtype),
            pltpu.VMEM(basis.shape, basis.dtype),
            pltpu.VMEM((2, hours // 2, rank), jnp.float32),
            pltpu.SemaphoreType.DMA((2, tiles)),
        ],
        compiler_params=pltpu.CompilerParams(vmem_limit_bytes=58 * 2**20),
        cost_estimate=FREE,
        name="project",
    )(core[None], snapshots, basis)


def rebuild_kernel(tiles, place, energy, vectors, *refs):
    count = (len(refs) - 9) // 2
    held, coeffs, refs = refs[:count], refs[count : 2 * count], refs[2 * count :]
    operator, modes, fields, known, turned, scaled, made, arrived, sent = refs
    hours, cells = held[0].shape
    tile = cells // tiles
    half = hours // 2
    first = [pl.multiple_of(lax.rem(place[0] + k, count) * hours, hours) for k in range(count)]
    inputs = [pltpu.make_async_copy(vectors, turned, arrived.at[count])]
    for k, block in enumerate(coeffs):
        for own in range(2):
            at = pl.multiple_of(first[k] + lax.rem(place[1] + own, 2) * half, half)
            inputs.append(
                pltpu.make_async_copy(
                    block.at[own], known.at[pl.ds(at, half)], arrived.at[count + 1 + 2 * k + own]
                )
            )
    blocks = [
        pltpu.make_async_copy(block, fields.at[pl.ds(k * hours, hours)], arrived.at[k])
        for k, block in enumerate(held)
    ]
    for copy in inputs + blocks:
        copy.start()
    for copy in inputs:
        copy.wait()
    every = known[...]
    hour = lax.broadcasted_iota(jnp.int32, every.shape, 0)
    scaled[...] = jnp.where(hour == 0, 0.0, pltpu.roll(every, 1, 0)) * energy[...]
    ordered = jnp.concatenate([scaled[pl.ds(at, hours)] for at in first], axis=0)
    high, low = in_parts(ordered)
    weights = (product(turned[...], high, LAST) + product(turned[...], low, LAST)).astype(
        jnp.bfloat16
    )
    for copy in blocks:
        copy.wait()
    outgoing = []
    for i in range(tiles):
        span = pl.ds(i * tile, tile)
        made[:, span] = product(weights, fields[:, span], ROWS).astype(made.dtype)
        copy = pltpu.make_async_copy(made.at[:, span], modes.at[:, span], sent.at[i])
        copy.start()
        outgoing.append(copy)
    high, low = in_parts(every)
    s_high, s_low = in_parts(scaled[...])
    operator[...] = (
        product(high, s_high, FIRST) + product(high, s_low, FIRST) + product(low, s_high, FIRST)
    )
    for copy in outgoing:
        copy.wait()


def rebuild(place, energy, vectors, held, coeffs, tiles):
    hours, cells = held[0].shape
    total, rank = len(held) * hours, coeffs[0].shape[2]
    modes = vectors.shape[0]
    anywhere = pl.BlockSpec(memory_space=pl.ANY)
    return pl.pallas_call(
        functools.partial(rebuild_kernel, tiles),
        out_shape=(
            jax.ShapeDtypeStruct((rank, rank), jnp.float32),
            jax.ShapeDtypeStruct((modes, cells), jnp.bfloat16),
        ),
        in_specs=[
            pl.BlockSpec(memory_space=pltpu.SMEM),
            pl.BlockSpec(memory_space=pltpu.VMEM),
        ]
        + [anywhere] * (1 + 2 * len(held)),
        out_specs=(pl.BlockSpec(memory_space=pltpu.VMEM), anywhere),
        scratch_shapes=[
            pltpu.VMEM((total, cells), held[0].dtype),
            pltpu.VMEM((total, rank), jnp.float32),
            pltpu.VMEM(vectors.shape, vectors.dtype),
            pltpu.VMEM((total, rank), jnp.float32),
            pltpu.VMEM((modes, cells), jnp.bfloat16),
            pltpu.SemaphoreType.DMA((3 * len(held) + 1,)),
            pltpu.SemaphoreType.DMA((tiles,)),
        ],
        compiler_params=pltpu.CompilerParams(vmem_limit_bytes=40 * 2**20),
        cost_estimate=FREE,
        name="rebuild",
    )(place, energy[None, :], vectors, *held, *coeffs)


def swapped(value, axis, bit):
    route = [(i ^ bit, i) for i in range(lax.axis_size(axis))]
    return lax.ppermute(value, axis, route)


def turned_round(value, axis):
    size = lax.axis_size(axis)
    routes = [[((i + k) % size, i) for i in range(size)] for k in range(1, size)]
    return [value] + [lax.ppermute(value, axis, route) for route in routes]


def per_device(eof_basis, snapshots, inverse_energy, eigen_vectors):
    tm, outer = lax.axis_size("tm"), lax.axis_size("outer")
    me, core = lax.axis_index("tm"), lax.axis_index("inner")
    fields = snapshots.T

    held = turned_round(fields, "tm")

    kept, given = project(core, fields, eof_basis, 8)
    mine = kept + swapped(given, "inner", 1)
    bit = 1
    while bit < outer:
        near = swapped(mine, "outer", bit)
        if 2 * bit < outer:
            far, both = (swapped(mine, "outer", b) for b in (2 * bit, 3 * bit))
            mine = (mine + near) + (far + both)
        else:
            mine = mine + near
        bit *= 4
    coeffs = turned_round(jnp.stack([mine, swapped(mine, "inner", 1)]), "tm")

    rows = eigen_vectors.shape[1] // tm
    vectors = lax.dynamic_slice_in_dim(eigen_vectors, me * rows, rows, 1)
    return rebuild(jnp.stack([me, core]), inverse_energy, vectors.T, held, coeffs, 8)


def solution(mesh):
    tm, space = mesh.shape["tm"], mesh.shape["space"]
    split = Mesh(mesh.devices.reshape(tm, space // 2, 2), ("tm", "outer", "inner"))
    cells = ("outer", "inner")
    in_specs = (P(cells, None), P(cells, "tm"), P(), P())
    out_specs = (P(), P("tm", cells))
    return jax.shard_map(
        per_device, mesh=split, in_specs=in_specs, out_specs=out_specs, check_vma=False
    )
```

time: 35.9 us -> 33.1 us (0.922)
  blocking collectives: 16 us -> 0 us
  waiting for transfers between devices: 4.09 us -> 13.4 us
  starting transfers between devices: 7.24 us -> 9.75 us
  other arithmetic: 0.02 us -> 0.86 us
  Pallas kernels: 7.52 us -> 8.11 us
    all_gather x1 -> x0, blocking collectives: 8.57 us -> none  [per_device(): lax.all_gather(mine, ('tm', 'inner'), axis=0).reshape(tm * hours, rank)]
    all_to_all x1 -> x0, blocking collectives: 7.38 us -> none  [per_device(): mine = jnp.sum(lax.all_to_all(pieces, 'inner', 0, 0, tiled=True), axis=0)]
    ppermute x1 -> x2, waiting for transfers between devices: 0.01 us -> 5.3 us  [turned_round(): return [value] + [lax.ppermute(value, axis, route) for route in routes]]
    ppermute x2 -> x6, waiting for transfers between devices: 4.09 us -> 8.09 us  [swapped(): return lax.ppermute(value, axis, route)]
    ppermute x2 -> x6, starting transfers between devices: 4.23 us -> 6.22 us  [swapped(): return lax.ppermute(value, axis, route)]
    add x2 -> x3, other arithmetic: 0.01 us -> 0.78 us  [the longest x1 0.76 us: per_device(): mine = kept + swapped(given, 'inner', 1)]
    pallas_call x1, Pallas kernels: 3.93 us -> 4.51 us  [rebuild(): pl.pallas_call(functools.partial(rebuild_kernel, tiles), out_shape=(jax.S...]
    ppermute x1 -> x2, starting transfers between devices: 3 us -> 3.54 us  [turned_round(): return [value] + [lax.ppermute(value, axis, route) for route in routes]]
  transfers between devices with their start and end apart: 3 -> 8, of which waited for: 2 -> 7; matrix products, arithmetic and copies ran while one was open for 0% -> 3% of each run, Pallas kernels for 10% -> 11%
where the time goes in v6:
time: 33.1 us; the launch traced here: 33 us
  waiting for transfers between devices  13.4 us (40%)
  starting transfers between devices  9.75 us (29%)
  Pallas kernels  8.11 us (25%)
  other arithmetic  0.86 us (3%)
  between operations  0.72 us (2%)
    ppermute x6, waiting for transfers between devices, swapped(): return lax.ppermute(value, axis, route)  8.09 us
    ppermute x6, starting transfers between devices, swapped(): return lax.ppermute(value, axis, route)  6.22 us
    ppermute x2, waiting for transfers between devices, turned_round(): return [value] + [lax.ppermute(value, axis, route) for route in routes]  5.3 us
    pallas_call x1, Pallas kernels, rebuild(): pl.pallas_call(functools.partial(rebuild_kernel, tiles), out_shape=(jax.S...  4.51 us
    pallas_call x1, Pallas kernels, project(): pl.pallas_call(functools.partial(project_kernel, tiles), out_shape=(half,...  3.6 us
    ppermute x2, starting transfers between devices, turned_round(): return [value] + [lax.ppermute(value, axis, route) for route in routes]  3.54 us
    add x1, other arithmetic, per_device(): mine = kept + swapped(given, 'inner', 1)  0.76 us
  transfers between devices with their start and end apart: 8, of which 7 were waited for; matrix products, arithmetic and copies ran while one was open for 3% of the time, Pallas kernels for 11%

profile of v6, /device:TPU:0, one launch (start us, length us, event | category | flops | bytes accessed | tf_op | source)
XLA Modules:
  0.0 33.0 jit_solution(11690796856547989567)
XLA Ops:
  0.6 0.0 copy-start
  0.6 0.0 copy-start.1
  0.7 0.0 copy-start.2
  0.7 3.0 %collective-permute-start = (bf16[64,8192]{1,0:T(8,128)(2,1)}, bf16[64,8192]{1,0:T(8,128)(2,1)S(1)}, u32[]{:S(2)}, u32[]{:S(2)}) collective-permute-start(bf16[64,8192]{1,0:T(8,128)(2,1)} %bitcast.7), channel_id=1, source_target_pairs={{16,0},{0,16},{17,1},{1,17},{18,2},{2,18},{19,3},{3,19},{20,4},{4,... | collective-permute-start | bytes 3145736 | tf_op jit(solution)/shard_map/ppermute | solution.py:166
  3.7 3.6 %project.1 = (f32[32,256]{1,0:T(8,128)}, f32[32,256]{1,0:T(8,128)}) custom-call(s32[1]{0:T(128)} %bitcast.1.core, bf16[64,8192]{1,0:T(8,128)(2,1)} %bitcast.8, bf16[8192,256]{1,0:T(8,128)(2,1)} %basis.1), custom_call_target="tpu_custom_call" | custom-call | tf_op jit(solution)/shard_map/project/pallas_call | solution.py:57
  7.3 0.1 collective-permute-start.1
  7.4 1.4 %collective-permute-done.1 = f32[32,256]{1,0:T(8,128)S(1)} collective-permute-done((f32[32,256]{1,0:T(8,128)}, f32[32,256]{1,0:T(8,128)S(1)}, u32[]{:S(2)}, u32[]{:S(2)}) %collective-permute-start.1) | collective-permute-done | bytes 32800 | tf_op jit(solution)/shard_map/ppermute | solution.py:160
  8.8 0.8 %add.19 = f32[32,256]{1,0:T(8,128)S(1)} add(f32[32,256]{1,0:T(8,128)} %get-tuple-element.4, f32[32,256]{1,0:T(8,128)S(1)} %collective-permute-done.1) | non-fusion elementwise | flops 8192 | bytes 98304 | tf_op jit(solution)/shard_map/add | solution.py:177
  9.5 2.5 %collective-permute-start.4 = (f32[32,256]{1,0:T(8,128)S(1)}, f32[32,256]{1,0:T(8,128)S(1)}, u32[]{:S(2)}, u32[]{:S(2)}) collective-permute-start(f32[32,256]{1,0:T(8,128)S(1)} %add.19), channel_id=1, source_target_pairs={{6,0},{4,2},{2,4},{0,6},{14,8},{12,10},{10,12},{8,14},{7,1},{5,3},... | collective-permute-start | bytes 98312 | tf_op jit(solution)/shard_map/ppermute | solution.py:160
  12.1 0.5 %collective-permute-start.3 = (f32[32,256]{1,0:T(8,128)S(1)}, f32[32,256]{1,0:T(8,128)S(1)}, u32[]{:S(2)}, u32[]{:S(2)}) collective-permute-start(f32[32,256]{1,0:T(8,128)S(1)} %add.19), channel_id=1, source_target_pairs={{4,0},{6,2},{0,4},{2,6},{12,8},{14,10},{8,12},{10,14},{5,1},{7,3},... | collective-permute-start | bytes 98312 | tf_op jit(solution)/shard_map/ppermute | solution.py:160
  12.5 0.5 %collective-permute-start.2 = (f32[32,256]{1,0:T(8,128)S(1)}, f32[32,256]{1,0:T(8,128)S(1)}, u32[]{:S(2)}, u32[]{:S(2)}) collective-permute-start(f32[32,256]{1,0:T(8,128)S(1)} %add.19), channel_id=1, source_target_pairs={{2,0},{0,2},{6,4},{4,6},{10,8},{8,10},{14,12},{12,14},{3,1},{1,3},... | collective-permute-start | bytes 98312 | tf_op jit(solution)/shard_map/ppermute | solution.py:160
  13.0 1.3 %collective-permute-done.4 = f32[32,256]{1,0:T(8,128)S(1)} collective-permute-done((f32[32,256]{1,0:T(8,128)S(1)}, f32[32,256]{1,0:T(8,128)S(1)}, u32[]{:S(2)}, u32[]{:S(2)}) %collective-permute-start.4) | collective-permute-done | bytes 32800 | tf_op jit(solution)/shard_map/ppermute | solution.py:160
  14.3 1.6 %collective-permute-done.3 = f32[32,256]{1,0:T(8,128)S(1)} collective-permute-done((f32[32,256]{1,0:T(8,128)S(1)}, f32[32,256]{1,0:T(8,128)S(1)}, u32[]{:S(2)}, u32[]{:S(2)}) %collective-permute-start.3) | collective-permute-done | bytes 32800 | tf_op jit(solution)/shard_map/ppermute | solution.py:160
  16.0 0.5 %collective-permute-done.2 = f32[32,256]{1,0:T(8,128)S(1)} collective-permute-done((f32[32,256]{1,0:T(8,128)S(1)}, f32[32,256]{1,0:T(8,128)S(1)}, u32[]{:S(2)}, u32[]{:S(2)}) %collective-permute-start.2) | collective-permute-done | bytes 32800 | tf_op jit(solution)/shard_map/ppermute | solution.py:160
  16.4 2.7 %collective-permute-start.5 = (f32[32,256]{1,0:T(8,128)S(1)}, f32[32,256]{1,0:T(8,128)S(1)}, u32[]{:S(2)}, u32[]{:S(2)}) collective-permute-start(f32[32,256]{1,0:T(8,128)S(1)} %add_add_fusion), channel_id=1, source_target_pairs={{8,0},{10,2},{12,4},{14,6},{0,8},{2,10},{4,12},{6,14},{9,1},{11,3}... | collective-permute-start | bytes 98312 | tf_op jit(solution)/shard_map/ppermute | solution.py:160
  19.1 2.2 %collective-permute-done.5 = f32[32,256]{1,0:T(8,128)S(1)} collective-permute-done((f32[32,256]{1,0:T(8,128)S(1)}, f32[32,256]{1,0:T(8,128)S(1)}, u32[]{:S(2)}, u32[]{:S(2)}) %collective-permute-start.5) | collective-permute-done | bytes 32800 | tf_op jit(solution)/shard_map/ppermute | solution.py:160
  21.3 0.0 collective-permute-start.6
  21.3 0.0 copy-done
  21.4 0.1 copy.7
  21.5 1.1 %collective-permute-done.6 = f32[32,256]{1,0:T(8,128)S(1)} collective-permute-done((f32[32,256]{1,0:T(8,128)S(1)}, f32[32,256]{1,0:T(8,128)S(1)}, u32[]{:S(2)}, u32[]{:S(2)}) %collective-permute-start.6) | collective-permute-done | bytes 32800 | tf_op jit(solution)/shard_map/ppermute | solution.py:160
  22.5 0.5 %collective-permute-start.7 = (f32[2,32,256]{2,1,0:T(8,128)S(1)}, f32[2,32,256]{2,1,0:T(8,128)S(1)}, u32[]{:S(2)}, u32[]{:S(2)}) collective-permute-start(f32[2,32,256]{2,1,0:T(8,128)S(1)} %pad_maximum_fusion.refs_2_), channel_id=1, source_target_pairs={{16,0},{0,16},{17,1},{1,17},{18,2},{2,18},{19,3},{3,19},{20,4},{4,... | collective-permute-start | bytes 196616 | tf_op jit(solution)/shard_map/ppermute | solution.py:166
  23.1 0.1 pad_add_fusion.place
  23.1 5.3 %collective-permute-done.7.refs_3_ = f32[2,32,256]{2,1,0:T(8,128)S(1)} collective-permute-done((f32[2,32,256]{2,1,0:T(8,128)S(1)}, f32[2,32,256]{2,1,0:T(8,128)S(1)}, u32[]{:S(2)}, u32[]{:S(2)}) %collective-permute-start.7) | collective-permute-done | bytes 65568 | tf_op jit(solution)/shard_map/ppermute | solution.py:166
  28.4 0.0 collective-permute-done.refs_1_
  28.4 0.0 copy-done.1
  28.4 0.0 copy-done.2
  28.5 4.5 %rebuild.1 = (f32[256,256]{1,0:T(8,128)}, bf16[256,8192]{1,0:T(8,128)(2,1)}) custom-call(s32[2]{0:T(128)S(1)} %pad_add_fusion.place, f32[1,256]{1,0:T(1,128)S(1)} %bitcast.11, bf16[256,256]{1,0:T(8,128)(2,1)S(1)} %bitcast.10, bf16[64,8192]{1,0:T(8,128)(2,1)S(1)} %bitcast.9, bf16[64,8192]{1,0:T(8,128)(2,1)S(1)} %collective-permute-done.refs_1_, ...), custom_call_target="tpu_custom_call" | custom-call | tf_op jit(solution)/shard_map/rebuild/pallas_call | solution.py:131
  (4 shorter events, 0.0 us)
Async XLA Ops:
  0.6 20.7 %copy-start = (bf16[256,512]{1,0:T(8,128)(2,1)S(1)}, bf16[256,512]{1,0:T(8,128)(2,1)}, u32[]{:S(2)}) copy-start(bf16[256,512]{1,0:T(8,128)(2,1)} %param.7) | copy-start | bytes 786436
  0.6 27.8 %copy-start.1 = (bf16[8192,64]{0,1:T(8,128)(2,1)S(1)}, bf16[8192,64]{0,1:T(8,128)(2,1)}, u32[]{:S(2)}) copy-start(bf16[8192,64]{0,1:T(8,128)(2,1)} %param.5) | copy-start | bytes 3145732
  0.7 27.8 %copy-start.2 = (f32[256]{0:T(256)S(1)}, f32[256]{0:T(256)}, u32[]{:S(2)}) copy-start(f32[256]{0:T(256)} %param.6) | copy-start | bytes 3076
  0.7 27.8 %collective-permute-start = (bf16[64,8192]{1,0:T(8,128)(2,1)}, bf16[64,8192]{1,0:T(8,128)(2,1)S(1)}, u32[]{:S(2)}, u32[]{:S(2)}) collective-permute-start(bf16[64,8192]{1,0:T(8,128)(2,1)} %bitcast.7), channel_id=1, source_target_pairs={{16,0},{0,16},{17,1},{1,17},{18,2},{2,18},{19,3},{3,19},{20,4},{4,... | collective-permute-start | bytes 3145736 | tf_op jit(solution)/shard_map/ppermute | solution.py:166
  7.3 1.5 %collective-permute-start.1 = (f32[32,256]{1,0:T(8,128)}, f32[32,256]{1,0:T(8,128)S(1)}, u32[]{:S(2)}, u32[]{:S(2)}) collective-permute-start(f32[32,256]{1,0:T(8,128)} %get-tuple-element.5), channel_id=1, source_target_pairs={{1,0},{0,1},{3,2},{2,3},{5,4},{4,5},{7,6},{6,7},{9,8},{8,9},{11,10... | collective-permute-start | bytes 98312 | tf_op jit(solution)/shard_map/ppermute | solution.py:160
  9.5 4.8 %collective-permute-start.4 = (f32[32,256]{1,0:T(8,128)S(1)}, f32[32,256]{1,0:T(8,128)S(1)}, u32[]{:S(2)}, u32[]{:S(2)}) collective-permute-start(f32[32,256]{1,0:T(8,128)S(1)} %add.19), channel_id=1, source_target_pairs={{6,0},{4,2},{2,4},{0,6},{14,8},{12,10},{10,12},{8,14},{7,1},{5,3},... | collective-permute-start | bytes 98312 | tf_op jit(solution)/shard_map/ppermute | solution.py:160
  12.1 3.9 %collective-permute-start.3 = (f32[32,256]{1,0:T(8,128)S(1)}, f32[32,256]{1,0:T(8,128)S(1)}, u32[]{:S(2)}, u32[]{:S(2)}) collective-permute-start(f32[32,256]{1,0:T(8,128)S(1)} %add.19), channel_id=1, source_target_pairs={{4,0},{6,2},{0,4},{2,6},{12,8},{14,10},{8,12},{10,14},{5,1},{7,3},... | collective-permute-start | bytes 98312 | tf_op jit(solution)/shard_map/ppermute | solution.py:160
  12.5 3.9 %collective-permute-start.2 = (f32[32,256]{1,0:T(8,128)S(1)}, f32[32,256]{1,0:T(8,128)S(1)}, u32[]{:S(2)}, u32[]{:S(2)}) collective-permute-start(f32[32,256]{1,0:T(8,128)S(1)} %add.19), channel_id=1, source_target_pairs={{2,0},{0,2},{6,4},{4,6},{10,8},{8,10},{14,12},{12,14},{3,1},{1,3},... | collective-permute-start | bytes 98312 | tf_op jit(solution)/shard_map/ppermute | solution.py:160
  16.4 4.9 %collective-permute-start.5 = (f32[32,256]{1,0:T(8,128)S(1)}, f32[32,256]{1,0:T(8,128)S(1)}, u32[]{:S(2)}, u32[]{:S(2)}) collective-permute-start(f32[32,256]{1,0:T(8,128)S(1)} %add_add_fusion), channel_id=1, source_target_pairs={{8,0},{10,2},{12,4},{14,6},{0,8},{2,10},{4,12},{6,14},{9,1},{11,3}... | collective-permute-start | bytes 98312 | tf_op jit(solution)/shard_map/ppermute | solution.py:160
  21.3 1.2 %collective-permute-start.6 = (f32[32,256]{1,0:T(8,128)S(1)}, f32[32,256]{1,0:T(8,128)S(1)}, u32[]{:S(2)}, u32[]{:S(2)}) collective-permute-start(f32[32,256]{1,0:T(8,128)S(1)} %add.23), channel_id=1, source_target_pairs={{1,0},{0,1},{3,2},{2,3},{5,4},{4,5},{7,6},{6,7},{9,8},{8,9},{11,10... | collective-permute-start | bytes 98312 | tf_op jit(solution)/shard_map/ppermute | solution.py:160
  22.5 5.9 %collective-permute-start.7 = (f32[2,32,256]{2,1,0:T(8,128)S(1)}, f32[2,32,256]{2,1,0:T(8,128)S(1)}, u32[]{:S(2)}, u32[]{:S(2)}) collective-permute-start(f32[2,32,256]{2,1,0:T(8,128)S(1)} %pad_maximum_fusion.refs_2_), channel_id=1, source_target_pairs={{16,0},{0,16},{17,1},{1,17},{18,2},{2,18},{19,3},{3,19},{20,4},{4,... | collective-permute-start | bytes 196616 | tf_op jit(solution)/shard_map/ppermute | solution.py:166

commit v7 on v6

--- a/solution.py
+++ b/solution.py
@@ -66,34 +66,38 @@
             pltpu.VMEM((2, hours // 2, rank), jnp.float32),
             pltpu.SemaphoreType.DMA((2, tiles)),
         ],
-        compiler_params=pltpu.CompilerParams(vmem_limit_bytes=58 * 2**20),
+        compiler_params=pltpu.CompilerParams(vmem_limit_bytes=53 * 2**20),
         cost_estimate=FREE,
         name="project",
     )(core[None], snapshots, basis)
 
 
 def rebuild_kernel(tiles, place, energy, vectors, *refs):
-    count = (len(refs) - 9) // 2
-    held, coeffs, refs = refs[:count], refs[count : 2 * count], refs[2 * count :]
-    operator, modes, fields, known, turned, scaled, made, arrived, sent = refs
+    count = (len(refs) - 10) // 3
+    held, coeffs, refs = refs[:count], refs[count : 3 * count], refs[3 * count :]
+    operator, modes, fields, known, turned, scaled, made, square, arrived, sent = refs
     hours, cells = held[0].shape
-    tile = cells // tiles
-    half = hours // 2
+    half, tile = hours // 2, cells // tiles
+    spans = [pl.ds(i * tile, tile) for i in range(tiles)]
     first = [pl.multiple_of(lax.rem(place[0] + k, count) * hours, hours) for k in range(count)]
-    inputs = [pltpu.make_async_copy(vectors, turned, arrived.at[count])]
-    for k, block in enumerate(coeffs):
-        for own in range(2):
-            at = pl.multiple_of(first[k] + lax.rem(place[1] + own, 2) * half, half)
-            inputs.append(
-                pltpu.make_async_copy(
-                    block.at[own], known.at[pl.ds(at, half)], arrived.at[count + 1 + 2 * k + own]
-                )
-            )
+    inputs = [pltpu.make_async_copy(vectors, turned, arrived.at[tiles, 0])]
+    for n, block in enumerate(coeffs):
+        at = pl.multiple_of(first[n // 2] + lax.rem(place[1] + n % 2, 2) * half, half)
+        inputs.append(
+            pltpu.make_async_copy(
+                block, known.at[pl.ds(at, half)], arrived.at[tiles + 1 + n % 2, n // 2]
+            )
+        )
     blocks = [
-        pltpu.make_async_copy(block, fields.at[pl.ds(k * hours, hours)], arrived.at[k])
-        for k, block in enumerate(held)
+        [
+            pltpu.make_async_copy(
+                block.at[:, span], fields.at[pl.ds(k * hours, hours), span], arrived.at[i, k]
+            )
+            for k, block in enumerate(held)
+        ]
+        for i, span in enumerate(spans)
     ]
-    for copy in inputs + blocks:
+    for copy in inputs + sum(blocks, []):
         copy.start()
     for copy in inputs:
         copy.wait()
@@ -105,27 +109,30 @@
     weights = (product(turned[...], high, LAST) + product(turned[...], low, LAST)).astype(
         jnp.bfloat16
     )
-    for copy in blocks:
-        copy.wait()
     outgoing = []
-    for i in range(tiles):
-        span = pl.ds(i * tile, tile)
+    for i, span in enumerate(spans):
+        if i == tiles - 1:
+            high, low = in_parts(every)
+            s_high, s_low = in_parts(scaled[...])
+            square[...] = (
+                product(high, s_high, FIRST)
+                + product(high, s_low, FIRST)
+                + product(low, s_high, FIRST)
+            )
+            outgoing.append(pltpu.make_async_copy(square, operator, sent.at[tiles]))
+            outgoing[-1].start()
+        for copy in blocks[i]:
+            copy.wait()
         made[:, span] = product(weights, fields[:, span], ROWS).astype(made.dtype)
-        copy = pltpu.make_async_copy(made.at[:, span], modes.at[:, span], sent.at[i])
-        copy.start()
-        outgoing.append(copy)
-    high, low = in_parts(every)
-    s_high, s_low = in_parts(scaled[...])
-    operator[...] = (
-        product(high, s_high, FIRST) + product(high, s_low, FIRST) + product(low, s_high, FIRST)
-    )
+        outgoing.append(pltpu.make_async_copy(made.at[:, span], modes.at[:, span], sent.at[i]))
+        outgoing[-1].start()
     for copy in outgoing:
         copy.wait()
 
 
 def rebuild(place, energy, vectors, held, coeffs, tiles):
     hours, cells = held[0].shape
-    total, rank = len(held) * hours, coeffs[0].shape[2]
+    total, rank = len(held) * hours, coeffs[0].shape[1]
     modes = vectors.shape[0]
     anywhere = pl.BlockSpec(memory_space=pl.ANY)
     return pl.pallas_call(
@@ -138,16 +145,17 @@
             pl.BlockSpec(memory_space=pltpu.SMEM),
             pl.BlockSpec(memory_space=pltpu.VMEM),
         ]
-        + [anywhere] * (1 + 2 * len(held)),
-        out_specs=(pl.BlockSpec(memory_space=pltpu.VMEM), anywhere),
+        + [anywhere] * (1 + 3 * len(held)),
+        out_specs=(anywhere, anywhere),
         scratch_shapes=[
             pltpu.VMEM((total, cells), held[0].dtype),
             pltpu.VMEM((total, rank), jnp.float32),
             pltpu.VMEM(vectors.shape, vectors.dtype),
             pltpu.VMEM((total, rank), jnp.float32),
             pltpu.VMEM((modes, cells), jnp.bfloat16),
-            pltpu.SemaphoreType.DMA((3 * len(held) + 1,)),
-            pltpu.SemaphoreType.DMA((tiles,)),
+            pltpu.VMEM((rank, rank), jnp.float32),
+            pltpu.SemaphoreType.DMA((tiles + 3, len(held))),
+            pltpu.SemaphoreType.DMA((tiles + 1,)),
         ],
         compiler_params=pltpu.CompilerParams(vmem_limit_bytes=40 * 2**20),
         cost_estimate=FREE,
@@ -160,10 +168,14 @@
     return lax.ppermute(value, axis, route)
 
 
-def turned_round(value, axis):
-    size = lax.axis_size(axis)
-    routes = [[((i + k) % size, i) for i in range(size)] for k in range(1, size)]
-    return [value] + [lax.ppermute(value, axis, route) for route in routes]
+def moved(value, by, swap):
+    size = lax.axis_size("tm")
+    route = [
+        (2 * ((i + by) % size) + (core ^ swap), 2 * i + core)
+        for i in range(size)
+        for core in range(2)
+    ]
+    return lax.ppermute(value, ("tm", "inner"), route)
 
 
 def per_device(eof_basis, snapshots, inverse_energy, eigen_vectors):
@@ -171,7 +183,7 @@
     me, core = lax.axis_index("tm"), lax.axis_index("inner")
     fields = snapshots.T
 
-    held = turned_round(fields, "tm")
+    held = [fields] + [moved(fields, k, 0) for k in range(1, tm)]
 
     kept, given = project(core, fields, eof_basis, 8)
     mine = kept + swapped(given, "inner", 1)
@@ -184,7 +196,9 @@
         else:
             mine = mine + near
         bit *= 4
-    coeffs = turned_round(jnp.stack([mine, swapped(mine, "inner", 1)]), "tm")
+    coeffs = [mine, moved(mine, 0, 1)]
+    for k in range(1, tm):
+        coeffs += [moved(mine, k, 0), moved(mine, k, 1)]
 
     rows = eigen_vectors.shape[1] // tm
     vectors = lax.dynamic_slice_in_dim(eigen_vectors, me * rows, rows, 1)

time: 33.1 us -> 33.8 us (1.021)
  starting transfers between devices: 9.75 us -> 11.1 us
  other arithmetic: 0.86 us -> 0.09 us
    ppermute x2 -> x4, waiting for transfers between devices: 5.3 us -> 6.68 us  [moved(): return lax.ppermute(value, ('tm', 'inner'), route)]
    ppermute x2 -> x4, starting transfers between devices: 3.54 us -> 4.86 us  [moved(): return lax.ppermute(value, ('tm', 'inner'), route)]
    ppermute x6 -> x5, waiting for transfers between devices: 8.09 us -> 6.81 us  [swapped(): return lax.ppermute(value, axis, route)]
    add x1, other arithmetic: 0.76 us -> 0.01 us  [per_device(): mine = kept + swapped(given, 'inner', 1)]
    pallas_call x1, Pallas kernels: 4.51 us -> 5.23 us  [rebuild(): pl.pallas_call(functools.partial(rebuild_kernel, tiles), out_shape=(jax.S...]
    pallas_call x1, Pallas kernels: 3.6 us -> 2.97 us  [project(): pl.pallas_call(functools.partial(project_kernel, tiles), out_shape=(half,...]
    ppermute x6 -> x5, starting transfers between devices: 6.22 us -> 6.22 us  [swapped(): return lax.ppermute(value, axis, route)]
  transfers between devices with their start and end apart: 8 -> 9, of which waited for: 7 -> 7; matrix products, arithmetic and copies ran while one was open for 3% -> 1% of each run, Pallas kernels for 11% -> 9%
where the time goes in v7:
time: 33.8 us; the launch traced here: 33.7 us
  waiting for transfers between devices  13.5 us (40%)
  starting transfers between devices  11.1 us (33%)
  Pallas kernels  8.2 us (24%)
  between operations  0.71 us (2%)
    ppermute x5, waiting for transfers between devices, swapped(): return lax.ppermute(value, axis, route)  6.81 us
    ppermute x4, waiting for transfers between devices, moved(): return lax.ppermute(value, ('tm', 'inner'), route)  6.68 us
    ppermute x5, starting transfers between devices, swapped(): return lax.ppermute(value, axis, route)  6.22 us
    pallas_call x1, Pallas kernels, rebuild(): pl.pallas_call(functools.partial(rebuild_kernel, tiles), out_shape=(jax.S...  5.23 us
    ppermute x4, starting transfers between devices, moved(): return lax.ppermute(value, ('tm', 'inner'), route)  4.86 us
    pallas_call x1, Pallas kernels, project(): pl.pallas_call(functools.partial(project_kernel, tiles), out_shape=(half,...  2.97 us
  transfers between devices with their start and end apart: 9, of which 7 were waited for; matrix products, arithmetic and copies ran while one was open for 1% of the time, Pallas kernels for 9%

profile of v7, /device:TPU:0, one launch (start us, length us, event | category | flops | bytes accessed | tf_op | source)
XLA Modules:
  0.0 33.7 jit_solution(11287947769822765615)
XLA Ops:
  0.6 0.0 copy-start
  0.6 0.0 copy-start.1
  0.7 0.0 copy-start.2
  0.7 3.0 %collective-permute-start = (bf16[64,8192]{1,0:T(8,128)(2,1)}, bf16[64,8192]{1,0:T(8,128)(2,1)S(1)}, u32[]{:S(2)}, u32[]{:S(2)}) collective-permute-start(bf16[64,8192]{1,0:T(8,128)(2,1)} %bitcast.5), channel_id=1, source_target_pairs={{16,0},{17,1},{0,16},{1,17},{18,2},{19,3},{2,18},{3,19},{20,4},{21... | collective-permute-start | bytes 3145736 | tf_op jit(solution)/shard_map/ppermute | solution.py:178
  3.7 3.0 %project.1 = (f32[32,256]{1,0:T(8,128)S(1)}, f32[32,256]{1,0:T(8,128)S(1)}) custom-call(s32[1]{0:T(128)} %bitcast.1.core, bf16[64,8192]{1,0:T(8,128)(2,1)} %bitcast.6, bf16[8192,256]{1,0:T(8,128)(2,1)} %basis.1), custom_call_target="tpu_custom_call" | custom-call | tf_op jit(solution)/shard_map/project/pallas_call | solution.py:57
  6.7 0.1 collective-permute-start.1
  6.7 1.2 %collective-permute-done.1 = f32[32,256]{1,0:T(8,128)S(1)} collective-permute-done((f32[32,256]{1,0:T(8,128)S(1)}, f32[32,256]{1,0:T(8,128)S(1)}, u32[]{:S(2)}, u32[]{:S(2)}) %collective-permute-start.1) | collective-permute-done | bytes 32800 | tf_op jit(solution)/shard_map/ppermute | solution.py:168
  7.9 2.5 %collective-permute-start.4 = (f32[32,256]{1,0:T(8,128)S(1)}, f32[32,256]{1,0:T(8,128)S(1)}, u32[]{:S(2)}, u32[]{:S(2)}) collective-permute-start(f32[32,256]{1,0:T(8,128)S(1)} %add.19), channel_id=1, source_target_pairs={{6,0},{4,2},{2,4},{0,6},{14,8},{12,10},{10,12},{8,14},{7,1},{5,3},... | collective-permute-start | bytes 98312 | tf_op jit(solution)/shard_map/ppermute | solution.py:168
  10.5 0.4 %collective-permute-start.3 = (f32[32,256]{1,0:T(8,128)S(1)}, f32[32,256]{1,0:T(8,128)S(1)}, u32[]{:S(2)}, u32[]{:S(2)}) collective-permute-start(f32[32,256]{1,0:T(8,128)S(1)} %add.19), channel_id=1, source_target_pairs={{4,0},{6,2},{0,4},{2,6},{12,8},{14,10},{8,12},{10,14},{5,1},{7,3},... | collective-permute-start | bytes 98312 | tf_op jit(solution)/shard_map/ppermute | solution.py:168
  10.9 0.5 %collective-permute-start.2 = (f32[32,256]{1,0:T(8,128)S(1)}, f32[32,256]{1,0:T(8,128)S(1)}, u32[]{:S(2)}, u32[]{:S(2)}) collective-permute-start(f32[32,256]{1,0:T(8,128)S(1)} %add.19), channel_id=1, source_target_pairs={{2,0},{0,2},{6,4},{4,6},{10,8},{8,10},{14,12},{12,14},{3,1},{1,3},... | collective-permute-start | bytes 98312 | tf_op jit(solution)/shard_map/ppermute | solution.py:168
  11.4 1.3 %collective-permute-done.4 = f32[32,256]{1,0:T(8,128)S(1)} collective-permute-done((f32[32,256]{1,0:T(8,128)S(1)}, f32[32,256]{1,0:T(8,128)S(1)}, u32[]{:S(2)}, u32[]{:S(2)}) %collective-permute-start.4) | collective-permute-done | bytes 32800 | tf_op jit(solution)/shard_map/ppermute | solution.py:168
  12.7 1.6 %collective-permute-done.3 = f32[32,256]{1,0:T(8,128)S(1)} collective-permute-done((f32[32,256]{1,0:T(8,128)S(1)}, f32[32,256]{1,0:T(8,128)S(1)}, u32[]{:S(2)}, u32[]{:S(2)}) %collective-permute-start.3) | collective-permute-done | bytes 32800 | tf_op jit(solution)/shard_map/ppermute | solution.py:168
  14.4 0.4 %collective-permute-done.2 = f32[32,256]{1,0:T(8,128)S(1)} collective-permute-done((f32[32,256]{1,0:T(8,128)S(1)}, f32[32,256]{1,0:T(8,128)S(1)}, u32[]{:S(2)}, u32[]{:S(2)}) %collective-permute-start.2) | collective-permute-done | bytes 32800 | tf_op jit(solution)/shard_map/ppermute | solution.py:168
  14.8 2.7 %collective-permute-start.5 = (f32[32,256]{1,0:T(8,128)S(1)}, f32[32,256]{1,0:T(8,128)S(1)}, u32[]{:S(2)}, u32[]{:S(2)}) collective-permute-start(f32[32,256]{1,0:T(8,128)S(1)} %add_add_fusion), channel_id=1, source_target_pairs={{8,0},{10,2},{12,4},{14,6},{0,8},{2,10},{4,12},{6,14},{9,1},{11,3}... | collective-permute-start | bytes 98312 | tf_op jit(solution)/shard_map/ppermute | solution.py:168
  17.5 0.0 copy-done
  17.5 2.2 %collective-permute-done.5 = f32[32,256]{1,0:T(8,128)S(1)} collective-permute-done((f32[32,256]{1,0:T(8,128)S(1)}, f32[32,256]{1,0:T(8,128)S(1)}, u32[]{:S(2)}, u32[]{:S(2)}) %collective-permute-start.5) | collective-permute-done | bytes 32800 | tf_op jit(solution)/shard_map/ppermute | solution.py:168
  19.7 0.0 collective-permute-start.8
  19.7 0.6 %collective-permute-start.7 = (f32[32,256]{1,0:T(8,128)S(1)}, f32[32,256]{1,0:T(8,128)S(1)}, u32[]{:S(2)}, u32[]{:S(2)}) collective-permute-start(f32[32,256]{1,0:T(8,128)S(1)} %add.23.refs_2_), channel_id=1, source_target_pairs={{16,0},{17,1},{0,16},{1,17},{18,2},{19,3},{2,18},{3,19},{20,4},{21... | collective-permute-start | bytes 98312 | tf_op jit(solution)/shard_map/ppermute | solution.py:178
  20.3 1.2 %collective-permute-start.6 = (f32[32,256]{1,0:T(8,128)S(1)}, f32[32,256]{1,0:T(8,128)S(1)}, u32[]{:S(2)}, u32[]{:S(2)}) collective-permute-start(f32[32,256]{1,0:T(8,128)S(1)} %add.23.refs_2_), channel_id=1, source_target_pairs={{1,0},{0,1},{17,16},{16,17},{3,2},{2,3},{19,18},{18,19},{5,4},{4,5... | collective-permute-start | bytes 98312 | tf_op jit(solution)/shard_map/ppermute | solution.py:178
  21.6 0.1 pad_add_fusion.place
  21.7 0.1 copy.7
  21.8 5.6 %collective-permute-done.8.refs_5_ = f32[32,256]{1,0:T(8,128)S(1)} collective-permute-done((f32[32,256]{1,0:T(8,128)S(1)}, f32[32,256]{1,0:T(8,128)S(1)}, u32[]{:S(2)}, u32[]{:S(2)}) %collective-permute-start.8) | collective-permute-done | bytes 32800 | tf_op jit(solution)/shard_map/ppermute | solution.py:178
  27.4 1.1 %collective-permute-done.7.refs_4_ = f32[32,256]{1,0:T(8,128)S(1)} collective-permute-done((f32[32,256]{1,0:T(8,128)S(1)}, f32[32,256]{1,0:T(8,128)S(1)}, u32[]{:S(2)}, u32[]{:S(2)}) %collective-permute-start.7) | collective-permute-done | bytes 32800 | tf_op jit(solution)/shard_map/ppermute | solution.py:178
  28.4 0.0 collective-permute-done.6.refs_3_
  28.4 0.0 collective-permute-done.refs_1_
  28.4 0.0 copy-done.1
  28.5 0.0 copy-done.2
  28.5 5.2 %rebuild.1 = (f32[256,256]{1,0:T(8,128)}, bf16[256,8192]{1,0:T(8,128)(2,1)}) custom-call(s32[2]{0:T(128)S(1)} %pad_add_fusion.place, f32[1,256]{1,0:T(1,128)S(1)} %bitcast.9, bf16[256,256]{1,0:T(8,128)(2,1)S(1)} %bitcast.8, bf16[64,8192]{1,0:T(8,128)(2,1)S(1)} %bitcast.7, bf16[64,8192]{1,0:T(8,128)(2,1)S(1)} %collective-permute-done.refs_1_, ...), custom_call_target="tpu_custom_call" | custom-call | tf_op jit(solution)/shard_map/rebuild/pallas_call | solution.py:138
  (4 shorter events, 0.0 us)
Async XLA Ops:
  0.6 16.9 %copy-start = (bf16[256,512]{1,0:T(8,128)(2,1)S(1)}, bf16[256,512]{1,0:T(8,128)(2,1)}, u32[]{:S(2)}) copy-start(bf16[256,512]{1,0:T(8,128)(2,1)} %param.7) | copy-start | bytes 786436
  0.6 27.8 %copy-start.1 = (bf16[8192,64]{0,1:T(8,128)(2,1)S(1)}, bf16[8192,64]{0,1:T(8,128)(2,1)}, u32[]{:S(2)}) copy-start(bf16[8192,64]{0,1:T(8,128)(2,1)} %param.5) | copy-start | bytes 3145732
  0.7 27.8 %copy-start.2 = (f32[256]{0:T(256)S(1)}, f32[256]{0:T(256)}, u32[]{:S(2)}) copy-start(f32[256]{0:T(256)} %param.6) | copy-start | bytes 3076
  0.7 27.8 %collective-permute-start = (bf16[64,8192]{1,0:T(8,128)(2,1)}, bf16[64,8192]{1,0:T(8,128)(2,1)S(1)}, u32[]{:S(2)}, u32[]{:S(2)}) collective-permute-start(bf16[64,8192]{1,0:T(8,128)(2,1)} %bitcast.5), channel_id=1, source_target_pairs={{16,0},{17,1},{0,16},{1,17},{18,2},{19,3},{2,18},{3,19},{20,4},{21... | collective-permute-start | bytes 3145736 | tf_op jit(solution)/shard_map/ppermute | solution.py:178
  6.7 1.3 %collective-permute-start.1 = (f32[32,256]{1,0:T(8,128)S(1)}, f32[32,256]{1,0:T(8,128)S(1)}, u32[]{:S(2)}, u32[]{:S(2)}) collective-permute-start(f32[32,256]{1,0:T(8,128)S(1)} %get-tuple-element.5), channel_id=1, source_target_pairs={{1,0},{0,1},{3,2},{2,3},{5,4},{4,5},{7,6},{6,7},{9,8},{8,9},{11,10... | collective-permute-start | bytes 98312 | tf_op jit(solution)/shard_map/ppermute | solution.py:168
  7.9 4.8 %collective-permute-start.4 = (f32[32,256]{1,0:T(8,128)S(1)}, f32[32,256]{1,0:T(8,128)S(1)}, u32[]{:S(2)}, u32[]{:S(2)}) collective-permute-start(f32[32,256]{1,0:T(8,128)S(1)} %add.19), channel_id=1, source_target_pairs={{6,0},{4,2},{2,4},{0,6},{14,8},{12,10},{10,12},{8,14},{7,1},{5,3},... | collective-permute-start | bytes 98312 | tf_op jit(solution)/shard_map/ppermute | solution.py:168
  10.5 3.9 %collective-permute-start.3 = (f32[32,256]{1,0:T(8,128)S(1)}, f32[32,256]{1,0:T(8,128)S(1)}, u32[]{:S(2)}, u32[]{:S(2)}) collective-permute-start(f32[32,256]{1,0:T(8,128)S(1)} %add.19), channel_id=1, source_target_pairs={{4,0},{6,2},{0,4},{2,6},{12,8},{14,10},{8,12},{10,14},{5,1},{7,3},... | collective-permute-start | bytes 98312 | tf_op jit(solution)/shard_map/ppermute | solution.py:168
  10.9 3.9 %collective-permute-start.2 = (f32[32,256]{1,0:T(8,128)S(1)}, f32[32,256]{1,0:T(8,128)S(1)}, u32[]{:S(2)}, u32[]{:S(2)}) collective-permute-start(f32[32,256]{1,0:T(8,128)S(1)} %add.19), channel_id=1, source_target_pairs={{2,0},{0,2},{6,4},{4,6},{10,8},{8,10},{14,12},{12,14},{3,1},{1,3},... | collective-permute-start | bytes 98312 | tf_op jit(solution)/shard_map/ppermute | solution.py:168
  14.8 4.9 %collective-permute-start.5 = (f32[32,256]{1,0:T(8,128)S(1)}, f32[32,256]{1,0:T(8,128)S(1)}, u32[]{:S(2)}, u32[]{:S(2)}) collective-permute-start(f32[32,256]{1,0:T(8,128)S(1)} %add_add_fusion), channel_id=1, source_target_pairs={{8,0},{10,2},{12,4},{14,6},{0,8},{2,10},{4,12},{6,14},{9,1},{11,3}... | collective-permute-start | bytes 98312 | tf_op jit(solution)/shard_map/ppermute | solution.py:168
  19.7 7.6 %collective-permute-start.8 = (f32[32,256]{1,0:T(8,128)S(1)}, f32[32,256]{1,0:T(8,128)S(1)}, u32[]{:S(2)}, u32[]{:S(2)}) collective-permute-start(f32[32,256]{1,0:T(8,128)S(1)} %add.23.refs_2_), channel_id=1, source_target_pairs={{17,0},{16,1},{1,16},{0,17},{19,2},{18,3},{3,18},{2,19},{21,4},{20... | collective-permute-start | bytes 98312 | tf_op jit(solution)/shard_map/ppermute | solution.py:178
  19.7 8.7 %collective-permute-start.7 = (f32[32,256]{1,0:T(8,128)S(1)}, f32[32,256]{1,0:T(8,128)S(1)}, u32[]{:S(2)}, u32[]{:S(2)}) collective-permute-start(f32[32,256]{1,0:T(8,128)S(1)} %add.23.refs_2_), channel_id=1, source_target_pairs={{16,0},{17,1},{0,16},{1,17},{18,2},{19,3},{2,18},{3,19},{20,4},{21... | collective-permute-start | bytes 98312 | tf_op jit(solution)/shard_map/ppermute | solution.py:178
  20.3 8.1 %collective-permute-start.6 = (f32[32,256]{1,0:T(8,128)S(1)}, f32[32,256]{1,0:T(8,128)S(1)}, u32[]{:S(2)}, u32[]{:S(2)}) collective-permute-start(f32[32,256]{1,0:T(8,128)S(1)} %add.23.refs_2_), channel_id=1, source_target_pairs={{1,0},{0,1},{17,16},{16,17},{3,2},{2,3},{19,18},{18,19},{5,4},{4,5... | collective-permute-start | bytes 98312 | tf_op jit(solution)/shard_map/ppermute | solution.py:178

commit v8 on v7

--- a/solution.py
+++ b/solution.py
@@ -72,45 +72,60 @@
     )(core[None], snapshots, basis)
 
 
-def rebuild_kernel(tiles, place, energy, vectors, *refs):
-    count = (len(refs) - 10) // 3
-    held, coeffs, refs = refs[:count], refs[count : 3 * count], refs[3 * count :]
+def started(copies):
+    for copy in copies:
+        copy.start()
+    return copies
+
+
+def waited(copies):
+    for copy in copies:
+        copy.wait()
+
+
+def gathered(held, fields, arrived):
+    rows = held[0].shape[0]
+    return [
+        pltpu.make_async_copy(block, fields.at[pl.ds(k * rows, rows)], arrived.at[k])
+        for k, block in enumerate(held)
+    ]
+
+
+def rebuild_kernel(tiles, place, energy, vectors, coeffs, *refs):
+    count = coeffs.shape[0] // 2
+    held, refs = refs[:count], refs[count:]
     operator, modes, fields, known, turned, scaled, made, square, arrived, sent = refs
-    hours, cells = held[0].shape
-    half, tile = hours // 2, cells // tiles
-    spans = [pl.ds(i * tile, tile) for i in range(tiles)]
-    first = [pl.multiple_of(lax.rem(place[0] + k, count) * hours, hours) for k in range(count)]
-    inputs = [pltpu.make_async_copy(vectors, turned, arrived.at[tiles, 0])]
-    for n, block in enumerate(coeffs):
-        at = pl.multiple_of(first[n // 2] + lax.rem(place[1] + n % 2, 2) * half, half)
-        inputs.append(
-            pltpu.make_async_copy(
-                block, known.at[pl.ds(at, half)], arrived.at[tiles + 1 + n % 2, n // 2]
-            )
-        )
-    blocks = [
+    half = coeffs.shape[1]
+    inputs = started(
         [
-            pltpu.make_async_copy(
-                block.at[:, span], fields.at[pl.ds(k * hours, hours), span], arrived.at[i, k]
-            )
-            for k, block in enumerate(held)
+            pltpu.make_async_copy(coeffs, known, arrived.at[len(held)]),
+            pltpu.make_async_copy(vectors, turned, arrived.at[len(held) + 1]),
         ]
-        for i, span in enumerate(spans)
+    )
+    blocks = started(gathered(held, fields, arrived))
+    waited(inputs)
+    order = [
+        2 * lax.rem(count + block - place[0], count) + lax.rem(2 + core - place[1], 2)
+        for block in range(count)
+        for core in range(2)
     ]
-    for copy in inputs + sum(blocks, []):
-        copy.start()
-    for copy in inputs:
-        copy.wait()
-    every = known[...]
+    every = jnp.concatenate([known[at] for at in order], axis=0)
     hour = lax.broadcasted_iota(jnp.int32, every.shape, 0)
     scaled[...] = jnp.where(hour == 0, 0.0, pltpu.roll(every, 1, 0)) * energy[...]
-    ordered = jnp.concatenate([scaled[pl.ds(at, hours)] for at in first], axis=0)
+    first = [lax.rem(place[0] + k, count) * 2 * half for k in range(count)]
+    ordered = jnp.concatenate(
+        [scaled[pl.ds(pl.multiple_of(at, half), 2 * half)] for at in first], axis=0
+    )
     high, low = in_parts(ordered)
     weights = (product(turned[...], high, LAST) + product(turned[...], low, LAST)).astype(
         jnp.bfloat16
     )
+
+    waited(blocks)
+    width = fields.shape[1] // tiles
     outgoing = []
-    for i, span in enumerate(spans):
+    for i in range(tiles):
+        span = pl.ds(i * width, width)
         if i == tiles - 1:
             high, low = in_parts(every)
             s_high, s_low = in_parts(scaled[...])
@@ -119,48 +134,44 @@
                 + product(high, s_low, FIRST)
                 + product(low, s_high, FIRST)
             )
-            outgoing.append(pltpu.make_async_copy(square, operator, sent.at[tiles]))
-            outgoing[-1].start()
-        for copy in blocks[i]:
-            copy.wait()
+            outgoing += started([pltpu.make_async_copy(square, operator, sent.at[tiles])])
         made[:, span] = product(weights, fields[:, span], ROWS).astype(made.dtype)
-        outgoing.append(pltpu.make_async_copy(made.at[:, span], modes.at[:, span], sent.at[i]))
-        outgoing[-1].start()
-    for copy in outgoing:
-        copy.wait()
-
-
-def rebuild(place, energy, vectors, held, coeffs, tiles):
-    hours, cells = held[0].shape
-    total, rank = len(held) * hours, coeffs[0].shape[1]
-    modes = vectors.shape[0]
-    anywhere = pl.BlockSpec(memory_space=pl.ANY)
+        copy = pltpu.make_async_copy(made.at[:, span], modes.at[:, span], sent.at[i])
+        outgoing += started([copy])
+    waited(outgoing)
+
+
+ANYWHERE = pl.BlockSpec(memory_space=pl.ANY)
+IN_VMEM = pl.BlockSpec(memory_space=pltpu.VMEM)
+
+
+def rebuild(place, energy, vectors, coeffs, held, tiles):
+    cells = held[0].shape[1]
+    blocks, half, rank = coeffs.shape
+    hours, modes = blocks * half, vectors.shape[0]
     return pl.pallas_call(
         functools.partial(rebuild_kernel, tiles),
         out_shape=(
             jax.ShapeDtypeStruct((rank, rank), jnp.float32),
             jax.ShapeDtypeStruct((modes, cells), jnp.bfloat16),
         ),
-        in_specs=[
-            pl.BlockSpec(memory_space=pltpu.SMEM),
-            pl.BlockSpec(memory_space=pltpu.VMEM),
-        ]
-        + [anywhere] * (1 + 3 * len(held)),
-        out_specs=(anywhere, anywhere),
+        in_specs=[pl.BlockSpec(memory_space=pltpu.SMEM), IN_VMEM]
+        + [ANYWHERE] * (2 + len(held)),
+        out_specs=(ANYWHERE, ANYWHERE),
         scratch_shapes=[
-            pltpu.VMEM((total, cells), held[0].dtype),
-            pltpu.VMEM((total, rank), jnp.float32),
+            pltpu.VMEM((hours, cells), jnp.bfloat16),
+            pltpu.VMEM(coeffs.shape, jnp.float32),
             pltpu.VMEM(vectors.shape, vectors.dtype),
-            pltpu.VMEM((total, rank), jnp.float32),
+            pltpu.VMEM((hours, rank), jnp.float32),
             pltpu.VMEM((modes, cells), jnp.bfloat16),
             pltpu.VMEM((rank, rank), jnp.float32),
-            pltpu.SemaphoreType.DMA((tiles + 3, len(held))),
+            pltpu.SemaphoreType.DMA((len(held) + 2,)),
             pltpu.SemaphoreType.DMA((tiles + 1,)),
         ],
         compiler_params=pltpu.CompilerParams(vmem_limit_bytes=40 * 2**20),
         cost_estimate=FREE,
         name="rebuild",
-    )(place, energy[None, :], vectors, *held, *coeffs)
+    )(place, energy[None, :], vectors, coeffs, *held)
 
 
 def swapped(value, axis, bit):
@@ -202,7 +213,8 @@
 
     rows = eigen_vectors.shape[1] // tm
     vectors = lax.dynamic_slice_in_dim(eigen_vectors, me * rows, rows, 1)
-    return rebuild(jnp.stack([me, core]), inverse_energy, vectors.T, held, coeffs, 8)
+    place = jnp.stack([me, core])
+    return rebuild(place, inverse_energy, vectors.T, jnp.stack(coeffs), held, 4)
 
 
 def solution(mesh):

time: 33.8 us -> 32.6 us (0.964)
  Pallas kernels: 8.2 us -> 6.96 us
    pallas_call x1, Pallas kernels: 5.23 us -> 3.98 us  [rebuild(): pl.pallas_call(functools.partial(rebuild_kernel, tiles), out_shape=(jax.S...]
where the time goes in v8:
time: 32.6 us; the launch traced here: 32.5 us
  waiting for transfers between devices  13.5 us (41%)
  starting transfers between devices  11.1 us (34%)
  Pallas kernels  6.96 us (21%)
  between operations  0.73 us (2%)
    ppermute x5, waiting for transfers between devices, swapped(): return lax.ppermute(value, axis, route)  6.81 us
    ppermute x4, waiting for transfers between devices, moved(): return lax.ppermute(value, ('tm', 'inner'), route)  6.68 us
    ppermute x5, starting transfers between devices, swapped(): return lax.ppermute(value, axis, route)  6.22 us
    ppermute x4, starting transfers between devices, moved(): return lax.ppermute(value, ('tm', 'inner'), route)  4.86 us
    pallas_call x1, Pallas kernels, rebuild(): pl.pallas_call(functools.partial(rebuild_kernel, tiles), out_shape=(jax.S...  3.98 us
    pallas_call x1, Pallas kernels, project(): pl.pallas_call(functools.partial(project_kernel, tiles), out_shape=(half,...  2.97 us
  transfers between devices with their start and end apart: 9, of which 7 were waited for; matrix products, arithmetic and copies ran while one was open for 1% of the time, Pallas kernels for 9%

profile of v8, /device:TPU:0, one launch (start us, length us, event | category | flops | bytes accessed | tf_op | source)
XLA Modules:
  0.0 32.5 jit_solution(1601931077622065416)
XLA Ops:
  0.6 0.0 copy-start
  0.6 0.0 copy-start.1
  0.7 0.0 copy-start.2
  0.7 3.0 %collective-permute-start.8 = (bf16[64,8192]{1,0:T(8,128)(2,1)}, bf16[64,8192]{1,0:T(8,128)(2,1)S(1)}, u32[]{:S(2)}, u32[]{:S(2)}) collective-permute-start(bf16[64,8192]{1,0:T(8,128)(2,1)} %bitcast.9), channel_id=1, source_target_pairs={{16,0},{17,1},{0,16},{1,17},{18,2},{19,3},{2,18},{3,19},{20,4},{21... | collective-permute-start | bytes 3145736 | tf_op jit(solution)/shard_map/ppermute | solution.py:189
  3.7 3.0 %project.1 = (f32[32,256]{1,0:T(8,128)S(1)}, f32[32,256]{1,0:T(8,128)S(1)}) custom-call(s32[1]{0:T(128)} %bitcast.1.core, bf16[64,8192]{1,0:T(8,128)(2,1)} %bitcast.10, bf16[8192,256]{1,0:T(8,128)(2,1)} %basis.1), custom_call_target="tpu_custom_call" | custom-call | tf_op jit(solution)/shard_map/project/pallas_call | solution.py:57
  6.7 0.1 collective-permute-start
  6.7 1.2 %collective-permute-done = f32[32,256]{1,0:T(8,128)S(1)} collective-permute-done((f32[32,256]{1,0:T(8,128)S(1)}, f32[32,256]{1,0:T(8,128)S(1)}, u32[]{:S(2)}, u32[]{:S(2)}) %collective-permute-start) | collective-permute-done | bytes 32800 | tf_op jit(solution)/shard_map/ppermute | solution.py:179
  7.9 2.5 %collective-permute-start.3 = (f32[32,256]{1,0:T(8,128)S(1)}, f32[32,256]{1,0:T(8,128)S(1)}, u32[]{:S(2)}, u32[]{:S(2)}) collective-permute-start(f32[32,256]{1,0:T(8,128)S(1)} %add.19), channel_id=1, source_target_pairs={{6,0},{4,2},{2,4},{0,6},{14,8},{12,10},{10,12},{8,14},{7,1},{5,3},... | collective-permute-start | bytes 98312 | tf_op jit(solution)/shard_map/ppermute | solution.py:179
  10.5 0.4 %collective-permute-start.2 = (f32[32,256]{1,0:T(8,128)S(1)}, f32[32,256]{1,0:T(8,128)S(1)}, u32[]{:S(2)}, u32[]{:S(2)}) collective-permute-start(f32[32,256]{1,0:T(8,128)S(1)} %add.19), channel_id=1, source_target_pairs={{4,0},{6,2},{0,4},{2,6},{12,8},{14,10},{8,12},{10,14},{5,1},{7,3},... | collective-permute-start | bytes 98312 | tf_op jit(solution)/shard_map/ppermute | solution.py:179
  10.9 0.5 %collective-permute-start.1 = (f32[32,256]{1,0:T(8,128)S(1)}, f32[32,256]{1,0:T(8,128)S(1)}, u32[]{:S(2)}, u32[]{:S(2)}) collective-permute-start(f32[32,256]{1,0:T(8,128)S(1)} %add.19), channel_id=1, source_target_pairs={{2,0},{0,2},{6,4},{4,6},{10,8},{8,10},{14,12},{12,14},{3,1},{1,3},... | collective-permute-start | bytes 98312 | tf_op jit(solution)/shard_map/ppermute | solution.py:179
  11.4 1.3 %collective-permute-done.3 = f32[32,256]{1,0:T(8,128)S(1)} collective-permute-done((f32[32,256]{1,0:T(8,128)S(1)}, f32[32,256]{1,0:T(8,128)S(1)}, u32[]{:S(2)}, u32[]{:S(2)}) %collective-permute-start.3) | collective-permute-done | bytes 32800 | tf_op jit(solution)/shard_map/ppermute | solution.py:179
  12.7 1.6 %collective-permute-done.2 = f32[32,256]{1,0:T(8,128)S(1)} collective-permute-done((f32[32,256]{1,0:T(8,128)S(1)}, f32[32,256]{1,0:T(8,128)S(1)}, u32[]{:S(2)}, u32[]{:S(2)}) %collective-permute-start.2) | collective-permute-done | bytes 32800 | tf_op jit(solution)/shard_map/ppermute | solution.py:179
  14.4 0.4 %collective-permute-done.1 = f32[32,256]{1,0:T(8,128)S(1)} collective-permute-done((f32[32,256]{1,0:T(8,128)S(1)}, f32[32,256]{1,0:T(8,128)S(1)}, u32[]{:S(2)}, u32[]{:S(2)}) %collective-permute-start.1) | collective-permute-done | bytes 32800 | tf_op jit(solution)/shard_map/ppermute | solution.py:179
  14.8 2.7 %collective-permute-start.4 = (f32[32,256]{1,0:T(8,128)S(1)}, f32[32,256]{1,0:T(8,128)S(1)}, u32[]{:S(2)}, u32[]{:S(2)}) collective-permute-start(f32[32,256]{1,0:T(8,128)S(1)} %add_add_fusion), channel_id=1, source_target_pairs={{8,0},{10,2},{12,4},{14,6},{0,8},{2,10},{4,12},{6,14},{9,1},{11,3}... | collective-permute-start | bytes 98312 | tf_op jit(solution)/shard_map/ppermute | solution.py:179
  17.5 0.0 copy-done
  17.5 2.2 %collective-permute-done.4 = f32[32,256]{1,0:T(8,128)S(1)} collective-permute-done((f32[32,256]{1,0:T(8,128)S(1)}, f32[32,256]{1,0:T(8,128)S(1)}, u32[]{:S(2)}, u32[]{:S(2)}) %collective-permute-start.4) | collective-permute-done | bytes 32800 | tf_op jit(solution)/shard_map/ppermute | solution.py:179
  19.7 0.0 collective-permute-start.7
  19.7 0.6 %collective-permute-start.6 = (f32[32,256]{1,0:T(8,128)S(1)}, f32[32,256]{1,0:T(8,128)S(1)}, u32[]{:S(2)}, u32[]{:S(2)}) collective-permute-start(f32[32,256]{1,0:T(8,128)S(1)} %add.23), channel_id=1, source_target_pairs={{16,0},{17,1},{0,16},{1,17},{18,2},{19,3},{2,18},{3,19},{20,4},{21... | collective-permute-start | bytes 98312 | tf_op jit(solution)/shard_map/ppermute | solution.py:189
  20.3 1.2 %collective-permute-start.5 = (f32[32,256]{1,0:T(8,128)S(1)}, f32[32,256]{1,0:T(8,128)S(1)}, u32[]{:S(2)}, u32[]{:S(2)}) collective-permute-start(f32[32,256]{1,0:T(8,128)S(1)} %add.23), channel_id=1, source_target_pairs={{1,0},{0,1},{17,16},{16,17},{3,2},{2,3},{19,18},{18,19},{5,4},{4,5... | collective-permute-start | bytes 98312 | tf_op jit(solution)/shard_map/ppermute | solution.py:189
  21.6 0.1 pad_add_fusion.place
  21.7 0.1 copy.7
  21.8 5.6 %collective-permute-done.7 = f32[32,256]{1,0:T(8,128)S(1)} collective-permute-done((f32[32,256]{1,0:T(8,128)S(1)}, f32[32,256]{1,0:T(8,128)S(1)}, u32[]{:S(2)}, u32[]{:S(2)}) %collective-permute-start.7) | collective-permute-done | bytes 32800 | tf_op jit(solution)/shard_map/ppermute | solution.py:189
  27.4 1.1 %collective-permute-done.6 = f32[32,256]{1,0:T(8,128)S(1)} collective-permute-done((f32[32,256]{1,0:T(8,128)S(1)}, f32[32,256]{1,0:T(8,128)S(1)}, u32[]{:S(2)}, u32[]{:S(2)}) %collective-permute-start.6) | collective-permute-done | bytes 32800 | tf_op jit(solution)/shard_map/ppermute | solution.py:189
  28.4 0.0 collective-permute-done.5
  28.5 0.0 collective-permute-done.8.refs_1_
  28.5 0.0 copy-done.1
  28.5 0.0 copy-done.2
  28.5 4.0 %rebuild.1 = (f32[256,256]{1,0:T(8,128)}, bf16[256,8192]{1,0:T(8,128)(2,1)}) custom-call(s32[2]{0:T(128)S(1)} %pad_add_fusion.place, f32[1,256]{1,0:T(1,128)S(1)} %bitcast.13, bf16[256,256]{1,0:T(8,128)(2,1)S(1)} %bitcast.12, f32[4,32,256]{2,1,0:T(8,128)S(1)} %pad_maximum_fusion.coeffs, bf16[64,8192]{1,0:T(8,128)(2,1)S(1)} %bitcast.11, ...), custom_call_target="tpu_custom_call" | custom-call | tf_op jit(solution)/shard_map/rebuild/pallas_call | solution.py:152
  (5 shorter events, 0.0 us)
Async XLA Ops:
  0.6 16.9 %copy-start = (bf16[256,512]{1,0:T(8,128)(2,1)S(1)}, bf16[256,512]{1,0:T(8,128)(2,1)}, u32[]{:S(2)}) copy-start(bf16[256,512]{1,0:T(8,128)(2,1)} %param.7) | copy-start | bytes 786436
  0.6 27.8 %copy-start.1 = (bf16[8192,64]{0,1:T(8,128)(2,1)S(1)}, bf16[8192,64]{0,1:T(8,128)(2,1)}, u32[]{:S(2)}) copy-start(bf16[8192,64]{0,1:T(8,128)(2,1)} %param.5) | copy-start | bytes 3145732
  0.7 27.8 %copy-start.2 = (f32[256]{0:T(256)S(1)}, f32[256]{0:T(256)}, u32[]{:S(2)}) copy-start(f32[256]{0:T(256)} %param.6) | copy-start | bytes 3076
  0.7 27.8 %collective-permute-start.8 = (bf16[64,8192]{1,0:T(8,128)(2,1)}, bf16[64,8192]{1,0:T(8,128)(2,1)S(1)}, u32[]{:S(2)}, u32[]{:S(2)}) collective-permute-start(bf16[64,8192]{1,0:T(8,128)(2,1)} %bitcast.9), channel_id=1, source_target_pairs={{16,0},{17,1},{0,16},{1,17},{18,2},{19,3},{2,18},{3,19},{20,4},{21... | collective-permute-start | bytes 3145736 | tf_op jit(solution)/shard_map/ppermute | solution.py:189
  6.7 1.3 %collective-permute-start = (f32[32,256]{1,0:T(8,128)S(1)}, f32[32,256]{1,0:T(8,128)S(1)}, u32[]{:S(2)}, u32[]{:S(2)}) collective-permute-start(f32[32,256]{1,0:T(8,128)S(1)} %get-tuple-element.5), channel_id=1, source_target_pairs={{1,0},{0,1},{3,2},{2,3},{5,4},{4,5},{7,6},{6,7},{9,8},{8,9},{11,10... | collective-permute-start | bytes 98312 | tf_op jit(solution)/shard_map/ppermute | solution.py:179
  7.9 4.8 %collective-permute-start.3 = (f32[32,256]{1,0:T(8,128)S(1)}, f32[32,256]{1,0:T(8,128)S(1)}, u32[]{:S(2)}, u32[]{:S(2)}) collective-permute-start(f32[32,256]{1,0:T(8,128)S(1)} %add.19), channel_id=1, source_target_pairs={{6,0},{4,2},{2,4},{0,6},{14,8},{12,10},{10,12},{8,14},{7,1},{5,3},... | collective-permute-start | bytes 98312 | tf_op jit(solution)/shard_map/ppermute | solution.py:179
  10.5 3.9 %collective-permute-start.2 = (f32[32,256]{1,0:T(8,128)S(1)}, f32[32,256]{1,0:T(8,128)S(1)}, u32[]{:S(2)}, u32[]{:S(2)}) collective-permute-start(f32[32,256]{1,0:T(8,128)S(1)} %add.19), channel_id=1, source_target_pairs={{4,0},{6,2},{0,4},{2,6},{12,8},{14,10},{8,12},{10,14},{5,1},{7,3},... | collective-permute-start | bytes 98312 | tf_op jit(solution)/shard_map/ppermute | solution.py:179
  10.9 3.9 %collective-permute-start.1 = (f32[32,256]{1,0:T(8,128)S(1)}, f32[32,256]{1,0:T(8,128)S(1)}, u32[]{:S(2)}, u32[]{:S(2)}) collective-permute-start(f32[32,256]{1,0:T(8,128)S(1)} %add.19), channel_id=1, source_target_pairs={{2,0},{0,2},{6,4},{4,6},{10,8},{8,10},{14,12},{12,14},{3,1},{1,3},... | collective-permute-start | bytes 98312 | tf_op jit(solution)/shard_map/ppermute | solution.py:179
  14.8 4.9 %collective-permute-start.4 = (f32[32,256]{1,0:T(8,128)S(1)}, f32[32,256]{1,0:T(8,128)S(1)}, u32[]{:S(2)}, u32[]{:S(2)}) collective-permute-start(f32[32,256]{1,0:T(8,128)S(1)} %add_add_fusion), channel_id=1, source_target_pairs={{8,0},{10,2},{12,4},{14,6},{0,8},{2,10},{4,12},{6,14},{9,1},{11,3}... | collective-permute-start | bytes 98312 | tf_op jit(solution)/shard_map/ppermute | solution.py:179
  19.7 7.6 %collective-permute-start.7 = (f32[32,256]{1,0:T(8,128)S(1)}, f32[32,256]{1,0:T(8,128)S(1)}, u32[]{:S(2)}, u32[]{:S(2)}) collective-permute-start(f32[32,256]{1,0:T(8,128)S(1)} %add.23), channel_id=1, source_target_pairs={{17,0},{16,1},{1,16},{0,17},{19,2},{18,3},{3,18},{2,19},{21,4},{20... | collective-permute-start | bytes 98312 | tf_op jit(solution)/shard_map/ppermute | solution.py:189
  19.7 8.7 %collective-permute-start.6 = (f32[32,256]{1,0:T(8,128)S(1)}, f32[32,256]{1,0:T(8,128)S(1)}, u32[]{:S(2)}, u32[]{:S(2)}) collective-permute-start(f32[32,256]{1,0:T(8,128)S(1)} %add.23), channel_id=1, source_target_pairs={{16,0},{17,1},{0,16},{1,17},{18,2},{19,3},{2,18},{3,19},{20,4},{21... | collective-permute-start | bytes 98312 | tf_op jit(solution)/shard_map/ppermute | solution.py:189
  20.3 8.1 %collective-permute-start.5 = (f32[32,256]{1,0:T(8,128)S(1)}, f32[32,256]{1,0:T(8,128)S(1)}, u32[]{:S(2)}, u32[]{:S(2)}) collective-permute-start(f32[32,256]{1,0:T(8,128)S(1)} %add.23), channel_id=1, source_target_pairs={{1,0},{0,1},{17,16},{16,17},{3,2},{2,3},{19,18},{18,19},{5,4},{4,5... | collective-permute-start | bytes 98312 | tf_op jit(solution)/shard_map/ppermute | solution.py:189

commit v9 on v8

--- a/solution.py
+++ b/solution.py
@@ -11,6 +11,7 @@
 FIRST = (((0,), (0,)), ((), ()))
 LAST = (((1,), (1,)), ((), ()))
 FREE = pl.CostEstimate(flops=0, bytes_accessed=0, transcendentals=0)
+COST_A = pl.CostEstimate(flops=6 * 10**9, bytes_accessed=0, transcendentals=0)
 
 
 def in_parts(value):
@@ -83,26 +84,47 @@
         copy.wait()
 
 
-def gathered(held, fields, arrived):
-    rows = held[0].shape[0]
-    return [
-        pltpu.make_async_copy(block, fields.at[pl.ds(k * rows, rows)], arrived.at[k])
-        for k, block in enumerate(held)
-    ]
-
-
-def rebuild_kernel(tiles, place, energy, vectors, coeffs, *refs):
+def gathered(held, fields, begin, arrived):
+    width = fields.shape[1]
+    copies, row = [], 0
+    for n, (block, offset) in enumerate(held):
+        rows = block.shape[0]
+        copies.append(
+            pltpu.make_async_copy(
+                block.at[:, pl.ds(begin - offset, width)],
+                fields.at[pl.ds(row, rows)],
+                arrived.at[n],
+            )
+        )
+        row += rows
+    return copies
+
+
+def rebuilt(weights, fields, made, modes, begin, tiles, sent, between):
+    width = fields.shape[1] // tiles
+    copies = []
+    for i in range(tiles):
+        span = pl.ds(i * width, width)
+        if i == tiles - 1:
+            copies += between()
+        made[:, span] = product(weights, fields[:, span], ROWS).astype(made.dtype)
+        target = modes.at[:, pl.ds(begin + i * width, width)]
+        copies += started([pltpu.make_async_copy(made.at[:, span], target, sent.at[i])])
+    return copies
+
+
+def first_kernel(offsets, tiles, place, energy, vectors, coeffs, *refs):
+    held, refs = refs[: len(offsets)], refs[len(offsets) :]
+    operator, modes, weights, fields, known, turned, scaled, made, square, arrived, sent = refs
+    half = coeffs.shape[1]
     count = coeffs.shape[0] // 2
-    held, refs = refs[:count], refs[count:]
-    operator, modes, fields, known, turned, scaled, made, square, arrived, sent = refs
-    half = coeffs.shape[1]
     inputs = started(
         [
             pltpu.make_async_copy(coeffs, known, arrived.at[len(held)]),
             pltpu.make_async_copy(vectors, turned, arrived.at[len(held) + 1]),
         ]
     )
-    blocks = started(gathered(held, fields, arrived))
+    blocks = started(gathered(list(zip(held, offsets)), fields, 0, arrived))
     waited(inputs)
     order = [
         2 * lax.rem(count + block - place[0], count) + lax.rem(2 + core - place[1], 2)
@@ -117,61 +139,82 @@
         [scaled[pl.ds(pl.multiple_of(at, half), 2 * half)] for at in first], axis=0
     )
     high, low = in_parts(ordered)
-    weights = (product(turned[...], high, LAST) + product(turned[...], low, LAST)).astype(
+    weights[...] = (product(turned[...], high, LAST) + product(turned[...], low, LAST)).astype(
         jnp.bfloat16
     )
 
+    def rest():
+        high, low = in_parts(every)
+        s_high, s_low = in_parts(scaled[...])
+        square[...] = (
+            product(high, s_high, FIRST)
+            + product(high, s_low, FIRST)
+            + product(low, s_high, FIRST)
+        )
+        return started([pltpu.make_async_copy(square, operator, sent.at[tiles])])
+
     waited(blocks)
-    width = fields.shape[1] // tiles
-    outgoing = []
-    for i in range(tiles):
-        span = pl.ds(i * width, width)
-        if i == tiles - 1:
-            high, low = in_parts(every)
-            s_high, s_low = in_parts(scaled[...])
-            square[...] = (
-                product(high, s_high, FIRST)
-                + product(high, s_low, FIRST)
-                + product(low, s_high, FIRST)
-            )
-            outgoing += started([pltpu.make_async_copy(square, operator, sent.at[tiles])])
-        made[:, span] = product(weights, fields[:, span], ROWS).astype(made.dtype)
-        copy = pltpu.make_async_copy(made.at[:, span], modes.at[:, span], sent.at[i])
-        outgoing += started([copy])
-    waited(outgoing)
+    waited(rebuilt(weights[...], fields, made, modes, 0, tiles, sent, rest))
+
+
+def last_kernel(offsets, begin, tiles, weights, *refs):
+    held, refs = refs[: len(offsets)], refs[len(offsets) :]
+    _, modes, fields, made, arrived, sent = refs
+    waited(started(gathered(list(zip(held, offsets)), fields, begin, arrived)))
+    waited(rebuilt(weights[...], fields, made, modes, begin, tiles, sent, list))
 
 
 ANYWHERE = pl.BlockSpec(memory_space=pl.ANY)
 IN_VMEM = pl.BlockSpec(memory_space=pltpu.VMEM)
 
 
-def rebuild(place, energy, vectors, coeffs, held, tiles):
-    cells = held[0].shape[1]
+def rebuild_first(place, energy, vectors, coeffs, held, cells, width, tiles):
     blocks, half, rank = coeffs.shape
     hours, modes = blocks * half, vectors.shape[0]
     return pl.pallas_call(
-        functools.partial(rebuild_kernel, tiles),
+        functools.partial(first_kernel, [0] * len(held), tiles),
         out_shape=(
             jax.ShapeDtypeStruct((rank, rank), jnp.float32),
             jax.ShapeDtypeStruct((modes, cells), jnp.bfloat16),
+            jax.ShapeDtypeStruct((modes, hours), jnp.bfloat16),
         ),
         in_specs=[pl.BlockSpec(memory_space=pltpu.SMEM), IN_VMEM]
         + [ANYWHERE] * (2 + len(held)),
-        out_specs=(ANYWHERE, ANYWHERE),
+        out_specs=(ANYWHERE, ANYWHERE, IN_VMEM),
         scratch_shapes=[
-            pltpu.VMEM((hours, cells), jnp.bfloat16),
+            pltpu.VMEM((hours, width), jnp.bfloat16),
             pltpu.VMEM(coeffs.shape, jnp.float32),
             pltpu.VMEM(vectors.shape, vectors.dtype),
             pltpu.VMEM((hours, rank), jnp.float32),
-            pltpu.VMEM((modes, cells), jnp.bfloat16),
+            pltpu.VMEM((modes, width), jnp.bfloat16),
             pltpu.VMEM((rank, rank), jnp.float32),
             pltpu.SemaphoreType.DMA((len(held) + 2,)),
             pltpu.SemaphoreType.DMA((tiles + 1,)),
         ],
         compiler_params=pltpu.CompilerParams(vmem_limit_bytes=40 * 2**20),
+        cost_estimate=COST_A,
+        name="rebuild_first",
+    )(place, energy[None, :], vectors, coeffs, *held)
+
+
+def rebuild_last(weights, held, offsets, modes, begin, tiles):
+    width = modes.shape[1] - begin
+    return pl.pallas_call(
+        functools.partial(last_kernel, offsets, begin, tiles),
+        out_shape=jax.ShapeDtypeStruct(modes.shape, modes.dtype),
+        in_specs=[IN_VMEM] + [ANYWHERE] * (len(held) + 1),
+        out_specs=ANYWHERE,
+        scratch_shapes=[
+            pltpu.VMEM((weights.shape[1], width), jnp.bfloat16),
+            pltpu.VMEM((modes.shape[0], width), jnp.bfloat16),
+            pltpu.SemaphoreType.DMA((len(held),)),
+            pltpu.SemaphoreType.DMA((tiles,)),
+        ],
+        input_output_aliases={1 + len(held): 0},
+        compiler_params=pltpu.CompilerParams(vmem_limit_bytes=40 * 2**20),
         cost_estimate=FREE,
-        name="rebuild",
-    )(place, energy[None, :], vectors, coeffs, *held)
+        name="rebuild_last",
+    )(weights, *held, modes)
 
 
 def swapped(value, axis, bit):
@@ -194,7 +237,13 @@
     me, core = lax.axis_index("tm"), lax.axis_index("inner")
     fields = snapshots.T
 
-    held = [fields] + [moved(fields, k, 0) for k in range(1, tm)]
+    cells = fields.shape[1]
+    begin = cells // 4 * 3
+
+    first, last, offsets = [fields], [fields], [0]
+    for k in range(1, tm):
+        first.append(moved(fields[:, :begin], k, 0))
+        offsets.append(begin)
 
     kept, given = project(core, fields, eof_basis, 8)
     mine = kept + swapped(given, "inner", 1)
@@ -207,6 +256,8 @@
         else:
             mine = mine + near
         bit *= 4
+    mine, rest = lax.optimization_barrier((mine, fields[:, begin:]))
+    last += [moved(rest, k, 0) for k in range(1, tm)]
     coeffs = [mine, moved(mine, 0, 1)]
     for k in range(1, tm):
         coeffs += [moved(mine, k, 0), moved(mine, k, 1)]
@@ -214,7 +265,10 @@
     rows = eigen_vectors.shape[1] // tm
     vectors = lax.dynamic_slice_in_dim(eigen_vectors, me * rows, rows, 1)
     place = jnp.stack([me, core])
-    return rebuild(place, inverse_energy, vectors.T, jnp.stack(coeffs), held, 4)
+    operator, modes, weights = rebuild_first(
+        place, inverse_energy, vectors.T, jnp.stack(coeffs), first, cells, begin, 3
+    )
+    return operator, rebuild_last(weights, last, offsets, modes, begin, 2)
 
 
 def solution(mesh):

time: 32.6 us -> 32.8 us (level)
  waiting for transfers between devices: 13.5 us -> 10.8 us
  local copies, waits for them, and re-layouts: 0.12 us -> 1.43 us
  Pallas kernels: 6.96 us -> 7.91 us
  starting transfers between devices: 11.1 us -> 11.7 us
    ppermute x4 -> x5, waiting for transfers between devices: 6.68 us -> 4.03 us  [moved(): return lax.ppermute(value, ('tm', 'inner'), route)]
    slice x0 -> x2, local copies, waits for them, and re-layouts: none -> 1.3 us  [the longest x1 1.28 us: per_device(): first.append(moved(fields[:, :begin], k, 0))]
    pallas_call x1 -> x2, Pallas kernels: 3.98 us -> 4.93 us  [the longest x1 3.6 us: rebuild_first(): pl.pallas_call(functools.partial(first_kernel, [0] * len(held), tiles), o...]
    ppermute x4 -> x5, starting transfers between devices: 4.86 us -> 5.46 us  [moved(): return lax.ppermute(value, ('tm', 'inner'), route)]
  transfers between devices with their start and end apart: 9 -> 10, of which waited for: 7 -> 8; matrix products, arithmetic and copies ran while one was open for 1% -> 1% of each run, Pallas kernels for 9% -> 20%
where the time goes in v9:
time: 32.8 us; the launch traced here: 32.7 us
  starting transfers between devices  11.7 us (36%)
  waiting for transfers between devices  10.8 us (33%)
  Pallas kernels  7.91 us (24%)
  local copies, waits for them, and re-layouts  1.43 us (4%)
  between operations  0.75 us (2%)
    ppermute x5, waiting for transfers between devices, swapped(): return lax.ppermute(value, axis, route)  6.77 us
    ppermute x5, starting transfers between devices, swapped(): return lax.ppermute(value, axis, route)  6.22 us
    ppermute x5, starting transfers between devices, moved(): return lax.ppermute(value, ('tm', 'inner'), route)  5.46 us
    ppermute x5, waiting for transfers between devices, moved(): return lax.ppermute(value, ('tm', 'inner'), route)  4.03 us
    pallas_call x1, Pallas kernels, rebuild_first(): pl.pallas_call(functools.partial(first_kernel, [0] * len(held), tiles), o...  3.6 us
    pallas_call x1, Pallas kernels, project(): pl.pallas_call(functools.partial(project_kernel, tiles), out_shape=(half,...  2.98 us
    pallas_call x1, Pallas kernels, rebuild_last(): pl.pallas_call(functools.partial(last_kernel, offsets, begin, tiles), out...  1.32 us
    slice x1, local copies, waits for them, and re-layouts, per_device(): first.append(moved(fields[:, :begin], k, 0))  1.28 us
  transfers between devices with their start and end apart: 10, of which 8 were waited for; matrix products, arithmetic and copies ran while one was open for 1% of the time, Pallas kernels for 20%

profile of v9, /device:TPU:0, one launch (start us, length us, event | category | flops | bytes accessed | tf_op | source)
XLA Modules:
  0.0 32.7 jit_solution(15155479800414105809)
XLA Ops:
  0.6 0.0 copy-start
  0.6 0.0 copy-start.1
  0.7 0.0 copy-start.2
  0.7 1.3 %slice.9 = bf16[64,6144]{1,0:T(8,128)(2,1)S(1)} slice(bf16[64,8192]{1,0:T(8,128)(2,1)} %bitcast.9), slice={[0:64], [0:6144]} | slice | bytes 1572864 | tf_op jit(solution)/shard_map/slice | solution.py:245
  2.0 3.0 %collective-permute-start.8 = (bf16[64,6144]{1,0:T(8,128)(2,1)S(1)}, bf16[64,6144]{1,0:T(8,128)(2,1)S(1)}, u32[]{:S(2)}, u32[]{:S(2)}) collective-permute-start(bf16[64,6144]{1,0:T(8,128)(2,1)S(1)} %slice.9), channel_id=1, source_target_pairs={{16,0},{17,1},{0,16},{1,17},{18,2},{19,3},{2,18},{3,19},{20,4},{21... | collective-permute-start | bytes 2359304 | tf_op jit(solution)/shard_map/ppermute | solution.py:232
  5.0 3.0 %project.1 = (f32[32,256]{1,0:T(8,128)S(1)}, f32[32,256]{1,0:T(8,128)S(1)}) custom-call(s32[1]{0:T(128)} %bitcast.1.core, bf16[64,8192]{1,0:T(8,128)(2,1)} %bitcast.10, bf16[8192,256]{1,0:T(8,128)(2,1)} %basis.1), custom_call_target="tpu_custom_call" | custom-call | tf_op jit(solution)/shard_map/project/pallas_call | solution.py:58
  7.9 0.1 collective-permute-start
  8.0 1.2 %collective-permute-done = f32[32,256]{1,0:T(8,128)S(1)} collective-permute-done((f32[32,256]{1,0:T(8,128)S(1)}, f32[32,256]{1,0:T(8,128)S(1)}, u32[]{:S(2)}, u32[]{:S(2)}) %collective-permute-start) | collective-permute-done | bytes 32800 | tf_op jit(solution)/shard_map/ppermute | solution.py:222
  9.2 2.5 %collective-permute-start.3 = (f32[32,256]{1,0:T(8,128)S(1)}, f32[32,256]{1,0:T(8,128)S(1)}, u32[]{:S(2)}, u32[]{:S(2)}) collective-permute-start(f32[32,256]{1,0:T(8,128)S(1)} %add.19), channel_id=1, source_target_pairs={{6,0},{4,2},{2,4},{0,6},{14,8},{12,10},{10,12},{8,14},{7,1},{5,3},... | collective-permute-start | bytes 98312 | tf_op jit(solution)/shard_map/ppermute | solution.py:222
  11.8 0.4 %collective-permute-start.2 = (f32[32,256]{1,0:T(8,128)S(1)}, f32[32,256]{1,0:T(8,128)S(1)}, u32[]{:S(2)}, u32[]{:S(2)}) collective-permute-start(f32[32,256]{1,0:T(8,128)S(1)} %add.19), channel_id=1, source_target_pairs={{4,0},{6,2},{0,4},{2,6},{12,8},{14,10},{8,12},{10,14},{5,1},{7,3},... | collective-permute-start | bytes 98312 | tf_op jit(solution)/shard_map/ppermute | solution.py:222
  12.2 0.5 %collective-permute-start.1 = (f32[32,256]{1,0:T(8,128)S(1)}, f32[32,256]{1,0:T(8,128)S(1)}, u32[]{:S(2)}, u32[]{:S(2)}) collective-permute-start(f32[32,256]{1,0:T(8,128)S(1)} %add.19), channel_id=1, source_target_pairs={{2,0},{0,2},{6,4},{4,6},{10,8},{8,10},{14,12},{12,14},{3,1},{1,3},... | collective-permute-start | bytes 98312 | tf_op jit(solution)/shard_map/ppermute | solution.py:222
  12.7 1.3 %collective-permute-done.3 = f32[32,256]{1,0:T(8,128)S(1)} collective-permute-done((f32[32,256]{1,0:T(8,128)S(1)}, f32[32,256]{1,0:T(8,128)S(1)}, u32[]{:S(2)}, u32[]{:S(2)}) %collective-permute-start.3) | collective-permute-done | bytes 32800 | tf_op jit(solution)/shard_map/ppermute | solution.py:222
  14.0 1.6 %collective-permute-done.2 = f32[32,256]{1,0:T(8,128)S(1)} collective-permute-done((f32[32,256]{1,0:T(8,128)S(1)}, f32[32,256]{1,0:T(8,128)S(1)}, u32[]{:S(2)}, u32[]{:S(2)}) %collective-permute-start.2) | collective-permute-done | bytes 32800 | tf_op jit(solution)/shard_map/ppermute | solution.py:222
  15.7 0.4 %collective-permute-done.1 = f32[32,256]{1,0:T(8,128)S(1)} collective-permute-done((f32[32,256]{1,0:T(8,128)S(1)}, f32[32,256]{1,0:T(8,128)S(1)}, u32[]{:S(2)}, u32[]{:S(2)}) %collective-permute-start.1) | collective-permute-done | bytes 32800 | tf_op jit(solution)/shard_map/ppermute | solution.py:222
  16.1 2.7 %collective-permute-start.4 = (f32[32,256]{1,0:T(8,128)S(1)}, f32[32,256]{1,0:T(8,128)S(1)}, u32[]{:S(2)}, u32[]{:S(2)}) collective-permute-start(f32[32,256]{1,0:T(8,128)S(1)} %add_add_fusion), channel_id=1, source_target_pairs={{8,0},{10,2},{12,4},{14,6},{0,8},{2,10},{4,12},{6,14},{9,1},{11,3}... | collective-permute-start | bytes 98312 | tf_op jit(solution)/shard_map/ppermute | solution.py:222
  18.8 0.0 copy-done
  18.8 0.0 copy-done.1
  18.8 2.2 %collective-permute-done.4 = f32[32,256]{1,0:T(8,128)S(1)} collective-permute-done((f32[32,256]{1,0:T(8,128)S(1)}, f32[32,256]{1,0:T(8,128)S(1)}, u32[]{:S(2)}, u32[]{:S(2)}) %collective-permute-start.4) | collective-permute-done | bytes 32800 | tf_op jit(solution)/shard_map/ppermute | solution.py:222
  21.0 0.0 collective-permute-start.7
  21.0 0.6 %collective-permute-start.6 = (f32[32,256]{1,0:T(8,128)S(1)}, f32[32,256]{1,0:T(8,128)S(1)}, u32[]{:S(2)}, u32[]{:S(2)}) collective-permute-start(f32[32,256]{1,0:T(8,128)S(1)} %add.23), channel_id=1, source_target_pairs={{16,0},{17,1},{0,16},{1,17},{18,2},{19,3},{2,18},{3,19},{20,4},{21... | collective-permute-start | bytes 98312 | tf_op jit(solution)/shard_map/ppermute | solution.py:232
  21.6 1.2 %collective-permute-start.5 = (f32[32,256]{1,0:T(8,128)S(1)}, f32[32,256]{1,0:T(8,128)S(1)}, u32[]{:S(2)}, u32[]{:S(2)}) collective-permute-start(f32[32,256]{1,0:T(8,128)S(1)} %add.23), channel_id=1, source_target_pairs={{1,0},{0,1},{17,16},{16,17},{3,2},{2,3},{19,18},{18,19},{5,4},{4,5... | collective-permute-start | bytes 98312 | tf_op jit(solution)/shard_map/ppermute | solution.py:232
  22.9 0.1 pad_add_fusion.place
  23.0 0.1 copy.8
  23.1 0.6 %collective-permute-start.9 = (bf16[64,2048]{1,0:T(8,128)(2,1)S(1)}, bf16[64,2048]{1,0:T(8,128)(2,1)S(1)}, u32[]{:S(2)}, u32[]{:S(2)}) collective-permute-start(bf16[64,2048]{1,0:T(8,128)(2,1)S(1)} %slice.8), channel_id=1, source_target_pairs={{16,0},{17,1},{0,16},{1,17},{18,2},{19,3},{2,18},{3,19},{20,4},{21... | collective-permute-start | bytes 786440 | tf_op jit(solution)/shard_map/ppermute | solution.py:232
  23.7 0.7 %collective-permute-done.7 = f32[32,256]{1,0:T(8,128)S(1)} collective-permute-done((f32[32,256]{1,0:T(8,128)S(1)}, f32[32,256]{1,0:T(8,128)S(1)}, u32[]{:S(2)}, u32[]{:S(2)}) %collective-permute-start.7) | collective-permute-done | bytes 32800 | tf_op jit(solution)/shard_map/ppermute | solution.py:232
  24.4 0.7 %collective-permute-done.6 = f32[32,256]{1,0:T(8,128)S(1)} collective-permute-done((f32[32,256]{1,0:T(8,128)S(1)}, f32[32,256]{1,0:T(8,128)S(1)}, u32[]{:S(2)}, u32[]{:S(2)}) %collective-permute-start.6) | collective-permute-done | bytes 32800 | tf_op jit(solution)/shard_map/ppermute | solution.py:232
  25.1 0.0 collective-permute-done.5
  25.1 0.0 collective-permute-done.8.refs_1_
  25.1 0.0 copy-done.2
  25.1 3.6 %rebuild_first.1 = (f32[256,256]{1,0:T(8,128)}, bf16[256,8192]{1,0:T(8,128)(2,1)}, bf16[256,128]{1,0:T(8,128)(2,1)S(1)}) custom-call(s32[2]{0:T(128)S(1)} %pad_add_fusion.place, f32[1,256]{1,0:T(1,128)S(1)} %bitcast.15, bf16[256,256]{1,0:T(8,128)(2,1)S(1)} %bitcast.14, f32[4,32,256]{2,1,0:T(8,128)S(1)} %pad_maximum_fusion.coeffs, ...), custom_call_target="tpu_custom_call" | custom-call | flops 6000000000 | tf_op jit(solution)/shard_map/rebuild_first/pallas_call | solution.py:174
  28.7 2.6 %collective-permute-done.9.refs_1_ = bf16[64,2048]{1,0:T(8,128)(2,1)S(1)} collective-permute-done((bf16[64,2048]{1,0:T(8,128)(2,1)S(1)}, bf16[64,2048]{1,0:T(8,128)(2,1)S(1)}, u32[]{:S(2)}, u32[]{:S(2)}) %collective-permute-start.9) | collective-permute-done | bytes 262176 | tf_op jit(solution)/shard_map/ppermute | solution.py:232
  31.3 1.3 %rebuild_last.1 = bf16[256,8192]{1,0:T(8,128)(2,1)} custom-call(bf16[256,128]{1,0:T(8,128)(2,1)S(1)} %get-tuple-element.13.weights, bf16[64,8192]{1,0:T(8,128)(2,1)S(1)} %bitcast.13, bf16[64,2048]{1,0:T(8,128)(2,1)S(1)} %collective-permute-done.9.refs_1_, bf16[256,8192]{1,0:T(8,128)(2,1)} %get-tuple-element.15.refs_2_), custom_call_target="tpu_custom_call", output_to_operand_aliasing={{}: (3, {})} | custom-call | tf_op jit(solution)/shard_map/rebuild_last/pallas_call | solution.py:202
  (6 shorter events, 0.1 us)
Async XLA Ops:
  0.6 18.2 %copy-start = (bf16[256,512]{1,0:T(8,128)(2,1)S(1)}, bf16[256,512]{1,0:T(8,128)(2,1)}, u32[]{:S(2)}) copy-start(bf16[256,512]{1,0:T(8,128)(2,1)} %param.7) | copy-start | bytes 786436
  0.6 18.2 %copy-start.1 = (bf16[8192,64]{0,1:T(8,128)(2,1)S(1)}, bf16[8192,64]{0,1:T(8,128)(2,1)}, u32[]{:S(2)}) copy-start(bf16[8192,64]{0,1:T(8,128)(2,1)} %param.5) | copy-start | bytes 3145732
  0.7 24.4 %copy-start.2 = (f32[256]{0:T(256)S(1)}, f32[256]{0:T(256)}, u32[]{:S(2)}) copy-start(f32[256]{0:T(256)} %param.6) | copy-start | bytes 3076
  2.0 23.1 %collective-permute-start.8 = (bf16[64,6144]{1,0:T(8,128)(2,1)S(1)}, bf16[64,6144]{1,0:T(8,128)(2,1)S(1)}, u32[]{:S(2)}, u32[]{:S(2)}) collective-permute-start(bf16[64,6144]{1,0:T(8,128)(2,1)S(1)} %slice.9), channel_id=1, source_target_pairs={{16,0},{17,1},{0,16},{1,17},{18,2},{19,3},{2,18},{3,19},{20,4},{21... | collective-permute-start | bytes 2359304 | tf_op jit(solution)/shard_map/ppermute | solution.py:232
  7.9 1.3 %collective-permute-start = (f32[32,256]{1,0:T(8,128)S(1)}, f32[32,256]{1,0:T(8,128)S(1)}, u32[]{:S(2)}, u32[]{:S(2)}) collective-permute-start(f32[32,256]{1,0:T(8,128)S(1)} %get-tuple-element.10), channel_id=1, source_target_pairs={{1,0},{0,1},{3,2},{2,3},{5,4},{4,5},{7,6},{6,7},{9,8},{8,9},{11,10... | collective-permute-start | bytes 98312 | tf_op jit(solution)/shard_map/ppermute | solution.py:222
  9.2 4.8 %collective-permute-start.3 = (f32[32,256]{1,0:T(8,128)S(1)}, f32[32,256]{1,0:T(8,128)S(1)}, u32[]{:S(2)}, u32[]{:S(2)}) collective-permute-start(f32[32,256]{1,0:T(8,128)S(1)} %add.19), channel_id=1, source_target_pairs={{6,0},{4,2},{2,4},{0,6},{14,8},{12,10},{10,12},{8,14},{7,1},{5,3},... | collective-permute-start | bytes 98312 | tf_op jit(solution)/shard_map/ppermute | solution.py:222
  11.8 3.9 %collective-permute-start.2 = (f32[32,256]{1,0:T(8,128)S(1)}, f32[32,256]{1,0:T(8,128)S(1)}, u32[]{:S(2)}, u32[]{:S(2)}) collective-permute-start(f32[32,256]{1,0:T(8,128)S(1)} %add.19), channel_id=1, source_target_pairs={{4,0},{6,2},{0,4},{2,6},{12,8},{14,10},{8,12},{10,14},{5,1},{7,3},... | collective-permute-start | bytes 98312 | tf_op jit(solution)/shard_map/ppermute | solution.py:222
  12.2 3.9 %collective-permute-start.1 = (f32[32,256]{1,0:T(8,128)S(1)}, f32[32,256]{1,0:T(8,128)S(1)}, u32[]{:S(2)}, u32[]{:S(2)}) collective-permute-start(f32[32,256]{1,0:T(8,128)S(1)} %add.19), channel_id=1, source_target_pairs={{2,0},{0,2},{6,4},{4,6},{10,8},{8,10},{14,12},{12,14},{3,1},{1,3},... | collective-permute-start | bytes 98312 | tf_op jit(solution)/shard_map/ppermute | solution.py:222
  16.1 4.9 %collective-permute-start.4 = (f32[32,256]{1,0:T(8,128)S(1)}, f32[32,256]{1,0:T(8,128)S(1)}, u32[]{:S(2)}, u32[]{:S(2)}) collective-permute-start(f32[32,256]{1,0:T(8,128)S(1)} %add_add_fusion), channel_id=1, source_target_pairs={{8,0},{10,2},{12,4},{14,6},{0,8},{2,10},{4,12},{6,14},{9,1},{11,3}... | collective-permute-start | bytes 98312 | tf_op jit(solution)/shard_map/ppermute | solution.py:222
  21.0 3.3 %collective-permute-start.7 = (f32[32,256]{1,0:T(8,128)S(1)}, f32[32,256]{1,0:T(8,128)S(1)}, u32[]{:S(2)}, u32[]{:S(2)}) collective-permute-start(f32[32,256]{1,0:T(8,128)S(1)} %add.23), channel_id=1, source_target_pairs={{17,0},{16,1},{1,16},{0,17},{19,2},{18,3},{3,18},{2,19},{21,4},{20... | collective-permute-start | bytes 98312 | tf_op jit(solution)/shard_map/ppermute | solution.py:232
  21.0 4.0 %collective-permute-start.6 = (f32[32,256]{1,0:T(8,128)S(1)}, f32[32,256]{1,0:T(8,128)S(1)}, u32[]{:S(2)}, u32[]{:S(2)}) collective-permute-start(f32[32,256]{1,0:T(8,128)S(1)} %add.23), channel_id=1, source_target_pairs={{16,0},{17,1},{0,16},{1,17},{18,2},{19,3},{2,18},{3,19},{20,4},{21... | collective-permute-start | bytes 98312 | tf_op jit(solution)/shard_map/ppermute | solution.py:232
  21.6 3.4 %collective-permute-start.5 = (f32[32,256]{1,0:T(8,128)S(1)}, f32[32,256]{1,0:T(8,128)S(1)}, u32[]{:S(2)}, u32[]{:S(2)}) collective-permute-start(f32[32,256]{1,0:T(8,128)S(1)} %add.23), channel_id=1, source_target_pairs={{1,0},{0,1},{17,16},{16,17},{3,2},{2,3},{19,18},{18,19},{5,4},{4,5... | collective-permute-start | bytes 98312 | tf_op jit(solution)/shard_map/ppermute | solution.py:232
  23.1 8.3 %collective-permute-start.9 = (bf16[64,2048]{1,0:T(8,128)(2,1)S(1)}, bf16[64,2048]{1,0:T(8,128)(2,1)S(1)}, u32[]{:S(2)}, u32[]{:S(2)}) collective-permute-start(bf16[64,2048]{1,0:T(8,128)(2,1)S(1)} %slice.8), channel_id=1, source_target_pairs={{16,0},{17,1},{0,16},{1,17},{18,2},{19,3},{2,18},{3,19},{20,4},{21... | collective-permute-start | bytes 786440 | tf_op jit(solution)/shard_map/ppermute | solution.py:232

commit v10 on v9

v10 whole, which is shorter than its diff:
```python
import functools

import jax
import jax.numpy as jnp
from jax import lax
from jax.experimental import pallas as pl
from jax.experimental.pallas import tpu as pltpu
from jax.sharding import Mesh, PartitionSpec as P

ROWS = (((1,), (0,)), ((), ()))
FIRST = (((0,), (0,)), ((), ()))
LAST = (((1,), (1,)), ((), ()))
FREE = pl.CostEstimate(flops=0, bytes_accessed=0, transcendentals=0)
COST_A = pl.CostEstimate(flops=6 * 10**9, bytes_accessed=0, transcendentals=0)
ANYWHERE = pl.BlockSpec(memory_space=pl.ANY)
IN_VMEM = pl.BlockSpec(memory_space=pltpu.VMEM)


def started(copies):
    for copy in copies:
        copy.start()
    return copies


def waited(copies):
    for copy in copies:
        copy.wait()


def in_parts(value):
    high = value.astype(jnp.bfloat16)
    return high, (value - high.astype(jnp.float32)).astype(jnp.bfloat16)


def product(left, right, dims):
    return lax.dot_general(left, right, dims, preferred_element_type=jnp.float32)


def cut_kernel(fields, early, late, sent):
    begin = early.shape[1]
    waited(
        started(
            [
                pltpu.make_async_copy(fields.at[:, pl.ds(0, begin)], early, sent.at[0]),
                pltpu.make_async_copy(fields.at[:, pl.ds(begin, late.shape[1])], late, sent.at[1]),
            ]
        )
    )


def cut(fields, begin):
    hours, cells = fields.shape
    return pl.pallas_call(
        cut_kernel,
        out_shape=(
            jax.ShapeDtypeStruct((hours, begin), fields.dtype),
            jax.ShapeDtypeStruct((hours, cells - begin), fields.dtype),
        ),
        in_specs=[ANYWHERE],
        out_specs=(ANYWHERE, ANYWHERE),
        scratch_shapes=[pltpu.SemaphoreType.DMA((2,))],
        compiler_params=pltpu.CompilerParams(vmem_limit_bytes=53 * 2**20),
        cost_estimate=FREE,
        name="cut",
    )(fields)


def project_kernel(tiles, snapshots, basis, kept, given, fields, patterns, halves, arrived):
    cells = snapshots.shape[1]
    tile = cells // tiles
    copies = []
    for i in range(tiles):
        span = pl.ds(i * tile, tile)
        copies.append(
            (
                pltpu.make_async_copy(snapshots.at[:, span], fields.at[:, span], arrived.at[0, i]),
                pltpu.make_async_copy(basis.at[span], patterns.at[span], arrived.at[1, i]),
            )
        )
    for pair in copies:
        for copy in pair:
            copy.start()
    total = jnp.zeros((fields.shape[0], patterns.shape[1]), jnp.float32)
    for i, pair in enumerate(copies):
        for copy in pair:
            copy.wait()
        span = pl.ds(i * tile, tile)
        total += product(fields[:, span], patterns[span], ROWS)
    half = kept.shape[0]
    core = lax.axis_index("inner")
    halves[0] = total[:half]
    halves[1] = total[half:]
    kept[...] = halves[core]
    given[...] = halves[1 - core]


def project(snapshots, basis, tiles):
    hours = snapshots.shape[0]
    rank = basis.shape[1]
    half = jax.ShapeDtypeStruct((hours // 2, rank), jnp.float32)
    return pl.pallas_call(
        functools.partial(project_kernel, tiles),
        out_shape=(half, half),
        in_specs=[ANYWHERE] * 2,
        out_specs=(pl.BlockSpec(memory_space=pltpu.VMEM),) * 2,
        scratch_shapes=[
            pltpu.VMEM(snapshots.shape, snapshots.dtype),
            pltpu.VMEM(basis.shape, basis.dtype),
            pltpu.VMEM((2, hours // 2, rank), jnp.float32),
            pltpu.SemaphoreType.DMA((2, tiles)),
        ],
        compiler_params=pltpu.CompilerParams(vmem_limit_bytes=53 * 2**20),
        cost_estimate=FREE,
        name="project",
    )(snapshots, basis)


def gathered(held, fields, begin, arrived):
    width = fields.shape[1]
    copies, row = [], 0
    for n, (block, offset) in enumerate(held):
        rows = block.shape[0]
        copies.append(
            pltpu.make_async_copy(
                block.at[:, pl.ds(begin - offset, width)],
                fields.at[pl.ds(row, rows)],
                arrived.at[n],
            )
        )
        row += rows
    return copies


def rebuilt(weights, fields, made, modes, begin, tiles, sent):
    width = fields.shape[1] // tiles
    copies = []
    for i in range(tiles):
        span = pl.ds(i * width, width)
        made[:, span] = product(weights, fields[:, span], ROWS).astype(made.dtype)
        target = modes.at[:, pl.ds(begin + i * width, width)]
        copies += started([pltpu.make_async_copy(made.at[:, span], target, sent.at[i])])
    return copies


def by_hours(known):
    me, core = lax.axis_index("tm"), lax.axis_index("inner")
    count = known.shape[0] // 2
    order = [
        2 * lax.rem(count + block - me, count) + lax.rem(2 + half - core, 2)
        for block in range(count)
        for half in range(2)
    ]
    return jnp.concatenate([known[at] for at in order], axis=0)


def lagged_and_scaled(every, energy):
    hour = lax.broadcasted_iota(jnp.int32, every.shape, 0)
    return jnp.where(hour == 0, 0.0, pltpu.roll(every, 1, 0)) * energy


def first_kernel(offsets, tiles, energy, vectors, coeffs, *refs):
    held, refs = refs[: len(offsets)], refs[len(offsets) :]
    modes, weights, fields, known, turned, scale, scaled, made, arrived, sent = refs
    count, hours = coeffs.shape[0] // 2, 2 * coeffs.shape[1]
    inputs = started(
        [
            pltpu.make_async_copy(source, target, arrived.at[len(held) + n])
            for n, (source, target) in enumerate(
                ((coeffs, known), (vectors, turned), (energy, scale))
            )
        ]
    )
    blocks = started(gathered(list(zip(held, offsets)), fields, 0, arrived))
    waited(inputs)
    scaled[...] = lagged_and_scaled(by_hours(known), scale[...])
    me = lax.axis_index("tm")
    first = [lax.rem(me + k, count) * hours for k in range(count)]
    ordered = jnp.concatenate(
        [scaled[pl.ds(pl.multiple_of(at, hours), hours)] for at in first], axis=0
    )
    high, low = in_parts(ordered)
    weights[...] = (product(turned[...], high, LAST) + product(turned[...], low, LAST)).astype(
        jnp.bfloat16
    )
    waited(blocks)
    waited(rebuilt(weights[...], fields, made, modes, 0, tiles, sent))


def operator_kernel(energy, coeffs, operator, scale, known, arrived):
    waited(
        started(
            [
                pltpu.make_async_copy(coeffs, known, arrived.at[0]),
                pltpu.make_async_copy(energy, scale, arrived.at[1]),
            ]
        )
    )
    every = by_hours(known)
    high, low = in_parts(every)
    s_high, s_low = in_parts(lagged_and_scaled(every, scale[...]))
    operator[...] = (
        product(high, s_high, FIRST) + product(high, s_low, FIRST) + product(low, s_high, FIRST)
    )


def last_kernel(offsets, begin, tiles, weights, *refs):
    held, refs = refs[: len(offsets)], refs[len(offsets) :]
    _, modes, fields, made, arrived, sent = refs
    waited(started(gathered(list(zip(held, offsets)), fields, begin, arrived)))
    waited(rebuilt(weights[...], fields, made, modes, begin, tiles, sent))


def rebuild_first(energy, vectors, coeffs, held, cells, width, tiles):
    blocks, half, rank = coeffs.shape
    hours, modes = blocks * half, vectors.shape[0]
    return pl.pallas_call(
        functools.partial(first_kernel, [0] * len(held), tiles),
        out_shape=(
            jax.ShapeDtypeStruct((modes, cells), jnp.bfloat16),
            jax.ShapeDtypeStruct((modes, hours), jnp.bfloat16),
        ),
        in_specs=[ANYWHERE] * (3 + len(held)),
        out_specs=(ANYWHERE, IN_VMEM),
        scratch_shapes=[
            pltpu.VMEM((hours, width), jnp.bfloat16),
            pltpu.VMEM(coeffs.shape, jnp.float32),
            pltpu.VMEM(vectors.shape, vectors.dtype),
            pltpu.VMEM(energy.shape, energy.dtype),
            pltpu.VMEM((hours, rank), jnp.float32),
            pltpu.VMEM((modes, width), jnp.bfloat16),
            pltpu.SemaphoreType.DMA((len(held) + 3,)),
            pltpu.SemaphoreType.DMA((tiles,)),
        ],
        compiler_params=pltpu.CompilerParams(vmem_limit_bytes=40 * 2**20),
        cost_estimate=COST_A,
        name="rebuild_first",
    )(energy, vectors, coeffs, *held)


def operate(energy, coeffs):
    rank = coeffs.shape[2]
    return pl.pallas_call(
        operator_kernel,
        out_shape=jax.ShapeDtypeStruct((rank, rank), jnp.float32),
        in_specs=[ANYWHERE] * 2,
        out_specs=IN_VMEM,
        scratch_shapes=[
            pltpu.VMEM(energy.shape, energy.dtype),
            pltpu.VMEM(coeffs.shape, coeffs.dtype),
            pltpu.SemaphoreType.DMA((2,)),
        ],
        cost_estimate=FREE,
        name="operate",
    )(energy, coeffs)


def rebuild_last(weights, held, offsets, modes, begin, tiles):
    width = modes.shape[1] - begin
    return pl.pallas_call(
        functools.partial(last_kernel, offsets, begin, tiles),
        out_shape=jax.ShapeDtypeStruct(modes.shape, modes.dtype),
        in_specs=[IN_VMEM] + [ANYWHERE] * (len(held) + 1),
        out_specs=ANYWHERE,
        scratch_shapes=[
            pltpu.VMEM((weights.shape[1], width), jnp.bfloat16),
            pltpu.VMEM((modes.shape[0], width), jnp.bfloat16),
            pltpu.SemaphoreType.DMA((len(held),)),
            pltpu.SemaphoreType.DMA((tiles,)),
        ],
        input_output_aliases={1 + len(held): 0},
        compiler_params=pltpu.CompilerParams(vmem_limit_bytes=40 * 2**20),
        cost_estimate=FREE,
        name="rebuild_last",
    )(weights, *held, modes)


def swapped(value, axis, bit):
    route = [(i ^ bit, i) for i in range(lax.axis_size(axis))]
    return lax.ppermute(value, axis, route)


def moved(value, by, swap):
    size = lax.axis_size("tm")
    route = [
        (2 * ((i + by) % size) + (core ^ swap), 2 * i + core)
        for i in range(size)
        for core in range(2)
    ]
    return lax.ppermute(value, ("tm", "inner"), route)


def per_device(eof_basis, snapshots, inverse_energy, eigen_vectors):
    tm, outer = lax.axis_size("tm"), lax.axis_size("outer")
    me = lax.axis_index("tm")
    fields = snapshots.T

    cells = fields.shape[1]
    begin = cells // 16 * 13

    early, late = cut(fields, begin)
    first, last, offsets = [fields], [late], [begin]
    for k in range(1, tm):
        first.append(moved(early, k, 0))
        offsets.append(begin)

    kept, given = project(fields, eof_basis, 8)
    mine = kept + swapped(given, "inner", 1)
    bit = 1
    while bit < outer:
        near = swapped(mine, "outer", bit)
        if 2 * bit < outer:
            far, both = (swapped(mine, "outer", b) for b in (2 * bit, 3 * bit))
            mine = (mine + near) + (far + both)
        else:
            mine = mine + near
        bit *= 4
    mine, late = lax.optimization_barrier((mine, late))
    last += [moved(late, k, 0) for k in range(1, tm)]
    coeffs = [mine, moved(mine, 0, 1)]
    for k in range(1, tm):
        coeffs += [moved(mine, k, 0), moved(mine, k, 1)]

    rows = eigen_vectors.shape[1] // tm
    vectors = lax.dynamic_slice_in_dim(eigen_vectors, me * rows, rows, 1)
    energy, coeffs = inverse_energy[None, :], jnp.stack(coeffs)
    modes, weights = rebuild_first(energy, vectors.T, coeffs, first, cells, begin, 4)
    weights, coeffs = lax.optimization_barrier((weights, coeffs))
    operator = operate(energy, coeffs)
    return operator, rebuild_last(weights, last, offsets, modes, begin, 2)


def solution(mesh):
    tm, space = mesh.shape["tm"], mesh.shape["space"]
    split = Mesh(mesh.devices.reshape(tm, space // 2, 2), ("tm", "outer", "inner"))
    cells = ("outer", "inner")
    in_specs = (P(cells, None), P(cells, "tm"), P(), P())
    out_specs = (P(), P("tm", cells))
    return jax.shard_map(
        per_device, mesh=split, in_specs=in_specs, out_specs=out_specs, check_vma=False
    )
```

time: 32.8 us -> 58.2 us (1.77)
  Pallas kernels: 7.91 us -> 36.7 us
  waiting for transfers between devices: 10.8 us -> 8.73 us
  local copies, waits for them, and re-layouts: 1.43 us -> 0.13 us
    pallas_call x0 -> x2, Pallas kernels: none -> 28.8 us  [the longest x1 26.9 us: cut(): pl.pallas_call(cut_kernel, out_shape=(jax.ShapeDtypeStruct((hours, begin)...]
    ppermute x5, waiting for transfers between devices: 4.03 us -> 1.91 us  [moved(): return lax.ppermute(value, ('tm', 'inner'), route)]
    slice x2 -> x0, local copies, waits for them, and re-layouts: 1.3 us -> none  [the longest x1 1.28 us: per_device(): first.append(moved(fields[:, :begin], k, 0))]
  transfers between devices with their start and end apart: 10 -> 10, of which waited for: 8 -> 7; matrix products, arithmetic and copies ran while one was open for 1% -> 0% of each run, Pallas kernels for 20% -> 14%
where the time goes in v10:
time: 58.2 us; the launch traced here: 58 us
  Pallas kernels  36.7 us (63%)
  starting transfers between devices  11.7 us (20%)
  waiting for transfers between devices  8.73 us (15%)
  between operations  0.78 us (1%)
    pallas_call x1, Pallas kernels, cut(): pl.pallas_call(cut_kernel, out_shape=(jax.ShapeDtypeStruct((hours, begin)...  26.9 us
    ppermute x5, waiting for transfers between devices, swapped(): return lax.ppermute(value, axis, route)  6.82 us
    ppermute x5, starting transfers between devices, swapped(): return lax.ppermute(value, axis, route)  6.22 us
    ppermute x5, starting transfers between devices, moved(): return lax.ppermute(value, ('tm', 'inner'), route)  5.46 us
    pallas_call x1, Pallas kernels, rebuild_first(): pl.pallas_call(functools.partial(first_kernel, [0] * len(held), tiles), o...  3.16 us
    pallas_call x1, Pallas kernels, project(): pl.pallas_call(functools.partial(project_kernel, tiles), out_shape=(half,...  2.99 us
    pallas_call x1, Pallas kernels, operate(): pl.pallas_call(operator_kernel, out_shape=jax.ShapeDtypeStruct((rank, ran...  1.92 us
    ppermute x5, waiting for transfers between devices, moved(): return lax.ppermute(value, ('tm', 'inner'), route)  1.91 us
  transfers between devices with their start and end apart: 10, of which 7 were waited for; matrix products, arithmetic and copies ran while one was open for 0% of the time, Pallas kernels for 14%

profile of v10, /device:TPU:0, one launch (start us, length us, event | category | flops | bytes accessed | tf_op | source)
XLA Modules:
  0.0 58.0 jit_solution(321152003405237658)
XLA Ops:
  0.6 0.0 copy-start
  0.6 0.0 copy-start.1
  0.7 0.0 copy-start.3
  0.7 26.9 %cut.1 = (bf16[64,6656]{1,0:T(8,128)(2,1)}, bf16[64,1536]{1,0:T(8,128)(2,1)S(1)}) custom-call(bf16[64,8192]{1,0:T(8,128)(2,1)} %bitcast.7), custom_call_target="tpu_custom_call" | custom-call | tf_op jit(solution)/shard_map/cut/pallas_call | solution.py:53
  27.6 3.0 %collective-permute-start.8 = (bf16[64,6656]{1,0:T(8,128)(2,1)}, bf16[64,6656]{1,0:T(8,128)(2,1)S(1)}, u32[]{:S(2)}, u32[]{:S(2)}) collective-permute-start(bf16[64,6656]{1,0:T(8,128)(2,1)} %get-tuple-element.16), channel_id=1, source_target_pairs={{16,0},{17,1},{0,16},{1,17},{18,2},{19,3},{2,18},{3,19},{20,4},{21... | collective-permute-start | bytes 2555912 | tf_op jit(solution)/shard_map/ppermute | solution.py:289
  30.6 3.0 %project.1 = (f32[32,256]{1,0:T(8,128)S(1)}, f32[32,256]{1,0:T(8,128)S(1)}) custom-call(bf16[64,8192]{1,0:T(8,128)(2,1)} %bitcast.8, bf16[8192,256]{1,0:T(8,128)(2,1)} %basis.1), custom_call_target="tpu_custom_call" | custom-call | tf_op jit(solution)/shard_map/project/pallas_call | solution.py:101
  33.6 0.1 collective-permute-start
  33.7 1.2 %collective-permute-done = f32[32,256]{1,0:T(8,128)S(1)} collective-permute-done((f32[32,256]{1,0:T(8,128)S(1)}, f32[32,256]{1,0:T(8,128)S(1)}, u32[]{:S(2)}, u32[]{:S(2)}) %collective-permute-start) | collective-permute-done | bytes 32800 | tf_op jit(solution)/shard_map/ppermute | solution.py:279
  34.9 2.5 %collective-permute-start.3 = (f32[32,256]{1,0:T(8,128)S(1)}, f32[32,256]{1,0:T(8,128)S(1)}, u32[]{:S(2)}, u32[]{:S(2)}) collective-permute-start(f32[32,256]{1,0:T(8,128)S(1)} %add.19), channel_id=1, source_target_pairs={{6,0},{4,2},{2,4},{0,6},{14,8},{12,10},{10,12},{8,14},{7,1},{5,3},... | collective-permute-start | bytes 98312 | tf_op jit(solution)/shard_map/ppermute | solution.py:279
  37.4 0.4 collective-permute-start.2
  37.9 0.5 collective-permute-start.1
  38.4 1.3 %collective-permute-done.3 = f32[32,256]{1,0:T(8,128)S(1)} collective-permute-done((f32[32,256]{1,0:T(8,128)S(1)}, f32[32,256]{1,0:T(8,128)S(1)}, u32[]{:S(2)}, u32[]{:S(2)}) %collective-permute-start.3) | collective-permute-done | bytes 32800 | tf_op jit(solution)/shard_map/ppermute | solution.py:279
  39.7 1.6 %collective-permute-done.2 = f32[32,256]{1,0:T(8,128)S(1)} collective-permute-done((f32[32,256]{1,0:T(8,128)S(1)}, f32[32,256]{1,0:T(8,128)S(1)}, u32[]{:S(2)}, u32[]{:S(2)}) %collective-permute-start.2) | collective-permute-done | bytes 32800 | tf_op jit(solution)/shard_map/ppermute | solution.py:279
  41.3 0.4 collective-permute-done.1
  41.8 2.7 %collective-permute-start.4 = (f32[32,256]{1,0:T(8,128)S(1)}, f32[32,256]{1,0:T(8,128)S(1)}, u32[]{:S(2)}, u32[]{:S(2)}) collective-permute-start(f32[32,256]{1,0:T(8,128)S(1)} %add_add_fusion), channel_id=1, source_target_pairs={{8,0},{10,2},{12,4},{14,6},{0,8},{2,10},{4,12},{6,14},{9,1},{11,3}... | collective-permute-start | bytes 98312 | tf_op jit(solution)/shard_map/ppermute | solution.py:279
  44.5 2.2 %collective-permute-done.4 = f32[32,256]{1,0:T(8,128)S(1)} collective-permute-done((f32[32,256]{1,0:T(8,128)S(1)}, f32[32,256]{1,0:T(8,128)S(1)}, u32[]{:S(2)}, u32[]{:S(2)}) %collective-permute-start.4) | collective-permute-done | bytes 32800 | tf_op jit(solution)/shard_map/ppermute | solution.py:279
  46.7 0.0 collective-permute-start.7
  46.7 0.6 %collective-permute-start.6 = (f32[32,256]{1,0:T(8,128)S(1)}, f32[32,256]{1,0:T(8,128)S(1)}, u32[]{:S(2)}, u32[]{:S(2)}) collective-permute-start(f32[32,256]{1,0:T(8,128)S(1)} %add.23), channel_id=1, source_target_pairs={{16,0},{17,1},{0,16},{1,17},{18,2},{19,3},{2,18},{3,19},{20,4},{21... | collective-permute-start | bytes 98312 | tf_op jit(solution)/shard_map/ppermute | solution.py:289
  47.3 1.3 %collective-permute-start.5 = (f32[32,256]{1,0:T(8,128)S(1)}, f32[32,256]{1,0:T(8,128)S(1)}, u32[]{:S(2)}, u32[]{:S(2)}) collective-permute-start(f32[32,256]{1,0:T(8,128)S(1)} %add.23), channel_id=1, source_target_pairs={{1,0},{0,1},{17,16},{16,17},{3,2},{2,3},{19,18},{18,19},{5,4},{4,5... | collective-permute-start | bytes 98312 | tf_op jit(solution)/shard_map/ppermute | solution.py:289
  48.5 0.0 copy-done
  48.6 0.1 copy.8
  48.7 0.6 %collective-permute-start.9 = (bf16[64,1536]{1,0:T(8,128)(2,1)S(1)}, bf16[64,1536]{1,0:T(8,128)(2,1)S(1)}, u32[]{:S(2)}, u32[]{:S(2)}) collective-permute-start(bf16[64,1536]{1,0:T(8,128)(2,1)S(1)} %get-tuple-element.20.refs_0_), channel_id=1, source_target_pairs={{16,0},{17,1},{0,16},{1,17},{18,2},{19,3},{2,18},{3,19},{20,4},{21... | collective-permute-start | bytes 589832 | tf_op jit(solution)/shard_map/ppermute | solution.py:289
  49.3 1.2 %collective-permute-done.7 = f32[32,256]{1,0:T(8,128)S(1)} collective-permute-done((f32[32,256]{1,0:T(8,128)S(1)}, f32[32,256]{1,0:T(8,128)S(1)}, u32[]{:S(2)}, u32[]{:S(2)}) %collective-permute-start.7) | collective-permute-done | bytes 32800 | tf_op jit(solution)/shard_map/ppermute | solution.py:289
  50.5 0.7 %collective-permute-done.6 = f32[32,256]{1,0:T(8,128)S(1)} collective-permute-done((f32[32,256]{1,0:T(8,128)S(1)}, f32[32,256]{1,0:T(8,128)S(1)}, u32[]{:S(2)}, u32[]{:S(2)}) %collective-permute-start.6) | collective-permute-done | bytes 32800 | tf_op jit(solution)/shard_map/ppermute | solution.py:289
  51.2 0.0 collective-permute-done.5
  51.2 0.0 copy-start.2
  51.2 0.0 collective-permute-done.8.refs_1_
  51.2 0.0 copy-done.1
  51.2 0.0 copy-done.3
  51.2 3.2 %rebuild_first.1 = (bf16[256,8192]{1,0:T(8,128)(2,1)}, bf16[256,128]{1,0:T(8,128)(2,1)S(1)}) custom-call(f32[1,256]{1,0:T(1,128)S(1)} %bitcast.12, bf16[256,256]{1,0:T(8,128)(2,1)S(1)} %bitcast.10, f32[4,32,256]{2,1,0:T(8,128)S(1)} %pad_maximum_fusion.coeffs, bf16[64,8192]{1,0:T(8,128)(2,1)S(1)} %bitcast.9, bf16[64,6656]{1,0:T(8,128)(2,1)S(1)} %collective-permute-done.8.refs_1_), custom_call_target="tpu_custom_call" | custom-call | flops 6000000000 | tf_op jit(solution)/shard_map/rebuild_first/pallas_call | solution.py:216
  54.4 0.0 copy-done.2
  54.4 1.9 %operate.1 = f32[256,256]{1,0:T(8,128)} custom-call(f32[1,256]{1,0:T(1,128)} %bitcast.11, f32[4,32,256]{2,1,0:T(8,128)} %copy-done.2), custom_call_target="tpu_custom_call" | custom-call | tf_op jit(solution)/shard_map/operate/pallas_call | solution.py:242
  56.3 0.0 collective-permute-done.9.refs_1_
  56.3 1.7 %rebuild_last.1 = bf16[256,8192]{1,0:T(8,128)(2,1)} custom-call(bf16[256,128]{1,0:T(8,128)(2,1)S(1)} %get-tuple-element.19.weights, bf16[64,1536]{1,0:T(8,128)(2,1)S(1)} %get-tuple-element.20.refs_0_, bf16[64,1536]{1,0:T(8,128)(2,1)S(1)} %collective-permute-done.9.refs_1_, bf16[256,8192]{1,0:T(8,128)(2,1)} %get-tuple-element.21.refs_2_), custom_call_target="tpu_custom_call", output_to_operand_aliasing={{}: (3, {})} | custom-call | tf_op jit(solution)/shard_map/rebuild_last/pallas_call | solution.py:259
  (5 shorter events, 0.0 us)
Async XLA Ops:
  0.6 47.9 %copy-start = (bf16[256,512]{1,0:T(8,128)(2,1)S(1)}, bf16[256,512]{1,0:T(8,128)(2,1)}, u32[]{:S(2)}) copy-start(bf16[256,512]{1,0:T(8,128)(2,1)} %param.7) | copy-start | bytes 786436
  0.6 50.6 %copy-start.1 = (bf16[8192,64]{0,1:T(8,128)(2,1)S(1)}, bf16[8192,64]{0,1:T(8,128)(2,1)}, u32[]{:S(2)}) copy-start(bf16[8192,64]{0,1:T(8,128)(2,1)} %param.5) | copy-start | bytes 3145732
  0.7 50.6 %copy-start.3 = (f32[256]{0:T(256)S(1)}, f32[256]{0:T(256)}, u32[]{:S(2)}) copy-start(f32[256]{0:T(256)} %param.6) | copy-start | bytes 3076
  27.6 23.6 %collective-permute-start.8 = (bf16[64,6656]{1,0:T(8,128)(2,1)}, bf16[64,6656]{1,0:T(8,128)(2,1)S(1)}, u32[]{:S(2)}, u32[]{:S(2)}) collective-permute-start(bf16[64,6656]{1,0:T(8,128)(2,1)} %get-tuple-element.16), channel_id=1, source_target_pairs={{16,0},{17,1},{0,16},{1,17},{18,2},{19,3},{2,18},{3,19},{20,4},{21... | collective-permute-start | bytes 2555912 | tf_op jit(solution)/shard_map/ppermute | solution.py:289
  33.6 1.3 %collective-permute-start = (f32[32,256]{1,0:T(8,128)S(1)}, f32[32,256]{1,0:T(8,128)S(1)}, u32[]{:S(2)}, u32[]{:S(2)}) collective-permute-start(f32[32,256]{1,0:T(8,128)S(1)} %get-tuple-element.13), channel_id=1, source_target_pairs={{1,0},{0,1},{3,2},{2,3},{5,4},{4,5},{7,6},{6,7},{9,8},{8,9},{11,10... | collective-permute-start | bytes 98312 | tf_op jit(solution)/shard_map/ppermute | solution.py:279
  34.9 4.8 %collective-permute-start.3 = (f32[32,256]{1,0:T(8,128)S(1)}, f32[32,256]{1,0:T(8,128)S(1)}, u32[]{:S(2)}, u32[]{:S(2)}) collective-permute-start(f32[32,256]{1,0:T(8,128)S(1)} %add.19), channel_id=1, source_target_pairs={{6,0},{4,2},{2,4},{0,6},{14,8},{12,10},{10,12},{8,14},{7,1},{5,3},... | collective-permute-start | bytes 98312 | tf_op jit(solution)/shard_map/ppermute | solution.py:279
  37.4 3.9 %collective-permute-start.2 = (f32[32,256]{1,0:T(8,128)S(1)}, f32[32,256]{1,0:T(8,128)S(1)}, u32[]{:S(2)}, u32[]{:S(2)}) collective-permute-start(f32[32,256]{1,0:T(8,128)S(1)} %add.19), channel_id=1, source_target_pairs={{4,0},{6,2},{0,4},{2,6},{12,8},{14,10},{8,12},{10,14},{5,1},{7,3},... | collective-permute-start | bytes 98312 | tf_op jit(solution)/shard_map/ppermute | solution.py:279
  37.9 3.9 %collective-permute-start.1 = (f32[32,256]{1,0:T(8,128)S(1)}, f32[32,256]{1,0:T(8,128)S(1)}, u32[]{:S(2)}, u32[]{:S(2)}) collective-permute-start(f32[32,256]{1,0:T(8,128)S(1)} %add.19), channel_id=1, source_target_pairs={{2,0},{0,2},{6,4},{4,6},{10,8},{8,10},{14,12},{12,14},{3,1},{1,3},... | collective-permute-start | bytes 98312 | tf_op jit(solution)/shard_map/ppermute | solution.py:279
  41.8 4.9 %collective-permute-start.4 = (f32[32,256]{1,0:T(8,128)S(1)}, f32[32,256]{1,0:T(8,128)S(1)}, u32[]{:S(2)}, u32[]{:S(2)}) collective-permute-start(f32[32,256]{1,0:T(8,128)S(1)} %add_add_fusion), channel_id=1, source_target_pairs={{8,0},{10,2},{12,4},{14,6},{0,8},{2,10},{4,12},{6,14},{9,1},{11,3}... | collective-permute-start | bytes 98312 | tf_op jit(solution)/shard_map/ppermute | solution.py:279
  46.7 3.8 %collective-permute-start.7 = (f32[32,256]{1,0:T(8,128)S(1)}, f32[32,256]{1,0:T(8,128)S(1)}, u32[]{:S(2)}, u32[]{:S(2)}) collective-permute-start(f32[32,256]{1,0:T(8,128)S(1)} %add.23), channel_id=1, source_target_pairs={{17,0},{16,1},{1,16},{0,17},{19,2},{18,3},{3,18},{2,19},{21,4},{20... | collective-permute-start | bytes 98312 | tf_op jit(solution)/shard_map/ppermute | solution.py:289
  46.7 4.5 %collective-permute-start.6 = (f32[32,256]{1,0:T(8,128)S(1)}, f32[32,256]{1,0:T(8,128)S(1)}, u32[]{:S(2)}, u32[]{:S(2)}) collective-permute-start(f32[32,256]{1,0:T(8,128)S(1)} %add.23), channel_id=1, source_target_pairs={{16,0},{17,1},{0,16},{1,17},{18,2},{19,3},{2,18},{3,19},{20,4},{21... | collective-permute-start | bytes 98312 | tf_op jit(solution)/shard_map/ppermute | solution.py:289
  47.3 3.9 %collective-permute-start.5 = (f32[32,256]{1,0:T(8,128)S(1)}, f32[32,256]{1,0:T(8,128)S(1)}, u32[]{:S(2)}, u32[]{:S(2)}) collective-permute-start(f32[32,256]{1,0:T(8,128)S(1)} %add.23), channel_id=1, source_target_pairs={{1,0},{0,1},{17,16},{16,17},{3,2},{2,3},{19,18},{18,19},{5,4},{4,5... | collective-permute-start | bytes 98312 | tf_op jit(solution)/shard_map/ppermute | solution.py:289
  48.7 7.7 %collective-permute-start.9 = (bf16[64,1536]{1,0:T(8,128)(2,1)S(1)}, bf16[64,1536]{1,0:T(8,128)(2,1)S(1)}, u32[]{:S(2)}, u32[]{:S(2)}) collective-permute-start(bf16[64,1536]{1,0:T(8,128)(2,1)S(1)} %get-tuple-element.20.refs_0_), channel_id=1, source_target_pairs={{16,0},{17,1},{0,16},{1,17},{18,2},{19,3},{2,18},{3,19},{20,4},{21... | collective-permute-start | bytes 589832 | tf_op jit(solution)/shard_map/ppermute | solution.py:289
  51.2 3.2 %copy-start.2 = (f32[4,32,256]{2,1,0:T(8,128)}, f32[4,32,256]{2,1,0:T(8,128)S(1)}, u32[]{:S(2)}) copy-start(f32[4,32,256]{2,1,0:T(8,128)S(1)} %pad_maximum_fusion.coeffs) | copy-start | bytes 393220

commit v11 on v10

--- a/solution.py
+++ b/solution.py
@@ -11,7 +11,7 @@
 FIRST = (((0,), (0,)), ((), ()))
 LAST = (((1,), (1,)), ((), ()))
 FREE = pl.CostEstimate(flops=0, bytes_accessed=0, transcendentals=0)
-COST_A = pl.CostEstimate(flops=6 * 10**9, bytes_accessed=0, transcendentals=0)
+COST_A = pl.CostEstimate(flops=10**9, bytes_accessed=0, transcendentals=0)
 ANYWHERE = pl.BlockSpec(memory_space=pl.ANY)
 IN_VMEM = pl.BlockSpec(memory_space=pltpu.VMEM)
 
@@ -59,7 +59,7 @@
         in_specs=[ANYWHERE],
         out_specs=(ANYWHERE, ANYWHERE),
         scratch_shapes=[pltpu.SemaphoreType.DMA((2,))],
-        compiler_params=pltpu.CompilerParams(vmem_limit_bytes=53 * 2**20),
+        compiler_params=pltpu.CompilerParams(vmem_limit_bytes=52 * 2**20),
         cost_estimate=FREE,
         name="cut",
     )(fields)
@@ -131,11 +131,13 @@
     return copies
 
 
-def rebuilt(weights, fields, made, modes, begin, tiles, sent):
+def rebuilt(weights, fields, made, modes, begin, tiles, sent, between):
     width = fields.shape[1] // tiles
     copies = []
     for i in range(tiles):
         span = pl.ds(i * width, width)
+        if i == tiles - 1:
+            copies += between()
         made[:, span] = product(weights, fields[:, span], ROWS).astype(made.dtype)
         target = modes.at[:, pl.ds(begin + i * width, width)]
         copies += started([pltpu.make_async_copy(made.at[:, span], target, sent.at[i])])
@@ -160,7 +162,7 @@
 
 def first_kernel(offsets, tiles, energy, vectors, coeffs, *refs):
     held, refs = refs[: len(offsets)], refs[len(offsets) :]
-    modes, weights, fields, known, turned, scale, scaled, made, arrived, sent = refs
+    operator, modes, weights, fields, known, turned, scale, scaled, made, square, arrived, sent = refs
     count, hours = coeffs.shape[0] // 2, 2 * coeffs.shape[1]
     inputs = started(
         [
@@ -172,7 +174,8 @@
     )
     blocks = started(gathered(list(zip(held, offsets)), fields, 0, arrived))
     waited(inputs)
-    scaled[...] = lagged_and_scaled(by_hours(known), scale[...])
+    every = by_hours(known)
+    scaled[...] = lagged_and_scaled(every, scale[...])
     me = lax.axis_index("tm")
     first = [lax.rem(me + k, count) * hours for k in range(count)]
     ordered = jnp.concatenate(
@@ -183,31 +186,25 @@
         jnp.bfloat16
     )
     waited(blocks)
-    waited(rebuilt(weights[...], fields, made, modes, 0, tiles, sent))
-
-
-def operator_kernel(energy, coeffs, operator, scale, known, arrived):
-    waited(
-        started(
-            [
-                pltpu.make_async_copy(coeffs, known, arrived.at[0]),
-                pltpu.make_async_copy(energy, scale, arrived.at[1]),
-            ]
+
+    def rest():
+        high, low = in_parts(every)
+        s_high, s_low = in_parts(scaled[...])
+        square[...] = (
+            product(high, s_high, FIRST)
+            + product(high, s_low, FIRST)
+            + product(low, s_high, FIRST)
         )
-    )
-    every = by_hours(known)
-    high, low = in_parts(every)
-    s_high, s_low = in_parts(lagged_and_scaled(every, scale[...]))
-    operator[...] = (
-        product(high, s_high, FIRST) + product(high, s_low, FIRST) + product(low, s_high, FIRST)
-    )
+        return started([pltpu.make_async_copy(square, operator, sent.at[tiles])])
+
+    waited(rebuilt(weights[...], fields, made, modes, 0, tiles, sent, rest))
 
 
 def last_kernel(offsets, begin, tiles, weights, *refs):
     held, refs = refs[: len(offsets)], refs[len(offsets) :]
     _, modes, fields, made, arrived, sent = refs
     waited(started(gathered(list(zip(held, offsets)), fields, begin, arrived)))
-    waited(rebuilt(weights[...], fields, made, modes, begin, tiles, sent))
+    waited(rebuilt(weights[...], fields, made, modes, begin, tiles, sent, list))
 
 
 def rebuild_first(energy, vectors, coeffs, held, cells, width, tiles):
@@ -216,11 +213,12 @@
     return pl.pallas_call(
         functools.partial(first_kernel, [0] * len(held), tiles),
         out_shape=(
+            jax.ShapeDtypeStruct((rank, rank), jnp.float32),
             jax.ShapeDtypeStruct((modes, cells), jnp.bfloat16),
             jax.ShapeDtypeStruct((modes, hours), jnp.bfloat16),
         ),
         in_specs=[ANYWHERE] * (3 + len(held)),
-        out_specs=(ANYWHERE, IN_VMEM),
+        out_specs=(ANYWHERE, ANYWHERE, IN_VMEM),
         scratch_shapes=[
             pltpu.VMEM((hours, width), jnp.bfloat16),
             pltpu.VMEM(coeffs.shape, jnp.float32),
@@ -228,30 +226,14 @@
             pltpu.VMEM(energy.shape, energy.dtype),
             pltpu.VMEM((hours, rank), jnp.float32),
             pltpu.VMEM((modes, width), jnp.bfloat16),
+            pltpu.VMEM((rank, rank), jnp.float32),
             pltpu.SemaphoreType.DMA((len(held) + 3,)),
-            pltpu.SemaphoreType.DMA((tiles,)),
+            pltpu.SemaphoreType.DMA((tiles + 1,)),
         ],
         compiler_params=pltpu.CompilerParams(vmem_limit_bytes=40 * 2**20),
         cost_estimate=COST_A,
         name="rebuild_first",
     )(energy, vectors, coeffs, *held)
-
-
-def operate(energy, coeffs):
-    rank = coeffs.shape[2]
-    return pl.pallas_call(
-        operator_kernel,
-        out_shape=jax.ShapeDtypeStruct((rank, rank), jnp.float32),
-        in_specs=[ANYWHERE] * 2,
-        out_specs=IN_VMEM,
-        scratch_shapes=[
-            pltpu.VMEM(energy.shape, energy.dtype),
-            pltpu.VMEM(coeffs.shape, coeffs.dtype),
-            pltpu.SemaphoreType.DMA((2,)),
-        ],
-        cost_estimate=FREE,
-        name="operate",
-    )(energy, coeffs)
 
 
 def rebuild_last(weights, held, offsets, modes, begin, tiles):
@@ -295,10 +277,10 @@
     fields = snapshots.T
 
     cells = fields.shape[1]
-    begin = cells // 16 * 13
+    begin = cells // 4 * 3
 
     early, late = cut(fields, begin)
-    first, last, offsets = [fields], [late], [begin]
+    first, last, offsets = [fields], [fields], [0]
     for k in range(1, tm):
         first.append(moved(early, k, 0))
         offsets.append(begin)
@@ -318,14 +300,13 @@
     last += [moved(late, k, 0) for k in range(1, tm)]
     coeffs = [mine, moved(mine, 0, 1)]
     for k in range(1, tm):
-        coeffs += [moved(mine, k, 0), moved(mine, k, 1)]
+        theirs = moved(mine, k, 0)
+        coeffs += [theirs, moved(theirs, 0, 1)]
 
     rows = eigen_vectors.shape[1] // tm
     vectors = lax.dynamic_slice_in_dim(eigen_vectors, me * rows, rows, 1)
     energy, coeffs = inverse_energy[None, :], jnp.stack(coeffs)
-    modes, weights = rebuild_first(energy, vectors.T, coeffs, first, cells, begin, 4)
-    weights, coeffs = lax.optimization_barrier((weights, coeffs))
-    operator = operate(energy, coeffs)
+    operator, modes, weights = rebuild_first(energy, vectors.T, coeffs, first, cells, begin, 3)
     return operator, rebuild_last(weights, last, offsets, modes, begin, 2)
 
 

time: 58.2 us -> 33.5 us (0.58)
  Pallas kernels: 36.7 us -> 8.69 us
  local copies, waits for them, and re-layouts: 0.13 us -> 1.69 us
  other arithmetic: 0.03 us -> 1.45 us
  waiting for transfers between devices: 8.73 us -> 9.38 us
    pallas_call x1, Pallas kernels: 26.9 us -> 1.3 us  [cut(): pl.pallas_call(cut_kernel, out_shape=(jax.ShapeDtypeStruct((hours, begin)...]
    pallas_call x1 -> x0, Pallas kernels: 1.92 us -> none  [operate(): pl.pallas_call(operator_kernel, out_shape=jax.ShapeDtypeStruct((rank, ran...]
    unnamed x9 -> x7, local copies, waits for them, and re-layouts: 0.13 us -> 1.02 us
    another operation x1, other arithmetic: 0.01 us -> 0.82 us  [per_device(): energy, coeffs = (inverse_energy[None, :], jnp.stack(coeffs))]
    dynamic_slice x1, local copies, waits for them, and re-layouts: 0.01 us -> 0.67 us  [per_device(): vectors = lax.dynamic_slice_in_dim(eigen_vectors, me * rows, rows, 1)]
    ppermute x5, waiting for transfers between devices: 1.91 us -> 2.56 us  [moved(): return lax.ppermute(value, ('tm', 'inner'), route)]
    add x1, other arithmetic: 0.01 us -> 0.62 us  [per_device(): mine = mine + near]
  transfers between devices with their start and end apart: 10 -> 10, of which waited for: 7 -> 6; matrix products, arithmetic and copies ran while one was open for 0% -> 9% of each run, Pallas kernels for 14% -> 18%
where the time goes in v11:
time: 33.5 us; the launch traced here: 33.2 us
  starting transfers between devices  11.3 us (34%)
  waiting for transfers between devices  9.38 us (28%)
  Pallas kernels  8.69 us (26%)
  local copies, waits for them, and re-layouts  1.69 us (5%)
  other arithmetic  1.45 us (4%)
  between operations  0.76 us (2%)
    ppermute x5, waiting for transfers between devices, swapped(): return lax.ppermute(value, axis, route)  6.82 us
    ppermute x5, starting transfers between devices, swapped(): return lax.ppermute(value, axis, route)  6.22 us
    ppermute x5, starting transfers between devices, moved(): return lax.ppermute(value, ('tm', 'inner'), route)  5.03 us
    pallas_call x1, Pallas kernels, rebuild_first(): pl.pallas_call(functools.partial(first_kernel, [0] * len(held), tiles), o...  3.07 us
    pallas_call x1, Pallas kernels, project(): pl.pallas_call(functools.partial(project_kernel, tiles), out_shape=(half,...  2.99 us
    ppermute x5, waiting for transfers between devices, moved(): return lax.ppermute(value, ('tm', 'inner'), route)  2.56 us
    pallas_call x1, Pallas kernels, rebuild_last(): pl.pallas_call(functools.partial(last_kernel, offsets, begin, tiles), out...  1.33 us
    pallas_call x1, Pallas kernels, cut(): pl.pallas_call(cut_kernel, out_shape=(jax.ShapeDtypeStruct((hours, begin)...  1.3 us
  transfers between devices with their start and end apart: 10, of which 6 were waited for; matrix products, arithmetic and copies ran while one was open for 9% of the time, Pallas kernels for 18%

profile of v11, /device:TPU:0, one launch (start us, length us, event | category | flops | bytes accessed | tf_op | source)
XLA Modules:
  0.0 33.2 jit_solution(12211143248888856194)
XLA Ops:
  0.6 0.0 copy-start
  0.6 0.0 copy-start.1
  0.7 0.0 copy-start.2
  0.7 1.3 %cut.1 = (bf16[64,6144]{1,0:T(8,128)(2,1)S(1)}, bf16[64,2048]{1,0:T(8,128)(2,1)S(1)}) custom-call(bf16[64,8192]{1,0:T(8,128)(2,1)} %bitcast.7), custom_call_target="tpu_custom_call" | custom-call | tf_op jit(solution)/shard_map/cut/pallas_call | solution.py:53
  2.0 3.0 %collective-permute-start.8 = (bf16[64,6144]{1,0:T(8,128)(2,1)S(1)}, bf16[64,6144]{1,0:T(8,128)(2,1)S(1)}, u32[]{:S(2)}, u32[]{:S(2)}) collective-permute-start(bf16[64,6144]{1,0:T(8,128)(2,1)S(1)} %get-tuple-element.15), channel_id=1, source_target_pairs={{16,0},{17,1},{0,16},{1,17},{18,2},{19,3},{2,18},{3,19},{20,4},{21... | collective-permute-start | bytes 2359304 | tf_op jit(solution)/shard_map/ppermute | solution.py:271
  5.0 3.0 %project.1 = (f32[32,256]{1,0:T(8,128)S(1)}, f32[32,256]{1,0:T(8,128)S(1)}) custom-call(bf16[64,8192]{1,0:T(8,128)(2,1)} %bitcast.8, bf16[8192,256]{1,0:T(8,128)(2,1)} %basis.1), custom_call_target="tpu_custom_call" | custom-call | tf_op jit(solution)/shard_map/project/pallas_call | solution.py:101
  8.0 0.1 collective-permute-start
  8.1 1.2 %collective-permute-done = f32[32,256]{1,0:T(8,128)S(1)} collective-permute-done((f32[32,256]{1,0:T(8,128)S(1)}, f32[32,256]{1,0:T(8,128)S(1)}, u32[]{:S(2)}, u32[]{:S(2)}) %collective-permute-start) | collective-permute-done | bytes 32800 | tf_op jit(solution)/shard_map/ppermute | solution.py:261
  9.3 2.5 %collective-permute-start.3 = (f32[32,256]{1,0:T(8,128)S(1)}, f32[32,256]{1,0:T(8,128)S(1)}, u32[]{:S(2)}, u32[]{:S(2)}) collective-permute-start(f32[32,256]{1,0:T(8,128)S(1)} %add.19), channel_id=1, source_target_pairs={{6,0},{4,2},{2,4},{0,6},{14,8},{12,10},{10,12},{8,14},{7,1},{5,3},... | collective-permute-start | bytes 98312 | tf_op jit(solution)/shard_map/ppermute | solution.py:261
  11.8 0.4 %collective-permute-start.2 = (f32[32,256]{1,0:T(8,128)S(1)}, f32[32,256]{1,0:T(8,128)S(1)}, u32[]{:S(2)}, u32[]{:S(2)}) collective-permute-start(f32[32,256]{1,0:T(8,128)S(1)} %add.19), channel_id=1, source_target_pairs={{4,0},{6,2},{0,4},{2,6},{12,8},{14,10},{8,12},{10,14},{5,1},{7,3},... | collective-permute-start | bytes 98312 | tf_op jit(solution)/shard_map/ppermute | solution.py:261
  12.2 0.5 %collective-permute-start.1 = (f32[32,256]{1,0:T(8,128)S(1)}, f32[32,256]{1,0:T(8,128)S(1)}, u32[]{:S(2)}, u32[]{:S(2)}) collective-permute-start(f32[32,256]{1,0:T(8,128)S(1)} %add.19), channel_id=1, source_target_pairs={{2,0},{0,2},{6,4},{4,6},{10,8},{8,10},{14,12},{12,14},{3,1},{1,3},... | collective-permute-start | bytes 98312 | tf_op jit(solution)/shard_map/ppermute | solution.py:261
  12.7 1.3 %collective-permute-done.3 = f32[32,256]{1,0:T(8,128)S(1)} collective-permute-done((f32[32,256]{1,0:T(8,128)S(1)}, f32[32,256]{1,0:T(8,128)S(1)}, u32[]{:S(2)}, u32[]{:S(2)}) %collective-permute-start.3) | collective-permute-done | bytes 32800 | tf_op jit(solution)/shard_map/ppermute | solution.py:261
  14.1 1.6 %collective-permute-done.2 = f32[32,256]{1,0:T(8,128)S(1)} collective-permute-done((f32[32,256]{1,0:T(8,128)S(1)}, f32[32,256]{1,0:T(8,128)S(1)}, u32[]{:S(2)}, u32[]{:S(2)}) %collective-permute-start.2) | collective-permute-done | bytes 32800 | tf_op jit(solution)/shard_map/ppermute | solution.py:261
  15.7 0.4 %collective-permute-done.1 = f32[32,256]{1,0:T(8,128)S(1)} collective-permute-done((f32[32,256]{1,0:T(8,128)S(1)}, f32[32,256]{1,0:T(8,128)S(1)}, u32[]{:S(2)}, u32[]{:S(2)}) %collective-permute-start.1) | collective-permute-done | bytes 32800 | tf_op jit(solution)/shard_map/ppermute | solution.py:261
  16.2 2.7 %collective-permute-start.4 = (f32[32,256]{1,0:T(8,128)S(1)}, f32[32,256]{1,0:T(8,128)S(1)}, u32[]{:S(2)}, u32[]{:S(2)}) collective-permute-start(f32[32,256]{1,0:T(8,128)S(1)} %add_add_fusion), channel_id=1, source_target_pairs={{8,0},{10,2},{12,4},{14,6},{0,8},{2,10},{4,12},{6,14},{9,1},{11,3}... | collective-permute-start | bytes 98312 | tf_op jit(solution)/shard_map/ppermute | solution.py:261
  18.8 2.2 %collective-permute-done.4 = f32[32,256]{1,0:T(8,128)S(1)} collective-permute-done((f32[32,256]{1,0:T(8,128)S(1)}, f32[32,256]{1,0:T(8,128)S(1)}, u32[]{:S(2)}, u32[]{:S(2)}) %collective-permute-start.4) | collective-permute-done | bytes 32800 | tf_op jit(solution)/shard_map/ppermute | solution.py:261
  21.0 0.6 %add.23 = f32[32,256]{1,0:T(8,128)} add(f32[32,256]{1,0:T(8,128)S(1)} %add_add_fusion, f32[32,256]{1,0:T(8,128)S(1)} %collective-permute-done.4) | non-fusion elementwise | flops 8192 | bytes 98304 | tf_op jit(solution)/shard_map/add | solution.py:297
  21.7 0.5 %collective-permute-start.6 = (f32[32,256]{1,0:T(8,128)}, f32[32,256]{1,0:T(8,128)}, u32[]{:S(2)}, u32[]{:S(2)}) collective-permute-start(f32[32,256]{1,0:T(8,128)} %add.23), channel_id=1, source_target_pairs={{16,0},{17,1},{0,16},{1,17},{18,2},{19,3},{2,18},{3,19},{20,4},{21... | collective-permute-start | bytes 98312 | tf_op jit(solution)/shard_map/ppermute | solution.py:271
  22.2 0.0 collective-permute-start.5
  22.2 1.5 %collective-permute-start.9 = (bf16[64,2048]{1,0:T(8,128)(2,1)S(1)}, bf16[64,2048]{1,0:T(8,128)(2,1)S(1)}, u32[]{:S(2)}, u32[]{:S(2)}) collective-permute-start(bf16[64,2048]{1,0:T(8,128)(2,1)S(1)} %get-tuple-element.18), channel_id=1, source_target_pairs={{16,0},{17,1},{0,16},{1,17},{18,2},{19,3},{2,18},{3,19},{20,4},{21... | collective-permute-start | bytes 786440 | tf_op jit(solution)/shard_map/ppermute | solution.py:271
  23.7 2.5 %collective-permute-done.6 = f32[32,256]{1,0:T(8,128)} collective-permute-done((f32[32,256]{1,0:T(8,128)}, f32[32,256]{1,0:T(8,128)}, u32[]{:S(2)}, u32[]{:S(2)}) %collective-permute-start.6) | collective-permute-done | bytes 32800 | tf_op jit(solution)/shard_map/ppermute | solution.py:271
  26.2 0.0 collective-permute-start.7
  26.2 0.0 copy-done
  26.2 0.7 %constant_dynamic-slice_fusion = bf16[256,256]{1,0:T(8,128)(2,1)} fusion(bf16[256,512]{1,0:T(8,128)(2,1)S(1)} %copy-done, s32[]{:T(128)S(6)} %select_n.3), kind=kLoop, calls=%fused_computation.2 | loop fusion | bytes 262148 | tf_op jit(solution)/shard_map/dynamic_slice | solution.py:307
  26.9 1.0 %copy.8 = bf16[256,256]{0,1:T(8,128)(2,1)S(1)} copy(bf16[256,256]{1,0:T(8,128)(2,1)} %constant_dynamic-slice_fusion) | data formatting | bytes 262144
  27.9 0.0 collective-permute-done.5
  27.9 0.0 collective-permute-done.7
  27.9 0.8 %pad_maximum_fusion.coeffs = f32[4,32,256]{2,1,0:T(8,128)S(1)} fusion(f32[1,32,256]{2,1,0:T(8,128)} %bitcast.6, f32[1,32,256]{2,1,0:T(8,128)} %bitcast.5, f32[1,32,256]{2,1,0:T(8,128)} %bitcast.4, f32[1,32,256]{2,1,0:T(8,128)} %bitcast.3), kind=kLoop, calls=%fused_computation | loop fusion | flops 98304 | bytes 262144 | tf_op jit(solution)/shard_map/stack | solution.py:308
  28.8 0.0 collective-permute-done.8.refs_1_
  28.8 0.0 copy-done.1
  28.8 0.0 copy-done.2
  28.8 3.1 %rebuild_first.1 = (f32[256,256]{1,0:T(8,128)}, bf16[256,8192]{1,0:T(8,128)(2,1)}, bf16[256,128]{1,0:T(8,128)(2,1)S(1)}) custom-call(f32[1,256]{1,0:T(1,128)S(1)} %bitcast.12, bf16[256,256]{1,0:T(8,128)(2,1)S(1)} %bitcast.11, f32[4,32,256]{2,1,0:T(8,128)S(1)} %pad_maximum_fusion.coeffs, bf16[64,8192]{1,0:T(8,128)(2,1)S(1)} %bitcast.9, ...), custom_call_target="tpu_custom_call" | custom-call | flops 1000000000 | tf_op jit(solution)/shard_map/rebuild_first/pallas_call | solution.py:213
  31.9 0.0 collective-permute-done.9.refs_1_
  31.9 1.3 %rebuild_last.1 = bf16[256,8192]{1,0:T(8,128)(2,1)} custom-call(bf16[256,128]{1,0:T(8,128)(2,1)S(1)} %get-tuple-element.17.weights, bf16[64,8192]{1,0:T(8,128)(2,1)S(1)} %bitcast.10, bf16[64,2048]{1,0:T(8,128)(2,1)S(1)} %collective-permute-done.9.refs_1_, bf16[256,8192]{1,0:T(8,128)(2,1)} %get-tuple-element.19.refs_2_), custom_call_target="tpu_custom_call", output_to_operand_aliasing={{}: (3, {})} | custom-call | tf_op jit(solution)/shard_map/rebuild_last/pallas_call | solution.py:241
  (2 shorter events, 0.0 us)
Async XLA Ops:
  0.6 25.6 %copy-start = (bf16[256,512]{1,0:T(8,128)(2,1)S(1)}, bf16[256,512]{1,0:T(8,128)(2,1)}, u32[]{:S(2)}) copy-start(bf16[256,512]{1,0:T(8,128)(2,1)} %param.7) | copy-start | bytes 786436
  0.6 28.1 %copy-start.1 = (bf16[8192,64]{0,1:T(8,128)(2,1)S(1)}, bf16[8192,64]{0,1:T(8,128)(2,1)}, u32[]{:S(2)}) copy-start(bf16[8192,64]{0,1:T(8,128)(2,1)} %param.5) | copy-start | bytes 3145732
  0.7 28.1 %copy-start.2 = (f32[256]{0:T(256)S(1)}, f32[256]{0:T(256)}, u32[]{:S(2)}) copy-start(f32[256]{0:T(256)} %param.6) | copy-start | bytes 3076
  2.0 26.8 %collective-permute-start.8 = (bf16[64,6144]{1,0:T(8,128)(2,1)S(1)}, bf16[64,6144]{1,0:T(8,128)(2,1)S(1)}, u32[]{:S(2)}, u32[]{:S(2)}) collective-permute-start(bf16[64,6144]{1,0:T(8,128)(2,1)S(1)} %get-tuple-element.15), channel_id=1, source_target_pairs={{16,0},{17,1},{0,16},{1,17},{18,2},{19,3},{2,18},{3,19},{20,4},{21... | collective-permute-start | bytes 2359304 | tf_op jit(solution)/shard_map/ppermute | solution.py:271
  8.0 1.3 %collective-permute-start = (f32[32,256]{1,0:T(8,128)S(1)}, f32[32,256]{1,0:T(8,128)S(1)}, u32[]{:S(2)}, u32[]{:S(2)}) collective-permute-start(f32[32,256]{1,0:T(8,128)S(1)} %get-tuple-element.12), channel_id=1, source_target_pairs={{1,0},{0,1},{3,2},{2,3},{5,4},{4,5},{7,6},{6,7},{9,8},{8,9},{11,10... | collective-permute-start | bytes 98312 | tf_op jit(solution)/shard_map/ppermute | solution.py:261
  9.3 4.8 %collective-permute-start.3 = (f32[32,256]{1,0:T(8,128)S(1)}, f32[32,256]{1,0:T(8,128)S(1)}, u32[]{:S(2)}, u32[]{:S(2)}) collective-permute-start(f32[32,256]{1,0:T(8,128)S(1)} %add.19), channel_id=1, source_target_pairs={{6,0},{4,2},{2,4},{0,6},{14,8},{12,10},{10,12},{8,14},{7,1},{5,3},... | collective-permute-start | bytes 98312 | tf_op jit(solution)/shard_map/ppermute | solution.py:261
  11.8 3.9 %collective-permute-start.2 = (f32[32,256]{1,0:T(8,128)S(1)}, f32[32,256]{1,0:T(8,128)S(1)}, u32[]{:S(2)}, u32[]{:S(2)}) collective-permute-start(f32[32,256]{1,0:T(8,128)S(1)} %add.19), channel_id=1, source_target_pairs={{4,0},{6,2},{0,4},{2,6},{12,8},{14,10},{8,12},{10,14},{5,1},{7,3},... | collective-permute-start | bytes 98312 | tf_op jit(solution)/shard_map/ppermute | solution.py:261
  12.2 3.9 %collective-permute-start.1 = (f32[32,256]{1,0:T(8,128)S(1)}, f32[32,256]{1,0:T(8,128)S(1)}, u32[]{:S(2)}, u32[]{:S(2)}) collective-permute-start(f32[32,256]{1,0:T(8,128)S(1)} %add.19), channel_id=1, source_target_pairs={{2,0},{0,2},{6,4},{4,6},{10,8},{8,10},{14,12},{12,14},{3,1},{1,3},... | collective-permute-start | bytes 98312 | tf_op jit(solution)/shard_map/ppermute | solution.py:261
  16.2 4.9 %collective-permute-start.4 = (f32[32,256]{1,0:T(8,128)S(1)}, f32[32,256]{1,0:T(8,128)S(1)}, u32[]{:S(2)}, u32[]{:S(2)}) collective-permute-start(f32[32,256]{1,0:T(8,128)S(1)} %add_add_fusion), channel_id=1, source_target_pairs={{8,0},{10,2},{12,4},{14,6},{0,8},{2,10},{4,12},{6,14},{9,1},{11,3}... | collective-permute-start | bytes 98312 | tf_op jit(solution)/shard_map/ppermute | solution.py:261
  21.7 4.6 %collective-permute-start.6 = (f32[32,256]{1,0:T(8,128)}, f32[32,256]{1,0:T(8,128)}, u32[]{:S(2)}, u32[]{:S(2)}) collective-permute-start(f32[32,256]{1,0:T(8,128)} %add.23), channel_id=1, source_target_pairs={{16,0},{17,1},{0,16},{1,17},{18,2},{19,3},{2,18},{3,19},{20,4},{21... | collective-permute-start | bytes 98312 | tf_op jit(solution)/shard_map/ppermute | solution.py:271
  22.2 5.7 %collective-permute-start.5 = (f32[32,256]{1,0:T(8,128)}, f32[32,256]{1,0:T(8,128)}, u32[]{:S(2)}, u32[]{:S(2)}) collective-permute-start(f32[32,256]{1,0:T(8,128)} %add.23), channel_id=1, source_target_pairs={{1,0},{0,1},{17,16},{16,17},{3,2},{2,3},{19,18},{18,19},{5,4},{4,5... | collective-permute-start | bytes 98312 | tf_op jit(solution)/shard_map/ppermute | solution.py:271
  22.2 9.7 %collective-permute-start.9 = (bf16[64,2048]{1,0:T(8,128)(2,1)S(1)}, bf16[64,2048]{1,0:T(8,128)(2,1)S(1)}, u32[]{:S(2)}, u32[]{:S(2)}) collective-permute-start(bf16[64,2048]{1,0:T(8,128)(2,1)S(1)} %get-tuple-element.18), channel_id=1, source_target_pairs={{16,0},{17,1},{0,16},{1,17},{18,2},{19,3},{2,18},{3,19},{20,4},{21... | collective-permute-start | bytes 786440 | tf_op jit(solution)/shard_map/ppermute | solution.py:271
  26.2 1.7 %collective-permute-start.7 = (f32[32,256]{1,0:T(8,128)}, f32[32,256]{1,0:T(8,128)}, u32[]{:S(2)}, u32[]{:S(2)}) collective-permute-start(f32[32,256]{1,0:T(8,128)} %collective-permute-done.6), channel_id=1, source_target_pairs={{1,0},{0,1},{17,16},{16,17},{3,2},{2,3},{19,18},{18,19},{5,4},{4,5... | collective-permute-start | bytes 98312 | tf_op jit(solution)/shard_map/ppermute | solution.py:271

commit v12 on v8

v12 whole, which is shorter than its diff:
```python
import functools

import jax
import jax.numpy as jnp
from jax import lax
from jax.experimental import pallas as pl
from jax.experimental.pallas import tpu as pltpu
from jax.sharding import Mesh, PartitionSpec as P

ROWS = (((1,), (0,)), ((), ()))
FIRST = (((0,), (0,)), ((), ()))
LAST = (((1,), (1,)), ((), ()))
STRIP = 256
FREE = pl.CostEstimate(flops=0, bytes_accessed=0, transcendentals=0)
ANYWHERE = pl.BlockSpec(memory_space=pl.ANY)
IN_VMEM = pl.BlockSpec(memory_space=pltpu.VMEM)


def started(copies):
    for copy in copies:
        copy.start()
    return copies


def waited(copies):
    for copy in copies:
        copy.wait()


def in_parts(value):
    high = value.astype(jnp.bfloat16)
    return high, (value - high.astype(jnp.float32)).astype(jnp.bfloat16)


def product(left, right, dims):
    return lax.dot_general(left, right, dims, preferred_element_type=jnp.float32)


def project_kernel(tiles, snapshots, basis, kept, given, fields, patterns, halves, arrived):
    cells = snapshots.shape[1]
    tile = cells // tiles
    copies = []
    for i in range(tiles):
        span = pl.ds(i * tile, tile)
        copies.append(
            (
                pltpu.make_async_copy(snapshots.at[:, span], fields.at[:, span], arrived.at[0, i]),
                pltpu.make_async_copy(basis.at[span], patterns.at[span], arrived.at[1, i]),
            )
        )
    for pair in copies:
        for copy in pair:
            copy.start()
    total = jnp.zeros((fields.shape[0], patterns.shape[1]), jnp.float32)
    for i, pair in enumerate(copies):
        for copy in pair:
            copy.wait()
        span = pl.ds(i * tile, tile)
        total += product(fields[:, span], patterns[span], ROWS)
    half = kept.shape[0]
    core = lax.axis_index("inner")
    halves[0] = total[:half]
    halves[1] = total[half:]
    kept[...] = halves[core]
    given[...] = halves[1 - core]


def project(snapshots, basis, tiles):
    hours = snapshots.shape[0]
    rank = basis.shape[1]
    half = jax.ShapeDtypeStruct((hours // 2, rank), jnp.float32)
    return pl.pallas_call(
        functools.partial(project_kernel, tiles),
        out_shape=(half, half),
        in_specs=[ANYWHERE] * 2,
        out_specs=(pl.BlockSpec(memory_space=pltpu.VMEM),) * 2,
        scratch_shapes=[
            pltpu.VMEM(snapshots.shape, snapshots.dtype),
            pltpu.VMEM(basis.shape, basis.dtype),
            pltpu.VMEM((2, hours // 2, rank), jnp.float32),
            pltpu.SemaphoreType.DMA((2, tiles)),
        ],
        compiler_params=pltpu.CompilerParams(vmem_limit_bytes=53 * 2**20),
        cost_estimate=FREE,
        name="project",
    )(snapshots, basis)


def gathered(held, fields, begin, width, arrived):
    rows = held[0].shape[0]
    span = pl.ds(begin, width)
    return [
        pltpu.make_async_copy(
            block.at[:, span], fields.at[pl.ds(k * rows, rows), span], arrived.at[k]
        )
        for k, block in enumerate(held)
    ]


def by_hours(known):
    me, core = lax.axis_index("tm"), lax.axis_index("inner")
    count = known.shape[0] // 2
    order = [
        2 * lax.rem(count + block - me, count) + lax.rem(2 + half - core, 2)
        for block in range(count)
        for half in range(2)
    ]
    return jnp.concatenate([known[at] for at in order], axis=0)


def lagged_and_scaled(every, energy):
    hour = lax.broadcasted_iota(jnp.int32, every.shape, 0)
    return jnp.where(hour == 0, 0.0, pltpu.roll(every, 1, 0)) * energy


def rebuild_kernel(parts, tiles, energy, vectors, coeffs, *refs):
    count, hours = coeffs.shape[0] // 2, 2 * coeffs.shape[1]
    held, refs = refs[:count], refs[count:]
    operator, modes, fields, known, turned, scale, scaled, made, square, arrived, sent = refs
    cells = modes.shape[1]
    sources = ((coeffs, known), (vectors, turned), (energy, scale))
    inputs = started(
        [
            pltpu.make_async_copy(source, target, arrived.at[parts + n, 0])
            for n, (source, target) in enumerate(sources)
        ]
    )
    width = cells // parts
    blocks = [
        started(gathered(held, fields, i * width, width, arrived.at[i])) for i in range(parts)
    ]
    waited(inputs)
    every = by_hours(known)
    scaled[...] = lagged_and_scaled(every.astype(jnp.float32), scale[...])
    me = lax.axis_index("tm")
    first = [lax.rem(me + k, count) * hours for k in range(count)]
    ordered = jnp.concatenate(
        [scaled[pl.ds(pl.multiple_of(at, hours), hours)] for at in first], axis=0
    )
    high, low = in_parts(ordered)
    weights = (product(turned[...], high, LAST) + product(turned[...], low, LAST)).astype(
        jnp.bfloat16
    )
    width = cells // tiles
    outgoing = []
    for i in range(tiles):
        if i % (tiles // parts) == 0:
            waited(blocks[i // (tiles // parts)])
        if i == tiles - 1:
            high, low = in_parts(scaled[...])
            square[...] = product(every, high, FIRST) + product(every, low, FIRST)
            outgoing += started([pltpu.make_async_copy(square, operator, sent.at[tiles])])
        for at in range(i * width, (i + 1) * width, STRIP):
            span = pl.ds(at, STRIP)
            made[:, span] = product(weights, fields[:, span], ROWS).astype(made.dtype)
        span = pl.ds(i * width, width)
        copy = pltpu.make_async_copy(made.at[:, span], modes.at[:, span], sent.at[i])
        outgoing += started([copy])
    waited(outgoing)


def rebuild(energy, vectors, coeffs, held, parts, tiles):
    blocks, half, rank = coeffs.shape
    hours, modes, cells = blocks * half, vectors.shape[0], held[0].shape[1]
    return pl.pallas_call(
        functools.partial(rebuild_kernel, parts, tiles),
        out_shape=(
            jax.ShapeDtypeStruct((rank, rank), jnp.float32),
            jax.ShapeDtypeStruct((modes, cells), jnp.bfloat16),
        ),
        in_specs=[ANYWHERE] * (3 + len(held)),
        out_specs=(ANYWHERE, ANYWHERE),
        scratch_shapes=[
            pltpu.VMEM((hours, cells), jnp.bfloat16),
            pltpu.VMEM(coeffs.shape, coeffs.dtype),
            pltpu.VMEM(vectors.shape, vectors.dtype),
            pltpu.VMEM(energy.shape, energy.dtype),
            pltpu.VMEM((hours, rank), jnp.float32),
            pltpu.VMEM((modes, cells), jnp.bfloat16),
            pltpu.VMEM((rank, rank), jnp.float32),
            pltpu.SemaphoreType.DMA((parts + 3, len(held))),
            pltpu.SemaphoreType.DMA((tiles + 1,)),
        ],
        compiler_params=pltpu.CompilerParams(vmem_limit_bytes=40 * 2**20),
        cost_estimate=FREE,
        name="rebuild",
    )(energy, vectors, coeffs, *held)


def swapped(value, axis, bit):
    route = [(i ^ bit, i) for i in range(lax.axis_size(axis))]
    return lax.ppermute(value, axis, route)


def moved(value, by, swap):
    size = lax.axis_size("tm")
    route = [
        (2 * ((i + by) % size) + (core ^ swap), 2 * i + core)
        for i in range(size)
        for core in range(2)
    ]
    return lax.ppermute(value, ("tm", "inner"), route)


def per_device(eof_basis, snapshots, inverse_energy, eigen_vectors):
    tm, outer = lax.axis_size("tm"), lax.axis_size("outer")
    me = lax.axis_index("tm")
    fields = snapshots.T

    held = [fields] + [moved(fields, k, 0) for k in range(1, tm)]

    kept, given = project(fields, eof_basis, 8)
    mine = kept + swapped(given, "inner", 1)
    bit = 1
    while bit < outer:
        near = swapped(mine, "outer", bit)
        if 2 * bit < outer:
            far, both = (swapped(mine, "outer", b) for b in (2 * bit, 3 * bit))
            mine = (mine + near) + (far + both)
        else:
            mine = mine + near
        bit *= 4
    mine = mine.astype(jnp.bfloat16)
    coeffs = [mine, moved(mine, 0, 1)]
    for k in range(1, tm):
        coeffs += [moved(mine, k, 0), moved(mine, k, 1)]

    rows = eigen_vectors.shape[1] // tm
    vectors = lax.dynamic_slice_in_dim(eigen_vectors, me * rows, rows, 1)
    energy, coeffs = inverse_energy[None, :], jnp.stack(coeffs)
    return rebuild(energy, vectors.T, coeffs, held, 2, 4)


def solution(mesh):
    tm, space = mesh.shape["tm"], mesh.shape["space"]
    split = Mesh(mesh.devices.reshape(tm, space // 2, 2), ("tm", "outer", "inner"))
    cells = ("outer", "inner")
    in_specs = (P(cells, None), P(cells, "tm"), P(), P())
    out_specs = (P(), P("tm", cells))
    return jax.shard_map(
        per_device, mesh=split, in_specs=in_specs, out_specs=out_specs, check_vma=False
    )
```

time: 32.6 us -> 31.4 us (0.963)
  waiting for transfers between devices: 13.5 us -> 12.9 us
  Pallas kernels: 6.96 us -> 6.44 us
    ppermute x4, waiting for transfers between devices: 6.68 us -> 6.03 us  [moved(): return lax.ppermute(value, ('tm', 'inner'), route)]
    pallas_call x1, Pallas kernels: 3.98 us -> 3.46 us  [rebuild(): pl.pallas_call(functools.partial(rebuild_kernel, parts, tiles), out_shape...]
  transfers between devices with their start and end apart: 9 -> 9, of which waited for: 7 -> 7; matrix products, arithmetic and copies ran while one was open for 1% -> 0% of each run, Pallas kernels for 9% -> 10%
where the time goes in v12:
time: 31.4 us; the launch traced here: 31.2 us
  waiting for transfers between devices  12.9 us (41%)
  starting transfers between devices  11.1 us (35%)
  Pallas kernels  6.44 us (21%)
  between operations  0.73 us (2%)
    ppermute x5, waiting for transfers between devices, swapped(): return lax.ppermute(value, axis, route)  6.82 us
    ppermute x5, starting transfers between devices, swapped(): return lax.ppermute(value, axis, route)  6.22 us
    ppermute x4, waiting for transfers between devices, moved(): return lax.ppermute(value, ('tm', 'inner'), route)  6.03 us
    ppermute x4, starting transfers between devices, moved(): return lax.ppermute(value, ('tm', 'inner'), route)  4.86 us
    pallas_call x1, Pallas kernels, rebuild(): pl.pallas_call(functools.partial(rebuild_kernel, parts, tiles), out_shape...  3.46 us
    pallas_call x1, Pallas kernels, project(): pl.pallas_call(functools.partial(project_kernel, tiles), out_shape=(half,...  2.98 us
  transfers between devices with their start and end apart: 9, of which 7 were waited for; matrix products, arithmetic and copies ran while one was open for 0% of the time, Pallas kernels for 10%

profile of v12, /device:TPU:0, one launch (start us, length us, event | category | flops | bytes accessed | tf_op | source)
XLA Modules:
  0.0 31.2 jit_solution(17344700925450761884)
XLA Ops:
  0.6 0.0 copy-start
  0.6 0.0 copy-start.1
  0.7 0.0 copy-start.2
  0.7 3.0 %collective-permute-start.8 = (bf16[64,8192]{1,0:T(8,128)(2,1)}, bf16[64,8192]{1,0:T(8,128)(2,1)S(1)}, u32[]{:S(2)}, u32[]{:S(2)}) collective-permute-start(bf16[64,8192]{1,0:T(8,128)(2,1)} %bitcast.7), channel_id=1, source_target_pairs={{16,0},{17,1},{0,16},{1,17},{18,2},{19,3},{2,18},{3,19},{20,4},{21... | collective-permute-start | bytes 3145736 | tf_op jit(solution)/shard_map/ppermute | solution.py:202
  3.7 3.0 %project.1 = (f32[32,256]{1,0:T(8,128)S(1)}, f32[32,256]{1,0:T(8,128)S(1)}) custom-call(bf16[64,8192]{1,0:T(8,128)(2,1)} %bitcast.8, bf16[8192,256]{1,0:T(8,128)(2,1)} %basis.1), custom_call_target="tpu_custom_call" | custom-call | tf_op jit(solution)/shard_map/project/pallas_call | solution.py:72
  6.7 0.1 collective-permute-start
  6.7 1.2 %collective-permute-done = f32[32,256]{1,0:T(8,128)S(1)} collective-permute-done((f32[32,256]{1,0:T(8,128)S(1)}, f32[32,256]{1,0:T(8,128)S(1)}, u32[]{:S(2)}, u32[]{:S(2)}) %collective-permute-start) | collective-permute-done | bytes 32800 | tf_op jit(solution)/shard_map/ppermute | solution.py:192
  7.9 2.5 %collective-permute-start.3 = (f32[32,256]{1,0:T(8,128)S(1)}, f32[32,256]{1,0:T(8,128)S(1)}, u32[]{:S(2)}, u32[]{:S(2)}) collective-permute-start(f32[32,256]{1,0:T(8,128)S(1)} %add.19), channel_id=1, source_target_pairs={{6,0},{4,2},{2,4},{0,6},{14,8},{12,10},{10,12},{8,14},{7,1},{5,3},... | collective-permute-start | bytes 98312 | tf_op jit(solution)/shard_map/ppermute | solution.py:192
  10.5 0.4 %collective-permute-start.2 = (f32[32,256]{1,0:T(8,128)S(1)}, f32[32,256]{1,0:T(8,128)S(1)}, u32[]{:S(2)}, u32[]{:S(2)}) collective-permute-start(f32[32,256]{1,0:T(8,128)S(1)} %add.19), channel_id=1, source_target_pairs={{4,0},{6,2},{0,4},{2,6},{12,8},{14,10},{8,12},{10,14},{5,1},{7,3},... | collective-permute-start | bytes 98312 | tf_op jit(solution)/shard_map/ppermute | solution.py:192
  10.9 0.5 %collective-permute-start.1 = (f32[32,256]{1,0:T(8,128)S(1)}, f32[32,256]{1,0:T(8,128)S(1)}, u32[]{:S(2)}, u32[]{:S(2)}) collective-permute-start(f32[32,256]{1,0:T(8,128)S(1)} %add.19), channel_id=1, source_target_pairs={{2,0},{0,2},{6,4},{4,6},{10,8},{8,10},{14,12},{12,14},{3,1},{1,3},... | collective-permute-start | bytes 98312 | tf_op jit(solution)/shard_map/ppermute | solution.py:192
  11.4 1.3 %collective-permute-done.3 = f32[32,256]{1,0:T(8,128)S(1)} collective-permute-done((f32[32,256]{1,0:T(8,128)S(1)}, f32[32,256]{1,0:T(8,128)S(1)}, u32[]{:S(2)}, u32[]{:S(2)}) %collective-permute-start.3) | collective-permute-done | bytes 32800 | tf_op jit(solution)/shard_map/ppermute | solution.py:192
  12.7 1.6 %collective-permute-done.2 = f32[32,256]{1,0:T(8,128)S(1)} collective-permute-done((f32[32,256]{1,0:T(8,128)S(1)}, f32[32,256]{1,0:T(8,128)S(1)}, u32[]{:S(2)}, u32[]{:S(2)}) %collective-permute-start.2) | collective-permute-done | bytes 32800 | tf_op jit(solution)/shard_map/ppermute | solution.py:192
  14.4 0.4 %collective-permute-done.1 = f32[32,256]{1,0:T(8,128)S(1)} collective-permute-done((f32[32,256]{1,0:T(8,128)S(1)}, f32[32,256]{1,0:T(8,128)S(1)}, u32[]{:S(2)}, u32[]{:S(2)}) %collective-permute-start.1) | collective-permute-done | bytes 32800 | tf_op jit(solution)/shard_map/ppermute | solution.py:192
  14.8 2.7 %collective-permute-start.4 = (f32[32,256]{1,0:T(8,128)S(1)}, f32[32,256]{1,0:T(8,128)S(1)}, u32[]{:S(2)}, u32[]{:S(2)}) collective-permute-start(f32[32,256]{1,0:T(8,128)S(1)} %add_add_fusion), channel_id=1, source_target_pairs={{8,0},{10,2},{12,4},{14,6},{0,8},{2,10},{4,12},{6,14},{9,1},{11,3}... | collective-permute-start | bytes 98312 | tf_op jit(solution)/shard_map/ppermute | solution.py:192
  17.5 2.2 %collective-permute-done.4 = f32[32,256]{1,0:T(8,128)S(1)} collective-permute-done((f32[32,256]{1,0:T(8,128)S(1)}, f32[32,256]{1,0:T(8,128)S(1)}, u32[]{:S(2)}, u32[]{:S(2)}) %collective-permute-start.4) | collective-permute-done | bytes 32800 | tf_op jit(solution)/shard_map/ppermute | solution.py:192
  19.7 0.0 collective-permute-start.7
  19.7 0.6 %collective-permute-start.6 = (bf16[32,256]{1,0:T(8,128)(2,1)S(1)}, bf16[32,256]{1,0:T(8,128)(2,1)S(1)}, u32[]{:S(2)}, u32[]{:S(2)}) collective-permute-start(bf16[32,256]{1,0:T(8,128)(2,1)S(1)} %add_convert_fusion), channel_id=1, source_target_pairs={{16,0},{17,1},{0,16},{1,17},{18,2},{19,3},{2,18},{3,19},{20,4},{21... | collective-permute-start | bytes 49160 | tf_op jit(solution)/shard_map/ppermute | solution.py:202
  20.3 1.3 %collective-permute-start.5 = (bf16[32,256]{1,0:T(8,128)(2,1)S(1)}, bf16[32,256]{1,0:T(8,128)(2,1)S(1)}, u32[]{:S(2)}, u32[]{:S(2)}) collective-permute-start(bf16[32,256]{1,0:T(8,128)(2,1)S(1)} %add_convert_fusion), channel_id=1, source_target_pairs={{1,0},{0,1},{17,16},{16,17},{3,2},{2,3},{19,18},{18,19},{5,4},{4,5... | collective-permute-start | bytes 49160 | tf_op jit(solution)/shard_map/ppermute | solution.py:202
  21.6 0.0 copy-done
  21.6 0.1 copy.7
  21.7 5.1 %collective-permute-done.7 = bf16[32,256]{1,0:T(8,128)(2,1)S(1)} collective-permute-done((bf16[32,256]{1,0:T(8,128)(2,1)S(1)}, bf16[32,256]{1,0:T(8,128)(2,1)S(1)}, u32[]{:S(2)}, u32[]{:S(2)}) %collective-permute-start.7) | collective-permute-done | bytes 16416 | tf_op jit(solution)/shard_map/ppermute | solution.py:202
  26.8 0.9 %collective-permute-done.6 = bf16[32,256]{1,0:T(8,128)(2,1)S(1)} collective-permute-done((bf16[32,256]{1,0:T(8,128)(2,1)S(1)}, bf16[32,256]{1,0:T(8,128)(2,1)S(1)}, u32[]{:S(2)}, u32[]{:S(2)}) %collective-permute-start.6) | collective-permute-done | bytes 16416 | tf_op jit(solution)/shard_map/ppermute | solution.py:202
  27.7 0.0 collective-permute-done.5
  27.8 0.0 collective-permute-done.8.refs_1_
  27.8 0.0 copy-done.1
  27.8 0.0 copy-done.2
  27.8 3.5 %rebuild.1 = (f32[256,256]{1,0:T(8,128)}, bf16[256,8192]{1,0:T(8,128)(2,1)}) custom-call(f32[1,256]{1,0:T(1,128)S(1)} %bitcast.11, bf16[256,256]{1,0:T(8,128)(2,1)S(1)} %bitcast.10, bf16[4,32,256]{2,1,0:T(8,128)(2,1)S(1)} %pad_maximum_fusion.coeffs, bf16[64,8192]{1,0:T(8,128)(2,1)S(1)} %bitcast.9, bf16[64,8192]{1,0:T(8,128)(2,1)S(1)} %collective-permute-done.8.refs_1_), custom_call_target="tpu_custom_call" | custom-call | tf_op jit(solution)/shard_map/rebuild/pallas_call | solution.py:165
  (5 shorter events, 0.0 us)
Async XLA Ops:
  0.6 21.0 %copy-start = (bf16[256,512]{1,0:T(8,128)(2,1)S(1)}, bf16[256,512]{1,0:T(8,128)(2,1)}, u32[]{:S(2)}) copy-start(bf16[256,512]{1,0:T(8,128)(2,1)} %param.7) | copy-start | bytes 786436
  0.6 27.1 %copy-start.1 = (bf16[8192,64]{0,1:T(8,128)(2,1)S(1)}, bf16[8192,64]{0,1:T(8,128)(2,1)}, u32[]{:S(2)}) copy-start(bf16[8192,64]{0,1:T(8,128)(2,1)} %param.5) | copy-start | bytes 3145732
  0.7 27.1 %copy-start.2 = (f32[256]{0:T(256)S(1)}, f32[256]{0:T(256)}, u32[]{:S(2)}) copy-start(f32[256]{0:T(256)} %param.6) | copy-start | bytes 3076
  0.7 27.1 %collective-permute-start.8 = (bf16[64,8192]{1,0:T(8,128)(2,1)}, bf16[64,8192]{1,0:T(8,128)(2,1)S(1)}, u32[]{:S(2)}, u32[]{:S(2)}) collective-permute-start(bf16[64,8192]{1,0:T(8,128)(2,1)} %bitcast.7), channel_id=1, source_target_pairs={{16,0},{17,1},{0,16},{1,17},{18,2},{19,3},{2,18},{3,19},{20,4},{21... | collective-permute-start | bytes 3145736 | tf_op jit(solution)/shard_map/ppermute | solution.py:202
  6.7 1.3 %collective-permute-start = (f32[32,256]{1,0:T(8,128)S(1)}, f32[32,256]{1,0:T(8,128)S(1)}, u32[]{:S(2)}, u32[]{:S(2)}) collective-permute-start(f32[32,256]{1,0:T(8,128)S(1)} %get-tuple-element.5), channel_id=1, source_target_pairs={{1,0},{0,1},{3,2},{2,3},{5,4},{4,5},{7,6},{6,7},{9,8},{8,9},{11,10... | collective-permute-start | bytes 98312 | tf_op jit(solution)/shard_map/ppermute | solution.py:192
  7.9 4.8 %collective-permute-start.3 = (f32[32,256]{1,0:T(8,128)S(1)}, f32[32,256]{1,0:T(8,128)S(1)}, u32[]{:S(2)}, u32[]{:S(2)}) collective-permute-start(f32[32,256]{1,0:T(8,128)S(1)} %add.19), channel_id=1, source_target_pairs={{6,0},{4,2},{2,4},{0,6},{14,8},{12,10},{10,12},{8,14},{7,1},{5,3},... | collective-permute-start | bytes 98312 | tf_op jit(solution)/shard_map/ppermute | solution.py:192
  10.5 3.9 %collective-permute-start.2 = (f32[32,256]{1,0:T(8,128)S(1)}, f32[32,256]{1,0:T(8,128)S(1)}, u32[]{:S(2)}, u32[]{:S(2)}) collective-permute-start(f32[32,256]{1,0:T(8,128)S(1)} %add.19), channel_id=1, source_target_pairs={{4,0},{6,2},{0,4},{2,6},{12,8},{14,10},{8,12},{10,14},{5,1},{7,3},... | collective-permute-start | bytes 98312 | tf_op jit(solution)/shard_map/ppermute | solution.py:192
  10.9 3.9 %collective-permute-start.1 = (f32[32,256]{1,0:T(8,128)S(1)}, f32[32,256]{1,0:T(8,128)S(1)}, u32[]{:S(2)}, u32[]{:S(2)}) collective-permute-start(f32[32,256]{1,0:T(8,128)S(1)} %add.19), channel_id=1, source_target_pairs={{2,0},{0,2},{6,4},{4,6},{10,8},{8,10},{14,12},{12,14},{3,1},{1,3},... | collective-permute-start | bytes 98312 | tf_op jit(solution)/shard_map/ppermute | solution.py:192
  14.8 4.9 %collective-permute-start.4 = (f32[32,256]{1,0:T(8,128)S(1)}, f32[32,256]{1,0:T(8,128)S(1)}, u32[]{:S(2)}, u32[]{:S(2)}) collective-permute-start(f32[32,256]{1,0:T(8,128)S(1)} %add_add_fusion), channel_id=1, source_target_pairs={{8,0},{10,2},{12,4},{14,6},{0,8},{2,10},{4,12},{6,14},{9,1},{11,3}... | collective-permute-start | bytes 98312 | tf_op jit(solution)/shard_map/ppermute | solution.py:192
  19.7 7.1 %collective-permute-start.7 = (bf16[32,256]{1,0:T(8,128)(2,1)S(1)}, bf16[32,256]{1,0:T(8,128)(2,1)S(1)}, u32[]{:S(2)}, u32[]{:S(2)}) collective-permute-start(bf16[32,256]{1,0:T(8,128)(2,1)S(1)} %add_convert_fusion), channel_id=1, source_target_pairs={{17,0},{16,1},{1,16},{0,17},{19,2},{18,3},{3,18},{2,19},{21,4},{20... | collective-permute-start | bytes 49160 | tf_op jit(solution)/shard_map/ppermute | solution.py:202
  19.7 8.0 %collective-permute-start.6 = (bf16[32,256]{1,0:T(8,128)(2,1)S(1)}, bf16[32,256]{1,0:T(8,128)(2,1)S(1)}, u32[]{:S(2)}, u32[]{:S(2)}) collective-permute-start(bf16[32,256]{1,0:T(8,128)(2,1)S(1)} %add_convert_fusion), channel_id=1, source_target_pairs={{16,0},{17,1},{0,16},{1,17},{18,2},{19,3},{2,18},{3,19},{20,4},{21... | collective-permute-start | bytes 49160 | tf_op jit(solution)/shard_map/ppermute | solution.py:202
  20.3 7.4 %collective-permute-start.5 = (bf16[32,256]{1,0:T(8,128)(2,1)S(1)}, bf16[32,256]{1,0:T(8,128)(2,1)S(1)}, u32[]{:S(2)}, u32[]{:S(2)}) collective-permute-start(bf16[32,256]{1,0:T(8,128)(2,1)S(1)} %add_convert_fusion), channel_id=1, source_target_pairs={{1,0},{0,1},{17,16},{16,17},{3,2},{2,3},{19,18},{18,19},{5,4},{4,5... | collective-permute-start | bytes 49160 | tf_op jit(solution)/shard_map/ppermute | solution.py:202

commit v13 on v12

--- a/solution.py
+++ b/solution.py
@@ -113,16 +113,19 @@
     return jnp.where(hour == 0, 0.0, pltpu.roll(every, 1, 0)) * energy
 
 
-def rebuild_kernel(parts, tiles, energy, vectors, coeffs, *refs):
-    count, hours = coeffs.shape[0] // 2, 2 * coeffs.shape[1]
-    held, refs = refs[:count], refs[count:]
+def rebuild_kernel(parts, tiles, energy, vectors, *refs):
+    count = (len(refs) - 11) // 2
+    held, coeffs, refs = refs[:count], refs[count : 2 * count], refs[2 * count :]
     operator, modes, fields, known, turned, scale, scaled, made, square, arrived, sent = refs
-    cells = modes.shape[1]
-    sources = ((coeffs, known), (vectors, turned), (energy, scale))
+    hours, cells = held[0].shape
     inputs = started(
         [
-            pltpu.make_async_copy(source, target, arrived.at[parts + n, 0])
-            for n, (source, target) in enumerate(sources)
+            pltpu.make_async_copy(block, known.at[pl.ds(2 * k, 2)], arrived.at[parts, k])
+            for k, block in enumerate(coeffs)
+        ]
+        + [
+            pltpu.make_async_copy(energy, scale, arrived.at[parts + 1, 0]),
+            pltpu.make_async_copy(vectors, turned, arrived.at[parts + 2, 0]),
         ]
     )
     width = cells // parts
@@ -146,33 +149,33 @@
     for i in range(tiles):
         if i % (tiles // parts) == 0:
             waited(blocks[i // (tiles // parts)])
-        if i == tiles - 1:
-            high, low = in_parts(scaled[...])
-            square[...] = product(every, high, FIRST) + product(every, low, FIRST)
-            outgoing += started([pltpu.make_async_copy(square, operator, sent.at[tiles])])
         for at in range(i * width, (i + 1) * width, STRIP):
             span = pl.ds(at, STRIP)
             made[:, span] = product(weights, fields[:, span], ROWS).astype(made.dtype)
         span = pl.ds(i * width, width)
         copy = pltpu.make_async_copy(made.at[:, span], modes.at[:, span], sent.at[i])
         outgoing += started([copy])
+    high, low = in_parts(scaled[...])
+    square[...] = product(every, high, FIRST) + product(every, low, FIRST)
+    outgoing += started([pltpu.make_async_copy(square, operator, sent.at[tiles])])
     waited(outgoing)
 
 
-def rebuild(energy, vectors, coeffs, held, parts, tiles):
-    blocks, half, rank = coeffs.shape
-    hours, modes, cells = blocks * half, vectors.shape[0], held[0].shape[1]
+def rebuild(energy, vectors, held, coeffs, parts, tiles):
+    _, half, rank = coeffs[0].shape
+    hours, cells = held[0].shape
+    hours, modes = len(held) * hours, vectors.shape[0]
     return pl.pallas_call(
         functools.partial(rebuild_kernel, parts, tiles),
         out_shape=(
             jax.ShapeDtypeStruct((rank, rank), jnp.float32),
             jax.ShapeDtypeStruct((modes, cells), jnp.bfloat16),
         ),
-        in_specs=[ANYWHERE] * (3 + len(held)),
+        in_specs=[ANYWHERE] * (2 + 2 * len(held)),
         out_specs=(ANYWHERE, ANYWHERE),
         scratch_shapes=[
             pltpu.VMEM((hours, cells), jnp.bfloat16),
-            pltpu.VMEM(coeffs.shape, coeffs.dtype),
+            pltpu.VMEM((2 * len(held), half, rank), coeffs[0].dtype),
             pltpu.VMEM(vectors.shape, vectors.dtype),
             pltpu.VMEM(energy.shape, energy.dtype),
             pltpu.VMEM((hours, rank), jnp.float32),
@@ -184,7 +187,7 @@
         compiler_params=pltpu.CompilerParams(vmem_limit_bytes=40 * 2**20),
         cost_estimate=FREE,
         name="rebuild",
-    )(energy, vectors, coeffs, *held)
+    )(energy, vectors, *held, *coeffs)
 
 
 def swapped(value, axis, bit):
@@ -221,14 +224,12 @@
             mine = mine + near
         bit *= 4
     mine = mine.astype(jnp.bfloat16)
-    coeffs = [mine, moved(mine, 0, 1)]
-    for k in range(1, tm):
-        coeffs += [moved(mine, k, 0), moved(mine, k, 1)]
+    both = jnp.stack([mine, moved(mine, 0, 1)])
+    coeffs = [both] + [moved(both, k, 0) for k in range(1, tm)]
 
     rows = eigen_vectors.shape[1] // tm
     vectors = lax.dynamic_slice_in_dim(eigen_vectors, me * rows, rows, 1)
-    energy, coeffs = inverse_energy[None, :], jnp.stack(coeffs)
-    return rebuild(energy, vectors.T, coeffs, held, 2, 4)
+    return rebuild(inverse_energy[None, :], vectors.T, held, coeffs, 2, 4)
 
 
 def solution(mesh):

time: 31.4 us -> 31.4 us (level)
  starting transfers between devices: 11.1 us -> 9.76 us
  waiting for transfers between devices: 12.9 us -> 14.2 us
    ppermute x4 -> x3, starting transfers between devices: 4.86 us -> 3.54 us  [moved(): return lax.ppermute(value, ('tm', 'inner'), route)]
    ppermute x4 -> x3, waiting for transfers between devices: 6.03 us -> 7.33 us  [moved(): return lax.ppermute(value, ('tm', 'inner'), route)]
  transfers between devices with their start and end apart: 9 -> 8, of which waited for: 7 -> 7; matrix products, arithmetic and copies ran while one was open for 0% -> 0% of each run, Pallas kernels for 10% -> 10%
where the time goes in v13:
time: 31.4 us; the launch traced here: 31.2 us
  waiting for transfers between devices  14.2 us (45%)
  starting transfers between devices  9.76 us (31%)
  Pallas kernels  6.43 us (20%)
  between operations  0.71 us (2%)
    ppermute x3, waiting for transfers between devices, moved(): return lax.ppermute(value, ('tm', 'inner'), route)  7.33 us
    ppermute x5, waiting for transfers between devices, swapped(): return lax.ppermute(value, axis, route)  6.82 us
    ppermute x5, starting transfers between devices, swapped(): return lax.ppermute(value, axis, route)  6.22 us
    ppermute x3, starting transfers between devices, moved(): return lax.ppermute(value, ('tm', 'inner'), route)  3.54 us
    pallas_call x1, Pallas kernels, rebuild(): pl.pallas_call(functools.partial(rebuild_kernel, parts, tiles), out_shape...  3.45 us
    pallas_call x1, Pallas kernels, project(): pl.pallas_call(functools.partial(project_kernel, tiles), out_shape=(half,...  2.98 us
  transfers between devices with their start and end apart: 8, of which 7 were waited for; matrix products, arithmetic and copies ran while one was open for 0% of the time, Pallas kernels for 10%

profile of v13, /device:TPU:0, one launch (start us, length us, event | category | flops | bytes accessed | tf_op | source)
XLA Modules:
  0.0 31.2 jit_solution(7873721618649210959)
XLA Ops:
  0.6 0.0 copy-start
  0.6 0.0 copy-start.1
  0.7 0.0 copy-start.2
  0.7 3.0 %collective-permute-start = (bf16[64,8192]{1,0:T(8,128)(2,1)}, bf16[64,8192]{1,0:T(8,128)(2,1)S(1)}, u32[]{:S(2)}, u32[]{:S(2)}) collective-permute-start(bf16[64,8192]{1,0:T(8,128)(2,1)} %bitcast.5), channel_id=1, source_target_pairs={{16,0},{17,1},{0,16},{1,17},{18,2},{19,3},{2,18},{3,19},{20,4},{21... | collective-permute-start | bytes 3145736 | tf_op jit(solution)/shard_map/ppermute | solution.py:205
  3.7 3.0 %project.1 = (f32[32,256]{1,0:T(8,128)S(1)}, f32[32,256]{1,0:T(8,128)S(1)}) custom-call(bf16[64,8192]{1,0:T(8,128)(2,1)} %bitcast.6, bf16[8192,256]{1,0:T(8,128)(2,1)} %basis.1), custom_call_target="tpu_custom_call" | custom-call | tf_op jit(solution)/shard_map/project/pallas_call | solution.py:72
  6.7 0.1 collective-permute-start.1
  6.7 1.2 %collective-permute-done.1 = f32[32,256]{1,0:T(8,128)S(1)} collective-permute-done((f32[32,256]{1,0:T(8,128)S(1)}, f32[32,256]{1,0:T(8,128)S(1)}, u32[]{:S(2)}, u32[]{:S(2)}) %collective-permute-start.1) | collective-permute-done | bytes 32800 | tf_op jit(solution)/shard_map/ppermute | solution.py:195
  7.9 2.5 %collective-permute-start.4 = (f32[32,256]{1,0:T(8,128)S(1)}, f32[32,256]{1,0:T(8,128)S(1)}, u32[]{:S(2)}, u32[]{:S(2)}) collective-permute-start(f32[32,256]{1,0:T(8,128)S(1)} %add.19), channel_id=1, source_target_pairs={{6,0},{4,2},{2,4},{0,6},{14,8},{12,10},{10,12},{8,14},{7,1},{5,3},... | collective-permute-start | bytes 98312 | tf_op jit(solution)/shard_map/ppermute | solution.py:195
  10.5 0.4 %collective-permute-start.3 = (f32[32,256]{1,0:T(8,128)S(1)}, f32[32,256]{1,0:T(8,128)S(1)}, u32[]{:S(2)}, u32[]{:S(2)}) collective-permute-start(f32[32,256]{1,0:T(8,128)S(1)} %add.19), channel_id=1, source_target_pairs={{4,0},{6,2},{0,4},{2,6},{12,8},{14,10},{8,12},{10,14},{5,1},{7,3},... | collective-permute-start | bytes 98312 | tf_op jit(solution)/shard_map/ppermute | solution.py:195
  10.9 0.5 %collective-permute-start.2 = (f32[32,256]{1,0:T(8,128)S(1)}, f32[32,256]{1,0:T(8,128)S(1)}, u32[]{:S(2)}, u32[]{:S(2)}) collective-permute-start(f32[32,256]{1,0:T(8,128)S(1)} %add.19), channel_id=1, source_target_pairs={{2,0},{0,2},{6,4},{4,6},{10,8},{8,10},{14,12},{12,14},{3,1},{1,3},... | collective-permute-start | bytes 98312 | tf_op jit(solution)/shard_map/ppermute | solution.py:195
  11.4 1.3 %collective-permute-done.4 = f32[32,256]{1,0:T(8,128)S(1)} collective-permute-done((f32[32,256]{1,0:T(8,128)S(1)}, f32[32,256]{1,0:T(8,128)S(1)}, u32[]{:S(2)}, u32[]{:S(2)}) %collective-permute-start.4) | collective-permute-done | bytes 32800 | tf_op jit(solution)/shard_map/ppermute | solution.py:195
  12.7 1.6 %collective-permute-done.3 = f32[32,256]{1,0:T(8,128)S(1)} collective-permute-done((f32[32,256]{1,0:T(8,128)S(1)}, f32[32,256]{1,0:T(8,128)S(1)}, u32[]{:S(2)}, u32[]{:S(2)}) %collective-permute-start.3) | collective-permute-done | bytes 32800 | tf_op jit(solution)/shard_map/ppermute | solution.py:195
  14.4 0.4 %collective-permute-done.2 = f32[32,256]{1,0:T(8,128)S(1)} collective-permute-done((f32[32,256]{1,0:T(8,128)S(1)}, f32[32,256]{1,0:T(8,128)S(1)}, u32[]{:S(2)}, u32[]{:S(2)}) %collective-permute-start.2) | collective-permute-done | bytes 32800 | tf_op jit(solution)/shard_map/ppermute | solution.py:195
  14.8 2.7 %collective-permute-start.5 = (f32[32,256]{1,0:T(8,128)S(1)}, f32[32,256]{1,0:T(8,128)S(1)}, u32[]{:S(2)}, u32[]{:S(2)}) collective-permute-start(f32[32,256]{1,0:T(8,128)S(1)} %add_add_fusion), channel_id=1, source_target_pairs={{8,0},{10,2},{12,4},{14,6},{0,8},{2,10},{4,12},{6,14},{9,1},{11,3}... | collective-permute-start | bytes 98312 | tf_op jit(solution)/shard_map/ppermute | solution.py:195
  17.5 2.2 %collective-permute-done.5 = f32[32,256]{1,0:T(8,128)S(1)} collective-permute-done((f32[32,256]{1,0:T(8,128)S(1)}, f32[32,256]{1,0:T(8,128)S(1)}, u32[]{:S(2)}, u32[]{:S(2)}) %collective-permute-start.5) | collective-permute-done | bytes 32800 | tf_op jit(solution)/shard_map/ppermute | solution.py:195
  19.7 0.0 collective-permute-start.6
  19.7 1.2 %collective-permute-done.6 = bf16[32,256]{1,0:T(8,128)(2,1)S(1)} collective-permute-done((bf16[32,256]{1,0:T(8,128)(2,1)S(1)}, bf16[32,256]{1,0:T(8,128)(2,1)S(1)}, u32[]{:S(2)}, u32[]{:S(2)}) %collective-permute-start.6) | collective-permute-done | bytes 16416 | tf_op jit(solution)/shard_map/ppermute | solution.py:205
  20.9 0.5 %collective-permute-start.7 = (bf16[2,32,256]{2,1,0:T(8,128)(2,1)S(1)}, bf16[2,32,256]{2,1,0:T(8,128)(2,1)S(1)}, u32[]{:S(2)}, u32[]{:S(2)}) collective-permute-start(bf16[2,32,256]{2,1,0:T(8,128)(2,1)S(1)} %pad_maximum_fusion.refs_2_), channel_id=1, source_target_pairs={{16,0},{17,1},{0,16},{1,17},{18,2},{19,3},{2,18},{3,19},{20,4},{21... | collective-permute-start | bytes 98312 | tf_op jit(solution)/shard_map/ppermute | solution.py:205
  21.5 0.0 copy-done
  21.5 0.1 copy.7
  21.6 6.2 %collective-permute-done.7.refs_3_ = bf16[2,32,256]{2,1,0:T(8,128)(2,1)S(1)} collective-permute-done((bf16[2,32,256]{2,1,0:T(8,128)(2,1)S(1)}, bf16[2,32,256]{2,1,0:T(8,128)(2,1)S(1)}, u32[]{:S(2)}, u32[]{:S(2)}) %collective-permute-start.7) | collective-permute-done | bytes 32800 | tf_op jit(solution)/shard_map/ppermute | solution.py:205
  27.7 0.0 collective-permute-done.refs_1_
  27.7 0.0 copy-done.1
  27.7 0.0 copy-done.2
  27.8 3.5 %rebuild.1 = (f32[256,256]{1,0:T(8,128)}, bf16[256,8192]{1,0:T(8,128)(2,1)}) custom-call(f32[1,256]{1,0:T(1,128)S(1)} %bitcast.9, bf16[256,256]{1,0:T(8,128)(2,1)S(1)} %bitcast.8, bf16[64,8192]{1,0:T(8,128)(2,1)S(1)} %bitcast.7, bf16[64,8192]{1,0:T(8,128)(2,1)S(1)} %collective-permute-done.refs_1_, bf16[2,32,256]{2,1,0:T(8,128)(2,1)S(1)} %pad_maximum_fusion.refs_2_, ...), custom_call_target="tpu_custom_call" | custom-call | tf_op jit(solution)/shard_map/rebuild/pallas_call | solution.py:168
  (5 shorter events, 0.0 us)
Async XLA Ops:
  0.6 20.8 %copy-start = (bf16[256,512]{1,0:T(8,128)(2,1)S(1)}, bf16[256,512]{1,0:T(8,128)(2,1)}, u32[]{:S(2)}) copy-start(bf16[256,512]{1,0:T(8,128)(2,1)} %param.7) | copy-start | bytes 786436
  0.6 27.1 %copy-start.1 = (bf16[8192,64]{0,1:T(8,128)(2,1)S(1)}, bf16[8192,64]{0,1:T(8,128)(2,1)}, u32[]{:S(2)}) copy-start(bf16[8192,64]{0,1:T(8,128)(2,1)} %param.5) | copy-start | bytes 3145732
  0.7 27.1 %copy-start.2 = (f32[256]{0:T(256)S(1)}, f32[256]{0:T(256)}, u32[]{:S(2)}) copy-start(f32[256]{0:T(256)} %param.6) | copy-start | bytes 3076
  0.7 27.1 %collective-permute-start = (bf16[64,8192]{1,0:T(8,128)(2,1)}, bf16[64,8192]{1,0:T(8,128)(2,1)S(1)}, u32[]{:S(2)}, u32[]{:S(2)}) collective-permute-start(bf16[64,8192]{1,0:T(8,128)(2,1)} %bitcast.5), channel_id=1, source_target_pairs={{16,0},{17,1},{0,16},{1,17},{18,2},{19,3},{2,18},{3,19},{20,4},{21... | collective-permute-start | bytes 3145736 | tf_op jit(solution)/shard_map/ppermute | solution.py:205
  6.7 1.3 %collective-permute-start.1 = (f32[32,256]{1,0:T(8,128)S(1)}, f32[32,256]{1,0:T(8,128)S(1)}, u32[]{:S(2)}, u32[]{:S(2)}) collective-permute-start(f32[32,256]{1,0:T(8,128)S(1)} %get-tuple-element.5), channel_id=1, source_target_pairs={{1,0},{0,1},{3,2},{2,3},{5,4},{4,5},{7,6},{6,7},{9,8},{8,9},{11,10... | collective-permute-start | bytes 98312 | tf_op jit(solution)/shard_map/ppermute | solution.py:195
  7.9 4.8 %collective-permute-start.4 = (f32[32,256]{1,0:T(8,128)S(1)}, f32[32,256]{1,0:T(8,128)S(1)}, u32[]{:S(2)}, u32[]{:S(2)}) collective-permute-start(f32[32,256]{1,0:T(8,128)S(1)} %add.19), channel_id=1, source_target_pairs={{6,0},{4,2},{2,4},{0,6},{14,8},{12,10},{10,12},{8,14},{7,1},{5,3},... | collective-permute-start | bytes 98312 | tf_op jit(solution)/shard_map/ppermute | solution.py:195
  10.5 3.9 %collective-permute-start.3 = (f32[32,256]{1,0:T(8,128)S(1)}, f32[32,256]{1,0:T(8,128)S(1)}, u32[]{:S(2)}, u32[]{:S(2)}) collective-permute-start(f32[32,256]{1,0:T(8,128)S(1)} %add.19), channel_id=1, source_target_pairs={{4,0},{6,2},{0,4},{2,6},{12,8},{14,10},{8,12},{10,14},{5,1},{7,3},... | collective-permute-start | bytes 98312 | tf_op jit(solution)/shard_map/ppermute | solution.py:195
  10.9 3.9 %collective-permute-start.2 = (f32[32,256]{1,0:T(8,128)S(1)}, f32[32,256]{1,0:T(8,128)S(1)}, u32[]{:S(2)}, u32[]{:S(2)}) collective-permute-start(f32[32,256]{1,0:T(8,128)S(1)} %add.19), channel_id=1, source_target_pairs={{2,0},{0,2},{6,4},{4,6},{10,8},{8,10},{14,12},{12,14},{3,1},{1,3},... | collective-permute-start | bytes 98312 | tf_op jit(solution)/shard_map/ppermute | solution.py:195
  14.8 4.9 %collective-permute-start.5 = (f32[32,256]{1,0:T(8,128)S(1)}, f32[32,256]{1,0:T(8,128)S(1)}, u32[]{:S(2)}, u32[]{:S(2)}) collective-permute-start(f32[32,256]{1,0:T(8,128)S(1)} %add_add_fusion), channel_id=1, source_target_pairs={{8,0},{10,2},{12,4},{14,6},{0,8},{2,10},{4,12},{6,14},{9,1},{11,3}... | collective-permute-start | bytes 98312 | tf_op jit(solution)/shard_map/ppermute | solution.py:195
  19.7 1.2 %collective-permute-start.6 = (bf16[32,256]{1,0:T(8,128)(2,1)S(1)}, bf16[32,256]{1,0:T(8,128)(2,1)S(1)}, u32[]{:S(2)}, u32[]{:S(2)}) collective-permute-start(bf16[32,256]{1,0:T(8,128)(2,1)S(1)} %add_convert_fusion), channel_id=1, source_target_pairs={{1,0},{0,1},{17,16},{16,17},{3,2},{2,3},{19,18},{18,19},{5,4},{4,5... | collective-permute-start | bytes 49160 | tf_op jit(solution)/shard_map/ppermute | solution.py:205
  20.9 6.8 %collective-permute-start.7 = (bf16[2,32,256]{2,1,0:T(8,128)(2,1)S(1)}, bf16[2,32,256]{2,1,0:T(8,128)(2,1)S(1)}, u32[]{:S(2)}, u32[]{:S(2)}) collective-permute-start(bf16[2,32,256]{2,1,0:T(8,128)(2,1)S(1)} %pad_maximum_fusion.refs_2_), channel_id=1, source_target_pairs={{16,0},{17,1},{0,16},{1,17},{18,2},{19,3},{2,18},{3,19},{20,4},{21... | collective-permute-start | bytes 98312 | tf_op jit(solution)/shard_map/ppermute | solution.py:205

commit v14 on v13

--- a/solution.py
+++ b/solution.py
@@ -86,17 +86,6 @@
     )(snapshots, basis)
 
 
-def gathered(held, fields, begin, width, arrived):
-    rows = held[0].shape[0]
-    span = pl.ds(begin, width)
-    return [
-        pltpu.make_async_copy(
-            block.at[:, span], fields.at[pl.ds(k * rows, rows), span], arrived.at[k]
-        )
-        for k, block in enumerate(held)
-    ]
-
-
 def by_hours(known):
     me, core = lax.axis_index("tm"), lax.axis_index("inner")
     count = known.shape[0] // 2
@@ -113,25 +102,21 @@
     return jnp.where(hour == 0, 0.0, pltpu.roll(every, 1, 0)) * energy
 
 
-def rebuild_kernel(parts, tiles, energy, vectors, *refs):
-    count = (len(refs) - 11) // 2
+def rebuild_kernel(tiles, energy, vectors, *refs):
+    count = (len(refs) - 10) // 2
     held, coeffs, refs = refs[:count], refs[count : 2 * count], refs[2 * count :]
-    operator, modes, fields, known, turned, scale, scaled, made, square, arrived, sent = refs
+    operator, modes, known, turned, scale, scaled, made, square, arrived, sent = refs
     hours, cells = held[0].shape
     inputs = started(
         [
-            pltpu.make_async_copy(block, known.at[pl.ds(2 * k, 2)], arrived.at[parts, k])
+            pltpu.make_async_copy(block, known.at[pl.ds(2 * k, 2)], arrived.at[0, k])
             for k, block in enumerate(coeffs)
         ]
         + [
-            pltpu.make_async_copy(energy, scale, arrived.at[parts + 1, 0]),
-            pltpu.make_async_copy(vectors, turned, arrived.at[parts + 2, 0]),
+            pltpu.make_async_copy(energy, scale, arrived.at[1, 0]),
+            pltpu.make_async_copy(vectors, turned, arrived.at[2, 0]),
         ]
     )
-    width = cells // parts
-    blocks = [
-        started(gathered(held, fields, i * width, width, arrived.at[i])) for i in range(parts)
-    ]
     waited(inputs)
     every = by_hours(known)
     scaled[...] = lagged_and_scaled(every.astype(jnp.float32), scale[...])
@@ -147,11 +132,10 @@
     width = cells // tiles
     outgoing = []
     for i in range(tiles):
-        if i % (tiles // parts) == 0:
-            waited(blocks[i // (tiles // parts)])
         for at in range(i * width, (i + 1) * width, STRIP):
             span = pl.ds(at, STRIP)
-            made[:, span] = product(weights, fields[:, span], ROWS).astype(made.dtype)
+            fields = jnp.concatenate([block[:, span] for block in held], axis=0)
+            made[:, span] = product(weights, fields, ROWS).astype(made.dtype)
         span = pl.ds(i * width, width)
         copy = pltpu.make_async_copy(made.at[:, span], modes.at[:, span], sent.at[i])
         outgoing += started([copy])
@@ -161,27 +145,26 @@
     waited(outgoing)
 
 
-def rebuild(energy, vectors, held, coeffs, parts, tiles):
+def rebuild(energy, vectors, held, coeffs, tiles):
     _, half, rank = coeffs[0].shape
     hours, cells = held[0].shape
     hours, modes = len(held) * hours, vectors.shape[0]
     return pl.pallas_call(
-        functools.partial(rebuild_kernel, parts, tiles),
+        functools.partial(rebuild_kernel, tiles),
         out_shape=(
             jax.ShapeDtypeStruct((rank, rank), jnp.float32),
             jax.ShapeDtypeStruct((modes, cells), jnp.bfloat16),
         ),
-        in_specs=[ANYWHERE] * (2 + 2 * len(held)),
+        in_specs=[ANYWHERE] * 2 + [IN_VMEM] * len(held) + [ANYWHERE] * len(held),
         out_specs=(ANYWHERE, ANYWHERE),
         scratch_shapes=[
-            pltpu.VMEM((hours, cells), jnp.bfloat16),
             pltpu.VMEM((2 * len(held), half, rank), coeffs[0].dtype),
             pltpu.VMEM(vectors.shape, vectors.dtype),
             pltpu.VMEM(energy.shape, energy.dtype),
             pltpu.VMEM((hours, rank), jnp.float32),
             pltpu.VMEM((modes, cells), jnp.bfloat16),
             pltpu.VMEM((rank, rank), jnp.float32),
-            pltpu.SemaphoreType.DMA((parts + 3, len(held))),
+            pltpu.SemaphoreType.DMA((3, len(held))),
             pltpu.SemaphoreType.DMA((tiles + 1,)),
         ],
         compiler_params=pltpu.CompilerParams(vmem_limit_bytes=40 * 2**20),
@@ -229,7 +212,7 @@
 
     rows = eigen_vectors.shape[1] // tm
     vectors = lax.dynamic_slice_in_dim(eigen_vectors, me * rows, rows, 1)
-    return rebuild(inverse_energy[None, :], vectors.T, held, coeffs, 2, 4)
+    return rebuild(inverse_energy[None, :], vectors.T, held, coeffs, 4)
 
 
 def solution(mesh):

time: 31.4 us -> 31.1 us (level)
  no operation moved by 1% of the time
where the time goes in v14:
time: 31.1 us; the launch traced here: 30.9 us
  waiting for transfers between devices  14.2 us (46%)
  starting transfers between devices  9.76 us (31%)
  Pallas kernels  6.17 us (20%)
  between operations  0.71 us (2%)
    ppermute x3, waiting for transfers between devices, moved(): return lax.ppermute(value, ('tm', 'inner'), route)  7.33 us
    ppermute x5, waiting for transfers between devices, swapped(): return lax.ppermute(value, axis, route)  6.82 us
    ppermute x5, starting transfers between devices, swapped(): return lax.ppermute(value, axis, route)  6.22 us
    ppermute x3, starting transfers between devices, moved(): return lax.ppermute(value, ('tm', 'inner'), route)  3.54 us
    pallas_call x1, Pallas kernels, rebuild(): pl.pallas_call(functools.partial(rebuild_kernel, tiles), out_shape=(jax.S...  3.2 us
    pallas_call x1, Pallas kernels, project(): pl.pallas_call(functools.partial(project_kernel, tiles), out_shape=(half,...  2.98 us
  transfers between devices with their start and end apart: 8, of which 7 were waited for; matrix products, arithmetic and copies ran while one was open for 0% of the time, Pallas kernels for 10%

profile of v14, /device:TPU:0, one launch (start us, length us, event | category | flops | bytes accessed | tf_op | source)
XLA Modules:
  0.0 30.9 jit_solution(9418423192592794585)
XLA Ops:
  0.6 0.0 copy-start
  0.6 0.0 copy-start.1
  0.7 0.0 copy-start.2
  0.7 3.0 %collective-permute-start = (bf16[64,8192]{1,0:T(8,128)(2,1)}, bf16[64,8192]{1,0:T(8,128)(2,1)S(1)}, u32[]{:S(2)}, u32[]{:S(2)}) collective-permute-start(bf16[64,8192]{1,0:T(8,128)(2,1)} %bitcast.5), channel_id=1, source_target_pairs={{16,0},{17,1},{0,16},{1,17},{18,2},{19,3},{2,18},{3,19},{20,4},{21... | collective-permute-start | bytes 3145736 | tf_op jit(solution)/shard_map/ppermute | solution.py:188
  3.7 3.0 %project.1 = (f32[32,256]{1,0:T(8,128)S(1)}, f32[32,256]{1,0:T(8,128)S(1)}) custom-call(bf16[64,8192]{1,0:T(8,128)(2,1)} %bitcast.6, bf16[8192,256]{1,0:T(8,128)(2,1)} %basis.1), custom_call_target="tpu_custom_call" | custom-call | tf_op jit(solution)/shard_map/project/pallas_call | solution.py:72
  6.7 0.1 collective-permute-start.1
  6.7 1.2 %collective-permute-done.1 = f32[32,256]{1,0:T(8,128)S(1)} collective-permute-done((f32[32,256]{1,0:T(8,128)S(1)}, f32[32,256]{1,0:T(8,128)S(1)}, u32[]{:S(2)}, u32[]{:S(2)}) %collective-permute-start.1) | collective-permute-done | bytes 32800 | tf_op jit(solution)/shard_map/ppermute | solution.py:178
  7.9 2.5 %collective-permute-start.4 = (f32[32,256]{1,0:T(8,128)S(1)}, f32[32,256]{1,0:T(8,128)S(1)}, u32[]{:S(2)}, u32[]{:S(2)}) collective-permute-start(f32[32,256]{1,0:T(8,128)S(1)} %add.19), channel_id=1, source_target_pairs={{6,0},{4,2},{2,4},{0,6},{14,8},{12,10},{10,12},{8,14},{7,1},{5,3},... | collective-permute-start | bytes 98312 | tf_op jit(solution)/shard_map/ppermute | solution.py:178
  10.5 0.4 %collective-permute-start.3 = (f32[32,256]{1,0:T(8,128)S(1)}, f32[32,256]{1,0:T(8,128)S(1)}, u32[]{:S(2)}, u32[]{:S(2)}) collective-permute-start(f32[32,256]{1,0:T(8,128)S(1)} %add.19), channel_id=1, source_target_pairs={{4,0},{6,2},{0,4},{2,6},{12,8},{14,10},{8,12},{10,14},{5,1},{7,3},... | collective-permute-start | bytes 98312 | tf_op jit(solution)/shard_map/ppermute | solution.py:178
  10.9 0.5 %collective-permute-start.2 = (f32[32,256]{1,0:T(8,128)S(1)}, f32[32,256]{1,0:T(8,128)S(1)}, u32[]{:S(2)}, u32[]{:S(2)}) collective-permute-start(f32[32,256]{1,0:T(8,128)S(1)} %add.19), channel_id=1, source_target_pairs={{2,0},{0,2},{6,4},{4,6},{10,8},{8,10},{14,12},{12,14},{3,1},{1,3},... | collective-permute-start | bytes 98312 | tf_op jit(solution)/shard_map/ppermute | solution.py:178
  11.4 1.3 %collective-permute-done.4 = f32[32,256]{1,0:T(8,128)S(1)} collective-permute-done((f32[32,256]{1,0:T(8,128)S(1)}, f32[32,256]{1,0:T(8,128)S(1)}, u32[]{:S(2)}, u32[]{:S(2)}) %collective-permute-start.4) | collective-permute-done | bytes 32800 | tf_op jit(solution)/shard_map/ppermute | solution.py:178
  12.7 1.6 %collective-permute-done.3 = f32[32,256]{1,0:T(8,128)S(1)} collective-permute-done((f32[32,256]{1,0:T(8,128)S(1)}, f32[32,256]{1,0:T(8,128)S(1)}, u32[]{:S(2)}, u32[]{:S(2)}) %collective-permute-start.3) | collective-permute-done | bytes 32800 | tf_op jit(solution)/shard_map/ppermute | solution.py:178
  14.4 0.4 %collective-permute-done.2 = f32[32,256]{1,0:T(8,128)S(1)} collective-permute-done((f32[32,256]{1,0:T(8,128)S(1)}, f32[32,256]{1,0:T(8,128)S(1)}, u32[]{:S(2)}, u32[]{:S(2)}) %collective-permute-start.2) | collective-permute-done | bytes 32800 | tf_op jit(solution)/shard_map/ppermute | solution.py:178
  14.8 2.7 %collective-permute-start.5 = (f32[32,256]{1,0:T(8,128)S(1)}, f32[32,256]{1,0:T(8,128)S(1)}, u32[]{:S(2)}, u32[]{:S(2)}) collective-permute-start(f32[32,256]{1,0:T(8,128)S(1)} %add_add_fusion), channel_id=1, source_target_pairs={{8,0},{10,2},{12,4},{14,6},{0,8},{2,10},{4,12},{6,14},{9,1},{11,3}... | collective-permute-start | bytes 98312 | tf_op jit(solution)/shard_map/ppermute | solution.py:178
  17.5 2.2 %collective-permute-done.5 = f32[32,256]{1,0:T(8,128)S(1)} collective-permute-done((f32[32,256]{1,0:T(8,128)S(1)}, f32[32,256]{1,0:T(8,128)S(1)}, u32[]{:S(2)}, u32[]{:S(2)}) %collective-permute-start.5) | collective-permute-done | bytes 32800 | tf_op jit(solution)/shard_map/ppermute | solution.py:178
  19.7 0.0 collective-permute-start.6
  19.7 1.2 %collective-permute-done.6 = bf16[32,256]{1,0:T(8,128)(2,1)S(1)} collective-permute-done((bf16[32,256]{1,0:T(8,128)(2,1)S(1)}, bf16[32,256]{1,0:T(8,128)(2,1)S(1)}, u32[]{:S(2)}, u32[]{:S(2)}) %collective-permute-start.6) | collective-permute-done | bytes 16416 | tf_op jit(solution)/shard_map/ppermute | solution.py:188
  20.9 0.5 %collective-permute-start.7 = (bf16[2,32,256]{2,1,0:T(8,128)(2,1)S(1)}, bf16[2,32,256]{2,1,0:T(8,128)(2,1)S(1)}, u32[]{:S(2)}, u32[]{:S(2)}) collective-permute-start(bf16[2,32,256]{2,1,0:T(8,128)(2,1)S(1)} %pad_maximum_fusion.refs_2_), channel_id=1, source_target_pairs={{16,0},{17,1},{0,16},{1,17},{18,2},{19,3},{2,18},{3,19},{20,4},{21... | collective-permute-start | bytes 98312 | tf_op jit(solution)/shard_map/ppermute | solution.py:188
  21.5 0.0 copy-done
  21.5 0.1 copy.7
  21.6 6.2 %collective-permute-done.7.refs_3_ = bf16[2,32,256]{2,1,0:T(8,128)(2,1)S(1)} collective-permute-done((bf16[2,32,256]{2,1,0:T(8,128)(2,1)S(1)}, bf16[2,32,256]{2,1,0:T(8,128)(2,1)S(1)}, u32[]{:S(2)}, u32[]{:S(2)}) %collective-permute-start.7) | collective-permute-done | bytes 32800 | tf_op jit(solution)/shard_map/ppermute | solution.py:188
  27.7 0.0 collective-permute-done.refs_1_
  27.7 0.0 copy-done.1
  27.7 0.0 copy-done.2
  27.8 3.2 %rebuild.1 = (f32[256,256]{1,0:T(8,128)}, bf16[256,8192]{1,0:T(8,128)(2,1)}) custom-call(f32[1,256]{1,0:T(1,128)S(1)} %bitcast.9, bf16[256,256]{1,0:T(8,128)(2,1)S(1)} %bitcast.8, bf16[64,8192]{1,0:T(8,128)(2,1)S(1)} %bitcast.7, bf16[64,8192]{1,0:T(8,128)(2,1)S(1)} %collective-permute-done.refs_1_, bf16[2,32,256]{2,1,0:T(8,128)(2,1)S(1)} %pad_maximum_fusion.refs_2_, ...), custom_call_target="tpu_custom_call" | custom-call | tf_op jit(solution)/shard_map/rebuild/pallas_call | solution.py:152
  (5 shorter events, 0.0 us)
Async XLA Ops:
  0.6 20.8 %copy-start = (bf16[256,512]{1,0:T(8,128)(2,1)S(1)}, bf16[256,512]{1,0:T(8,128)(2,1)}, u32[]{:S(2)}) copy-start(bf16[256,512]{1,0:T(8,128)(2,1)} %param.7) | copy-start | bytes 786436
  0.6 27.1 %copy-start.1 = (bf16[8192,64]{0,1:T(8,128)(2,1)S(1)}, bf16[8192,64]{0,1:T(8,128)(2,1)}, u32[]{:S(2)}) copy-start(bf16[8192,64]{0,1:T(8,128)(2,1)} %param.5) | copy-start | bytes 3145732
  0.7 27.1 %copy-start.2 = (f32[256]{0:T(256)S(1)}, f32[256]{0:T(256)}, u32[]{:S(2)}) copy-start(f32[256]{0:T(256)} %param.6) | copy-start | bytes 3076
  0.7 27.1 %collective-permute-start = (bf16[64,8192]{1,0:T(8,128)(2,1)}, bf16[64,8192]{1,0:T(8,128)(2,1)S(1)}, u32[]{:S(2)}, u32[]{:S(2)}) collective-permute-start(bf16[64,8192]{1,0:T(8,128)(2,1)} %bitcast.5), channel_id=1, source_target_pairs={{16,0},{17,1},{0,16},{1,17},{18,2},{19,3},{2,18},{3,19},{20,4},{21... | collective-permute-start | bytes 3145736 | tf_op jit(solution)/shard_map/ppermute | solution.py:188
  6.7 1.3 %collective-permute-start.1 = (f32[32,256]{1,0:T(8,128)S(1)}, f32[32,256]{1,0:T(8,128)S(1)}, u32[]{:S(2)}, u32[]{:S(2)}) collective-permute-start(f32[32,256]{1,0:T(8,128)S(1)} %get-tuple-element.5), channel_id=1, source_target_pairs={{1,0},{0,1},{3,2},{2,3},{5,4},{4,5},{7,6},{6,7},{9,8},{8,9},{11,10... | collective-permute-start | bytes 98312 | tf_op jit(solution)/shard_map/ppermute | solution.py:178
  7.9 4.8 %collective-permute-start.4 = (f32[32,256]{1,0:T(8,128)S(1)}, f32[32,256]{1,0:T(8,128)S(1)}, u32[]{:S(2)}, u32[]{:S(2)}) collective-permute-start(f32[32,256]{1,0:T(8,128)S(1)} %add.19), channel_id=1, source_target_pairs={{6,0},{4,2},{2,4},{0,6},{14,8},{12,10},{10,12},{8,14},{7,1},{5,3},... | collective-permute-start | bytes 98312 | tf_op jit(solution)/shard_map/ppermute | solution.py:178
  10.5 3.9 %collective-permute-start.3 = (f32[32,256]{1,0:T(8,128)S(1)}, f32[32,256]{1,0:T(8,128)S(1)}, u32[]{:S(2)}, u32[]{:S(2)}) collective-permute-start(f32[32,256]{1,0:T(8,128)S(1)} %add.19), channel_id=1, source_target_pairs={{4,0},{6,2},{0,4},{2,6},{12,8},{14,10},{8,12},{10,14},{5,1},{7,3},... | collective-permute-start | bytes 98312 | tf_op jit(solution)/shard_map/ppermute | solution.py:178
  10.9 3.9 %collective-permute-start.2 = (f32[32,256]{1,0:T(8,128)S(1)}, f32[32,256]{1,0:T(8,128)S(1)}, u32[]{:S(2)}, u32[]{:S(2)}) collective-permute-start(f32[32,256]{1,0:T(8,128)S(1)} %add.19), channel_id=1, source_target_pairs={{2,0},{0,2},{6,4},{4,6},{10,8},{8,10},{14,12},{12,14},{3,1},{1,3},... | collective-permute-start | bytes 98312 | tf_op jit(solution)/shard_map/ppermute | solution.py:178
  14.8 4.9 %collective-permute-start.5 = (f32[32,256]{1,0:T(8,128)S(1)}, f32[32,256]{1,0:T(8,128)S(1)}, u32[]{:S(2)}, u32[]{:S(2)}) collective-permute-start(f32[32,256]{1,0:T(8,128)S(1)} %add_add_fusion), channel_id=1, source_target_pairs={{8,0},{10,2},{12,4},{14,6},{0,8},{2,10},{4,12},{6,14},{9,1},{11,3}... | collective-permute-start | bytes 98312 | tf_op jit(solution)/shard_map/ppermute | solution.py:178
  19.7 1.2 %collective-permute-start.6 = (bf16[32,256]{1,0:T(8,128)(2,1)S(1)}, bf16[32,256]{1,0:T(8,128)(2,1)S(1)}, u32[]{:S(2)}, u32[]{:S(2)}) collective-permute-start(bf16[32,256]{1,0:T(8,128)(2,1)S(1)} %add_convert_fusion), channel_id=1, source_target_pairs={{1,0},{0,1},{17,16},{16,17},{3,2},{2,3},{19,18},{18,19},{5,4},{4,5... | collective-permute-start | bytes 49160 | tf_op jit(solution)/shard_map/ppermute | solution.py:188
  20.9 6.8 %collective-permute-start.7 = (bf16[2,32,256]{2,1,0:T(8,128)(2,1)S(1)}, bf16[2,32,256]{2,1,0:T(8,128)(2,1)S(1)}, u32[]{:S(2)}, u32[]{:S(2)}) collective-permute-start(bf16[2,32,256]{2,1,0:T(8,128)(2,1)S(1)} %pad_maximum_fusion.refs_2_), channel_id=1, source_target_pairs={{16,0},{17,1},{0,16},{1,17},{18,2},{19,3},{2,18},{3,19},{20,4},{21... | collective-permute-start | bytes 98312 | tf_op jit(solution)/shard_map/ppermute | solution.py:188

commit v15 on v14

--- a/solution.py
+++ b/solution.py
@@ -86,47 +86,30 @@
     )(snapshots, basis)
 
 
-def by_hours(known):
-    me, core = lax.axis_index("tm"), lax.axis_index("inner")
-    count = known.shape[0] // 2
-    order = [
-        2 * lax.rem(count + block - me, count) + lax.rem(2 + half - core, 2)
-        for block in range(count)
-        for half in range(2)
-    ]
-    return jnp.concatenate([known[at] for at in order], axis=0)
-
-
 def lagged_and_scaled(every, energy):
     hour = lax.broadcasted_iota(jnp.int32, every.shape, 0)
     return jnp.where(hour == 0, 0.0, pltpu.roll(every, 1, 0)) * energy
 
 
 def rebuild_kernel(tiles, energy, vectors, *refs):
-    count = (len(refs) - 10) // 2
+    count = (len(refs) - 7) // 2
     held, coeffs, refs = refs[:count], refs[count : 2 * count], refs[2 * count :]
-    operator, modes, known, turned, scale, scaled, made, square, arrived, sent = refs
+    operator, modes, known, scaled, made, square, sent = refs
     hours, cells = held[0].shape
-    inputs = started(
-        [
-            pltpu.make_async_copy(block, known.at[pl.ds(2 * k, 2)], arrived.at[0, k])
-            for k, block in enumerate(coeffs)
-        ]
-        + [
-            pltpu.make_async_copy(energy, scale, arrived.at[1, 0]),
-            pltpu.make_async_copy(vectors, turned, arrived.at[2, 0]),
-        ]
-    )
-    waited(inputs)
-    every = by_hours(known)
-    scaled[...] = lagged_and_scaled(every.astype(jnp.float32), scale[...])
-    me = lax.axis_index("tm")
+    half = hours // 2
+    me, core = lax.axis_index("tm"), lax.axis_index("inner")
     first = [lax.rem(me + k, count) * hours for k in range(count)]
+    for k, block in enumerate(coeffs):
+        for n in range(2):
+            at = pl.multiple_of(first[k] + lax.rem(core + n, 2) * half, half)
+            known[pl.ds(at, half)] = block[n].astype(jnp.float32)
+    every = known[...].astype(jnp.bfloat16)
+    scaled[...] = lagged_and_scaled(known[...], energy[...])
     ordered = jnp.concatenate(
         [scaled[pl.ds(pl.multiple_of(at, hours), hours)] for at in first], axis=0
     )
     high, low = in_parts(ordered)
-    weights = (product(turned[...], high, LAST) + product(turned[...], low, LAST)).astype(
+    weights = (product(vectors[...], high, LAST) + product(vectors[...], low, LAST)).astype(
         jnp.bfloat16
     )
     width = cells // tiles
@@ -146,7 +129,7 @@
 
 
 def rebuild(energy, vectors, held, coeffs, tiles):
-    _, half, rank = coeffs[0].shape
+    rank = coeffs[0].shape[2]
     hours, cells = held[0].shape
     hours, modes = len(held) * hours, vectors.shape[0]
     return pl.pallas_call(
@@ -155,16 +138,13 @@
             jax.ShapeDtypeStruct((rank, rank), jnp.float32),
             jax.ShapeDtypeStruct((modes, cells), jnp.bfloat16),
         ),
-        in_specs=[ANYWHERE] * 2 + [IN_VMEM] * len(held) + [ANYWHERE] * len(held),
+        in_specs=[IN_VMEM] * (2 + 2 * len(held)),
         out_specs=(ANYWHERE, ANYWHERE),
         scratch_shapes=[
-            pltpu.VMEM((2 * len(held), half, rank), coeffs[0].dtype),
-            pltpu.VMEM(vectors.shape, vectors.dtype),
-            pltpu.VMEM(energy.shape, energy.dtype),
+            pltpu.VMEM((hours, rank), jnp.float32),
             pltpu.VMEM((hours, rank), jnp.float32),
             pltpu.VMEM((modes, cells), jnp.bfloat16),
             pltpu.VMEM((rank, rank), jnp.float32),
-            pltpu.SemaphoreType.DMA((3, len(held))),
             pltpu.SemaphoreType.DMA((tiles + 1,)),
         ],
         compiler_params=pltpu.CompilerParams(vmem_limit_bytes=40 * 2**20),

time: 31.1 us -> 30.8 us (level)
  no operation moved by 1% of the time
where the time goes in v15:
time: 30.8 us; the launch traced here: 30.7 us
  waiting for transfers between devices  14.2 us (46%)
  starting transfers between devices  9.76 us (32%)
  Pallas kernels  5.88 us (19%)
  between operations  0.71 us (2%)
    ppermute x3, waiting for transfers between devices, moved(): return lax.ppermute(value, ('tm', 'inner'), route)  7.33 us
    ppermute x5, waiting for transfers between devices, swapped(): return lax.ppermute(value, axis, route)  6.82 us
    ppermute x5, starting transfers between devices, swapped(): return lax.ppermute(value, axis, route)  6.22 us
    ppermute x3, starting transfers between devices, moved(): return lax.ppermute(value, ('tm', 'inner'), route)  3.54 us
    pallas_call x1, Pallas kernels, project(): pl.pallas_call(functools.partial(project_kernel, tiles), out_shape=(half,...  2.98 us
    pallas_call x1, Pallas kernels, rebuild(): pl.pallas_call(functools.partial(rebuild_kernel, tiles), out_shape=(jax.S...  2.9 us
  transfers between devices with their start and end apart: 8, of which 7 were waited for; matrix products, arithmetic and copies ran while one was open for 0% of the time, Pallas kernels for 10%

profile of v15, /device:TPU:0, one launch (start us, length us, event | category | flops | bytes accessed | tf_op | source)
XLA Modules:
  0.0 30.7 jit_solution(3575193137702225395)
XLA Ops:
  0.6 0.0 copy-start
  0.6 0.0 copy-start.1
  0.7 0.0 copy-start.2
  0.7 3.0 %collective-permute-start = (bf16[64,8192]{1,0:T(8,128)(2,1)}, bf16[64,8192]{1,0:T(8,128)(2,1)S(1)}, u32[]{:S(2)}, u32[]{:S(2)}) collective-permute-start(bf16[64,8192]{1,0:T(8,128)(2,1)} %bitcast.5), channel_id=1, source_target_pairs={{16,0},{17,1},{0,16},{1,17},{18,2},{19,3},{2,18},{3,19},{20,4},{21... | collective-permute-start | bytes 3145736 | tf_op jit(solution)/shard_map/ppermute | solution.py:168
  3.7 3.0 %project.1 = (f32[32,256]{1,0:T(8,128)S(1)}, f32[32,256]{1,0:T(8,128)S(1)}) custom-call(bf16[64,8192]{1,0:T(8,128)(2,1)} %bitcast.6, bf16[8192,256]{1,0:T(8,128)(2,1)} %basis.1), custom_call_target="tpu_custom_call" | custom-call | tf_op jit(solution)/shard_map/project/pallas_call | solution.py:72
  6.7 0.1 collective-permute-start.1
  6.7 1.2 %collective-permute-done.1 = f32[32,256]{1,0:T(8,128)S(1)} collective-permute-done((f32[32,256]{1,0:T(8,128)S(1)}, f32[32,256]{1,0:T(8,128)S(1)}, u32[]{:S(2)}, u32[]{:S(2)}) %collective-permute-start.1) | collective-permute-done | bytes 32800 | tf_op jit(solution)/shard_map/ppermute | solution.py:158
  7.9 2.5 %collective-permute-start.4 = (f32[32,256]{1,0:T(8,128)S(1)}, f32[32,256]{1,0:T(8,128)S(1)}, u32[]{:S(2)}, u32[]{:S(2)}) collective-permute-start(f32[32,256]{1,0:T(8,128)S(1)} %add.19), channel_id=1, source_target_pairs={{6,0},{4,2},{2,4},{0,6},{14,8},{12,10},{10,12},{8,14},{7,1},{5,3},... | collective-permute-start | bytes 98312 | tf_op jit(solution)/shard_map/ppermute | solution.py:158
  10.5 0.4 %collective-permute-start.3 = (f32[32,256]{1,0:T(8,128)S(1)}, f32[32,256]{1,0:T(8,128)S(1)}, u32[]{:S(2)}, u32[]{:S(2)}) collective-permute-start(f32[32,256]{1,0:T(8,128)S(1)} %add.19), channel_id=1, source_target_pairs={{4,0},{6,2},{0,4},{2,6},{12,8},{14,10},{8,12},{10,14},{5,1},{7,3},... | collective-permute-start | bytes 98312 | tf_op jit(solution)/shard_map/ppermute | solution.py:158
  10.9 0.5 %collective-permute-start.2 = (f32[32,256]{1,0:T(8,128)S(1)}, f32[32,256]{1,0:T(8,128)S(1)}, u32[]{:S(2)}, u32[]{:S(2)}) collective-permute-start(f32[32,256]{1,0:T(8,128)S(1)} %add.19), channel_id=1, source_target_pairs={{2,0},{0,2},{6,4},{4,6},{10,8},{8,10},{14,12},{12,14},{3,1},{1,3},... | collective-permute-start | bytes 98312 | tf_op jit(solution)/shard_map/ppermute | solution.py:158
  11.4 1.3 %collective-permute-done.4 = f32[32,256]{1,0:T(8,128)S(1)} collective-permute-done((f32[32,256]{1,0:T(8,128)S(1)}, f32[32,256]{1,0:T(8,128)S(1)}, u32[]{:S(2)}, u32[]{:S(2)}) %collective-permute-start.4) | collective-permute-done | bytes 32800 | tf_op jit(solution)/shard_map/ppermute | solution.py:158
  12.7 1.6 %collective-permute-done.3 = f32[32,256]{1,0:T(8,128)S(1)} collective-permute-done((f32[32,256]{1,0:T(8,128)S(1)}, f32[32,256]{1,0:T(8,128)S(1)}, u32[]{:S(2)}, u32[]{:S(2)}) %collective-permute-start.3) | collective-permute-done | bytes 32800 | tf_op jit(solution)/shard_map/ppermute | solution.py:158
  14.4 0.4 %collective-permute-done.2 = f32[32,256]{1,0:T(8,128)S(1)} collective-permute-done((f32[32,256]{1,0:T(8,128)S(1)}, f32[32,256]{1,0:T(8,128)S(1)}, u32[]{:S(2)}, u32[]{:S(2)}) %collective-permute-start.2) | collective-permute-done | bytes 32800 | tf_op jit(solution)/shard_map/ppermute | solution.py:158
  14.8 2.7 %collective-permute-start.5 = (f32[32,256]{1,0:T(8,128)S(1)}, f32[32,256]{1,0:T(8,128)S(1)}, u32[]{:S(2)}, u32[]{:S(2)}) collective-permute-start(f32[32,256]{1,0:T(8,128)S(1)} %add_add_fusion), channel_id=1, source_target_pairs={{8,0},{10,2},{12,4},{14,6},{0,8},{2,10},{4,12},{6,14},{9,1},{11,3}... | collective-permute-start | bytes 98312 | tf_op jit(solution)/shard_map/ppermute | solution.py:158
  17.5 2.2 %collective-permute-done.5 = f32[32,256]{1,0:T(8,128)S(1)} collective-permute-done((f32[32,256]{1,0:T(8,128)S(1)}, f32[32,256]{1,0:T(8,128)S(1)}, u32[]{:S(2)}, u32[]{:S(2)}) %collective-permute-start.5) | collective-permute-done | bytes 32800 | tf_op jit(solution)/shard_map/ppermute | solution.py:158
  19.7 0.0 collective-permute-start.6
  19.7 1.2 %collective-permute-done.6 = bf16[32,256]{1,0:T(8,128)(2,1)S(1)} collective-permute-done((bf16[32,256]{1,0:T(8,128)(2,1)S(1)}, bf16[32,256]{1,0:T(8,128)(2,1)S(1)}, u32[]{:S(2)}, u32[]{:S(2)}) %collective-permute-start.6) | collective-permute-done | bytes 16416 | tf_op jit(solution)/shard_map/ppermute | solution.py:168
  20.9 0.5 %collective-permute-start.7 = (bf16[2,32,256]{2,1,0:T(8,128)(2,1)S(1)}, bf16[2,32,256]{2,1,0:T(8,128)(2,1)S(1)}, u32[]{:S(2)}, u32[]{:S(2)}) collective-permute-start(bf16[2,32,256]{2,1,0:T(8,128)(2,1)S(1)} %pad_maximum_fusion.refs_2_), channel_id=1, source_target_pairs={{16,0},{17,1},{0,16},{1,17},{18,2},{19,3},{2,18},{3,19},{20,4},{21... | collective-permute-start | bytes 98312 | tf_op jit(solution)/shard_map/ppermute | solution.py:168
  21.5 0.0 copy-done
  21.5 0.1 copy.7
  21.6 6.2 %collective-permute-done.7.refs_3_ = bf16[2,32,256]{2,1,0:T(8,128)(2,1)S(1)} collective-permute-done((bf16[2,32,256]{2,1,0:T(8,128)(2,1)S(1)}, bf16[2,32,256]{2,1,0:T(8,128)(2,1)S(1)}, u32[]{:S(2)}, u32[]{:S(2)}) %collective-permute-start.7) | collective-permute-done | bytes 32800 | tf_op jit(solution)/shard_map/ppermute | solution.py:168
  27.7 0.0 collective-permute-done.refs_1_
  27.7 0.0 copy-done.1
  27.7 0.0 copy-done.2
  27.8 2.9 %rebuild.1 = (f32[256,256]{1,0:T(8,128)}, bf16[256,8192]{1,0:T(8,128)(2,1)}) custom-call(f32[1,256]{1,0:T(1,128)S(1)} %bitcast.9, bf16[256,256]{1,0:T(8,128)(2,1)S(1)} %bitcast.8, bf16[64,8192]{1,0:T(8,128)(2,1)S(1)} %bitcast.7, bf16[64,8192]{1,0:T(8,128)(2,1)S(1)} %collective-permute-done.refs_1_, bf16[2,32,256]{2,1,0:T(8,128)(2,1)S(1)} %pad_maximum_fusion.refs_2_, ...), custom_call_target="tpu_custom_call" | custom-call | tf_op jit(solution)/shard_map/rebuild/pallas_call | solution.py:135
  (5 shorter events, 0.0 us)
Async XLA Ops:
  0.6 20.8 %copy-start = (bf16[256,512]{1,0:T(8,128)(2,1)S(1)}, bf16[256,512]{1,0:T(8,128)(2,1)}, u32[]{:S(2)}) copy-start(bf16[256,512]{1,0:T(8,128)(2,1)} %param.7) | copy-start | bytes 786436
  0.6 27.1 %copy-start.1 = (bf16[8192,64]{0,1:T(8,128)(2,1)S(1)}, bf16[8192,64]{0,1:T(8,128)(2,1)}, u32[]{:S(2)}) copy-start(bf16[8192,64]{0,1:T(8,128)(2,1)} %param.5) | copy-start | bytes 3145732
  0.7 27.1 %copy-start.2 = (f32[256]{0:T(256)S(1)}, f32[256]{0:T(256)}, u32[]{:S(2)}) copy-start(f32[256]{0:T(256)} %param.6) | copy-start | bytes 3076
  0.7 27.1 %collective-permute-start = (bf16[64,8192]{1,0:T(8,128)(2,1)}, bf16[64,8192]{1,0:T(8,128)(2,1)S(1)}, u32[]{:S(2)}, u32[]{:S(2)}) collective-permute-start(bf16[64,8192]{1,0:T(8,128)(2,1)} %bitcast.5), channel_id=1, source_target_pairs={{16,0},{17,1},{0,16},{1,17},{18,2},{19,3},{2,18},{3,19},{20,4},{21... | collective-permute-start | bytes 3145736 | tf_op jit(solution)/shard_map/ppermute | solution.py:168
  6.7 1.3 %collective-permute-start.1 = (f32[32,256]{1,0:T(8,128)S(1)}, f32[32,256]{1,0:T(8,128)S(1)}, u32[]{:S(2)}, u32[]{:S(2)}) collective-permute-start(f32[32,256]{1,0:T(8,128)S(1)} %get-tuple-element.5), channel_id=1, source_target_pairs={{1,0},{0,1},{3,2},{2,3},{5,4},{4,5},{7,6},{6,7},{9,8},{8,9},{11,10... | collective-permute-start | bytes 98312 | tf_op jit(solution)/shard_map/ppermute | solution.py:158
  7.9 4.8 %collective-permute-start.4 = (f32[32,256]{1,0:T(8,128)S(1)}, f32[32,256]{1,0:T(8,128)S(1)}, u32[]{:S(2)}, u32[]{:S(2)}) collective-permute-start(f32[32,256]{1,0:T(8,128)S(1)} %add.19), channel_id=1, source_target_pairs={{6,0},{4,2},{2,4},{0,6},{14,8},{12,10},{10,12},{8,14},{7,1},{5,3},... | collective-permute-start | bytes 98312 | tf_op jit(solution)/shard_map/ppermute | solution.py:158
  10.5 3.9 %collective-permute-start.3 = (f32[32,256]{1,0:T(8,128)S(1)}, f32[32,256]{1,0:T(8,128)S(1)}, u32[]{:S(2)}, u32[]{:S(2)}) collective-permute-start(f32[32,256]{1,0:T(8,128)S(1)} %add.19), channel_id=1, source_target_pairs={{4,0},{6,2},{0,4},{2,6},{12,8},{14,10},{8,12},{10,14},{5,1},{7,3},... | collective-permute-start | bytes 98312 | tf_op jit(solution)/shard_map/ppermute | solution.py:158
  10.9 3.9 %collective-permute-start.2 = (f32[32,256]{1,0:T(8,128)S(1)}, f32[32,256]{1,0:T(8,128)S(1)}, u32[]{:S(2)}, u32[]{:S(2)}) collective-permute-start(f32[32,256]{1,0:T(8,128)S(1)} %add.19), channel_id=1, source_target_pairs={{2,0},{0,2},{6,4},{4,6},{10,8},{8,10},{14,12},{12,14},{3,1},{1,3},... | collective-permute-start | bytes 98312 | tf_op jit(solution)/shard_map/ppermute | solution.py:158
  14.8 4.9 %collective-permute-start.5 = (f32[32,256]{1,0:T(8,128)S(1)}, f32[32,256]{1,0:T(8,128)S(1)}, u32[]{:S(2)}, u32[]{:S(2)}) collective-permute-start(f32[32,256]{1,0:T(8,128)S(1)} %add_add_fusion), channel_id=1, source_target_pairs={{8,0},{10,2},{12,4},{14,6},{0,8},{2,10},{4,12},{6,14},{9,1},{11,3}... | collective-permute-start | bytes 98312 | tf_op jit(solution)/shard_map/ppermute | solution.py:158
  19.7 1.2 %collective-permute-start.6 = (bf16[32,256]{1,0:T(8,128)(2,1)S(1)}, bf16[32,256]{1,0:T(8,128)(2,1)S(1)}, u32[]{:S(2)}, u32[]{:S(2)}) collective-permute-start(bf16[32,256]{1,0:T(8,128)(2,1)S(1)} %add_convert_fusion), channel_id=1, source_target_pairs={{1,0},{0,1},{17,16},{16,17},{3,2},{2,3},{19,18},{18,19},{5,4},{4,5... | collective-permute-start | bytes 49160 | tf_op jit(solution)/shard_map/ppermute | solution.py:168
  20.9 6.8 %collective-permute-start.7 = (bf16[2,32,256]{2,1,0:T(8,128)(2,1)S(1)}, bf16[2,32,256]{2,1,0:T(8,128)(2,1)S(1)}, u32[]{:S(2)}, u32[]{:S(2)}) collective-permute-start(bf16[2,32,256]{2,1,0:T(8,128)(2,1)S(1)} %pad_maximum_fusion.refs_2_), channel_id=1, source_target_pairs={{16,0},{17,1},{0,16},{1,17},{18,2},{19,3},{2,18},{3,19},{20,4},{21... | collective-permute-start | bytes 98312 | tf_op jit(solution)/shard_map/ppermute | solution.py:168

commit v16 on v15

--- a/solution.py
+++ b/solution.py
@@ -12,6 +12,7 @@
 LAST = (((1,), (1,)), ((), ()))
 STRIP = 256
 FREE = pl.CostEstimate(flops=0, bytes_accessed=0, transcendentals=0)
+LONG = pl.CostEstimate(flops=3 * 10**9, bytes_accessed=0, transcendentals=0)
 ANYWHERE = pl.BlockSpec(memory_space=pl.ANY)
 IN_VMEM = pl.BlockSpec(memory_space=pltpu.VMEM)
 
@@ -34,6 +35,37 @@
 
 def product(left, right, dims):
     return lax.dot_general(left, right, dims, preferred_element_type=jnp.float32)
+
+
+def cut_kernel(rows, parts, fields, early, sent):
+    width = early.shape[1] // parts
+    waited(
+        started(
+            [
+                pltpu.make_async_copy(
+                    fields.at[pl.ds(at, rows), pl.ds(i * width, width)],
+                    early.at[pl.ds(at, rows), pl.ds(i * width, width)],
+                    sent.at[at // rows, i],
+                )
+                for at in range(0, fields.shape[0], rows)
+                for i in range(parts)
+            ]
+        )
+    )
+
+
+def cut(fields, width, rows, parts):
+    hours = fields.shape[0]
+    return pl.pallas_call(
+        functools.partial(cut_kernel, rows, parts),
+        out_shape=jax.ShapeDtypeStruct((hours, width), fields.dtype),
+        in_specs=[ANYWHERE],
+        out_specs=ANYWHERE,
+        scratch_shapes=[pltpu.SemaphoreType.DMA((hours // rows, parts))],
+        compiler_params=pltpu.CompilerParams(vmem_limit_bytes=52 * 2**20),
+        cost_estimate=FREE,
+        name="cut",
+    )(fields)
 
 
 def project_kernel(tiles, snapshots, basis, kept, given, fields, patterns, halves, arrived):
@@ -91,11 +123,28 @@
     return jnp.where(hour == 0, 0.0, pltpu.roll(every, 1, 0)) * energy
 
 
-def rebuild_kernel(tiles, energy, vectors, *refs):
-    count = (len(refs) - 7) // 2
+def columns(held, begin, width):
+    return jnp.concatenate([b[:, pl.ds(begin - at, width)] for b, at in held], axis=0)
+
+
+def rebuilt(weights, held, made, modes, begin, tiles, sent):
+    width = made.shape[1] // tiles
+    outgoing = []
+    for i in range(tiles):
+        for at in range(i * width, (i + 1) * width, STRIP):
+            fields = columns(held, begin + at, STRIP)
+            made[:, pl.ds(at, STRIP)] = product(weights, fields, ROWS).astype(made.dtype)
+        target = modes.at[:, pl.ds(begin + i * width, width)]
+        copy = pltpu.make_async_copy(made.at[:, pl.ds(i * width, width)], target, sent.at[i])
+        outgoing += started([copy])
+    return outgoing
+
+
+def first_kernel(tiles, energy, vectors, *refs):
+    count = (len(refs) - 8) // 2
     held, coeffs, refs = refs[:count], refs[count : 2 * count], refs[2 * count :]
-    operator, modes, known, scaled, made, square, sent = refs
-    hours, cells = held[0].shape
+    operator, modes, weights, known, scaled, made, square, sent = refs
+    hours = held[0].shape[0]
     half = hours // 2
     me, core = lax.axis_index("tm"), lax.axis_index("inner")
     first = [lax.rem(me + k, count) * hours for k in range(count)]
@@ -109,48 +158,64 @@
         [scaled[pl.ds(pl.multiple_of(at, hours), hours)] for at in first], axis=0
     )
     high, low = in_parts(ordered)
-    weights = (product(vectors[...], high, LAST) + product(vectors[...], low, LAST)).astype(
+    value = (product(vectors[...], high, LAST) + product(vectors[...], low, LAST)).astype(
         jnp.bfloat16
     )
-    width = cells // tiles
-    outgoing = []
-    for i in range(tiles):
-        for at in range(i * width, (i + 1) * width, STRIP):
-            span = pl.ds(at, STRIP)
-            fields = jnp.concatenate([block[:, span] for block in held], axis=0)
-            made[:, span] = product(weights, fields, ROWS).astype(made.dtype)
-        span = pl.ds(i * width, width)
-        copy = pltpu.make_async_copy(made.at[:, span], modes.at[:, span], sent.at[i])
-        outgoing += started([copy])
+    weights[...] = value
+    outgoing = rebuilt(value, [(b, 0) for b in held], made, modes, 0, tiles, sent)
     high, low = in_parts(scaled[...])
     square[...] = product(every, high, FIRST) + product(every, low, FIRST)
     outgoing += started([pltpu.make_async_copy(square, operator, sent.at[tiles])])
     waited(outgoing)
 
 
-def rebuild(energy, vectors, held, coeffs, tiles):
+def last_kernel(begin, tiles, weights, *refs):
+    held, (_, modes, made, sent) = refs[:-4], refs[-4:]
+    blocks = [(held[0], 0)] + [(b, begin) for b in held[1:]]
+    waited(rebuilt(weights[...], blocks, made, modes, begin, tiles, sent))
+
+
+def rebuild_first(energy, vectors, held, coeffs, width, tiles):
     rank = coeffs[0].shape[2]
     hours, cells = held[0].shape
     hours, modes = len(held) * hours, vectors.shape[0]
     return pl.pallas_call(
-        functools.partial(rebuild_kernel, tiles),
+        functools.partial(first_kernel, tiles),
         out_shape=(
             jax.ShapeDtypeStruct((rank, rank), jnp.float32),
             jax.ShapeDtypeStruct((modes, cells), jnp.bfloat16),
+            jax.ShapeDtypeStruct((modes, hours), jnp.bfloat16),
         ),
         in_specs=[IN_VMEM] * (2 + 2 * len(held)),
-        out_specs=(ANYWHERE, ANYWHERE),
+        out_specs=(ANYWHERE, ANYWHERE, IN_VMEM),
         scratch_shapes=[
             pltpu.VMEM((hours, rank), jnp.float32),
             pltpu.VMEM((hours, rank), jnp.float32),
-            pltpu.VMEM((modes, cells), jnp.bfloat16),
+            pltpu.VMEM((modes, width), jnp.bfloat16),
             pltpu.VMEM((rank, rank), jnp.float32),
             pltpu.SemaphoreType.DMA((tiles + 1,)),
         ],
         compiler_params=pltpu.CompilerParams(vmem_limit_bytes=40 * 2**20),
+        cost_estimate=LONG,
+        name="rebuild_first",
+    )(energy, vectors, *held, *coeffs)
+
+
+def rebuild_last(weights, held, modes, begin, tiles):
+    return pl.pallas_call(
+        functools.partial(last_kernel, begin, tiles),
+        out_shape=jax.ShapeDtypeStruct(modes.shape, modes.dtype),
+        in_specs=[IN_VMEM] * (1 + len(held)) + [ANYWHERE],
+        out_specs=ANYWHERE,
+        scratch_shapes=[
+            pltpu.VMEM((modes.shape[0], modes.shape[1] - begin), modes.dtype),
+            pltpu.SemaphoreType.DMA((tiles,)),
+        ],
+        input_output_aliases={1 + len(held): 0},
+        compiler_params=pltpu.CompilerParams(vmem_limit_bytes=40 * 2**20),
         cost_estimate=FREE,
-        name="rebuild",
-    )(energy, vectors, *held, *coeffs)
+        name="rebuild_last",
+    )(weights, *held, modes)
 
 
 def swapped(value, axis, bit):
@@ -173,7 +238,10 @@
     me = lax.axis_index("tm")
     fields = snapshots.T
 
-    held = [fields] + [moved(fields, k, 0) for k in range(1, tm)]
+    begin = fields.shape[1] // 8 * 7
+
+    early, late = cut(fields, begin, 16, 2), fields[:, begin:]
+    first = [fields] + [moved(early, k, 0) for k in range(1, tm)]
 
     kept, given = project(fields, eof_basis, 8)
     mine = kept + swapped(given, "inner", 1)
@@ -188,11 +256,16 @@
         bit *= 4
     mine = mine.astype(jnp.bfloat16)
     both = jnp.stack([mine, moved(mine, 0, 1)])
+    both, late = lax.optimization_barrier((both, late))
+    last = [fields] + [moved(late, k, 0) for k in range(1, tm)]
     coeffs = [both] + [moved(both, k, 0) for k in range(1, tm)]
 
     rows = eigen_vectors.shape[1] // tm
     vectors = lax.dynamic_slice_in_dim(eigen_vectors, me * rows, rows, 1)
-    return rebuild(inverse_energy[None, :], vectors.T, held, coeffs, 4)
+    operator, modes, weights = rebuild_first(
+        inverse_energy[None, :], vectors.T, first, coeffs, begin, 4
+    )
+    return operator, rebuild_last(weights, last, modes, begin, 2)
 
 
 def solution(mesh):

time: 30.8 us -> 31 us (level)
  waiting for transfers between devices: 14.2 us -> 9.35 us
  local copies, waits for them, and re-layouts: 0.13 us -> 2.05 us
  starting transfers between devices: 9.76 us -> 11.3 us
  Pallas kernels: 5.88 us -> 7.4 us
    ppermute x3 -> x4, waiting for transfers between devices: 7.33 us -> 2.53 us  [moved(): return lax.ppermute(value, ('tm', 'inner'), route)]
    ppermute x3 -> x4, starting transfers between devices: 3.54 us -> 5.1 us  [moved(): return lax.ppermute(value, ('tm', 'inner'), route)]
    pallas_call x1 -> x3, Pallas kernels: 2.9 us -> 4.41 us  [the longest x1 2.72 us: rebuild_first(): pl.pallas_call(functools.partial(first_kernel, tiles), out_shape=(jax.Sha...]
    unnamed x7 -> x9, local copies, waits for them, and re-layouts: 0.12 us -> 1.38 us
    slice x0 -> x1, local copies, waits for them, and re-layouts: none -> 0.66 us  [per_device(): early, late = (cut(fields, begin, 16, 2), fields[:, begin:])]
  transfers between devices with their start and end apart: 8 -> 9, of which waited for: 7 -> 7; matrix products, arithmetic and copies ran while one was open for 0% -> 3% of each run, Pallas kernels for 10% -> 18%
where the time goes in v16:
time: 31 us; the launch traced here: 30.9 us
  starting transfers between devices  11.3 us (36%)
  waiting for transfers between devices  9.35 us (30%)
  Pallas kernels  7.4 us (24%)
  local copies, waits for them, and re-layouts  2.05 us (7%)
  between operations  0.73 us (2%)
    ppermute x5, waiting for transfers between devices, swapped(): return lax.ppermute(value, axis, route)  6.83 us
    ppermute x5, starting transfers between devices, swapped(): return lax.ppermute(value, axis, route)  6.21 us
    ppermute x4, starting transfers between devices, moved(): return lax.ppermute(value, ('tm', 'inner'), route)  5.1 us
    pallas_call x1, Pallas kernels, project(): pl.pallas_call(functools.partial(project_kernel, tiles), out_shape=(half,...  2.99 us
    pallas_call x1, Pallas kernels, rebuild_first(): pl.pallas_call(functools.partial(first_kernel, tiles), out_shape=(jax.Sha...  2.72 us
    ppermute x4, waiting for transfers between devices, moved(): return lax.ppermute(value, ('tm', 'inner'), route)  2.53 us
    unnamed x9, local copies, waits for them, and re-layouts  1.38 us
    pallas_call x1, Pallas kernels, rebuild_last(): pl.pallas_call(functools.partial(last_kernel, begin, tiles), out_shape=ja...  1.02 us
  transfers between devices with their start and end apart: 9, of which 7 were waited for; matrix products, arithmetic and copies ran while one was open for 3% of the time, Pallas kernels for 18%

profile of v16, /device:TPU:0, one launch (start us, length us, event | category | flops | bytes accessed | tf_op | source)
XLA Modules:
  0.0 30.9 jit_solution(15391466042969973553)
XLA Ops:
  0.6 0.0 copy-start
  0.6 0.0 copy-start.1
  0.7 1.3 %copy-done.1 = bf16[8192,64]{0,1:T(8,128)(2,1)S(1)} copy-done((bf16[8192,64]{0,1:T(8,128)(2,1)S(1)}, bf16[8192,64]{0,1:T(8,128)(2,1)}, u32[]{:S(2)}) %copy-start.1) | copy-done | bytes 1048600
  1.9 0.0 copy-start.2
  1.9 0.0 copy-start.3
  1.9 0.7 %cut.1 = bf16[64,7168]{1,0:T(8,128)(2,1)S(1)} custom-call(bf16[64,8192]{1,0:T(8,128)(2,1)S(1)} %bitcast.6), custom_call_target="tpu_custom_call" | custom-call | tf_op jit(solution)/shard_map/cut/pallas_call | solution.py:59
  2.6 3.0 %collective-permute-start = (bf16[64,7168]{1,0:T(8,128)(2,1)S(1)}, bf16[64,7168]{1,0:T(8,128)(2,1)S(1)}, u32[]{:S(2)}, u32[]{:S(2)}) collective-permute-start(bf16[64,7168]{1,0:T(8,128)(2,1)S(1)} %cut.1), channel_id=1, source_target_pairs={{16,0},{17,1},{0,16},{1,17},{18,2},{19,3},{2,18},{3,19},{20,4},{21... | collective-permute-start | bytes 2752520 | tf_op jit(solution)/shard_map/ppermute | solution.py:233
  5.6 3.0 %project.1 = (f32[32,256]{1,0:T(8,128)S(1)}, f32[32,256]{1,0:T(8,128)S(1)}) custom-call(bf16[64,8192]{1,0:T(8,128)(2,1)} %bitcast.5, bf16[8192,256]{1,0:T(8,128)(2,1)} %basis.1), custom_call_target="tpu_custom_call" | custom-call | tf_op jit(solution)/shard_map/project/pallas_call | solution.py:104
  8.6 0.1 collective-permute-start.1
  8.7 1.2 %collective-permute-done.1 = f32[32,256]{1,0:T(8,128)S(1)} collective-permute-done((f32[32,256]{1,0:T(8,128)S(1)}, f32[32,256]{1,0:T(8,128)S(1)}, u32[]{:S(2)}, u32[]{:S(2)}) %collective-permute-start.1) | collective-permute-done | bytes 32800 | tf_op jit(solution)/shard_map/ppermute | solution.py:223
  9.9 2.5 %collective-permute-start.4 = (f32[32,256]{1,0:T(8,128)S(1)}, f32[32,256]{1,0:T(8,128)S(1)}, u32[]{:S(2)}, u32[]{:S(2)}) collective-permute-start(f32[32,256]{1,0:T(8,128)S(1)} %add.19), channel_id=1, source_target_pairs={{6,0},{4,2},{2,4},{0,6},{14,8},{12,10},{10,12},{8,14},{7,1},{5,3},... | collective-permute-start | bytes 98312 | tf_op jit(solution)/shard_map/ppermute | solution.py:223
  12.4 0.4 %collective-permute-start.3 = (f32[32,256]{1,0:T(8,128)S(1)}, f32[32,256]{1,0:T(8,128)S(1)}, u32[]{:S(2)}, u32[]{:S(2)}) collective-permute-start(f32[32,256]{1,0:T(8,128)S(1)} %add.19), channel_id=1, source_target_pairs={{4,0},{6,2},{0,4},{2,6},{12,8},{14,10},{8,12},{10,14},{5,1},{7,3},... | collective-permute-start | bytes 98312 | tf_op jit(solution)/shard_map/ppermute | solution.py:223
  12.9 0.5 %collective-permute-start.2 = (f32[32,256]{1,0:T(8,128)S(1)}, f32[32,256]{1,0:T(8,128)S(1)}, u32[]{:S(2)}, u32[]{:S(2)}) collective-permute-start(f32[32,256]{1,0:T(8,128)S(1)} %add.19), channel_id=1, source_target_pairs={{2,0},{0,2},{6,4},{4,6},{10,8},{8,10},{14,12},{12,14},{3,1},{1,3},... | collective-permute-start | bytes 98312 | tf_op jit(solution)/shard_map/ppermute | solution.py:223
  13.4 1.3 %collective-permute-done.4 = f32[32,256]{1,0:T(8,128)S(1)} collective-permute-done((f32[32,256]{1,0:T(8,128)S(1)}, f32[32,256]{1,0:T(8,128)S(1)}, u32[]{:S(2)}, u32[]{:S(2)}) %collective-permute-start.4) | collective-permute-done | bytes 32800 | tf_op jit(solution)/shard_map/ppermute | solution.py:223
  14.7 1.6 %collective-permute-done.3 = f32[32,256]{1,0:T(8,128)S(1)} collective-permute-done((f32[32,256]{1,0:T(8,128)S(1)}, f32[32,256]{1,0:T(8,128)S(1)}, u32[]{:S(2)}, u32[]{:S(2)}) %collective-permute-start.3) | collective-permute-done | bytes 32800 | tf_op jit(solution)/shard_map/ppermute | solution.py:223
  16.3 0.4 %collective-permute-done.2 = f32[32,256]{1,0:T(8,128)S(1)} collective-permute-done((f32[32,256]{1,0:T(8,128)S(1)}, f32[32,256]{1,0:T(8,128)S(1)}, u32[]{:S(2)}, u32[]{:S(2)}) %collective-permute-start.2) | collective-permute-done | bytes 32800 | tf_op jit(solution)/shard_map/ppermute | solution.py:223
  16.8 2.7 %collective-permute-start.5 = (f32[32,256]{1,0:T(8,128)S(1)}, f32[32,256]{1,0:T(8,128)S(1)}, u32[]{:S(2)}, u32[]{:S(2)}) collective-permute-start(f32[32,256]{1,0:T(8,128)S(1)} %add_add_fusion), channel_id=1, source_target_pairs={{8,0},{10,2},{12,4},{14,6},{0,8},{2,10},{4,12},{6,14},{9,1},{11,3}... | collective-permute-start | bytes 98312 | tf_op jit(solution)/shard_map/ppermute | solution.py:223
  19.4 2.2 %collective-permute-done.5 = f32[32,256]{1,0:T(8,128)S(1)} collective-permute-done((f32[32,256]{1,0:T(8,128)S(1)}, f32[32,256]{1,0:T(8,128)S(1)}, u32[]{:S(2)}, u32[]{:S(2)}) %collective-permute-start.5) | collective-permute-done | bytes 32800 | tf_op jit(solution)/shard_map/ppermute | solution.py:223
  21.7 0.0 collective-permute-start.6
  21.7 0.0 copy-done.2
  21.7 0.7 %slice.4 = bf16[64,1024]{1,0:T(8,128)(2,1)} slice(bf16[64,8192]{1,0:T(8,128)(2,1)S(1)} %bitcast.7), slice={[0:64], [7168:8192]} | slice | bytes 262144 | tf_op jit(solution)/shard_map/slice | solution.py:243
  22.3 0.5 %collective-permute-done.6 = bf16[32,256]{1,0:T(8,128)(2,1)S(1)} collective-permute-done((bf16[32,256]{1,0:T(8,128)(2,1)S(1)}, bf16[32,256]{1,0:T(8,128)(2,1)S(1)}, u32[]{:S(2)}, u32[]{:S(2)}) %collective-permute-start.6) | collective-permute-done | bytes 16416 | tf_op jit(solution)/shard_map/ppermute | solution.py:233
  22.9 0.5 %collective-permute-start.7 = (bf16[2,32,256]{2,1,0:T(8,128)(2,1)S(1)}, bf16[2,32,256]{2,1,0:T(8,128)(2,1)S(1)}, u32[]{:S(2)}, u32[]{:S(2)}) collective-permute-start(bf16[2,32,256]{2,1,0:T(8,128)(2,1)S(1)} %pad_maximum_fusion.refs_2_), channel_id=1, source_target_pairs={{16,0},{17,1},{0,16},{1,17},{18,2},{19,3},{2,18},{3,19},{20,4},{21... | collective-permute-start | bytes 98312 | tf_op jit(solution)/shard_map/ppermute | solution.py:233
  23.4 0.0 copy-done
  23.4 0.1 copy.8
  23.5 1.6 %collective-permute-start.8 = (bf16[64,1024]{1,0:T(8,128)(2,1)}, bf16[64,1024]{1,0:T(8,128)(2,1)S(1)}, u32[]{:S(2)}, u32[]{:S(2)}) collective-permute-start(bf16[64,1024]{1,0:T(8,128)(2,1)} %slice.4), channel_id=1, source_target_pairs={{16,0},{17,1},{0,16},{1,17},{18,2},{19,3},{2,18},{3,19},{20,4},{21... | collective-permute-start | bytes 393224 | tf_op jit(solution)/shard_map/ppermute | solution.py:233
  25.1 2.0 %collective-permute-done.7.refs_3_ = bf16[2,32,256]{2,1,0:T(8,128)(2,1)S(1)} collective-permute-done((bf16[2,32,256]{2,1,0:T(8,128)(2,1)S(1)}, bf16[2,32,256]{2,1,0:T(8,128)(2,1)S(1)}, u32[]{:S(2)}, u32[]{:S(2)}) %collective-permute-start.7) | collective-permute-done | bytes 32800 | tf_op jit(solution)/shard_map/ppermute | solution.py:233
  27.1 0.0 collective-permute-done.refs_1_
  27.1 0.0 copy-done.3
  27.1 2.7 %rebuild_first.1 = (f32[256,256]{1,0:T(8,128)}, bf16[256,8192]{1,0:T(8,128)(2,1)}, bf16[256,128]{1,0:T(8,128)(2,1)S(1)}) custom-call(f32[1,256]{1,0:T(1,128)S(1)} %bitcast.11, bf16[256,256]{1,0:T(8,128)(2,1)S(1)} %bitcast.10, bf16[64,8192]{1,0:T(8,128)(2,1)S(1)} %bitcast.8, bf16[64,7168]{1,0:T(8,128)(2,1)S(1)} %collective-permute-done.refs_1_, ...), custom_call_target="tpu_custom_call" | custom-call | flops 3000000000 | tf_op jit(solution)/shard_map/rebuild_first/pallas_call | solution.py:182
  29.8 0.0 collective-permute-done.8.refs_1_
  29.8 1.0 %rebuild_last.1 = bf16[256,8192]{1,0:T(8,128)(2,1)} custom-call(bf16[256,128]{1,0:T(8,128)(2,1)S(1)} %get-tuple-element.13.weights, bf16[64,8192]{1,0:T(8,128)(2,1)S(1)} %bitcast.9, bf16[64,1024]{1,0:T(8,128)(2,1)S(1)} %collective-permute-done.8.refs_1_, bf16[256,8192]{1,0:T(8,128)(2,1)} %get-tuple-element.15.refs_2_), custom_call_target="tpu_custom_call", output_to_operand_aliasing={{}: (3, {})} | custom-call | tf_op jit(solution)/shard_map/rebuild_last/pallas_call | solution.py:205
  (5 shorter events, 0.0 us)
Async XLA Ops:
  0.6 22.8 %copy-start = (bf16[256,512]{1,0:T(8,128)(2,1)S(1)}, bf16[256,512]{1,0:T(8,128)(2,1)}, u32[]{:S(2)}) copy-start(bf16[256,512]{1,0:T(8,128)(2,1)} %param.7) | copy-start | bytes 786436
  0.6 1.3 %copy-start.1 = (bf16[8192,64]{0,1:T(8,128)(2,1)S(1)}, bf16[8192,64]{0,1:T(8,128)(2,1)}, u32[]{:S(2)}) copy-start(bf16[8192,64]{0,1:T(8,128)(2,1)} %param.5) | copy-start | bytes 3145732
  1.9 19.8 %copy-start.2 = (bf16[8192,64]{0,1:T(8,128)(2,1)S(1)}, bf16[8192,64]{0,1:T(8,128)(2,1)}, u32[]{:S(2)}) copy-start(bf16[8192,64]{0,1:T(8,128)(2,1)} %param.5) | copy-start | bytes 3145732
  1.9 25.2 %copy-start.3 = (f32[256]{0:T(256)S(1)}, f32[256]{0:T(256)}, u32[]{:S(2)}) copy-start(f32[256]{0:T(256)} %param.6) | copy-start | bytes 3076
  2.6 24.5 %collective-permute-start = (bf16[64,7168]{1,0:T(8,128)(2,1)S(1)}, bf16[64,7168]{1,0:T(8,128)(2,1)S(1)}, u32[]{:S(2)}, u32[]{:S(2)}) collective-permute-start(bf16[64,7168]{1,0:T(8,128)(2,1)S(1)} %cut.1), channel_id=1, source_target_pairs={{16,0},{17,1},{0,16},{1,17},{18,2},{19,3},{2,18},{3,19},{20,4},{21... | collective-permute-start | bytes 2752520 | tf_op jit(solution)/shard_map/ppermute | solution.py:233
  8.6 1.3 %collective-permute-start.1 = (f32[32,256]{1,0:T(8,128)S(1)}, f32[32,256]{1,0:T(8,128)S(1)}, u32[]{:S(2)}, u32[]{:S(2)}) collective-permute-start(f32[32,256]{1,0:T(8,128)S(1)} %get-tuple-element.10), channel_id=1, source_target_pairs={{1,0},{0,1},{3,2},{2,3},{5,4},{4,5},{7,6},{6,7},{9,8},{8,9},{11,10... | collective-permute-start | bytes 98312 | tf_op jit(solution)/shard_map/ppermute | solution.py:223
  9.9 4.8 %collective-permute-start.4 = (f32[32,256]{1,0:T(8,128)S(1)}, f32[32,256]{1,0:T(8,128)S(1)}, u32[]{:S(2)}, u32[]{:S(2)}) collective-permute-start(f32[32,256]{1,0:T(8,128)S(1)} %add.19), channel_id=1, source_target_pairs={{6,0},{4,2},{2,4},{0,6},{14,8},{12,10},{10,12},{8,14},{7,1},{5,3},... | collective-permute-start | bytes 98312 | tf_op jit(solution)/shard_map/ppermute | solution.py:223
  12.4 3.9 %collective-permute-start.3 = (f32[32,256]{1,0:T(8,128)S(1)}, f32[32,256]{1,0:T(8,128)S(1)}, u32[]{:S(2)}, u32[]{:S(2)}) collective-permute-start(f32[32,256]{1,0:T(8,128)S(1)} %add.19), channel_id=1, source_target_pairs={{4,0},{6,2},{0,4},{2,6},{12,8},{14,10},{8,12},{10,14},{5,1},{7,3},... | collective-permute-start | bytes 98312 | tf_op jit(solution)/shard_map/ppermute | solution.py:223
  12.9 3.9 %collective-permute-start.2 = (f32[32,256]{1,0:T(8,128)S(1)}, f32[32,256]{1,0:T(8,128)S(1)}, u32[]{:S(2)}, u32[]{:S(2)}) collective-permute-start(f32[32,256]{1,0:T(8,128)S(1)} %add.19), channel_id=1, source_target_pairs={{2,0},{0,2},{6,4},{4,6},{10,8},{8,10},{14,12},{12,14},{3,1},{1,3},... | collective-permute-start | bytes 98312 | tf_op jit(solution)/shard_map/ppermute | solution.py:223
  16.8 4.9 %collective-permute-start.5 = (f32[32,256]{1,0:T(8,128)S(1)}, f32[32,256]{1,0:T(8,128)S(1)}, u32[]{:S(2)}, u32[]{:S(2)}) collective-permute-start(f32[32,256]{1,0:T(8,128)S(1)} %add_add_fusion), channel_id=1, source_target_pairs={{8,0},{10,2},{12,4},{14,6},{0,8},{2,10},{4,12},{6,14},{9,1},{11,3}... | collective-permute-start | bytes 98312 | tf_op jit(solution)/shard_map/ppermute | solution.py:223
  21.7 1.2 %collective-permute-start.6 = (bf16[32,256]{1,0:T(8,128)(2,1)S(1)}, bf16[32,256]{1,0:T(8,128)(2,1)S(1)}, u32[]{:S(2)}, u32[]{:S(2)}) collective-permute-start(bf16[32,256]{1,0:T(8,128)(2,1)S(1)} %add_convert_fusion), channel_id=1, source_target_pairs={{1,0},{0,1},{17,16},{16,17},{3,2},{2,3},{19,18},{18,19},{5,4},{4,5... | collective-permute-start | bytes 49160 | tf_op jit(solution)/shard_map/ppermute | solution.py:233
  22.9 4.2 %collective-permute-start.7 = (bf16[2,32,256]{2,1,0:T(8,128)(2,1)S(1)}, bf16[2,32,256]{2,1,0:T(8,128)(2,1)S(1)}, u32[]{:S(2)}, u32[]{:S(2)}) collective-permute-start(bf16[2,32,256]{2,1,0:T(8,128)(2,1)S(1)} %pad_maximum_fusion.refs_2_), channel_id=1, source_target_pairs={{16,0},{17,1},{0,16},{1,17},{18,2},{19,3},{2,18},{3,19},{20,4},{21... | collective-permute-start | bytes 98312 | tf_op jit(solution)/shard_map/ppermute | solution.py:233
  23.5 6.3 %collective-permute-start.8 = (bf16[64,1024]{1,0:T(8,128)(2,1)}, bf16[64,1024]{1,0:T(8,128)(2,1)S(1)}, u32[]{:S(2)}, u32[]{:S(2)}) collective-permute-start(bf16[64,1024]{1,0:T(8,128)(2,1)} %slice.4), channel_id=1, source_target_pairs={{16,0},{17,1},{0,16},{1,17},{18,2},{19,3},{2,18},{3,19},{20,4},{21... | collective-permute-start | bytes 393224 | tf_op jit(solution)/shard_map/ppermute | solution.py:233

commit v17 on v16

--- a/solution.py
+++ b/solution.py
@@ -37,58 +37,54 @@
     return lax.dot_general(left, right, dims, preferred_element_type=jnp.float32)
 
 
-def cut_kernel(rows, parts, fields, early, sent):
-    width = early.shape[1] // parts
-    waited(
-        started(
-            [
-                pltpu.make_async_copy(
-                    fields.at[pl.ds(at, rows), pl.ds(i * width, width)],
-                    early.at[pl.ds(at, rows), pl.ds(i * width, width)],
-                    sent.at[at // rows, i],
-                )
-                for at in range(0, fields.shape[0], rows)
-                for i in range(parts)
-            ]
-        )
-    )
-
-
-def cut(fields, width, rows, parts):
-    hours = fields.shape[0]
-    return pl.pallas_call(
-        functools.partial(cut_kernel, rows, parts),
-        out_shape=jax.ShapeDtypeStruct((hours, width), fields.dtype),
+def cut_kernel(rows, begin, fields, early, late, sent):
+    half = begin // 2
+    copies = []
+    for n, at in enumerate(range(0, fields.shape[0], rows)):
+        here = pl.ds(at, rows)
+        for i in range(2):
+            span = pl.ds(i * half, half)
+            copies.append(
+                pltpu.make_async_copy(fields.at[here, span], early.at[here, span], sent.at[n, i])
+            )
+    span = pl.ds(begin, late.shape[1])
+    copies.append(pltpu.make_async_copy(fields.at[:, span], late, sent.at[0, 2]))
+    waited(started(copies))
+
+
+def cut(fields, begin, rows):
+    hours, cells = fields.shape
+    return pl.pallas_call(
+        functools.partial(cut_kernel, rows, begin),
+        out_shape=(
+            jax.ShapeDtypeStruct((hours, begin), fields.dtype),
+            jax.ShapeDtypeStruct((hours, cells - begin), fields.dtype),
+        ),
         in_specs=[ANYWHERE],
-        out_specs=ANYWHERE,
-        scratch_shapes=[pltpu.SemaphoreType.DMA((hours // rows, parts))],
+        out_specs=(ANYWHERE, ANYWHERE),
+        scratch_shapes=[pltpu.SemaphoreType.DMA((hours // rows, 3))],
         compiler_params=pltpu.CompilerParams(vmem_limit_bytes=52 * 2**20),
         cost_estimate=FREE,
         name="cut",
     )(fields)
 
 
-def project_kernel(tiles, snapshots, basis, kept, given, fields, patterns, halves, arrived):
-    cells = snapshots.shape[1]
-    tile = cells // tiles
-    copies = []
-    for i in range(tiles):
-        span = pl.ds(i * tile, tile)
-        copies.append(
-            (
-                pltpu.make_async_copy(snapshots.at[:, span], fields.at[:, span], arrived.at[0, i]),
-                pltpu.make_async_copy(basis.at[span], patterns.at[span], arrived.at[1, i]),
-            )
-        )
-    for pair in copies:
-        for copy in pair:
-            copy.start()
-    total = jnp.zeros((fields.shape[0], patterns.shape[1]), jnp.float32)
-    for i, pair in enumerate(copies):
-        for copy in pair:
-            copy.wait()
-        span = pl.ds(i * tile, tile)
-        total += product(fields[:, span], patterns[span], ROWS)
+def project_kernel(tiles, early, late, basis, kept, given, patterns, halves, arrived):
+    cells = basis.shape[0]
+    tile, begin = cells // tiles, early.shape[1]
+    spans = [pl.ds(i * tile, tile) for i in range(tiles)]
+    copies = started(
+        [
+            pltpu.make_async_copy(basis.at[span], patterns.at[span], arrived.at[i])
+            for i, span in enumerate(spans)
+        ]
+    )
+    total = jnp.zeros((early.shape[0], patterns.shape[1]), jnp.float32)
+    for i, span in enumerate(spans):
+        copies[i].wait()
+        at = i * tile
+        fields = early[:, span] if at < begin else late[:, pl.ds(at - begin, tile)]
+        total += product(fields, patterns[span], ROWS)
     half = kept.shape[0]
     core = lax.axis_index("inner")
     halves[0] = total[:half]
@@ -97,25 +93,23 @@
     given[...] = halves[1 - core]
 
 
-def project(snapshots, basis, tiles):
-    hours = snapshots.shape[0]
-    rank = basis.shape[1]
+def project(early, late, basis, tiles):
+    hours, rank = early.shape[0], basis.shape[1]
     half = jax.ShapeDtypeStruct((hours // 2, rank), jnp.float32)
     return pl.pallas_call(
         functools.partial(project_kernel, tiles),
         out_shape=(half, half),
-        in_specs=[ANYWHERE] * 2,
-        out_specs=(pl.BlockSpec(memory_space=pltpu.VMEM),) * 2,
+        in_specs=[IN_VMEM, IN_VMEM, ANYWHERE],
+        out_specs=(IN_VMEM, IN_VMEM),
         scratch_shapes=[
-            pltpu.VMEM(snapshots.shape, snapshots.dtype),
             pltpu.VMEM(basis.shape, basis.dtype),
             pltpu.VMEM((2, hours // 2, rank), jnp.float32),
-            pltpu.SemaphoreType.DMA((2, tiles)),
+            pltpu.SemaphoreType.DMA((tiles,)),
         ],
-        compiler_params=pltpu.CompilerParams(vmem_limit_bytes=53 * 2**20),
+        compiler_params=pltpu.CompilerParams(vmem_limit_bytes=52 * 2**20),
         cost_estimate=FREE,
         name="project",
-    )(snapshots, basis)
+    )(early, late, basis)
 
 
 def lagged_and_scaled(every, energy):
@@ -171,14 +165,13 @@
 
 def last_kernel(begin, tiles, weights, *refs):
     held, (_, modes, made, sent) = refs[:-4], refs[-4:]
-    blocks = [(held[0], 0)] + [(b, begin) for b in held[1:]]
+    blocks = [(b, begin) for b in held]
     waited(rebuilt(weights[...], blocks, made, modes, begin, tiles, sent))
 
 
-def rebuild_first(energy, vectors, held, coeffs, width, tiles):
+def rebuild_first(energy, vectors, held, coeffs, cells, tiles):
     rank = coeffs[0].shape[2]
-    hours, cells = held[0].shape
-    hours, modes = len(held) * hours, vectors.shape[0]
+    hours, modes = len(held) * held[0].shape[0], vectors.shape[0]
     return pl.pallas_call(
         functools.partial(first_kernel, tiles),
         out_shape=(
@@ -191,7 +184,7 @@
         scratch_shapes=[
             pltpu.VMEM((hours, rank), jnp.float32),
             pltpu.VMEM((hours, rank), jnp.float32),
-            pltpu.VMEM((modes, width), jnp.bfloat16),
+            pltpu.VMEM((modes, held[0].shape[1]), jnp.bfloat16),
             pltpu.VMEM((rank, rank), jnp.float32),
             pltpu.SemaphoreType.DMA((tiles + 1,)),
         ],
@@ -238,12 +231,13 @@
     me = lax.axis_index("tm")
     fields = snapshots.T
 
-    begin = fields.shape[1] // 8 * 7
-
-    early, late = cut(fields, begin, 16, 2), fields[:, begin:]
-    first = [fields] + [moved(early, k, 0) for k in range(1, tm)]
-
-    kept, given = project(fields, eof_basis, 8)
+    cells = fields.shape[1]
+    begin = cells // 8 * 7
+
+    early, late = cut(fields, begin, 16)
+    first = [early] + [moved(early, k, 0) for k in range(1, tm)]
+
+    kept, given = project(early, late, eof_basis, 8)
     mine = kept + swapped(given, "inner", 1)
     bit = 1
     while bit < outer:
@@ -256,14 +250,14 @@
         bit *= 4
     mine = mine.astype(jnp.bfloat16)
     both = jnp.stack([mine, moved(mine, 0, 1)])
-    both, late = lax.optimization_barrier((both, late))
-    last = [fields] + [moved(late, k, 0) for k in range(1, tm)]
+    both, behind = lax.optimization_barrier((both, late))
+    last = [late] + [moved(behind, k, 0) for k in range(1, tm)]
     coeffs = [both] + [moved(both, k, 0) for k in range(1, tm)]
 
     rows = eigen_vectors.shape[1] // tm
     vectors = lax.dynamic_slice_in_dim(eigen_vectors, me * rows, rows, 1)
     operator, modes, weights = rebuild_first(
-        inverse_energy[None, :], vectors.T, first, coeffs, begin, 4
+        inverse_energy[None, :], vectors.T, first, coeffs, cells, 4
     )
     return operator, rebuild_last(weights, last, modes, begin, 2)
 

time: 31 us -> 30.5 us (0.984)
  local copies, waits for them, and re-layouts: 2.05 us -> 0.12 us
  waiting for transfers between devices: 9.35 us -> 10.2 us
  Pallas kernels: 7.4 us -> 7.97 us
    unnamed x9 -> x5, local copies, waits for them, and re-layouts: 1.38 us -> 0.11 us
    ppermute x4, waiting for transfers between devices: 2.53 us -> 3.4 us  [moved(): return lax.ppermute(value, ('tm', 'inner'), route)]
    pallas_call x1, Pallas kernels: 0.66 us -> 1.43 us  [cut(): pl.pallas_call(functools.partial(cut_kernel, rows, begin), out_shape=(jax...]
    slice x1 -> x0, local copies, waits for them, and re-layouts: 0.66 us -> none  [per_device(): early, late = (cut(fields, begin, 16, 2), fields[:, begin:])]
  transfers between devices with their start and end apart: 9 -> 9, of which waited for: 7 -> 7; matrix products, arithmetic and copies ran while one was open for 3% -> 0% of each run, Pallas kernels for 18% -> 18%
where the time goes in v17:
time: 30.5 us; the launch traced here: 30.4 us
  starting transfers between devices  11.3 us (37%)
  waiting for transfers between devices  10.2 us (33%)
  Pallas kernels  7.97 us (26%)
  between operations  0.72 us (2%)
    ppermute x5, waiting for transfers between devices, swapped(): return lax.ppermute(value, axis, route)  6.82 us
    ppermute x5, starting transfers between devices, swapped(): return lax.ppermute(value, axis, route)  6.22 us
    ppermute x4, starting transfers between devices, moved(): return lax.ppermute(value, ('tm', 'inner'), route)  5.1 us
    ppermute x4, waiting for transfers between devices, moved(): return lax.ppermute(value, ('tm', 'inner'), route)  3.4 us
    pallas_call x1, Pallas kernels, project(): pl.pallas_call(functools.partial(project_kernel, tiles), out_shape=(half,...  2.79 us
    pallas_call x1, Pallas kernels, rebuild_first(): pl.pallas_call(functools.partial(first_kernel, tiles), out_shape=(jax.Sha...  2.72 us
    pallas_call x1, Pallas kernels, cut(): pl.pallas_call(functools.partial(cut_kernel, rows, begin), out_shape=(jax...  1.43 us
    pallas_call x1, Pallas kernels, rebuild_last(): pl.pallas_call(functools.partial(last_kernel, begin, tiles), out_shape=ja...  1.02 us
  transfers between devices with their start and end apart: 9, of which 7 were waited for; matrix products, arithmetic and copies ran while one was open for 0% of the time, Pallas kernels for 18%

profile of v17, /device:TPU:0, one launch (start us, length us, event | category | flops | bytes accessed | tf_op | source)
XLA Modules:
  0.0 30.4 jit_solution(9476893243176895309)
XLA Ops:
  0.6 0.0 copy-start
  0.6 0.0 copy-start.1
  0.7 1.4 %cut.1 = (bf16[64,7168]{1,0:T(8,128)(2,1)S(1)}, bf16[64,1024]{1,0:T(8,128)(2,1)S(1)}) custom-call(bf16[64,8192]{1,0:T(8,128)(2,1)} %bitcast.7), custom_call_target="tpu_custom_call" | custom-call | tf_op jit(solution)/shard_map/cut/pallas_call | solution.py:57
  2.1 3.0 %collective-permute-start = (bf16[64,7168]{1,0:T(8,128)(2,1)S(1)}, bf16[64,7168]{1,0:T(8,128)(2,1)S(1)}, u32[]{:S(2)}, u32[]{:S(2)}) collective-permute-start(bf16[64,7168]{1,0:T(8,128)(2,1)S(1)} %get-tuple-element.11.early.refs_0_), channel_id=1, source_target_pairs={{16,0},{17,1},{0,16},{1,17},{18,2},{19,3},{2,18},{3,19},{20,4},{21... | collective-permute-start | bytes 2752520 | tf_op jit(solution)/shard_map/ppermute | solution.py:226
  5.1 2.8 %project.1 = (f32[32,256]{1,0:T(8,128)S(1)}, f32[32,256]{1,0:T(8,128)S(1)}) custom-call(bf16[64,7168]{1,0:T(8,128)(2,1)S(1)} %get-tuple-element.11.early.refs_0_, bf16[64,1024]{1,0:T(8,128)(2,1)S(1)} %get-tuple-element.18.late.refs_0_, bf16[8192,256]{1,0:T(8,128)(2,1)} %basis.1), custom_call_target="tpu_custom_call" | custom-call | tf_op jit(solution)/shard_map/project/pallas_call | solution.py:99
  7.9 0.1 collective-permute-start.1
  8.0 1.2 %collective-permute-done.1 = f32[32,256]{1,0:T(8,128)S(1)} collective-permute-done((f32[32,256]{1,0:T(8,128)S(1)}, f32[32,256]{1,0:T(8,128)S(1)}, u32[]{:S(2)}, u32[]{:S(2)}) %collective-permute-start.1) | collective-permute-done | bytes 32800 | tf_op jit(solution)/shard_map/ppermute | solution.py:216
  9.2 2.5 %collective-permute-start.4 = (f32[32,256]{1,0:T(8,128)S(1)}, f32[32,256]{1,0:T(8,128)S(1)}, u32[]{:S(2)}, u32[]{:S(2)}) collective-permute-start(f32[32,256]{1,0:T(8,128)S(1)} %add.19), channel_id=1, source_target_pairs={{6,0},{4,2},{2,4},{0,6},{14,8},{12,10},{10,12},{8,14},{7,1},{5,3},... | collective-permute-start | bytes 98312 | tf_op jit(solution)/shard_map/ppermute | solution.py:216
  11.7 0.4 %collective-permute-start.3 = (f32[32,256]{1,0:T(8,128)S(1)}, f32[32,256]{1,0:T(8,128)S(1)}, u32[]{:S(2)}, u32[]{:S(2)}) collective-permute-start(f32[32,256]{1,0:T(8,128)S(1)} %add.19), channel_id=1, source_target_pairs={{4,0},{6,2},{0,4},{2,6},{12,8},{14,10},{8,12},{10,14},{5,1},{7,3},... | collective-permute-start | bytes 98312 | tf_op jit(solution)/shard_map/ppermute | solution.py:216
  12.2 0.5 %collective-permute-start.2 = (f32[32,256]{1,0:T(8,128)S(1)}, f32[32,256]{1,0:T(8,128)S(1)}, u32[]{:S(2)}, u32[]{:S(2)}) collective-permute-start(f32[32,256]{1,0:T(8,128)S(1)} %add.19), channel_id=1, source_target_pairs={{2,0},{0,2},{6,4},{4,6},{10,8},{8,10},{14,12},{12,14},{3,1},{1,3},... | collective-permute-start | bytes 98312 | tf_op jit(solution)/shard_map/ppermute | solution.py:216
  12.7 1.3 %collective-permute-done.4 = f32[32,256]{1,0:T(8,128)S(1)} collective-permute-done((f32[32,256]{1,0:T(8,128)S(1)}, f32[32,256]{1,0:T(8,128)S(1)}, u32[]{:S(2)}, u32[]{:S(2)}) %collective-permute-start.4) | collective-permute-done | bytes 32800 | tf_op jit(solution)/shard_map/ppermute | solution.py:216
  14.0 1.6 %collective-permute-done.3 = f32[32,256]{1,0:T(8,128)S(1)} collective-permute-done((f32[32,256]{1,0:T(8,128)S(1)}, f32[32,256]{1,0:T(8,128)S(1)}, u32[]{:S(2)}, u32[]{:S(2)}) %collective-permute-start.3) | collective-permute-done | bytes 32800 | tf_op jit(solution)/shard_map/ppermute | solution.py:216
  15.6 0.4 %collective-permute-done.2 = f32[32,256]{1,0:T(8,128)S(1)} collective-permute-done((f32[32,256]{1,0:T(8,128)S(1)}, f32[32,256]{1,0:T(8,128)S(1)}, u32[]{:S(2)}, u32[]{:S(2)}) %collective-permute-start.2) | collective-permute-done | bytes 32800 | tf_op jit(solution)/shard_map/ppermute | solution.py:216
  16.1 2.7 %collective-permute-start.5 = (f32[32,256]{1,0:T(8,128)S(1)}, f32[32,256]{1,0:T(8,128)S(1)}, u32[]{:S(2)}, u32[]{:S(2)}) collective-permute-start(f32[32,256]{1,0:T(8,128)S(1)} %add_add_fusion), channel_id=1, source_target_pairs={{8,0},{10,2},{12,4},{14,6},{0,8},{2,10},{4,12},{6,14},{9,1},{11,3}... | collective-permute-start | bytes 98312 | tf_op jit(solution)/shard_map/ppermute | solution.py:216
  18.7 2.2 %collective-permute-done.5 = f32[32,256]{1,0:T(8,128)S(1)} collective-permute-done((f32[32,256]{1,0:T(8,128)S(1)}, f32[32,256]{1,0:T(8,128)S(1)}, u32[]{:S(2)}, u32[]{:S(2)}) %collective-permute-start.5) | collective-permute-done | bytes 32800 | tf_op jit(solution)/shard_map/ppermute | solution.py:216
  21.0 0.0 collective-permute-start.6
  21.0 1.2 %collective-permute-done.6 = bf16[32,256]{1,0:T(8,128)(2,1)S(1)} collective-permute-done((bf16[32,256]{1,0:T(8,128)(2,1)S(1)}, bf16[32,256]{1,0:T(8,128)(2,1)S(1)}, u32[]{:S(2)}, u32[]{:S(2)}) %collective-permute-start.6) | collective-permute-done | bytes 16416 | tf_op jit(solution)/shard_map/ppermute | solution.py:226
  22.2 0.5 %collective-permute-start.7 = (bf16[2,32,256]{2,1,0:T(8,128)(2,1)S(1)}, bf16[2,32,256]{2,1,0:T(8,128)(2,1)S(1)}, u32[]{:S(2)}, u32[]{:S(2)}) collective-permute-start(bf16[2,32,256]{2,1,0:T(8,128)(2,1)S(1)} %pad_maximum_fusion.refs_2_), channel_id=1, source_target_pairs={{16,0},{17,1},{0,16},{1,17},{18,2},{19,3},{2,18},{3,19},{20,4},{21... | collective-permute-start | bytes 98312 | tf_op jit(solution)/shard_map/ppermute | solution.py:226
  22.7 0.0 copy-done
  22.7 0.1 copy.8
  22.8 1.6 %collective-permute-start.8 = (bf16[64,1024]{1,0:T(8,128)(2,1)S(1)}, bf16[64,1024]{1,0:T(8,128)(2,1)S(1)}, u32[]{:S(2)}, u32[]{:S(2)}) collective-permute-start(bf16[64,1024]{1,0:T(8,128)(2,1)S(1)} %get-tuple-element.18.late.refs_0_), channel_id=1, source_target_pairs={{16,0},{17,1},{0,16},{1,17},{18,2},{19,3},{2,18},{3,19},{20,4},{21... | collective-permute-start | bytes 393224 | tf_op jit(solution)/shard_map/ppermute | solution.py:226
  24.4 2.2 %collective-permute-done.7.refs_3_ = bf16[2,32,256]{2,1,0:T(8,128)(2,1)S(1)} collective-permute-done((bf16[2,32,256]{2,1,0:T(8,128)(2,1)S(1)}, bf16[2,32,256]{2,1,0:T(8,128)(2,1)S(1)}, u32[]{:S(2)}, u32[]{:S(2)}) %collective-permute-start.7) | collective-permute-done | bytes 32800 | tf_op jit(solution)/shard_map/ppermute | solution.py:226
  26.6 0.0 collective-permute-done.refs_1_
  26.6 0.0 copy-done.1
  26.6 2.7 %rebuild_first.1 = (f32[256,256]{1,0:T(8,128)}, bf16[256,8192]{1,0:T(8,128)(2,1)}, bf16[256,128]{1,0:T(8,128)(2,1)S(1)}) custom-call(f32[1,256]{1,0:T(1,128)S(1)} %bitcast.6, bf16[256,256]{1,0:T(8,128)(2,1)S(1)} %bitcast.5, bf16[64,7168]{1,0:T(8,128)(2,1)S(1)} %get-tuple-element.11.early.refs_0_, bf16[64,7168]{1,0:T(8,128)(2,1)S(1)} %collective-permute-done.refs_1_, ...), custom_call_target="tpu_custom_call" | custom-call | flops 3000000000 | tf_op jit(solution)/shard_map/rebuild_first/pallas_call | solution.py:175
  29.3 0.0 collective-permute-done.8.refs_1_
  29.4 1.0 %rebuild_last.1 = bf16[256,8192]{1,0:T(8,128)(2,1)} custom-call(bf16[256,128]{1,0:T(8,128)(2,1)S(1)} %get-tuple-element.17.weights, bf16[64,1024]{1,0:T(8,128)(2,1)S(1)} %get-tuple-element.18.late.refs_0_, bf16[64,1024]{1,0:T(8,128)(2,1)S(1)} %collective-permute-done.8.refs_1_, ...), custom_call_target="tpu_custom_call", output_to_operand_aliasing={{}: (3, {})} | custom-call | tf_op jit(solution)/shard_map/rebuild_last/pallas_call | solution.py:198
  (5 shorter events, 0.0 us)
Async XLA Ops:
  0.6 22.1 %copy-start = (bf16[256,512]{1,0:T(8,128)(2,1)S(1)}, bf16[256,512]{1,0:T(8,128)(2,1)}, u32[]{:S(2)}) copy-start(bf16[256,512]{1,0:T(8,128)(2,1)} %param.7) | copy-start | bytes 786436
  0.6 26.0 %copy-start.1 = (f32[256]{0:T(256)S(1)}, f32[256]{0:T(256)}, u32[]{:S(2)}) copy-start(f32[256]{0:T(256)} %param.6) | copy-start | bytes 3076
  2.1 24.5 %collective-permute-start = (bf16[64,7168]{1,0:T(8,128)(2,1)S(1)}, bf16[64,7168]{1,0:T(8,128)(2,1)S(1)}, u32[]{:S(2)}, u32[]{:S(2)}) collective-permute-start(bf16[64,7168]{1,0:T(8,128)(2,1)S(1)} %get-tuple-element.11.early.refs_0_), channel_id=1, source_target_pairs={{16,0},{17,1},{0,16},{1,17},{18,2},{19,3},{2,18},{3,19},{20,4},{21... | collective-permute-start | bytes 2752520 | tf_op jit(solution)/shard_map/ppermute | solution.py:226
  7.9 1.3 %collective-permute-start.1 = (f32[32,256]{1,0:T(8,128)S(1)}, f32[32,256]{1,0:T(8,128)S(1)}, u32[]{:S(2)}, u32[]{:S(2)}) collective-permute-start(f32[32,256]{1,0:T(8,128)S(1)} %get-tuple-element.14), channel_id=1, source_target_pairs={{1,0},{0,1},{3,2},{2,3},{5,4},{4,5},{7,6},{6,7},{9,8},{8,9},{11,10... | collective-permute-start | bytes 98312 | tf_op jit(solution)/shard_map/ppermute | solution.py:216
  9.2 4.8 %collective-permute-start.4 = (f32[32,256]{1,0:T(8,128)S(1)}, f32[32,256]{1,0:T(8,128)S(1)}, u32[]{:S(2)}, u32[]{:S(2)}) collective-permute-start(f32[32,256]{1,0:T(8,128)S(1)} %add.19), channel_id=1, source_target_pairs={{6,0},{4,2},{2,4},{0,6},{14,8},{12,10},{10,12},{8,14},{7,1},{5,3},... | collective-permute-start | bytes 98312 | tf_op jit(solution)/shard_map/ppermute | solution.py:216
  11.7 3.9 %collective-permute-start.3 = (f32[32,256]{1,0:T(8,128)S(1)}, f32[32,256]{1,0:T(8,128)S(1)}, u32[]{:S(2)}, u32[]{:S(2)}) collective-permute-start(f32[32,256]{1,0:T(8,128)S(1)} %add.19), channel_id=1, source_target_pairs={{4,0},{6,2},{0,4},{2,6},{12,8},{14,10},{8,12},{10,14},{5,1},{7,3},... | collective-permute-start | bytes 98312 | tf_op jit(solution)/shard_map/ppermute | solution.py:216
  12.2 3.9 %collective-permute-start.2 = (f32[32,256]{1,0:T(8,128)S(1)}, f32[32,256]{1,0:T(8,128)S(1)}, u32[]{:S(2)}, u32[]{:S(2)}) collective-permute-start(f32[32,256]{1,0:T(8,128)S(1)} %add.19), channel_id=1, source_target_pairs={{2,0},{0,2},{6,4},{4,6},{10,8},{8,10},{14,12},{12,14},{3,1},{1,3},... | collective-permute-start | bytes 98312 | tf_op jit(solution)/shard_map/ppermute | solution.py:216
  16.1 4.9 %collective-permute-start.5 = (f32[32,256]{1,0:T(8,128)S(1)}, f32[32,256]{1,0:T(8,128)S(1)}, u32[]{:S(2)}, u32[]{:S(2)}) collective-permute-start(f32[32,256]{1,0:T(8,128)S(1)} %add_add_fusion), channel_id=1, source_target_pairs={{8,0},{10,2},{12,4},{14,6},{0,8},{2,10},{4,12},{6,14},{9,1},{11,3}... | collective-permute-start | bytes 98312 | tf_op jit(solution)/shard_map/ppermute | solution.py:216
  21.0 1.2 %collective-permute-start.6 = (bf16[32,256]{1,0:T(8,128)(2,1)S(1)}, bf16[32,256]{1,0:T(8,128)(2,1)S(1)}, u32[]{:S(2)}, u32[]{:S(2)}) collective-permute-start(bf16[32,256]{1,0:T(8,128)(2,1)S(1)} %add_convert_fusion), channel_id=1, source_target_pairs={{1,0},{0,1},{17,16},{16,17},{3,2},{2,3},{19,18},{18,19},{5,4},{4,5... | collective-permute-start | bytes 49160 | tf_op jit(solution)/shard_map/ppermute | solution.py:226
  22.2 4.4 %collective-permute-start.7 = (bf16[2,32,256]{2,1,0:T(8,128)(2,1)S(1)}, bf16[2,32,256]{2,1,0:T(8,128)(2,1)S(1)}, u32[]{:S(2)}, u32[]{:S(2)}) collective-permute-start(bf16[2,32,256]{2,1,0:T(8,128)(2,1)S(1)} %pad_maximum_fusion.refs_2_), channel_id=1, source_target_pairs={{16,0},{17,1},{0,16},{1,17},{18,2},{19,3},{2,18},{3,19},{20,4},{21... | collective-permute-start | bytes 98312 | tf_op jit(solution)/shard_map/ppermute | solution.py:226
  22.8 6.5 %collective-permute-start.8 = (bf16[64,1024]{1,0:T(8,128)(2,1)S(1)}, bf16[64,1024]{1,0:T(8,128)(2,1)S(1)}, u32[]{:S(2)}, u32[]{:S(2)}) collective-permute-start(bf16[64,1024]{1,0:T(8,128)(2,1)S(1)} %get-tuple-element.18.late.refs_0_), channel_id=1, source_target_pairs={{16,0},{17,1},{0,16},{1,17},{18,2},{19,3},{2,18},{3,19},{20,4},{21... | collective-permute-start | bytes 393224 | tf_op jit(solution)/shard_map/ppermute | solution.py:226

commit v18 on v17

--- a/solution.py
+++ b/solution.py
@@ -37,32 +37,29 @@
     return lax.dot_general(left, right, dims, preferred_element_type=jnp.float32)
 
 
-def cut_kernel(rows, begin, fields, early, late, sent):
-    half = begin // 2
-    copies = []
-    for n, at in enumerate(range(0, fields.shape[0], rows)):
-        here = pl.ds(at, rows)
-        for i in range(2):
-            span = pl.ds(i * half, half)
-            copies.append(
-                pltpu.make_async_copy(fields.at[here, span], early.at[here, span], sent.at[n, i])
-            )
-    span = pl.ds(begin, late.shape[1])
-    copies.append(pltpu.make_async_copy(fields.at[:, span], late, sent.at[0, 2]))
-    waited(started(copies))
-
-
-def cut(fields, begin, rows):
+def cut_kernel(begin, fields, early, late, sent):
+    spans = pl.ds(0, begin), pl.ds(begin, late.shape[1])
+    waited(
+        started(
+            [
+                pltpu.make_async_copy(fields.at[:, span], piece, sent.at[i])
+                for i, (span, piece) in enumerate(zip(spans, (early, late)))
+            ]
+        )
+    )
+
+
+def cut(fields, begin):
     hours, cells = fields.shape
     return pl.pallas_call(
-        functools.partial(cut_kernel, rows, begin),
+        functools.partial(cut_kernel, begin),
         out_shape=(
             jax.ShapeDtypeStruct((hours, begin), fields.dtype),
             jax.ShapeDtypeStruct((hours, cells - begin), fields.dtype),
         ),
         in_specs=[ANYWHERE],
         out_specs=(ANYWHERE, ANYWHERE),
-        scratch_shapes=[pltpu.SemaphoreType.DMA((hours // rows, 3))],
+        scratch_shapes=[pltpu.SemaphoreType.DMA((2,))],
         compiler_params=pltpu.CompilerParams(vmem_limit_bytes=52 * 2**20),
         cost_estimate=FREE,
         name="cut",
@@ -121,10 +118,12 @@
     return jnp.concatenate([b[:, pl.ds(begin - at, width)] for b, at in held], axis=0)
 
 
-def rebuilt(weights, held, made, modes, begin, tiles, sent):
+def rebuilt(weights, held, made, modes, begin, tiles, sent, between=list):
     width = made.shape[1] // tiles
     outgoing = []
     for i in range(tiles):
+        if i == tiles - 1:
+            outgoing += between()
         for at in range(i * width, (i + 1) * width, STRIP):
             fields = columns(held, begin + at, STRIP)
             made[:, pl.ds(at, STRIP)] = product(weights, fields, ROWS).astype(made.dtype)
@@ -156,11 +155,13 @@
         jnp.bfloat16
     )
     weights[...] = value
-    outgoing = rebuilt(value, [(b, 0) for b in held], made, modes, 0, tiles, sent)
-    high, low = in_parts(scaled[...])
-    square[...] = product(every, high, FIRST) + product(every, low, FIRST)
-    outgoing += started([pltpu.make_async_copy(square, operator, sent.at[tiles])])
-    waited(outgoing)
+
+    def operate():
+        high, low = in_parts(scaled[...])
+        square[...] = product(every, high, FIRST) + product(every, low, FIRST)
+        return started([pltpu.make_async_copy(square, operator, sent.at[tiles])])
+
+    waited(rebuilt(value, [(b, 0) for b in held], made, modes, 0, tiles, sent, operate))
 
 
 def last_kernel(begin, tiles, weights, *refs):
@@ -234,7 +235,7 @@
     cells = fields.shape[1]
     begin = cells // 8 * 7
 
-    early, late = cut(fields, begin, 16)
+    early, late = cut(fields, begin)
     first = [early] + [moved(early, k, 0) for k in range(1, tm)]
 
     kept, given = project(early, late, eof_basis, 8)

time: 30.5 us -> 30.4 us (level)
  no operation moved by 1% of the time
where the time goes in v18:
time: 30.4 us; the launch traced here: 30.2 us
  starting transfers between devices  11.3 us (37%)
  waiting for transfers between devices  10.2 us (34%)
  Pallas kernels  7.79 us (26%)
  between operations  0.72 us (2%)
    ppermute x5, waiting for transfers between devices, swapped(): return lax.ppermute(value, axis, route)  6.83 us
    ppermute x5, starting transfers between devices, swapped(): return lax.ppermute(value, axis, route)  6.21 us
    ppermute x4, starting transfers between devices, moved(): return lax.ppermute(value, ('tm', 'inner'), route)  5.1 us
    ppermute x4, waiting for transfers between devices, moved(): return lax.ppermute(value, ('tm', 'inner'), route)  3.4 us
    pallas_call x1, Pallas kernels, project(): pl.pallas_call(functools.partial(project_kernel, tiles), out_shape=(half,...  2.79 us
    pallas_call x1, Pallas kernels, rebuild_first(): pl.pallas_call(functools.partial(first_kernel, tiles), out_shape=(jax.Sha...  2.73 us
    pallas_call x1, Pallas kernels, cut(): pl.pallas_call(functools.partial(cut_kernel, begin), out_shape=(jax.Shape...  1.24 us
    pallas_call x1, Pallas kernels, rebuild_last(): pl.pallas_call(functools.partial(last_kernel, begin, tiles), out_shape=ja...  1.03 us
  transfers between devices with their start and end apart: 9, of which 7 were waited for; matrix products, arithmetic and copies ran while one was open for 0% of the time, Pallas kernels for 18%

profile of v18, /device:TPU:0, one launch (start us, length us, event | category | flops | bytes accessed | tf_op | source)
XLA Modules:
  0.0 30.2 jit_solution(774494505025287369)
XLA Ops:
  0.6 0.0 copy-start
  0.6 0.0 copy-start.1
  0.7 1.2 %cut.1 = (bf16[64,7168]{1,0:T(8,128)(2,1)S(1)}, bf16[64,1024]{1,0:T(8,128)(2,1)S(1)}) custom-call(bf16[64,8192]{1,0:T(8,128)(2,1)} %bitcast.7), custom_call_target="tpu_custom_call" | custom-call | tf_op jit(solution)/shard_map/cut/pallas_call | solution.py:54
  1.9 3.0 %collective-permute-start = (bf16[64,7168]{1,0:T(8,128)(2,1)S(1)}, bf16[64,7168]{1,0:T(8,128)(2,1)S(1)}, u32[]{:S(2)}, u32[]{:S(2)}) collective-permute-start(bf16[64,7168]{1,0:T(8,128)(2,1)S(1)} %get-tuple-element.11.early.refs_0_), channel_id=1, source_target_pairs={{16,0},{17,1},{0,16},{1,17},{18,2},{19,3},{2,18},{3,19},{20,4},{21... | collective-permute-start | bytes 2752520 | tf_op jit(solution)/shard_map/ppermute | solution.py:227
  4.9 2.8 %project.1 = (f32[32,256]{1,0:T(8,128)S(1)}, f32[32,256]{1,0:T(8,128)S(1)}) custom-call(bf16[64,7168]{1,0:T(8,128)(2,1)S(1)} %get-tuple-element.11.early.refs_0_, bf16[64,1024]{1,0:T(8,128)(2,1)S(1)} %get-tuple-element.18.late.refs_0_, bf16[8192,256]{1,0:T(8,128)(2,1)} %basis.1), custom_call_target="tpu_custom_call" | custom-call | tf_op jit(solution)/shard_map/project/pallas_call | solution.py:96
  7.7 0.1 collective-permute-start.1
  7.8 1.2 %collective-permute-done.1 = f32[32,256]{1,0:T(8,128)S(1)} collective-permute-done((f32[32,256]{1,0:T(8,128)S(1)}, f32[32,256]{1,0:T(8,128)S(1)}, u32[]{:S(2)}, u32[]{:S(2)}) %collective-permute-start.1) | collective-permute-done | bytes 32800 | tf_op jit(solution)/shard_map/ppermute | solution.py:217
  9.0 2.5 %collective-permute-start.4 = (f32[32,256]{1,0:T(8,128)S(1)}, f32[32,256]{1,0:T(8,128)S(1)}, u32[]{:S(2)}, u32[]{:S(2)}) collective-permute-start(f32[32,256]{1,0:T(8,128)S(1)} %add.19), channel_id=1, source_target_pairs={{6,0},{4,2},{2,4},{0,6},{14,8},{12,10},{10,12},{8,14},{7,1},{5,3},... | collective-permute-start | bytes 98312 | tf_op jit(solution)/shard_map/ppermute | solution.py:217
  11.5 0.5 %collective-permute-start.3 = (f32[32,256]{1,0:T(8,128)S(1)}, f32[32,256]{1,0:T(8,128)S(1)}, u32[]{:S(2)}, u32[]{:S(2)}) collective-permute-start(f32[32,256]{1,0:T(8,128)S(1)} %add.19), channel_id=1, source_target_pairs={{4,0},{6,2},{0,4},{2,6},{12,8},{14,10},{8,12},{10,14},{5,1},{7,3},... | collective-permute-start | bytes 98312 | tf_op jit(solution)/shard_map/ppermute | solution.py:217
  12.0 0.5 %collective-permute-start.2 = (f32[32,256]{1,0:T(8,128)S(1)}, f32[32,256]{1,0:T(8,128)S(1)}, u32[]{:S(2)}, u32[]{:S(2)}) collective-permute-start(f32[32,256]{1,0:T(8,128)S(1)} %add.19), channel_id=1, source_target_pairs={{2,0},{0,2},{6,4},{4,6},{10,8},{8,10},{14,12},{12,14},{3,1},{1,3},... | collective-permute-start | bytes 98312 | tf_op jit(solution)/shard_map/ppermute | solution.py:217
  12.5 1.3 %collective-permute-done.4 = f32[32,256]{1,0:T(8,128)S(1)} collective-permute-done((f32[32,256]{1,0:T(8,128)S(1)}, f32[32,256]{1,0:T(8,128)S(1)}, u32[]{:S(2)}, u32[]{:S(2)}) %collective-permute-start.4) | collective-permute-done | bytes 32800 | tf_op jit(solution)/shard_map/ppermute | solution.py:217
  13.8 1.6 %collective-permute-done.3 = f32[32,256]{1,0:T(8,128)S(1)} collective-permute-done((f32[32,256]{1,0:T(8,128)S(1)}, f32[32,256]{1,0:T(8,128)S(1)}, u32[]{:S(2)}, u32[]{:S(2)}) %collective-permute-start.3) | collective-permute-done | bytes 32800 | tf_op jit(solution)/shard_map/ppermute | solution.py:217
  15.4 0.5 %collective-permute-done.2 = f32[32,256]{1,0:T(8,128)S(1)} collective-permute-done((f32[32,256]{1,0:T(8,128)S(1)}, f32[32,256]{1,0:T(8,128)S(1)}, u32[]{:S(2)}, u32[]{:S(2)}) %collective-permute-start.2) | collective-permute-done | bytes 32800 | tf_op jit(solution)/shard_map/ppermute | solution.py:217
  15.9 2.6 %collective-permute-start.5 = (f32[32,256]{1,0:T(8,128)S(1)}, f32[32,256]{1,0:T(8,128)S(1)}, u32[]{:S(2)}, u32[]{:S(2)}) collective-permute-start(f32[32,256]{1,0:T(8,128)S(1)} %add_add_fusion), channel_id=1, source_target_pairs={{8,0},{10,2},{12,4},{14,6},{0,8},{2,10},{4,12},{6,14},{9,1},{11,3}... | collective-permute-start | bytes 98312 | tf_op jit(solution)/shard_map/ppermute | solution.py:217
  18.5 2.2 %collective-permute-done.5 = f32[32,256]{1,0:T(8,128)S(1)} collective-permute-done((f32[32,256]{1,0:T(8,128)S(1)}, f32[32,256]{1,0:T(8,128)S(1)}, u32[]{:S(2)}, u32[]{:S(2)}) %collective-permute-start.5) | collective-permute-done | bytes 32800 | tf_op jit(solution)/shard_map/ppermute | solution.py:217
  20.8 0.0 collective-permute-start.6
  20.8 1.2 %collective-permute-done.6 = bf16[32,256]{1,0:T(8,128)(2,1)S(1)} collective-permute-done((bf16[32,256]{1,0:T(8,128)(2,1)S(1)}, bf16[32,256]{1,0:T(8,128)(2,1)S(1)}, u32[]{:S(2)}, u32[]{:S(2)}) %collective-permute-start.6) | collective-permute-done | bytes 16416 | tf_op jit(solution)/shard_map/ppermute | solution.py:227
  22.0 0.5 %collective-permute-start.7 = (bf16[2,32,256]{2,1,0:T(8,128)(2,1)S(1)}, bf16[2,32,256]{2,1,0:T(8,128)(2,1)S(1)}, u32[]{:S(2)}, u32[]{:S(2)}) collective-permute-start(bf16[2,32,256]{2,1,0:T(8,128)(2,1)S(1)} %pad_maximum_fusion.refs_2_), channel_id=1, source_target_pairs={{16,0},{17,1},{0,16},{1,17},{18,2},{19,3},{2,18},{3,19},{20,4},{21... | collective-permute-start | bytes 98312 | tf_op jit(solution)/shard_map/ppermute | solution.py:227
  22.5 0.0 copy-done
  22.5 0.1 copy.8
  22.6 1.6 %collective-permute-start.8 = (bf16[64,1024]{1,0:T(8,128)(2,1)S(1)}, bf16[64,1024]{1,0:T(8,128)(2,1)S(1)}, u32[]{:S(2)}, u32[]{:S(2)}) collective-permute-start(bf16[64,1024]{1,0:T(8,128)(2,1)S(1)} %get-tuple-element.18.late.refs_0_), channel_id=1, source_target_pairs={{16,0},{17,1},{0,16},{1,17},{18,2},{19,3},{2,18},{3,19},{20,4},{21... | collective-permute-start | bytes 393224 | tf_op jit(solution)/shard_map/ppermute | solution.py:227
  24.2 2.2 %collective-permute-done.7.refs_3_ = bf16[2,32,256]{2,1,0:T(8,128)(2,1)S(1)} collective-permute-done((bf16[2,32,256]{2,1,0:T(8,128)(2,1)S(1)}, bf16[2,32,256]{2,1,0:T(8,128)(2,1)S(1)}, u32[]{:S(2)}, u32[]{:S(2)}) %collective-permute-start.7) | collective-permute-done | bytes 32800 | tf_op jit(solution)/shard_map/ppermute | solution.py:227
  26.4 0.0 collective-permute-done.refs_1_
  26.4 0.0 copy-done.1
  26.4 2.7 %rebuild_first.1 = (f32[256,256]{1,0:T(8,128)}, bf16[256,8192]{1,0:T(8,128)(2,1)}, bf16[256,128]{1,0:T(8,128)(2,1)S(1)}) custom-call(f32[1,256]{1,0:T(1,128)S(1)} %bitcast.6, bf16[256,256]{1,0:T(8,128)(2,1)S(1)} %bitcast.5, bf16[64,7168]{1,0:T(8,128)(2,1)S(1)} %get-tuple-element.11.early.refs_0_, bf16[64,7168]{1,0:T(8,128)(2,1)S(1)} %collective-permute-done.refs_1_, ...), custom_call_target="tpu_custom_call" | custom-call | flops 3000000000 | tf_op jit(solution)/shard_map/rebuild_first/pallas_call | solution.py:176
  29.2 0.0 collective-permute-done.8.refs_1_
  29.2 1.0 %rebuild_last.1 = bf16[256,8192]{1,0:T(8,128)(2,1)} custom-call(bf16[256,128]{1,0:T(8,128)(2,1)S(1)} %get-tuple-element.17.weights, bf16[64,1024]{1,0:T(8,128)(2,1)S(1)} %get-tuple-element.18.late.refs_0_, bf16[64,1024]{1,0:T(8,128)(2,1)S(1)} %collective-permute-done.8.refs_1_, ...), custom_call_target="tpu_custom_call", output_to_operand_aliasing={{}: (3, {})} | custom-call | tf_op jit(solution)/shard_map/rebuild_last/pallas_call | solution.py:199
  (5 shorter events, 0.0 us)
Async XLA Ops:
  0.6 21.9 %copy-start = (bf16[256,512]{1,0:T(8,128)(2,1)S(1)}, bf16[256,512]{1,0:T(8,128)(2,1)}, u32[]{:S(2)}) copy-start(bf16[256,512]{1,0:T(8,128)(2,1)} %param.7) | copy-start | bytes 786436
  0.6 25.8 %copy-start.1 = (f32[256]{0:T(256)S(1)}, f32[256]{0:T(256)}, u32[]{:S(2)}) copy-start(f32[256]{0:T(256)} %param.6) | copy-start | bytes 3076
  1.9 24.5 %collective-permute-start = (bf16[64,7168]{1,0:T(8,128)(2,1)S(1)}, bf16[64,7168]{1,0:T(8,128)(2,1)S(1)}, u32[]{:S(2)}, u32[]{:S(2)}) collective-permute-start(bf16[64,7168]{1,0:T(8,128)(2,1)S(1)} %get-tuple-element.11.early.refs_0_), channel_id=1, source_target_pairs={{16,0},{17,1},{0,16},{1,17},{18,2},{19,3},{2,18},{3,19},{20,4},{21... | collective-permute-start | bytes 2752520 | tf_op jit(solution)/shard_map/ppermute | solution.py:227
  7.7 1.3 %collective-permute-start.1 = (f32[32,256]{1,0:T(8,128)S(1)}, f32[32,256]{1,0:T(8,128)S(1)}, u32[]{:S(2)}, u32[]{:S(2)}) collective-permute-start(f32[32,256]{1,0:T(8,128)S(1)} %get-tuple-element.14), channel_id=1, source_target_pairs={{1,0},{0,1},{3,2},{2,3},{5,4},{4,5},{7,6},{6,7},{9,8},{8,9},{11,10... | collective-permute-start | bytes 98312 | tf_op jit(solution)/shard_map/ppermute | solution.py:217
  9.0 4.8 %collective-permute-start.4 = (f32[32,256]{1,0:T(8,128)S(1)}, f32[32,256]{1,0:T(8,128)S(1)}, u32[]{:S(2)}, u32[]{:S(2)}) collective-permute-start(f32[32,256]{1,0:T(8,128)S(1)} %add.19), channel_id=1, source_target_pairs={{6,0},{4,2},{2,4},{0,6},{14,8},{12,10},{10,12},{8,14},{7,1},{5,3},... | collective-permute-start | bytes 98312 | tf_op jit(solution)/shard_map/ppermute | solution.py:217
  11.5 3.9 %collective-permute-start.3 = (f32[32,256]{1,0:T(8,128)S(1)}, f32[32,256]{1,0:T(8,128)S(1)}, u32[]{:S(2)}, u32[]{:S(2)}) collective-permute-start(f32[32,256]{1,0:T(8,128)S(1)} %add.19), channel_id=1, source_target_pairs={{4,0},{6,2},{0,4},{2,6},{12,8},{14,10},{8,12},{10,14},{5,1},{7,3},... | collective-permute-start | bytes 98312 | tf_op jit(solution)/shard_map/ppermute | solution.py:217
  12.0 3.9 %collective-permute-start.2 = (f32[32,256]{1,0:T(8,128)S(1)}, f32[32,256]{1,0:T(8,128)S(1)}, u32[]{:S(2)}, u32[]{:S(2)}) collective-permute-start(f32[32,256]{1,0:T(8,128)S(1)} %add.19), channel_id=1, source_target_pairs={{2,0},{0,2},{6,4},{4,6},{10,8},{8,10},{14,12},{12,14},{3,1},{1,3},... | collective-permute-start | bytes 98312 | tf_op jit(solution)/shard_map/ppermute | solution.py:217
  15.9 4.9 %collective-permute-start.5 = (f32[32,256]{1,0:T(8,128)S(1)}, f32[32,256]{1,0:T(8,128)S(1)}, u32[]{:S(2)}, u32[]{:S(2)}) collective-permute-start(f32[32,256]{1,0:T(8,128)S(1)} %add_add_fusion), channel_id=1, source_target_pairs={{8,0},{10,2},{12,4},{14,6},{0,8},{2,10},{4,12},{6,14},{9,1},{11,3}... | collective-permute-start | bytes 98312 | tf_op jit(solution)/shard_map/ppermute | solution.py:217
  20.8 1.2 %collective-permute-start.6 = (bf16[32,256]{1,0:T(8,128)(2,1)S(1)}, bf16[32,256]{1,0:T(8,128)(2,1)S(1)}, u32[]{:S(2)}, u32[]{:S(2)}) collective-permute-start(bf16[32,256]{1,0:T(8,128)(2,1)S(1)} %add_convert_fusion), channel_id=1, source_target_pairs={{1,0},{0,1},{17,16},{16,17},{3,2},{2,3},{19,18},{18,19},{5,4},{4,5... | collective-permute-start | bytes 49160 | tf_op jit(solution)/shard_map/ppermute | solution.py:227
  22.0 4.4 %collective-permute-start.7 = (bf16[2,32,256]{2,1,0:T(8,128)(2,1)S(1)}, bf16[2,32,256]{2,1,0:T(8,128)(2,1)S(1)}, u32[]{:S(2)}, u32[]{:S(2)}) collective-permute-start(bf16[2,32,256]{2,1,0:T(8,128)(2,1)S(1)} %pad_maximum_fusion.refs_2_), channel_id=1, source_target_pairs={{16,0},{17,1},{0,16},{1,17},{18,2},{19,3},{2,18},{3,19},{20,4},{21... | collective-permute-start | bytes 98312 | tf_op jit(solution)/shard_map/ppermute | solution.py:227
  22.6 6.5 %collective-permute-start.8 = (bf16[64,1024]{1,0:T(8,128)(2,1)S(1)}, bf16[64,1024]{1,0:T(8,128)(2,1)S(1)}, u32[]{:S(2)}, u32[]{:S(2)}) collective-permute-start(bf16[64,1024]{1,0:T(8,128)(2,1)S(1)} %get-tuple-element.18.late.refs_0_), channel_id=1, source_target_pairs={{16,0},{17,1},{0,16},{1,17},{18,2},{19,3},{2,18},{3,19},{20,4},{21... | collective-permute-start | bytes 393224 | tf_op jit(solution)/shard_map/ppermute | solution.py:227

commit v19 on v18

--- a/solution.py
+++ b/solution.py
@@ -119,17 +119,18 @@
 
 
 def rebuilt(weights, held, made, modes, begin, tiles, sent, between=list):
-    width = made.shape[1] // tiles
+    strips = made.shape[1] // STRIP
+    edges = [strips * i // tiles * STRIP for i in range(tiles + 1)]
     outgoing = []
     for i in range(tiles):
         if i == tiles - 1:
             outgoing += between()
-        for at in range(i * width, (i + 1) * width, STRIP):
+        for at in range(edges[i], edges[i + 1], STRIP):
             fields = columns(held, begin + at, STRIP)
             made[:, pl.ds(at, STRIP)] = product(weights, fields, ROWS).astype(made.dtype)
-        target = modes.at[:, pl.ds(begin + i * width, width)]
-        copy = pltpu.make_async_copy(made.at[:, pl.ds(i * width, width)], target, sent.at[i])
-        outgoing += started([copy])
+        width = edges[i + 1] - edges[i]
+        source, target = made.at[:, pl.ds(edges[i], width)], pl.ds(begin + edges[i], width)
+        outgoing += started([pltpu.make_async_copy(source, modes.at[:, target], sent.at[i])])
     return outgoing
 
 
@@ -233,12 +234,12 @@
     fields = snapshots.T
 
     cells = fields.shape[1]
-    begin = cells // 8 * 7
+    begin = cells // 16 * 13
 
     early, late = cut(fields, begin)
     first = [early] + [moved(early, k, 0) for k in range(1, tm)]
 
-    kept, given = project(early, late, eof_basis, 8)
+    kept, given = project(early, late, eof_basis, 16)
     mine = kept + swapped(given, "inner", 1)
     bit = 1
     while bit < outer:

time: 30.4 us -> 31.1 us (1.023)
  waiting for transfers between devices: 10.2 us -> 10.9 us
    ppermute x4, waiting for transfers between devices: 3.4 us -> 4.08 us  [moved(): return lax.ppermute(value, ('tm', 'inner'), route)]
  transfers between devices with their start and end apart: 9 -> 9, of which waited for: 7 -> 8; matrix products, arithmetic and copies ran while one was open for 0% -> 0% of each run, Pallas kernels for 18% -> 18%
where the time goes in v19:
time: 31.1 us; the launch traced here: 30.9 us
  starting transfers between devices  11.3 us (36%)
  waiting for transfers between devices  10.9 us (35%)
  Pallas kernels  7.85 us (25%)
  between operations  0.71 us (2%)
    ppermute x5, waiting for transfers between devices, swapped(): return lax.ppermute(value, axis, route)  6.83 us
    ppermute x5, starting transfers between devices, swapped(): return lax.ppermute(value, axis, route)  6.21 us
    ppermute x4, starting transfers between devices, moved(): return lax.ppermute(value, ('tm', 'inner'), route)  5.1 us
    ppermute x4, waiting for transfers between devices, moved(): return lax.ppermute(value, ('tm', 'inner'), route)  4.08 us
    pallas_call x1, Pallas kernels, project(): pl.pallas_call(functools.partial(project_kernel, tiles), out_shape=(half,...  2.81 us
    pallas_call x1, Pallas kernels, rebuild_first(): pl.pallas_call(functools.partial(first_kernel, tiles), out_shape=(jax.Sha...  2.63 us
    pallas_call x1, Pallas kernels, cut(): pl.pallas_call(functools.partial(cut_kernel, begin), out_shape=(jax.Shape...  1.24 us
    pallas_call x1, Pallas kernels, rebuild_last(): pl.pallas_call(functools.partial(last_kernel, begin, tiles), out_shape=ja...  1.17 us
  transfers between devices with their start and end apart: 9, of which 8 were waited for; matrix products, arithmetic and copies ran while one was open for 0% of the time, Pallas kernels for 18%

profile of v19, /device:TPU:0, one launch (start us, length us, event | category | flops | bytes accessed | tf_op | source)
XLA Modules:
  0.0 30.9 jit_solution(1746416497997421149)
XLA Ops:
  0.6 0.0 copy-start
  0.6 0.0 copy-start.1
  0.7 1.2 %cut.1 = (bf16[64,6656]{1,0:T(8,128)(2,1)S(1)}, bf16[64,1536]{1,0:T(8,128)(2,1)S(1)}) custom-call(bf16[64,8192]{1,0:T(8,128)(2,1)} %bitcast.7), custom_call_target="tpu_custom_call" | custom-call | tf_op jit(solution)/shard_map/cut/pallas_call | solution.py:54
  1.9 3.0 %collective-permute-start = (bf16[64,6656]{1,0:T(8,128)(2,1)S(1)}, bf16[64,6656]{1,0:T(8,128)(2,1)S(1)}, u32[]{:S(2)}, u32[]{:S(2)}) collective-permute-start(bf16[64,6656]{1,0:T(8,128)(2,1)S(1)} %get-tuple-element.11.early.refs_0_), channel_id=1, source_target_pairs={{16,0},{17,1},{0,16},{1,17},{18,2},{19,3},{2,18},{3,19},{20,4},{21... | collective-permute-start | bytes 2555912 | tf_op jit(solution)/shard_map/ppermute | solution.py:228
  4.9 2.8 %project.1 = (f32[32,256]{1,0:T(8,128)S(1)}, f32[32,256]{1,0:T(8,128)S(1)}) custom-call(bf16[64,6656]{1,0:T(8,128)(2,1)S(1)} %get-tuple-element.11.early.refs_0_, bf16[64,1536]{1,0:T(8,128)(2,1)S(1)} %get-tuple-element.18.late.refs_0_, bf16[8192,256]{1,0:T(8,128)(2,1)} %basis.1), custom_call_target="tpu_custom_call" | custom-call | tf_op jit(solution)/shard_map/project/pallas_call | solution.py:96
  7.7 0.1 collective-permute-start.1
  7.8 1.2 %collective-permute-done.1 = f32[32,256]{1,0:T(8,128)S(1)} collective-permute-done((f32[32,256]{1,0:T(8,128)S(1)}, f32[32,256]{1,0:T(8,128)S(1)}, u32[]{:S(2)}, u32[]{:S(2)}) %collective-permute-start.1) | collective-permute-done | bytes 32800 | tf_op jit(solution)/shard_map/ppermute | solution.py:218
  9.0 2.5 %collective-permute-start.4 = (f32[32,256]{1,0:T(8,128)S(1)}, f32[32,256]{1,0:T(8,128)S(1)}, u32[]{:S(2)}, u32[]{:S(2)}) collective-permute-start(f32[32,256]{1,0:T(8,128)S(1)} %add.19), channel_id=1, source_target_pairs={{6,0},{4,2},{2,4},{0,6},{14,8},{12,10},{10,12},{8,14},{7,1},{5,3},... | collective-permute-start | bytes 98312 | tf_op jit(solution)/shard_map/ppermute | solution.py:218
  11.5 0.5 %collective-permute-start.3 = (f32[32,256]{1,0:T(8,128)S(1)}, f32[32,256]{1,0:T(8,128)S(1)}, u32[]{:S(2)}, u32[]{:S(2)}) collective-permute-start(f32[32,256]{1,0:T(8,128)S(1)} %add.19), channel_id=1, source_target_pairs={{4,0},{6,2},{0,4},{2,6},{12,8},{14,10},{8,12},{10,14},{5,1},{7,3},... | collective-permute-start | bytes 98312 | tf_op jit(solution)/shard_map/ppermute | solution.py:218
  12.0 0.5 %collective-permute-start.2 = (f32[32,256]{1,0:T(8,128)S(1)}, f32[32,256]{1,0:T(8,128)S(1)}, u32[]{:S(2)}, u32[]{:S(2)}) collective-permute-start(f32[32,256]{1,0:T(8,128)S(1)} %add.19), channel_id=1, source_target_pairs={{2,0},{0,2},{6,4},{4,6},{10,8},{8,10},{14,12},{12,14},{3,1},{1,3},... | collective-permute-start | bytes 98312 | tf_op jit(solution)/shard_map/ppermute | solution.py:218
  12.5 1.3 %collective-permute-done.4 = f32[32,256]{1,0:T(8,128)S(1)} collective-permute-done((f32[32,256]{1,0:T(8,128)S(1)}, f32[32,256]{1,0:T(8,128)S(1)}, u32[]{:S(2)}, u32[]{:S(2)}) %collective-permute-start.4) | collective-permute-done | bytes 32800 | tf_op jit(solution)/shard_map/ppermute | solution.py:218
  13.8 1.6 %collective-permute-done.3 = f32[32,256]{1,0:T(8,128)S(1)} collective-permute-done((f32[32,256]{1,0:T(8,128)S(1)}, f32[32,256]{1,0:T(8,128)S(1)}, u32[]{:S(2)}, u32[]{:S(2)}) %collective-permute-start.3) | collective-permute-done | bytes 32800 | tf_op jit(solution)/shard_map/ppermute | solution.py:218
  15.5 0.5 %collective-permute-done.2 = f32[32,256]{1,0:T(8,128)S(1)} collective-permute-done((f32[32,256]{1,0:T(8,128)S(1)}, f32[32,256]{1,0:T(8,128)S(1)}, u32[]{:S(2)}, u32[]{:S(2)}) %collective-permute-start.2) | collective-permute-done | bytes 32800 | tf_op jit(solution)/shard_map/ppermute | solution.py:218
  15.9 2.7 %collective-permute-start.5 = (f32[32,256]{1,0:T(8,128)S(1)}, f32[32,256]{1,0:T(8,128)S(1)}, u32[]{:S(2)}, u32[]{:S(2)}) collective-permute-start(f32[32,256]{1,0:T(8,128)S(1)} %add_add_fusion), channel_id=1, source_target_pairs={{8,0},{10,2},{12,4},{14,6},{0,8},{2,10},{4,12},{6,14},{9,1},{11,3}... | collective-permute-start | bytes 98312 | tf_op jit(solution)/shard_map/ppermute | solution.py:218
  18.6 2.2 %collective-permute-done.5 = f32[32,256]{1,0:T(8,128)S(1)} collective-permute-done((f32[32,256]{1,0:T(8,128)S(1)}, f32[32,256]{1,0:T(8,128)S(1)}, u32[]{:S(2)}, u32[]{:S(2)}) %collective-permute-start.5) | collective-permute-done | bytes 32800 | tf_op jit(solution)/shard_map/ppermute | solution.py:218
  20.8 0.0 collective-permute-start.6
  20.8 1.2 %collective-permute-done.6 = bf16[32,256]{1,0:T(8,128)(2,1)S(1)} collective-permute-done((bf16[32,256]{1,0:T(8,128)(2,1)S(1)}, bf16[32,256]{1,0:T(8,128)(2,1)S(1)}, u32[]{:S(2)}, u32[]{:S(2)}) %collective-permute-start.6) | collective-permute-done | bytes 16416 | tf_op jit(solution)/shard_map/ppermute | solution.py:228
  22.0 0.5 %collective-permute-start.7 = (bf16[2,32,256]{2,1,0:T(8,128)(2,1)S(1)}, bf16[2,32,256]{2,1,0:T(8,128)(2,1)S(1)}, u32[]{:S(2)}, u32[]{:S(2)}) collective-permute-start(bf16[2,32,256]{2,1,0:T(8,128)(2,1)S(1)} %pad_maximum_fusion.refs_2_), channel_id=1, source_target_pairs={{16,0},{17,1},{0,16},{1,17},{18,2},{19,3},{2,18},{3,19},{20,4},{21... | collective-permute-start | bytes 98312 | tf_op jit(solution)/shard_map/ppermute | solution.py:228
  22.5 0.0 copy-done
  22.5 0.1 copy.8
  22.7 1.6 %collective-permute-start.8 = (bf16[64,1536]{1,0:T(8,128)(2,1)S(1)}, bf16[64,1536]{1,0:T(8,128)(2,1)S(1)}, u32[]{:S(2)}, u32[]{:S(2)}) collective-permute-start(bf16[64,1536]{1,0:T(8,128)(2,1)S(1)} %get-tuple-element.18.late.refs_0_), channel_id=1, source_target_pairs={{16,0},{17,1},{0,16},{1,17},{18,2},{19,3},{2,18},{3,19},{20,4},{21... | collective-permute-start | bytes 589832 | tf_op jit(solution)/shard_map/ppermute | solution.py:228
  24.2 2.0 %collective-permute-done.7.refs_3_ = bf16[2,32,256]{2,1,0:T(8,128)(2,1)S(1)} collective-permute-done((bf16[2,32,256]{2,1,0:T(8,128)(2,1)S(1)}, bf16[2,32,256]{2,1,0:T(8,128)(2,1)S(1)}, u32[]{:S(2)}, u32[]{:S(2)}) %collective-permute-start.7) | collective-permute-done | bytes 32800 | tf_op jit(solution)/shard_map/ppermute | solution.py:228
  26.2 0.0 collective-permute-done.refs_1_
  26.2 0.0 copy-done.1
  26.2 2.6 %rebuild_first.1 = (f32[256,256]{1,0:T(8,128)}, bf16[256,8192]{1,0:T(8,128)(2,1)}, bf16[256,128]{1,0:T(8,128)(2,1)S(1)}) custom-call(f32[1,256]{1,0:T(1,128)S(1)} %bitcast.6, bf16[256,256]{1,0:T(8,128)(2,1)S(1)} %bitcast.5, bf16[64,6656]{1,0:T(8,128)(2,1)S(1)} %get-tuple-element.11.early.refs_0_, bf16[64,6656]{1,0:T(8,128)(2,1)S(1)} %collective-permute-done.refs_1_, ...), custom_call_target="tpu_custom_call" | custom-call | flops 3000000000 | tf_op jit(solution)/shard_map/rebuild_first/pallas_call | solution.py:177
  28.8 1.0 %collective-permute-done.8.refs_1_ = bf16[64,1536]{1,0:T(8,128)(2,1)S(1)} collective-permute-done((bf16[64,1536]{1,0:T(8,128)(2,1)S(1)}, bf16[64,1536]{1,0:T(8,128)(2,1)S(1)}, u32[]{:S(2)}, u32[]{:S(2)}) %collective-permute-start.8) | collective-permute-done | bytes 196640 | tf_op jit(solution)/shard_map/ppermute | solution.py:228
  29.8 1.2 %rebuild_last.1 = bf16[256,8192]{1,0:T(8,128)(2,1)} custom-call(bf16[256,128]{1,0:T(8,128)(2,1)S(1)} %get-tuple-element.17.weights, bf16[64,1536]{1,0:T(8,128)(2,1)S(1)} %get-tuple-element.18.late.refs_0_, bf16[64,1536]{1,0:T(8,128)(2,1)S(1)} %collective-permute-done.8.refs_1_, ...), custom_call_target="tpu_custom_call", output_to_operand_aliasing={{}: (3, {})} | custom-call | tf_op jit(solution)/shard_map/rebuild_last/pallas_call | solution.py:200
  (5 shorter events, 0.0 us)
Async XLA Ops:
  0.6 21.9 %copy-start = (bf16[256,512]{1,0:T(8,128)(2,1)S(1)}, bf16[256,512]{1,0:T(8,128)(2,1)}, u32[]{:S(2)}) copy-start(bf16[256,512]{1,0:T(8,128)(2,1)} %param.7) | copy-start | bytes 786436
  0.6 25.5 %copy-start.1 = (f32[256]{0:T(256)S(1)}, f32[256]{0:T(256)}, u32[]{:S(2)}) copy-start(f32[256]{0:T(256)} %param.6) | copy-start | bytes 3076
  1.9 24.3 %collective-permute-start = (bf16[64,6656]{1,0:T(8,128)(2,1)S(1)}, bf16[64,6656]{1,0:T(8,128)(2,1)S(1)}, u32[]{:S(2)}, u32[]{:S(2)}) collective-permute-start(bf16[64,6656]{1,0:T(8,128)(2,1)S(1)} %get-tuple-element.11.early.refs_0_), channel_id=1, source_target_pairs={{16,0},{17,1},{0,16},{1,17},{18,2},{19,3},{2,18},{3,19},{20,4},{21... | collective-permute-start | bytes 2555912 | tf_op jit(solution)/shard_map/ppermute | solution.py:228
  7.7 1.3 %collective-permute-start.1 = (f32[32,256]{1,0:T(8,128)S(1)}, f32[32,256]{1,0:T(8,128)S(1)}, u32[]{:S(2)}, u32[]{:S(2)}) collective-permute-start(f32[32,256]{1,0:T(8,128)S(1)} %get-tuple-element.14), channel_id=1, source_target_pairs={{1,0},{0,1},{3,2},{2,3},{5,4},{4,5},{7,6},{6,7},{9,8},{8,9},{11,10... | collective-permute-start | bytes 98312 | tf_op jit(solution)/shard_map/ppermute | solution.py:218
  9.0 4.8 %collective-permute-start.4 = (f32[32,256]{1,0:T(8,128)S(1)}, f32[32,256]{1,0:T(8,128)S(1)}, u32[]{:S(2)}, u32[]{:S(2)}) collective-permute-start(f32[32,256]{1,0:T(8,128)S(1)} %add.19), channel_id=1, source_target_pairs={{6,0},{4,2},{2,4},{0,6},{14,8},{12,10},{10,12},{8,14},{7,1},{5,3},... | collective-permute-start | bytes 98312 | tf_op jit(solution)/shard_map/ppermute | solution.py:218
  11.5 3.9 %collective-permute-start.3 = (f32[32,256]{1,0:T(8,128)S(1)}, f32[32,256]{1,0:T(8,128)S(1)}, u32[]{:S(2)}, u32[]{:S(2)}) collective-permute-start(f32[32,256]{1,0:T(8,128)S(1)} %add.19), channel_id=1, source_target_pairs={{4,0},{6,2},{0,4},{2,6},{12,8},{14,10},{8,12},{10,14},{5,1},{7,3},... | collective-permute-start | bytes 98312 | tf_op jit(solution)/shard_map/ppermute | solution.py:218
  12.0 3.9 %collective-permute-start.2 = (f32[32,256]{1,0:T(8,128)S(1)}, f32[32,256]{1,0:T(8,128)S(1)}, u32[]{:S(2)}, u32[]{:S(2)}) collective-permute-start(f32[32,256]{1,0:T(8,128)S(1)} %add.19), channel_id=1, source_target_pairs={{2,0},{0,2},{6,4},{4,6},{10,8},{8,10},{14,12},{12,14},{3,1},{1,3},... | collective-permute-start | bytes 98312 | tf_op jit(solution)/shard_map/ppermute | solution.py:218
  15.9 4.9 %collective-permute-start.5 = (f32[32,256]{1,0:T(8,128)S(1)}, f32[32,256]{1,0:T(8,128)S(1)}, u32[]{:S(2)}, u32[]{:S(2)}) collective-permute-start(f32[32,256]{1,0:T(8,128)S(1)} %add_add_fusion), channel_id=1, source_target_pairs={{8,0},{10,2},{12,4},{14,6},{0,8},{2,10},{4,12},{6,14},{9,1},{11,3}... | collective-permute-start | bytes 98312 | tf_op jit(solution)/shard_map/ppermute | solution.py:218
  20.8 1.2 %collective-permute-start.6 = (bf16[32,256]{1,0:T(8,128)(2,1)S(1)}, bf16[32,256]{1,0:T(8,128)(2,1)S(1)}, u32[]{:S(2)}, u32[]{:S(2)}) collective-permute-start(bf16[32,256]{1,0:T(8,128)(2,1)S(1)} %add_convert_fusion), channel_id=1, source_target_pairs={{1,0},{0,1},{17,16},{16,17},{3,2},{2,3},{19,18},{18,19},{5,4},{4,5... | collective-permute-start | bytes 49160 | tf_op jit(solution)/shard_map/ppermute | solution.py:228
  22.0 4.2 %collective-permute-start.7 = (bf16[2,32,256]{2,1,0:T(8,128)(2,1)S(1)}, bf16[2,32,256]{2,1,0:T(8,128)(2,1)S(1)}, u32[]{:S(2)}, u32[]{:S(2)}) collective-permute-start(bf16[2,32,256]{2,1,0:T(8,128)(2,1)S(1)} %pad_maximum_fusion.refs_2_), channel_id=1, source_target_pairs={{16,0},{17,1},{0,16},{1,17},{18,2},{19,3},{2,18},{3,19},{20,4},{21... | collective-permute-start | bytes 98312 | tf_op jit(solution)/shard_map/ppermute | solution.py:228
  22.7 7.1 %collective-permute-start.8 = (bf16[64,1536]{1,0:T(8,128)(2,1)S(1)}, bf16[64,1536]{1,0:T(8,128)(2,1)S(1)}, u32[]{:S(2)}, u32[]{:S(2)}) collective-permute-start(bf16[64,1536]{1,0:T(8,128)(2,1)S(1)} %get-tuple-element.18.late.refs_0_), channel_id=1, source_target_pairs={{16,0},{17,1},{0,16},{1,17},{18,2},{19,3},{2,18},{3,19},{20,4},{21... | collective-permute-start | bytes 589832 | tf_op jit(solution)/shard_map/ppermute | solution.py:228

commit v20 on v19

--- a/solution.py
+++ b/solution.py
@@ -12,7 +12,7 @@
 LAST = (((1,), (1,)), ((), ()))
 STRIP = 256
 FREE = pl.CostEstimate(flops=0, bytes_accessed=0, transcendentals=0)
-LONG = pl.CostEstimate(flops=3 * 10**9, bytes_accessed=0, transcendentals=0)
+LONG = pl.CostEstimate(flops=2 * 10**9, bytes_accessed=0, transcendentals=0)
 ANYWHERE = pl.BlockSpec(memory_space=pl.ANY)
 IN_VMEM = pl.BlockSpec(memory_space=pltpu.VMEM)
 
@@ -135,17 +135,16 @@
 
 
 def first_kernel(tiles, energy, vectors, *refs):
-    count = (len(refs) - 8) // 2
-    held, coeffs, refs = refs[:count], refs[count : 2 * count], refs[2 * count :]
+    count = (len(refs) - 8) // 3
+    held, coeffs, refs = refs[:count], refs[count : 3 * count], refs[3 * count :]
     operator, modes, weights, known, scaled, made, square, sent = refs
     hours = held[0].shape[0]
     half = hours // 2
     me, core = lax.axis_index("tm"), lax.axis_index("inner")
     first = [lax.rem(me + k, count) * hours for k in range(count)]
-    for k, block in enumerate(coeffs):
-        for n in range(2):
-            at = pl.multiple_of(first[k] + lax.rem(core + n, 2) * half, half)
-            known[pl.ds(at, half)] = block[n].astype(jnp.float32)
+    for n, block in enumerate(coeffs):
+        at = pl.multiple_of(first[n // 2] + lax.rem(core + n % 2, 2) * half, half)
+        known[pl.ds(at, half)] = block[...].astype(jnp.float32)
     every = known[...].astype(jnp.bfloat16)
     scaled[...] = lagged_and_scaled(known[...], energy[...])
     ordered = jnp.concatenate(
@@ -172,7 +171,7 @@
 
 
 def rebuild_first(energy, vectors, held, coeffs, cells, tiles):
-    rank = coeffs[0].shape[2]
+    rank = coeffs[0].shape[1]
     hours, modes = len(held) * held[0].shape[0], vectors.shape[0]
     return pl.pallas_call(
         functools.partial(first_kernel, tiles),
@@ -181,7 +180,7 @@
             jax.ShapeDtypeStruct((modes, cells), jnp.bfloat16),
             jax.ShapeDtypeStruct((modes, hours), jnp.bfloat16),
         ),
-        in_specs=[IN_VMEM] * (2 + 2 * len(held)),
+        in_specs=[IN_VMEM] * (2 + 3 * len(held)),
         out_specs=(ANYWHERE, ANYWHERE, IN_VMEM),
         scratch_shapes=[
             pltpu.VMEM((hours, rank), jnp.float32),
@@ -251,10 +250,12 @@
             mine = mine + near
         bit *= 4
     mine = mine.astype(jnp.bfloat16)
-    both = jnp.stack([mine, moved(mine, 0, 1)])
-    both, behind = lax.optimization_barrier((both, late))
+    mine, behind = lax.optimization_barrier((mine, late))
+    coeffs = []
+    for k in range(tm):
+        theirs = moved(mine, k, 0) if k else mine
+        coeffs += [theirs, moved(theirs, 0, 1)]
     last = [late] + [moved(behind, k, 0) for k in range(1, tm)]
-    coeffs = [both] + [moved(both, k, 0) for k in range(1, tm)]
 
     rows = eigen_vectors.shape[1] // tm
     vectors = lax.dynamic_slice_in_dim(eigen_vectors, me * rows, rows, 1)

time: 31.1 us -> 30.1 us (0.968)
  waiting for transfers between devices: 10.9 us -> 9.98 us
    ppermute x4 -> x5, waiting for transfers between devices: 4.08 us -> 3.15 us  [moved(): return lax.ppermute(value, ('tm', 'inner'), route)]
    ppermute x4 -> x5, starting transfers between devices: 5.1 us -> 5.03 us  [moved(): return lax.ppermute(value, ('tm', 'inner'), route)]
  transfers between devices with their start and end apart: 9 -> 10, of which waited for: 8 -> 8; matrix products, arithmetic and copies ran while one was open for 0% -> 0% of each run, Pallas kernels for 18% -> 18%
where the time goes in v20:
time: 30.1 us; the launch traced here: 29.9 us
  starting transfers between devices  11.2 us (37%)
  waiting for transfers between devices  9.98 us (33%)
  Pallas kernels  7.85 us (26%)
  between operations  0.71 us (2%)
    ppermute x5, waiting for transfers between devices, swapped(): return lax.ppermute(value, axis, route)  6.83 us
    ppermute x5, starting transfers between devices, swapped(): return lax.ppermute(value, axis, route)  6.21 us
    ppermute x5, starting transfers between devices, moved(): return lax.ppermute(value, ('tm', 'inner'), route)  5.03 us
    ppermute x5, waiting for transfers between devices, moved(): return lax.ppermute(value, ('tm', 'inner'), route)  3.15 us
    pallas_call x1, Pallas kernels, project(): pl.pallas_call(functools.partial(project_kernel, tiles), out_shape=(half,...  2.81 us
    pallas_call x1, Pallas kernels, rebuild_first(): pl.pallas_call(functools.partial(first_kernel, tiles), out_shape=(jax.Sha...  2.63 us
    pallas_call x1, Pallas kernels, cut(): pl.pallas_call(functools.partial(cut_kernel, begin), out_shape=(jax.Shape...  1.24 us
    pallas_call x1, Pallas kernels, rebuild_last(): pl.pallas_call(functools.partial(last_kernel, begin, tiles), out_shape=ja...  1.17 us
  transfers between devices with their start and end apart: 10, of which 8 were waited for; matrix products, arithmetic and copies ran while one was open for 0% of the time, Pallas kernels for 18%

profile of v20, /device:TPU:0, one launch (start us, length us, event | category | flops | bytes accessed | tf_op | source)
XLA Modules:
  0.0 29.9 jit_solution(15702879868751246052)
XLA Ops:
  0.6 0.0 copy-start
  0.6 0.0 copy-start.1
  0.7 1.2 %cut.1 = (bf16[64,6656]{1,0:T(8,128)(2,1)S(1)}, bf16[64,1536]{1,0:T(8,128)(2,1)S(1)}) custom-call(bf16[64,8192]{1,0:T(8,128)(2,1)} %bitcast.5), custom_call_target="tpu_custom_call" | custom-call | tf_op jit(solution)/shard_map/cut/pallas_call | solution.py:54
  1.9 3.0 %collective-permute-start = (bf16[64,6656]{1,0:T(8,128)(2,1)S(1)}, bf16[64,6656]{1,0:T(8,128)(2,1)S(1)}, u32[]{:S(2)}, u32[]{:S(2)}) collective-permute-start(bf16[64,6656]{1,0:T(8,128)(2,1)S(1)} %get-tuple-element.11.early.refs_0_), channel_id=1, source_target_pairs={{16,0},{17,1},{0,16},{1,17},{18,2},{19,3},{2,18},{3,19},{20,4},{21... | collective-permute-start | bytes 2555912 | tf_op jit(solution)/shard_map/ppermute | solution.py:227
  4.9 2.8 %project.1 = (f32[32,256]{1,0:T(8,128)S(1)}, f32[32,256]{1,0:T(8,128)S(1)}) custom-call(bf16[64,6656]{1,0:T(8,128)(2,1)S(1)} %get-tuple-element.11.early.refs_0_, bf16[64,1536]{1,0:T(8,128)(2,1)S(1)} %get-tuple-element.18.late.refs_0_, bf16[8192,256]{1,0:T(8,128)(2,1)} %basis.1), custom_call_target="tpu_custom_call" | custom-call | tf_op jit(solution)/shard_map/project/pallas_call | solution.py:96
  7.7 0.1 collective-permute-start.1
  7.8 1.2 %collective-permute-done.1 = f32[32,256]{1,0:T(8,128)S(1)} collective-permute-done((f32[32,256]{1,0:T(8,128)S(1)}, f32[32,256]{1,0:T(8,128)S(1)}, u32[]{:S(2)}, u32[]{:S(2)}) %collective-permute-start.1) | collective-permute-done | bytes 32800 | tf_op jit(solution)/shard_map/ppermute | solution.py:217
  9.0 2.5 %collective-permute-start.4 = (f32[32,256]{1,0:T(8,128)S(1)}, f32[32,256]{1,0:T(8,128)S(1)}, u32[]{:S(2)}, u32[]{:S(2)}) collective-permute-start(f32[32,256]{1,0:T(8,128)S(1)} %add.19), channel_id=1, source_target_pairs={{6,0},{4,2},{2,4},{0,6},{14,8},{12,10},{10,12},{8,14},{7,1},{5,3},... | collective-permute-start | bytes 98312 | tf_op jit(solution)/shard_map/ppermute | solution.py:217
  11.5 0.5 %collective-permute-start.3 = (f32[32,256]{1,0:T(8,128)S(1)}, f32[32,256]{1,0:T(8,128)S(1)}, u32[]{:S(2)}, u32[]{:S(2)}) collective-permute-start(f32[32,256]{1,0:T(8,128)S(1)} %add.19), channel_id=1, source_target_pairs={{4,0},{6,2},{0,4},{2,6},{12,8},{14,10},{8,12},{10,14},{5,1},{7,3},... | collective-permute-start | bytes 98312 | tf_op jit(solution)/shard_map/ppermute | solution.py:217
  12.0 0.5 %collective-permute-start.2 = (f32[32,256]{1,0:T(8,128)S(1)}, f32[32,256]{1,0:T(8,128)S(1)}, u32[]{:S(2)}, u32[]{:S(2)}) collective-permute-start(f32[32,256]{1,0:T(8,128)S(1)} %add.19), channel_id=1, source_target_pairs={{2,0},{0,2},{6,4},{4,6},{10,8},{8,10},{14,12},{12,14},{3,1},{1,3},... | collective-permute-start | bytes 98312 | tf_op jit(solution)/shard_map/ppermute | solution.py:217
  12.5 1.3 %collective-permute-done.4 = f32[32,256]{1,0:T(8,128)S(1)} collective-permute-done((f32[32,256]{1,0:T(8,128)S(1)}, f32[32,256]{1,0:T(8,128)S(1)}, u32[]{:S(2)}, u32[]{:S(2)}) %collective-permute-start.4) | collective-permute-done | bytes 32800 | tf_op jit(solution)/shard_map/ppermute | solution.py:217
  13.8 1.6 %collective-permute-done.3 = f32[32,256]{1,0:T(8,128)S(1)} collective-permute-done((f32[32,256]{1,0:T(8,128)S(1)}, f32[32,256]{1,0:T(8,128)S(1)}, u32[]{:S(2)}, u32[]{:S(2)}) %collective-permute-start.3) | collective-permute-done | bytes 32800 | tf_op jit(solution)/shard_map/ppermute | solution.py:217
  15.5 0.5 %collective-permute-done.2 = f32[32,256]{1,0:T(8,128)S(1)} collective-permute-done((f32[32,256]{1,0:T(8,128)S(1)}, f32[32,256]{1,0:T(8,128)S(1)}, u32[]{:S(2)}, u32[]{:S(2)}) %collective-permute-start.2) | collective-permute-done | bytes 32800 | tf_op jit(solution)/shard_map/ppermute | solution.py:217
  15.9 2.7 %collective-permute-start.5 = (f32[32,256]{1,0:T(8,128)S(1)}, f32[32,256]{1,0:T(8,128)S(1)}, u32[]{:S(2)}, u32[]{:S(2)}) collective-permute-start(f32[32,256]{1,0:T(8,128)S(1)} %add_add_fusion), channel_id=1, source_target_pairs={{8,0},{10,2},{12,4},{14,6},{0,8},{2,10},{4,12},{6,14},{9,1},{11,3}... | collective-permute-start | bytes 98312 | tf_op jit(solution)/shard_map/ppermute | solution.py:217
  18.6 2.2 %collective-permute-done.5 = f32[32,256]{1,0:T(8,128)S(1)} collective-permute-done((f32[32,256]{1,0:T(8,128)S(1)}, f32[32,256]{1,0:T(8,128)S(1)}, u32[]{:S(2)}, u32[]{:S(2)}) %collective-permute-start.5) | collective-permute-done | bytes 32800 | tf_op jit(solution)/shard_map/ppermute | solution.py:217
  20.8 0.5 %collective-permute-start.7 = (bf16[32,256]{1,0:T(8,128)(2,1)S(1)}, bf16[32,256]{1,0:T(8,128)(2,1)S(1)}, u32[]{:S(2)}, u32[]{:S(2)}) collective-permute-start(bf16[32,256]{1,0:T(8,128)(2,1)S(1)} %add_convert_fusion.refs_2_), channel_id=1, source_target_pairs={{16,0},{17,1},{0,16},{1,17},{18,2},{19,3},{2,18},{3,19},{20,4},{21... | collective-permute-start | bytes 49160 | tf_op jit(solution)/shard_map/ppermute | solution.py:227
  21.3 0.0 collective-permute-start.6
  21.3 1.5 %collective-permute-start.9 = (bf16[64,1536]{1,0:T(8,128)(2,1)S(1)}, bf16[64,1536]{1,0:T(8,128)(2,1)S(1)}, u32[]{:S(2)}, u32[]{:S(2)}) collective-permute-start(bf16[64,1536]{1,0:T(8,128)(2,1)S(1)} %get-tuple-element.18.late.refs_0_), channel_id=1, source_target_pairs={{16,0},{17,1},{0,16},{1,17},{18,2},{19,3},{2,18},{3,19},{20,4},{21... | collective-permute-start | bytes 589832 | tf_op jit(solution)/shard_map/ppermute | solution.py:227
  22.8 1.8 %collective-permute-done.7.refs_4_ = bf16[32,256]{1,0:T(8,128)(2,1)S(1)} collective-permute-done((bf16[32,256]{1,0:T(8,128)(2,1)S(1)}, bf16[32,256]{1,0:T(8,128)(2,1)S(1)}, u32[]{:S(2)}, u32[]{:S(2)}) %collective-permute-start.7) | collective-permute-done | bytes 16416 | tf_op jit(solution)/shard_map/ppermute | solution.py:227
  24.6 0.0 collective-permute-start.8
  24.6 0.0 copy-done
  24.7 0.1 copy.8
  24.8 0.0 collective-permute-done.6.refs_3_
  24.8 1.0 %collective-permute-done.8.refs_5_ = bf16[32,256]{1,0:T(8,128)(2,1)S(1)} collective-permute-done((bf16[32,256]{1,0:T(8,128)(2,1)S(1)}, bf16[32,256]{1,0:T(8,128)(2,1)S(1)}, u32[]{:S(2)}, u32[]{:S(2)}) %collective-permute-start.8) | collective-permute-done | bytes 16416 | tf_op jit(solution)/shard_map/ppermute | solution.py:227
  25.8 0.0 collective-permute-done.refs_1_
  25.8 0.0 copy-done.1
  25.8 2.6 %rebuild_first.1 = (f32[256,256]{1,0:T(8,128)}, bf16[256,8192]{1,0:T(8,128)(2,1)}, bf16[256,128]{1,0:T(8,128)(2,1)S(1)}) custom-call(f32[1,256]{1,0:T(1,128)S(1)} %bitcast.4, bf16[256,256]{1,0:T(8,128)(2,1)S(1)} %bitcast.3, bf16[64,6656]{1,0:T(8,128)(2,1)S(1)} %get-tuple-element.11.early.refs_0_, bf16[64,6656]{1,0:T(8,128)(2,1)S(1)} %collective-permute-done.refs_1_, ...), custom_call_target="tpu_custom_call" | custom-call | flops 2000000000 | tf_op jit(solution)/shard_map/rebuild_first/pallas_call | solution.py:176
  28.5 0.3 collective-permute-done.9.refs_1_
  28.8 1.2 %rebuild_last.1 = bf16[256,8192]{1,0:T(8,128)(2,1)} custom-call(bf16[256,128]{1,0:T(8,128)(2,1)S(1)} %get-tuple-element.17.weights, bf16[64,1536]{1,0:T(8,128)(2,1)S(1)} %get-tuple-element.18.late.refs_0_, bf16[64,1536]{1,0:T(8,128)(2,1)S(1)} %collective-permute-done.9.refs_1_, ...), custom_call_target="tpu_custom_call", output_to_operand_aliasing={{}: (3, {})} | custom-call | tf_op jit(solution)/shard_map/rebuild_last/pallas_call | solution.py:199
  (4 shorter events, 0.0 us)
Async XLA Ops:
  0.6 24.0 %copy-start = (bf16[256,512]{1,0:T(8,128)(2,1)S(1)}, bf16[256,512]{1,0:T(8,128)(2,1)}, u32[]{:S(2)}) copy-start(bf16[256,512]{1,0:T(8,128)(2,1)} %param.7) | copy-start | bytes 786436
  0.6 25.2 %copy-start.1 = (f32[256]{0:T(256)S(1)}, f32[256]{0:T(256)}, u32[]{:S(2)}) copy-start(f32[256]{0:T(256)} %param.6) | copy-start | bytes 3076
  1.9 23.9 %collective-permute-start = (bf16[64,6656]{1,0:T(8,128)(2,1)S(1)}, bf16[64,6656]{1,0:T(8,128)(2,1)S(1)}, u32[]{:S(2)}, u32[]{:S(2)}) collective-permute-start(bf16[64,6656]{1,0:T(8,128)(2,1)S(1)} %get-tuple-element.11.early.refs_0_), channel_id=1, source_target_pairs={{16,0},{17,1},{0,16},{1,17},{18,2},{19,3},{2,18},{3,19},{20,4},{21... | collective-permute-start | bytes 2555912 | tf_op jit(solution)/shard_map/ppermute | solution.py:227
  7.7 1.3 %collective-permute-start.1 = (f32[32,256]{1,0:T(8,128)S(1)}, f32[32,256]{1,0:T(8,128)S(1)}, u32[]{:S(2)}, u32[]{:S(2)}) collective-permute-start(f32[32,256]{1,0:T(8,128)S(1)} %get-tuple-element.14), channel_id=1, source_target_pairs={{1,0},{0,1},{3,2},{2,3},{5,4},{4,5},{7,6},{6,7},{9,8},{8,9},{11,10... | collective-permute-start | bytes 98312 | tf_op jit(solution)/shard_map/ppermute | solution.py:217
  9.0 4.8 %collective-permute-start.4 = (f32[32,256]{1,0:T(8,128)S(1)}, f32[32,256]{1,0:T(8,128)S(1)}, u32[]{:S(2)}, u32[]{:S(2)}) collective-permute-start(f32[32,256]{1,0:T(8,128)S(1)} %add.19), channel_id=1, source_target_pairs={{6,0},{4,2},{2,4},{0,6},{14,8},{12,10},{10,12},{8,14},{7,1},{5,3},... | collective-permute-start | bytes 98312 | tf_op jit(solution)/shard_map/ppermute | solution.py:217
  11.5 3.9 %collective-permute-start.3 = (f32[32,256]{1,0:T(8,128)S(1)}, f32[32,256]{1,0:T(8,128)S(1)}, u32[]{:S(2)}, u32[]{:S(2)}) collective-permute-start(f32[32,256]{1,0:T(8,128)S(1)} %add.19), channel_id=1, source_target_pairs={{4,0},{6,2},{0,4},{2,6},{12,8},{14,10},{8,12},{10,14},{5,1},{7,3},... | collective-permute-start | bytes 98312 | tf_op jit(solution)/shard_map/ppermute | solution.py:217
  12.0 3.9 %collective-permute-start.2 = (f32[32,256]{1,0:T(8,128)S(1)}, f32[32,256]{1,0:T(8,128)S(1)}, u32[]{:S(2)}, u32[]{:S(2)}) collective-permute-start(f32[32,256]{1,0:T(8,128)S(1)} %add.19), channel_id=1, source_target_pairs={{2,0},{0,2},{6,4},{4,6},{10,8},{8,10},{14,12},{12,14},{3,1},{1,3},... | collective-permute-start | bytes 98312 | tf_op jit(solution)/shard_map/ppermute | solution.py:217
  15.9 4.9 %collective-permute-start.5 = (f32[32,256]{1,0:T(8,128)S(1)}, f32[32,256]{1,0:T(8,128)S(1)}, u32[]{:S(2)}, u32[]{:S(2)}) collective-permute-start(f32[32,256]{1,0:T(8,128)S(1)} %add_add_fusion), channel_id=1, source_target_pairs={{8,0},{10,2},{12,4},{14,6},{0,8},{2,10},{4,12},{6,14},{9,1},{11,3}... | collective-permute-start | bytes 98312 | tf_op jit(solution)/shard_map/ppermute | solution.py:217
  20.8 3.8 %collective-permute-start.7 = (bf16[32,256]{1,0:T(8,128)(2,1)S(1)}, bf16[32,256]{1,0:T(8,128)(2,1)S(1)}, u32[]{:S(2)}, u32[]{:S(2)}) collective-permute-start(bf16[32,256]{1,0:T(8,128)(2,1)S(1)} %add_convert_fusion.refs_2_), channel_id=1, source_target_pairs={{16,0},{17,1},{0,16},{1,17},{18,2},{19,3},{2,18},{3,19},{20,4},{21... | collective-permute-start | bytes 49160 | tf_op jit(solution)/shard_map/ppermute | solution.py:227
  21.3 3.4 %collective-permute-start.6 = (bf16[32,256]{1,0:T(8,128)(2,1)S(1)}, bf16[32,256]{1,0:T(8,128)(2,1)S(1)}, u32[]{:S(2)}, u32[]{:S(2)}) collective-permute-start(bf16[32,256]{1,0:T(8,128)(2,1)S(1)} %add_convert_fusion.refs_2_), channel_id=1, source_target_pairs={{1,0},{0,1},{17,16},{16,17},{3,2},{2,3},{19,18},{18,19},{5,4},{4,5... | collective-permute-start | bytes 49160 | tf_op jit(solution)/shard_map/ppermute | solution.py:227
  21.3 7.4 %collective-permute-start.9 = (bf16[64,1536]{1,0:T(8,128)(2,1)S(1)}, bf16[64,1536]{1,0:T(8,128)(2,1)S(1)}, u32[]{:S(2)}, u32[]{:S(2)}) collective-permute-start(bf16[64,1536]{1,0:T(8,128)(2,1)S(1)} %get-tuple-element.18.late.refs_0_), channel_id=1, source_target_pairs={{16,0},{17,1},{0,16},{1,17},{18,2},{19,3},{2,18},{3,19},{20,4},{21... | collective-permute-start | bytes 589832 | tf_op jit(solution)/shard_map/ppermute | solution.py:227
  24.6 1.2 %collective-permute-start.8 = (bf16[32,256]{1,0:T(8,128)(2,1)S(1)}, bf16[32,256]{1,0:T(8,128)(2,1)S(1)}, u32[]{:S(2)}, u32[]{:S(2)}) collective-permute-start(bf16[32,256]{1,0:T(8,128)(2,1)S(1)} %collective-permute-done.7.refs_4_), channel_id=1, source_target_pairs={{1,0},{0,1},{17,16},{16,17},{3,2},{2,3},{19,18},{18,19},{5,4},{4,5... | collective-permute-start | bytes 49160 | tf_op jit(solution)/shard_map/ppermute | solution.py:227

commit v21 on v20

--- a/solution.py
+++ b/solution.py
@@ -38,15 +38,15 @@
 
 
 def cut_kernel(begin, fields, early, late, sent):
-    spans = pl.ds(0, begin), pl.ds(begin, late.shape[1])
-    waited(
-        started(
-            [
-                pltpu.make_async_copy(fields.at[:, span], piece, sent.at[i])
-                for i, (span, piece) in enumerate(zip(spans, (early, late)))
-            ]
+    half = begin // 2
+    copies = [
+        pltpu.make_async_copy(
+            fields.at[:, pl.ds(at, half)], early.at[:, pl.ds(at, half)], sent.at[at // half]
         )
-    )
+        for at in (0, half)
+    ]
+    rest = fields.at[:, pl.ds(begin, late.shape[1])]
+    waited(started(copies + [pltpu.make_async_copy(rest, late, sent.at[2])]))
 
 
 def cut(fields, begin):
@@ -59,7 +59,7 @@
         ),
         in_specs=[ANYWHERE],
         out_specs=(ANYWHERE, ANYWHERE),
-        scratch_shapes=[pltpu.SemaphoreType.DMA((2,))],
+        scratch_shapes=[pltpu.SemaphoreType.DMA((3,))],
         compiler_params=pltpu.CompilerParams(vmem_limit_bytes=52 * 2**20),
         cost_estimate=FREE,
         name="cut",
@@ -260,9 +260,9 @@
     rows = eigen_vectors.shape[1] // tm
     vectors = lax.dynamic_slice_in_dim(eigen_vectors, me * rows, rows, 1)
     operator, modes, weights = rebuild_first(
-        inverse_energy[None, :], vectors.T, first, coeffs, cells, 4
-    )
-    return operator, rebuild_last(weights, last, modes, begin, 2)
+        inverse_energy[None, :], vectors.T, first, coeffs, cells, 6
+    )
+    return operator, rebuild_last(weights, last, modes, begin, 3)
 
 
 def solution(mesh):

time: 30.1 us -> 30 us (level)
  no operation moved by 1% of the time
where the time goes in v21:
time: 30 us; the launch traced here: 29.9 us
  starting transfers between devices  11.2 us (37%)
  waiting for transfers between devices  10 us (33%)
  Pallas kernels  7.76 us (26%)
  between operations  0.71 us (2%)
    ppermute x5, waiting for transfers between devices, swapped(): return lax.ppermute(value, axis, route)  6.83 us
    ppermute x5, starting transfers between devices, swapped(): return lax.ppermute(value, axis, route)  6.21 us
    ppermute x5, starting transfers between devices, moved(): return lax.ppermute(value, ('tm', 'inner'), route)  5.03 us
    ppermute x5, waiting for transfers between devices, moved(): return lax.ppermute(value, ('tm', 'inner'), route)  3.19 us
    pallas_call x1, Pallas kernels, project(): pl.pallas_call(functools.partial(project_kernel, tiles), out_shape=(half,...  2.81 us
    pallas_call x1, Pallas kernels, rebuild_first(): pl.pallas_call(functools.partial(first_kernel, tiles), out_shape=(jax.Sha...  2.58 us
    pallas_call x1, Pallas kernels, cut(): pl.pallas_call(functools.partial(cut_kernel, begin), out_shape=(jax.Shape...  1.25 us
    pallas_call x1, Pallas kernels, rebuild_last(): pl.pallas_call(functools.partial(last_kernel, begin, tiles), out_shape=ja...  1.11 us
  transfers between devices with their start and end apart: 10, of which 8 were waited for; matrix products, arithmetic and copies ran while one was open for 0% of the time, Pallas kernels for 18%

profile of v21, /device:TPU:0, one launch (start us, length us, event | category | flops | bytes accessed | tf_op | source)
XLA Modules:
  0.0 29.9 jit_solution(16452209714418947576)
XLA Ops:
  0.6 0.0 copy-start
  0.6 0.0 copy-start.1
  0.7 1.3 %cut.1 = (bf16[64,6656]{1,0:T(8,128)(2,1)S(1)}, bf16[64,1536]{1,0:T(8,128)(2,1)S(1)}) custom-call(bf16[64,8192]{1,0:T(8,128)(2,1)} %bitcast.5), custom_call_target="tpu_custom_call" | custom-call | tf_op jit(solution)/shard_map/cut/pallas_call | solution.py:54
  1.9 3.0 %collective-permute-start = (bf16[64,6656]{1,0:T(8,128)(2,1)S(1)}, bf16[64,6656]{1,0:T(8,128)(2,1)S(1)}, u32[]{:S(2)}, u32[]{:S(2)}) collective-permute-start(bf16[64,6656]{1,0:T(8,128)(2,1)S(1)} %get-tuple-element.11.early.refs_0_), channel_id=1, source_target_pairs={{16,0},{17,1},{0,16},{1,17},{18,2},{19,3},{2,18},{3,19},{20,4},{21... | collective-permute-start | bytes 2555912 | tf_op jit(solution)/shard_map/ppermute | solution.py:227
  4.9 2.8 %project.1 = (f32[32,256]{1,0:T(8,128)S(1)}, f32[32,256]{1,0:T(8,128)S(1)}) custom-call(bf16[64,6656]{1,0:T(8,128)(2,1)S(1)} %get-tuple-element.11.early.refs_0_, bf16[64,1536]{1,0:T(8,128)(2,1)S(1)} %get-tuple-element.18.late.refs_0_, bf16[8192,256]{1,0:T(8,128)(2,1)} %basis.1), custom_call_target="tpu_custom_call" | custom-call | tf_op jit(solution)/shard_map/project/pallas_call | solution.py:96
  7.7 0.1 collective-permute-start.1
  7.8 1.2 %collective-permute-done.1 = f32[32,256]{1,0:T(8,128)S(1)} collective-permute-done((f32[32,256]{1,0:T(8,128)S(1)}, f32[32,256]{1,0:T(8,128)S(1)}, u32[]{:S(2)}, u32[]{:S(2)}) %collective-permute-start.1) | collective-permute-done | bytes 32800 | tf_op jit(solution)/shard_map/ppermute | solution.py:217
  9.0 2.5 %collective-permute-start.4 = (f32[32,256]{1,0:T(8,128)S(1)}, f32[32,256]{1,0:T(8,128)S(1)}, u32[]{:S(2)}, u32[]{:S(2)}) collective-permute-start(f32[32,256]{1,0:T(8,128)S(1)} %add.19), channel_id=1, source_target_pairs={{6,0},{4,2},{2,4},{0,6},{14,8},{12,10},{10,12},{8,14},{7,1},{5,3},... | collective-permute-start | bytes 98312 | tf_op jit(solution)/shard_map/ppermute | solution.py:217
  11.5 0.5 %collective-permute-start.3 = (f32[32,256]{1,0:T(8,128)S(1)}, f32[32,256]{1,0:T(8,128)S(1)}, u32[]{:S(2)}, u32[]{:S(2)}) collective-permute-start(f32[32,256]{1,0:T(8,128)S(1)} %add.19), channel_id=1, source_target_pairs={{4,0},{6,2},{0,4},{2,6},{12,8},{14,10},{8,12},{10,14},{5,1},{7,3},... | collective-permute-start | bytes 98312 | tf_op jit(solution)/shard_map/ppermute | solution.py:217
  12.0 0.5 %collective-permute-start.2 = (f32[32,256]{1,0:T(8,128)S(1)}, f32[32,256]{1,0:T(8,128)S(1)}, u32[]{:S(2)}, u32[]{:S(2)}) collective-permute-start(f32[32,256]{1,0:T(8,128)S(1)} %add.19), channel_id=1, source_target_pairs={{2,0},{0,2},{6,4},{4,6},{10,8},{8,10},{14,12},{12,14},{3,1},{1,3},... | collective-permute-start | bytes 98312 | tf_op jit(solution)/shard_map/ppermute | solution.py:217
  12.5 1.3 %collective-permute-done.4 = f32[32,256]{1,0:T(8,128)S(1)} collective-permute-done((f32[32,256]{1,0:T(8,128)S(1)}, f32[32,256]{1,0:T(8,128)S(1)}, u32[]{:S(2)}, u32[]{:S(2)}) %collective-permute-start.4) | collective-permute-done | bytes 32800 | tf_op jit(solution)/shard_map/ppermute | solution.py:217
  13.8 1.6 %collective-permute-done.3 = f32[32,256]{1,0:T(8,128)S(1)} collective-permute-done((f32[32,256]{1,0:T(8,128)S(1)}, f32[32,256]{1,0:T(8,128)S(1)}, u32[]{:S(2)}, u32[]{:S(2)}) %collective-permute-start.3) | collective-permute-done | bytes 32800 | tf_op jit(solution)/shard_map/ppermute | solution.py:217
  15.5 0.5 %collective-permute-done.2 = f32[32,256]{1,0:T(8,128)S(1)} collective-permute-done((f32[32,256]{1,0:T(8,128)S(1)}, f32[32,256]{1,0:T(8,128)S(1)}, u32[]{:S(2)}, u32[]{:S(2)}) %collective-permute-start.2) | collective-permute-done | bytes 32800 | tf_op jit(solution)/shard_map/ppermute | solution.py:217
  15.9 2.7 %collective-permute-start.5 = (f32[32,256]{1,0:T(8,128)S(1)}, f32[32,256]{1,0:T(8,128)S(1)}, u32[]{:S(2)}, u32[]{:S(2)}) collective-permute-start(f32[32,256]{1,0:T(8,128)S(1)} %add_add_fusion), channel_id=1, source_target_pairs={{8,0},{10,2},{12,4},{14,6},{0,8},{2,10},{4,12},{6,14},{9,1},{11,3}... | collective-permute-start | bytes 98312 | tf_op jit(solution)/shard_map/ppermute | solution.py:217
  18.6 2.2 %collective-permute-done.5 = f32[32,256]{1,0:T(8,128)S(1)} collective-permute-done((f32[32,256]{1,0:T(8,128)S(1)}, f32[32,256]{1,0:T(8,128)S(1)}, u32[]{:S(2)}, u32[]{:S(2)}) %collective-permute-start.5) | collective-permute-done | bytes 32800 | tf_op jit(solution)/shard_map/ppermute | solution.py:217
  20.8 0.5 %collective-permute-start.7 = (bf16[32,256]{1,0:T(8,128)(2,1)S(1)}, bf16[32,256]{1,0:T(8,128)(2,1)S(1)}, u32[]{:S(2)}, u32[]{:S(2)}) collective-permute-start(bf16[32,256]{1,0:T(8,128)(2,1)S(1)} %add_convert_fusion.refs_2_), channel_id=1, source_target_pairs={{16,0},{17,1},{0,16},{1,17},{18,2},{19,3},{2,18},{3,19},{20,4},{21... | collective-permute-start | bytes 49160 | tf_op jit(solution)/shard_map/ppermute | solution.py:227
  21.3 0.0 collective-permute-start.6
  21.4 1.5 %collective-permute-start.9 = (bf16[64,1536]{1,0:T(8,128)(2,1)S(1)}, bf16[64,1536]{1,0:T(8,128)(2,1)S(1)}, u32[]{:S(2)}, u32[]{:S(2)}) collective-permute-start(bf16[64,1536]{1,0:T(8,128)(2,1)S(1)} %get-tuple-element.18.late.refs_0_), channel_id=1, source_target_pairs={{16,0},{17,1},{0,16},{1,17},{18,2},{19,3},{2,18},{3,19},{20,4},{21... | collective-permute-start | bytes 589832 | tf_op jit(solution)/shard_map/ppermute | solution.py:227
  22.8 1.8 %collective-permute-done.7.refs_4_ = bf16[32,256]{1,0:T(8,128)(2,1)S(1)} collective-permute-done((bf16[32,256]{1,0:T(8,128)(2,1)S(1)}, bf16[32,256]{1,0:T(8,128)(2,1)S(1)}, u32[]{:S(2)}, u32[]{:S(2)}) %collective-permute-start.7) | collective-permute-done | bytes 16416 | tf_op jit(solution)/shard_map/ppermute | solution.py:227
  24.7 0.0 collective-permute-start.8
  24.7 0.0 copy-done
  24.7 0.1 copy.8
  24.8 0.0 collective-permute-done.6.refs_3_
  24.8 1.0 %collective-permute-done.8.refs_5_ = bf16[32,256]{1,0:T(8,128)(2,1)S(1)} collective-permute-done((bf16[32,256]{1,0:T(8,128)(2,1)S(1)}, bf16[32,256]{1,0:T(8,128)(2,1)S(1)}, u32[]{:S(2)}, u32[]{:S(2)}) %collective-permute-start.8) | collective-permute-done | bytes 16416 | tf_op jit(solution)/shard_map/ppermute | solution.py:227
  25.8 0.0 collective-permute-done.refs_1_
  25.8 0.0 copy-done.1
  25.8 2.6 %rebuild_first.1 = (f32[256,256]{1,0:T(8,128)}, bf16[256,8192]{1,0:T(8,128)(2,1)}, bf16[256,128]{1,0:T(8,128)(2,1)S(1)}) custom-call(f32[1,256]{1,0:T(1,128)S(1)} %bitcast.4, bf16[256,256]{1,0:T(8,128)(2,1)S(1)} %bitcast.3, bf16[64,6656]{1,0:T(8,128)(2,1)S(1)} %get-tuple-element.11.early.refs_0_, bf16[64,6656]{1,0:T(8,128)(2,1)S(1)} %collective-permute-done.refs_1_, ...), custom_call_target="tpu_custom_call" | custom-call | flops 2000000000 | tf_op jit(solution)/shard_map/rebuild_first/pallas_call | solution.py:176
  28.4 0.3 %collective-permute-done.9.refs_1_ = bf16[64,1536]{1,0:T(8,128)(2,1)S(1)} collective-permute-done((bf16[64,1536]{1,0:T(8,128)(2,1)S(1)}, bf16[64,1536]{1,0:T(8,128)(2,1)S(1)}, u32[]{:S(2)}, u32[]{:S(2)}) %collective-permute-start.9) | collective-permute-done | bytes 196640 | tf_op jit(solution)/shard_map/ppermute | solution.py:227
  28.8 1.1 %rebuild_last.1 = bf16[256,8192]{1,0:T(8,128)(2,1)} custom-call(bf16[256,128]{1,0:T(8,128)(2,1)S(1)} %get-tuple-element.17.weights, bf16[64,1536]{1,0:T(8,128)(2,1)S(1)} %get-tuple-element.18.late.refs_0_, bf16[64,1536]{1,0:T(8,128)(2,1)S(1)} %collective-permute-done.9.refs_1_, ...), custom_call_target="tpu_custom_call", output_to_operand_aliasing={{}: (3, {})} | custom-call | tf_op jit(solution)/shard_map/rebuild_last/pallas_call | solution.py:199
  (4 shorter events, 0.0 us)
Async XLA Ops:
  0.6 24.0 %copy-start = (bf16[256,512]{1,0:T(8,128)(2,1)S(1)}, bf16[256,512]{1,0:T(8,128)(2,1)}, u32[]{:S(2)}) copy-start(bf16[256,512]{1,0:T(8,128)(2,1)} %param.7) | copy-start | bytes 786436
  0.6 25.2 %copy-start.1 = (f32[256]{0:T(256)S(1)}, f32[256]{0:T(256)}, u32[]{:S(2)}) copy-start(f32[256]{0:T(256)} %param.6) | copy-start | bytes 3076
  1.9 23.9 %collective-permute-start = (bf16[64,6656]{1,0:T(8,128)(2,1)S(1)}, bf16[64,6656]{1,0:T(8,128)(2,1)S(1)}, u32[]{:S(2)}, u32[]{:S(2)}) collective-permute-start(bf16[64,6656]{1,0:T(8,128)(2,1)S(1)} %get-tuple-element.11.early.refs_0_), channel_id=1, source_target_pairs={{16,0},{17,1},{0,16},{1,17},{18,2},{19,3},{2,18},{3,19},{20,4},{21... | collective-permute-start | bytes 2555912 | tf_op jit(solution)/shard_map/ppermute | solution.py:227
  7.7 1.3 %collective-permute-start.1 = (f32[32,256]{1,0:T(8,128)S(1)}, f32[32,256]{1,0:T(8,128)S(1)}, u32[]{:S(2)}, u32[]{:S(2)}) collective-permute-start(f32[32,256]{1,0:T(8,128)S(1)} %get-tuple-element.14), channel_id=1, source_target_pairs={{1,0},{0,1},{3,2},{2,3},{5,4},{4,5},{7,6},{6,7},{9,8},{8,9},{11,10... | collective-permute-start | bytes 98312 | tf_op jit(solution)/shard_map/ppermute | solution.py:217
  9.0 4.8 %collective-permute-start.4 = (f32[32,256]{1,0:T(8,128)S(1)}, f32[32,256]{1,0:T(8,128)S(1)}, u32[]{:S(2)}, u32[]{:S(2)}) collective-permute-start(f32[32,256]{1,0:T(8,128)S(1)} %add.19), channel_id=1, source_target_pairs={{6,0},{4,2},{2,4},{0,6},{14,8},{12,10},{10,12},{8,14},{7,1},{5,3},... | collective-permute-start | bytes 98312 | tf_op jit(solution)/shard_map/ppermute | solution.py:217
  11.5 3.9 %collective-permute-start.3 = (f32[32,256]{1,0:T(8,128)S(1)}, f32[32,256]{1,0:T(8,128)S(1)}, u32[]{:S(2)}, u32[]{:S(2)}) collective-permute-start(f32[32,256]{1,0:T(8,128)S(1)} %add.19), channel_id=1, source_target_pairs={{4,0},{6,2},{0,4},{2,6},{12,8},{14,10},{8,12},{10,14},{5,1},{7,3},... | collective-permute-start | bytes 98312 | tf_op jit(solution)/shard_map/ppermute | solution.py:217
  12.0 3.9 %collective-permute-start.2 = (f32[32,256]{1,0:T(8,128)S(1)}, f32[32,256]{1,0:T(8,128)S(1)}, u32[]{:S(2)}, u32[]{:S(2)}) collective-permute-start(f32[32,256]{1,0:T(8,128)S(1)} %add.19), channel_id=1, source_target_pairs={{2,0},{0,2},{6,4},{4,6},{10,8},{8,10},{14,12},{12,14},{3,1},{1,3},... | collective-permute-start | bytes 98312 | tf_op jit(solution)/shard_map/ppermute | solution.py:217
  15.9 4.9 %collective-permute-start.5 = (f32[32,256]{1,0:T(8,128)S(1)}, f32[32,256]{1,0:T(8,128)S(1)}, u32[]{:S(2)}, u32[]{:S(2)}) collective-permute-start(f32[32,256]{1,0:T(8,128)S(1)} %add_add_fusion), channel_id=1, source_target_pairs={{8,0},{10,2},{12,4},{14,6},{0,8},{2,10},{4,12},{6,14},{9,1},{11,3}... | collective-permute-start | bytes 98312 | tf_op jit(solution)/shard_map/ppermute | solution.py:217
  20.8 3.8 %collective-permute-start.7 = (bf16[32,256]{1,0:T(8,128)(2,1)S(1)}, bf16[32,256]{1,0:T(8,128)(2,1)S(1)}, u32[]{:S(2)}, u32[]{:S(2)}) collective-permute-start(bf16[32,256]{1,0:T(8,128)(2,1)S(1)} %add_convert_fusion.refs_2_), channel_id=1, source_target_pairs={{16,0},{17,1},{0,16},{1,17},{18,2},{19,3},{2,18},{3,19},{20,4},{21... | collective-permute-start | bytes 49160 | tf_op jit(solution)/shard_map/ppermute | solution.py:227
  21.3 3.4 %collective-permute-start.6 = (bf16[32,256]{1,0:T(8,128)(2,1)S(1)}, bf16[32,256]{1,0:T(8,128)(2,1)S(1)}, u32[]{:S(2)}, u32[]{:S(2)}) collective-permute-start(bf16[32,256]{1,0:T(8,128)(2,1)S(1)} %add_convert_fusion.refs_2_), channel_id=1, source_target_pairs={{1,0},{0,1},{17,16},{16,17},{3,2},{2,3},{19,18},{18,19},{5,4},{4,5... | collective-permute-start | bytes 49160 | tf_op jit(solution)/shard_map/ppermute | solution.py:227
  21.4 7.4 %collective-permute-start.9 = (bf16[64,1536]{1,0:T(8,128)(2,1)S(1)}, bf16[64,1536]{1,0:T(8,128)(2,1)S(1)}, u32[]{:S(2)}, u32[]{:S(2)}) collective-permute-start(bf16[64,1536]{1,0:T(8,128)(2,1)S(1)} %get-tuple-element.18.late.refs_0_), channel_id=1, source_target_pairs={{16,0},{17,1},{0,16},{1,17},{18,2},{19,3},{2,18},{3,19},{20,4},{21... | collective-permute-start | bytes 589832 | tf_op jit(solution)/shard_map/ppermute | solution.py:227
  24.7 1.2 %collective-permute-start.8 = (bf16[32,256]{1,0:T(8,128)(2,1)S(1)}, bf16[32,256]{1,0:T(8,128)(2,1)S(1)}, u32[]{:S(2)}, u32[]{:S(2)}) collective-permute-start(bf16[32,256]{1,0:T(8,128)(2,1)S(1)} %collective-permute-done.7.refs_4_), channel_id=1, source_target_pairs={{1,0},{0,1},{17,16},{16,17},{3,2},{2,3},{19,18},{18,19},{5,4},{4,5... | collective-permute-start | bytes 49160 | tf_op jit(solution)/shard_map/ppermute | solution.py:227

commit v22 on v20

--- a/solution.py
+++ b/solution.py
@@ -37,51 +37,55 @@
     return lax.dot_general(left, right, dims, preferred_element_type=jnp.float32)
 
 
-def cut_kernel(begin, fields, early, late, sent):
-    spans = pl.ds(0, begin), pl.ds(begin, late.shape[1])
+def cut_kernel(fields, early, sent):
+    half = early.shape[1] // 2
+    spans = [pl.ds(at, half) for at in (0, half)]
     waited(
         started(
             [
-                pltpu.make_async_copy(fields.at[:, span], piece, sent.at[i])
-                for i, (span, piece) in enumerate(zip(spans, (early, late)))
+                pltpu.make_async_copy(fields.at[:, span], early.at[:, span], sent.at[i])
+                for i, span in enumerate(spans)
             ]
         )
     )
 
 
-def cut(fields, begin):
-    hours, cells = fields.shape
-    return pl.pallas_call(
-        functools.partial(cut_kernel, begin),
-        out_shape=(
-            jax.ShapeDtypeStruct((hours, begin), fields.dtype),
-            jax.ShapeDtypeStruct((hours, cells - begin), fields.dtype),
-        ),
+def cut(fields, width):
+    return pl.pallas_call(
+        cut_kernel,
+        out_shape=jax.ShapeDtypeStruct((fields.shape[0], width), fields.dtype),
         in_specs=[ANYWHERE],
-        out_specs=(ANYWHERE, ANYWHERE),
+        out_specs=ANYWHERE,
         scratch_shapes=[pltpu.SemaphoreType.DMA((2,))],
-        compiler_params=pltpu.CompilerParams(vmem_limit_bytes=52 * 2**20),
+        compiler_params=pltpu.CompilerParams(vmem_limit_bytes=53 * 2**20),
         cost_estimate=FREE,
         name="cut",
     )(fields)
 
 
-def project_kernel(tiles, early, late, basis, kept, given, patterns, halves, arrived):
+def project_kernel(
+    tiles, early, fields, basis, kept, given, late, patterns, halves, arrived, landed
+):
     cells = basis.shape[0]
     tile, begin = cells // tiles, early.shape[1]
     spans = [pl.ds(i * tile, tile) for i in range(tiles)]
+    rest = fields.at[:, pl.ds(begin, late.shape[1])]
+    rest = pltpu.make_async_copy(rest, late, landed.at[0])
     copies = started(
         [
             pltpu.make_async_copy(basis.at[span], patterns.at[span], arrived.at[i])
             for i, span in enumerate(spans)
         ]
     )
+    rest.start()
     total = jnp.zeros((early.shape[0], patterns.shape[1]), jnp.float32)
     for i, span in enumerate(spans):
+        at = i * tile
+        if at == begin:
+            rest.wait()
         copies[i].wait()
-        at = i * tile
-        fields = early[:, span] if at < begin else late[:, pl.ds(at - begin, tile)]
-        total += product(fields, patterns[span], ROWS)
+        held = early[:, span] if at < begin else late[:, pl.ds(at - begin, tile)]
+        total += product(held, patterns[span], ROWS)
     half = kept.shape[0]
     core = lax.axis_index("inner")
     halves[0] = total[:half]
@@ -90,23 +94,28 @@
     given[...] = halves[1 - core]
 
 
-def project(early, late, basis, tiles):
-    hours, rank = early.shape[0], basis.shape[1]
+def project(early, fields, basis, tiles):
+    (hours, cells), rank = fields.shape, basis.shape[1]
     half = jax.ShapeDtypeStruct((hours // 2, rank), jnp.float32)
     return pl.pallas_call(
         functools.partial(project_kernel, tiles),
-        out_shape=(half, half),
-        in_specs=[IN_VMEM, IN_VMEM, ANYWHERE],
-        out_specs=(IN_VMEM, IN_VMEM),
+        out_shape=(
+            half,
+            half,
+            jax.ShapeDtypeStruct((hours, cells - early.shape[1]), fields.dtype),
+        ),
+        in_specs=[IN_VMEM, ANYWHERE, ANYWHERE],
+        out_specs=(IN_VMEM,) * 3,
         scratch_shapes=[
             pltpu.VMEM(basis.shape, basis.dtype),
             pltpu.VMEM((2, hours // 2, rank), jnp.float32),
             pltpu.SemaphoreType.DMA((tiles,)),
+            pltpu.SemaphoreType.DMA((1,)),
         ],
         compiler_params=pltpu.CompilerParams(vmem_limit_bytes=52 * 2**20),
         cost_estimate=FREE,
         name="project",
-    )(early, late, basis)
+    )(early, fields, basis)
 
 
 def lagged_and_scaled(every, energy):
@@ -235,10 +244,10 @@
     cells = fields.shape[1]
     begin = cells // 16 * 13
 
-    early, late = cut(fields, begin)
+    early = cut(fields, begin)
     first = [early] + [moved(early, k, 0) for k in range(1, tm)]
 
-    kept, given = project(early, late, eof_basis, 16)
+    kept, given, late = project(early, fields, eof_basis, 16)
     mine = kept + swapped(given, "inner", 1)
     bit = 1
     while bit < outer:
@@ -260,9 +269,9 @@
     rows = eigen_vectors.shape[1] // tm
     vectors = lax.dynamic_slice_in_dim(eigen_vectors, me * rows, rows, 1)
     operator, modes, weights = rebuild_first(
-        inverse_energy[None, :], vectors.T, first, coeffs, cells, 4
-    )
-    return operator, rebuild_last(weights, last, modes, begin, 2)
+        inverse_energy[None, :], vectors.T, first, coeffs, cells, 9
+    )
+    return operator, rebuild_last(weights, last, modes, begin, 6)
 
 
 def solution(mesh):

time: 30.1 us -> 30 us (level)
  no operation moved by 1% of the time
where the time goes in v22:
time: 30 us; the launch traced here: 29.9 us
  starting transfers between devices  11.2 us (37%)
  waiting for transfers between devices  10.1 us (34%)
  Pallas kernels  7.68 us (26%)
  between operations  0.71 us (2%)
    ppermute x5, waiting for transfers between devices, swapped(): return lax.ppermute(value, axis, route)  6.82 us
    ppermute x5, starting transfers between devices, swapped(): return lax.ppermute(value, axis, route)  6.21 us
    ppermute x5, starting transfers between devices, moved(): return lax.ppermute(value, ('tm', 'inner'), route)  5.03 us
    ppermute x5, waiting for transfers between devices, moved(): return lax.ppermute(value, ('tm', 'inner'), route)  3.25 us
    pallas_call x1, Pallas kernels, project(): pl.pallas_call(functools.partial(project_kernel, tiles), out_shape=(half,...  2.82 us
    pallas_call x1, Pallas kernels, rebuild_first(): pl.pallas_call(functools.partial(first_kernel, tiles), out_shape=(jax.Sha...  2.52 us
    pallas_call x1, Pallas kernels, cut(): pl.pallas_call(cut_kernel, out_shape=jax.ShapeDtypeStruct((fields.shape[0...  1.2 us
    pallas_call x1, Pallas kernels, rebuild_last(): pl.pallas_call(functools.partial(last_kernel, begin, tiles), out_shape=ja...  1.14 us
  transfers between devices with their start and end apart: 10, of which 8 were waited for; matrix products, arithmetic and copies ran while one was open for 0% of the time, Pallas kernels for 18%

profile of v22, /device:TPU:0, one launch (start us, length us, event | category | flops | bytes accessed | tf_op | source)
XLA Modules:
  0.0 29.9 jit_solution(5189885278840304149)
XLA Ops:
  0.6 0.0 copy-start
  0.6 0.0 copy-start.1
  0.7 1.2 %cut.1.early.refs_0_ = bf16[64,6656]{1,0:T(8,128)(2,1)S(1)} custom-call(bf16[64,8192]{1,0:T(8,128)(2,1)} %bitcast.5), custom_call_target="tpu_custom_call" | custom-call | tf_op jit(solution)/shard_map/cut/pallas_call | solution.py:54
  1.9 3.0 %collective-permute-start = (bf16[64,6656]{1,0:T(8,128)(2,1)S(1)}, bf16[64,6656]{1,0:T(8,128)(2,1)S(1)}, u32[]{:S(2)}, u32[]{:S(2)}) collective-permute-start(bf16[64,6656]{1,0:T(8,128)(2,1)S(1)} %cut.1.early.refs_0_), channel_id=1, source_target_pairs={{16,0},{17,1},{0,16},{1,17},{18,2},{19,3},{2,18},{3,19},{20,4},{21... | collective-permute-start | bytes 2555912 | tf_op jit(solution)/shard_map/ppermute | solution.py:236
  4.9 2.8 %project.1 = (f32[32,256]{1,0:T(8,128)S(1)}, f32[32,256]{1,0:T(8,128)S(1)}, bf16[64,1536]{1,0:T(8,128)(2,1)S(1)}) custom-call(bf16[64,6656]{1,0:T(8,128)(2,1)S(1)} %cut.1.early.refs_0_, bf16[64,8192]{1,0:T(8,128)(2,1)} %bitcast.6, bf16[8192,256]{1,0:T(8,128)(2,1)} %basis.1), custom_call_target="tpu_custom_call" | custom-call | tf_op jit(solution)/shard_map/project/pallas_call | solution.py:100
  7.7 0.1 collective-permute-start.1
  7.8 1.2 %collective-permute-done.1 = f32[32,256]{1,0:T(8,128)S(1)} collective-permute-done((f32[32,256]{1,0:T(8,128)S(1)}, f32[32,256]{1,0:T(8,128)S(1)}, u32[]{:S(2)}, u32[]{:S(2)}) %collective-permute-start.1) | collective-permute-done | bytes 32800 | tf_op jit(solution)/shard_map/ppermute | solution.py:226
  9.0 2.5 %collective-permute-start.4 = (f32[32,256]{1,0:T(8,128)S(1)}, f32[32,256]{1,0:T(8,128)S(1)}, u32[]{:S(2)}, u32[]{:S(2)}) collective-permute-start(f32[32,256]{1,0:T(8,128)S(1)} %add.19), channel_id=1, source_target_pairs={{6,0},{4,2},{2,4},{0,6},{14,8},{12,10},{10,12},{8,14},{7,1},{5,3},... | collective-permute-start | bytes 98312 | tf_op jit(solution)/shard_map/ppermute | solution.py:226
  11.5 0.4 %collective-permute-start.3 = (f32[32,256]{1,0:T(8,128)S(1)}, f32[32,256]{1,0:T(8,128)S(1)}, u32[]{:S(2)}, u32[]{:S(2)}) collective-permute-start(f32[32,256]{1,0:T(8,128)S(1)} %add.19), channel_id=1, source_target_pairs={{4,0},{6,2},{0,4},{2,6},{12,8},{14,10},{8,12},{10,14},{5,1},{7,3},... | collective-permute-start | bytes 98312 | tf_op jit(solution)/shard_map/ppermute | solution.py:226
  12.0 0.5 %collective-permute-start.2 = (f32[32,256]{1,0:T(8,128)S(1)}, f32[32,256]{1,0:T(8,128)S(1)}, u32[]{:S(2)}, u32[]{:S(2)}) collective-permute-start(f32[32,256]{1,0:T(8,128)S(1)} %add.19), channel_id=1, source_target_pairs={{2,0},{0,2},{6,4},{4,6},{10,8},{8,10},{14,12},{12,14},{3,1},{1,3},... | collective-permute-start | bytes 98312 | tf_op jit(solution)/shard_map/ppermute | solution.py:226
  12.5 1.3 %collective-permute-done.4 = f32[32,256]{1,0:T(8,128)S(1)} collective-permute-done((f32[32,256]{1,0:T(8,128)S(1)}, f32[32,256]{1,0:T(8,128)S(1)}, u32[]{:S(2)}, u32[]{:S(2)}) %collective-permute-start.4) | collective-permute-done | bytes 32800 | tf_op jit(solution)/shard_map/ppermute | solution.py:226
  13.8 1.6 %collective-permute-done.3 = f32[32,256]{1,0:T(8,128)S(1)} collective-permute-done((f32[32,256]{1,0:T(8,128)S(1)}, f32[32,256]{1,0:T(8,128)S(1)}, u32[]{:S(2)}, u32[]{:S(2)}) %collective-permute-start.3) | collective-permute-done | bytes 32800 | tf_op jit(solution)/shard_map/ppermute | solution.py:226
  15.4 0.4 %collective-permute-done.2 = f32[32,256]{1,0:T(8,128)S(1)} collective-permute-done((f32[32,256]{1,0:T(8,128)S(1)}, f32[32,256]{1,0:T(8,128)S(1)}, u32[]{:S(2)}, u32[]{:S(2)}) %collective-permute-start.2) | collective-permute-done | bytes 32800 | tf_op jit(solution)/shard_map/ppermute | solution.py:226
  15.9 2.7 %collective-permute-start.5 = (f32[32,256]{1,0:T(8,128)S(1)}, f32[32,256]{1,0:T(8,128)S(1)}, u32[]{:S(2)}, u32[]{:S(2)}) collective-permute-start(f32[32,256]{1,0:T(8,128)S(1)} %add_add_fusion), channel_id=1, source_target_pairs={{8,0},{10,2},{12,4},{14,6},{0,8},{2,10},{4,12},{6,14},{9,1},{11,3}... | collective-permute-start | bytes 98312 | tf_op jit(solution)/shard_map/ppermute | solution.py:226
  18.5 2.2 %collective-permute-done.5 = f32[32,256]{1,0:T(8,128)S(1)} collective-permute-done((f32[32,256]{1,0:T(8,128)S(1)}, f32[32,256]{1,0:T(8,128)S(1)}, u32[]{:S(2)}, u32[]{:S(2)}) %collective-permute-start.5) | collective-permute-done | bytes 32800 | tf_op jit(solution)/shard_map/ppermute | solution.py:226
  20.8 0.5 %collective-permute-start.7 = (bf16[32,256]{1,0:T(8,128)(2,1)S(1)}, bf16[32,256]{1,0:T(8,128)(2,1)S(1)}, u32[]{:S(2)}, u32[]{:S(2)}) collective-permute-start(bf16[32,256]{1,0:T(8,128)(2,1)S(1)} %add_convert_fusion.refs_2_), channel_id=1, source_target_pairs={{16,0},{17,1},{0,16},{1,17},{18,2},{19,3},{2,18},{3,19},{20,4},{21... | collective-permute-start | bytes 49160 | tf_op jit(solution)/shard_map/ppermute | solution.py:236
  21.3 0.0 collective-permute-start.6
  21.3 1.5 %collective-permute-start.9 = (bf16[64,1536]{1,0:T(8,128)(2,1)S(1)}, bf16[64,1536]{1,0:T(8,128)(2,1)S(1)}, u32[]{:S(2)}, u32[]{:S(2)}) collective-permute-start(bf16[64,1536]{1,0:T(8,128)(2,1)S(1)} %get-tuple-element.16.refs_0_), channel_id=1, source_target_pairs={{16,0},{17,1},{0,16},{1,17},{18,2},{19,3},{2,18},{3,19},{20,4},{21... | collective-permute-start | bytes 589832 | tf_op jit(solution)/shard_map/ppermute | solution.py:236
  22.8 1.8 %collective-permute-done.7.refs_4_ = bf16[32,256]{1,0:T(8,128)(2,1)S(1)} collective-permute-done((bf16[32,256]{1,0:T(8,128)(2,1)S(1)}, bf16[32,256]{1,0:T(8,128)(2,1)S(1)}, u32[]{:S(2)}, u32[]{:S(2)}) %collective-permute-start.7) | collective-permute-done | bytes 16416 | tf_op jit(solution)/shard_map/ppermute | solution.py:236
  24.6 0.0 collective-permute-start.8
  24.6 0.0 copy-done
  24.6 0.1 copy.8
  24.7 0.0 collective-permute-done.6.refs_3_
  24.7 1.0 %collective-permute-done.8.refs_5_ = bf16[32,256]{1,0:T(8,128)(2,1)S(1)} collective-permute-done((bf16[32,256]{1,0:T(8,128)(2,1)S(1)}, bf16[32,256]{1,0:T(8,128)(2,1)S(1)}, u32[]{:S(2)}, u32[]{:S(2)}) %collective-permute-start.8) | collective-permute-done | bytes 16416 | tf_op jit(solution)/shard_map/ppermute | solution.py:236
  25.8 0.0 collective-permute-done.refs_1_
  25.8 0.0 copy-done.1
  25.8 2.5 %rebuild_first.1 = (f32[256,256]{1,0:T(8,128)}, bf16[256,8192]{1,0:T(8,128)(2,1)}, bf16[256,128]{1,0:T(8,128)(2,1)S(1)}) custom-call(f32[1,256]{1,0:T(1,128)S(1)} %bitcast.4, bf16[256,256]{1,0:T(8,128)(2,1)S(1)} %bitcast.3, bf16[64,6656]{1,0:T(8,128)(2,1)S(1)} %cut.1.early.refs_0_, bf16[64,6656]{1,0:T(8,128)(2,1)S(1)} %collective-permute-done.refs_1_, ...), custom_call_target="tpu_custom_call" | custom-call | flops 2000000000 | tf_op jit(solution)/shard_map/rebuild_first/pallas_call | solution.py:185
  28.3 0.4 %collective-permute-done.9.refs_1_ = bf16[64,1536]{1,0:T(8,128)(2,1)S(1)} collective-permute-done((bf16[64,1536]{1,0:T(8,128)(2,1)S(1)}, bf16[64,1536]{1,0:T(8,128)(2,1)S(1)}, u32[]{:S(2)}, u32[]{:S(2)}) %collective-permute-start.9) | collective-permute-done | bytes 196640 | tf_op jit(solution)/shard_map/ppermute | solution.py:236
  28.7 1.1 %rebuild_last.1 = bf16[256,8192]{1,0:T(8,128)(2,1)} custom-call(bf16[256,128]{1,0:T(8,128)(2,1)S(1)} %get-tuple-element.15.weights, bf16[64,1536]{1,0:T(8,128)(2,1)S(1)} %get-tuple-element.16.refs_0_, bf16[64,1536]{1,0:T(8,128)(2,1)S(1)} %collective-permute-done.9.refs_1_, bf16[256,8192]{1,0:T(8,128)(2,1)} %get-tuple-element.17.refs_2_), custom_call_target="tpu_custom_call", output_to_operand_aliasing={{}: (3, {})} | custom-call | tf_op jit(solution)/shard_map/rebuild_last/pallas_call | solution.py:208
  (4 shorter events, 0.0 us)
Async XLA Ops:
  0.6 24.0 %copy-start = (bf16[256,512]{1,0:T(8,128)(2,1)S(1)}, bf16[256,512]{1,0:T(8,128)(2,1)}, u32[]{:S(2)}) copy-start(bf16[256,512]{1,0:T(8,128)(2,1)} %param.7) | copy-start | bytes 786436
  0.6 25.1 %copy-start.1 = (f32[256]{0:T(256)S(1)}, f32[256]{0:T(256)}, u32[]{:S(2)}) copy-start(f32[256]{0:T(256)} %param.6) | copy-start | bytes 3076
  1.9 23.9 %collective-permute-start = (bf16[64,6656]{1,0:T(8,128)(2,1)S(1)}, bf16[64,6656]{1,0:T(8,128)(2,1)S(1)}, u32[]{:S(2)}, u32[]{:S(2)}) collective-permute-start(bf16[64,6656]{1,0:T(8,128)(2,1)S(1)} %cut.1.early.refs_0_), channel_id=1, source_target_pairs={{16,0},{17,1},{0,16},{1,17},{18,2},{19,3},{2,18},{3,19},{20,4},{21... | collective-permute-start | bytes 2555912 | tf_op jit(solution)/shard_map/ppermute | solution.py:236
  7.7 1.3 %collective-permute-start.1 = (f32[32,256]{1,0:T(8,128)S(1)}, f32[32,256]{1,0:T(8,128)S(1)}, u32[]{:S(2)}, u32[]{:S(2)}) collective-permute-start(f32[32,256]{1,0:T(8,128)S(1)} %get-tuple-element.11), channel_id=1, source_target_pairs={{1,0},{0,1},{3,2},{2,3},{5,4},{4,5},{7,6},{6,7},{9,8},{8,9},{11,10... | collective-permute-start | bytes 98312 | tf_op jit(solution)/shard_map/ppermute | solution.py:226
  9.0 4.8 %collective-permute-start.4 = (f32[32,256]{1,0:T(8,128)S(1)}, f32[32,256]{1,0:T(8,128)S(1)}, u32[]{:S(2)}, u32[]{:S(2)}) collective-permute-start(f32[32,256]{1,0:T(8,128)S(1)} %add.19), channel_id=1, source_target_pairs={{6,0},{4,2},{2,4},{0,6},{14,8},{12,10},{10,12},{8,14},{7,1},{5,3},... | collective-permute-start | bytes 98312 | tf_op jit(solution)/shard_map/ppermute | solution.py:226
  11.5 3.9 %collective-permute-start.3 = (f32[32,256]{1,0:T(8,128)S(1)}, f32[32,256]{1,0:T(8,128)S(1)}, u32[]{:S(2)}, u32[]{:S(2)}) collective-permute-start(f32[32,256]{1,0:T(8,128)S(1)} %add.19), channel_id=1, source_target_pairs={{4,0},{6,2},{0,4},{2,6},{12,8},{14,10},{8,12},{10,14},{5,1},{7,3},... | collective-permute-start | bytes 98312 | tf_op jit(solution)/shard_map/ppermute | solution.py:226
  12.0 3.9 %collective-permute-start.2 = (f32[32,256]{1,0:T(8,128)S(1)}, f32[32,256]{1,0:T(8,128)S(1)}, u32[]{:S(2)}, u32[]{:S(2)}) collective-permute-start(f32[32,256]{1,0:T(8,128)S(1)} %add.19), channel_id=1, source_target_pairs={{2,0},{0,2},{6,4},{4,6},{10,8},{8,10},{14,12},{12,14},{3,1},{1,3},... | collective-permute-start | bytes 98312 | tf_op jit(solution)/shard_map/ppermute | solution.py:226
  15.9 4.9 %collective-permute-start.5 = (f32[32,256]{1,0:T(8,128)S(1)}, f32[32,256]{1,0:T(8,128)S(1)}, u32[]{:S(2)}, u32[]{:S(2)}) collective-permute-start(f32[32,256]{1,0:T(8,128)S(1)} %add_add_fusion), channel_id=1, source_target_pairs={{8,0},{10,2},{12,4},{14,6},{0,8},{2,10},{4,12},{6,14},{9,1},{11,3}... | collective-permute-start | bytes 98312 | tf_op jit(solution)/shard_map/ppermute | solution.py:226
  20.8 3.8 %collective-permute-start.7 = (bf16[32,256]{1,0:T(8,128)(2,1)S(1)}, bf16[32,256]{1,0:T(8,128)(2,1)S(1)}, u32[]{:S(2)}, u32[]{:S(2)}) collective-permute-start(bf16[32,256]{1,0:T(8,128)(2,1)S(1)} %add_convert_fusion.refs_2_), channel_id=1, source_target_pairs={{16,0},{17,1},{0,16},{1,17},{18,2},{19,3},{2,18},{3,19},{20,4},{21... | collective-permute-start | bytes 49160 | tf_op jit(solution)/shard_map/ppermute | solution.py:236
  21.3 3.4 %collective-permute-start.6 = (bf16[32,256]{1,0:T(8,128)(2,1)S(1)}, bf16[32,256]{1,0:T(8,128)(2,1)S(1)}, u32[]{:S(2)}, u32[]{:S(2)}) collective-permute-start(bf16[32,256]{1,0:T(8,128)(2,1)S(1)} %add_convert_fusion.refs_2_), channel_id=1, source_target_pairs={{1,0},{0,1},{17,16},{16,17},{3,2},{2,3},{19,18},{18,19},{5,4},{4,5... | collective-permute-start | bytes 49160 | tf_op jit(solution)/shard_map/ppermute | solution.py:236
  21.3 7.4 %collective-permute-start.9 = (bf16[64,1536]{1,0:T(8,128)(2,1)S(1)}, bf16[64,1536]{1,0:T(8,128)(2,1)S(1)}, u32[]{:S(2)}, u32[]{:S(2)}) collective-permute-start(bf16[64,1536]{1,0:T(8,128)(2,1)S(1)} %get-tuple-element.16.refs_0_), channel_id=1, source_target_pairs={{16,0},{17,1},{0,16},{1,17},{18,2},{19,3},{2,18},{3,19},{20,4},{21... | collective-permute-start | bytes 589832 | tf_op jit(solution)/shard_map/ppermute | solution.py:236
  24.6 1.2 %collective-permute-start.8 = (bf16[32,256]{1,0:T(8,128)(2,1)S(1)}, bf16[32,256]{1,0:T(8,128)(2,1)S(1)}, u32[]{:S(2)}, u32[]{:S(2)}) collective-permute-start(bf16[32,256]{1,0:T(8,128)(2,1)S(1)} %collective-permute-done.7.refs_4_), channel_id=1, source_target_pairs={{1,0},{0,1},{17,16},{16,17},{3,2},{2,3},{19,18},{18,19},{5,4},{4,5... | collective-permute-start | bytes 49160 | tf_op jit(solution)/shard_map/ppermute | solution.py:236

commit v23 on v22

--- a/solution.py
+++ b/solution.py
@@ -10,7 +10,7 @@
 ROWS = (((1,), (0,)), ((), ()))
 FIRST = (((0,), (0,)), ((), ()))
 LAST = (((1,), (1,)), ((), ()))
-STRIP = 256
+STRIP = 512
 FREE = pl.CostEstimate(flops=0, bytes_accessed=0, transcendentals=0)
 LONG = pl.CostEstimate(flops=2 * 10**9, bytes_accessed=0, transcendentals=0)
 ANYWHERE = pl.BlockSpec(memory_space=pl.ANY)
@@ -269,9 +269,9 @@
     rows = eigen_vectors.shape[1] // tm
     vectors = lax.dynamic_slice_in_dim(eigen_vectors, me * rows, rows, 1)
     operator, modes, weights = rebuild_first(
-        inverse_energy[None, :], vectors.T, first, coeffs, cells, 9
-    )
-    return operator, rebuild_last(weights, last, modes, begin, 6)
+        inverse_energy[None, :], vectors.T, first, coeffs, cells, 6
+    )
+    return operator, rebuild_last(weights, last, modes, begin, 3)
 
 
 def solution(mesh):

time: 30 us -> 30 us (level)
  no operation moved by 1% of the time
where the time goes in v23:
time: 30 us; the launch traced here: 29.8 us
  starting transfers between devices  11.2 us (37%)
  waiting for transfers between devices  10 us (33%)
  Pallas kernels  7.7 us (26%)
  between operations  0.71 us (2%)
    ppermute x5, waiting for transfers between devices, swapped(): return lax.ppermute(value, axis, route)  6.82 us
    ppermute x5, starting transfers between devices, swapped(): return lax.ppermute(value, axis, route)  6.21 us
    ppermute x5, starting transfers between devices, moved(): return lax.ppermute(value, ('tm', 'inner'), route)  5.03 us
    ppermute x5, waiting for transfers between devices, moved(): return lax.ppermute(value, ('tm', 'inner'), route)  3.21 us
    pallas_call x1, Pallas kernels, project(): pl.pallas_call(functools.partial(project_kernel, tiles), out_shape=(half,...  2.82 us
    pallas_call x1, Pallas kernels, rebuild_first(): pl.pallas_call(functools.partial(first_kernel, tiles), out_shape=(jax.Sha...  2.56 us
    pallas_call x1, Pallas kernels, cut(): pl.pallas_call(cut_kernel, out_shape=jax.ShapeDtypeStruct((fields.shape[0...  1.2 us
    pallas_call x1, Pallas kernels, rebuild_last(): pl.pallas_call(functools.partial(last_kernel, begin, tiles), out_shape=ja...  1.12 us
  transfers between devices with their start and end apart: 10, of which 8 were waited for; matrix products, arithmetic and copies ran while one was open for 0% of the time, Pallas kernels for 18%

profile of v23, /device:TPU:0, one launch (start us, length us, event | category | flops | bytes accessed | tf_op | source)
XLA Modules:
  0.0 29.8 jit_solution(15350968122547433760)
XLA Ops:
  0.6 0.0 copy-start
  0.6 0.0 copy-start.1
  0.7 1.2 %cut.1.early.refs_0_ = bf16[64,6656]{1,0:T(8,128)(2,1)S(1)} custom-call(bf16[64,8192]{1,0:T(8,128)(2,1)} %bitcast.5), custom_call_target="tpu_custom_call" | custom-call | tf_op jit(solution)/shard_map/cut/pallas_call | solution.py:54
  1.9 3.0 %collective-permute-start = (bf16[64,6656]{1,0:T(8,128)(2,1)S(1)}, bf16[64,6656]{1,0:T(8,128)(2,1)S(1)}, u32[]{:S(2)}, u32[]{:S(2)}) collective-permute-start(bf16[64,6656]{1,0:T(8,128)(2,1)S(1)} %cut.1.early.refs_0_), channel_id=1, source_target_pairs={{16,0},{17,1},{0,16},{1,17},{18,2},{19,3},{2,18},{3,19},{20,4},{21... | collective-permute-start | bytes 2555912 | tf_op jit(solution)/shard_map/ppermute | solution.py:236
  4.9 2.8 %project.1 = (f32[32,256]{1,0:T(8,128)S(1)}, f32[32,256]{1,0:T(8,128)S(1)}, bf16[64,1536]{1,0:T(8,128)(2,1)S(1)}) custom-call(bf16[64,6656]{1,0:T(8,128)(2,1)S(1)} %cut.1.early.refs_0_, bf16[64,8192]{1,0:T(8,128)(2,1)} %bitcast.6, bf16[8192,256]{1,0:T(8,128)(2,1)} %basis.1), custom_call_target="tpu_custom_call" | custom-call | tf_op jit(solution)/shard_map/project/pallas_call | solution.py:100
  7.7 0.1 collective-permute-start.1
  7.8 1.2 %collective-permute-done.1 = f32[32,256]{1,0:T(8,128)S(1)} collective-permute-done((f32[32,256]{1,0:T(8,128)S(1)}, f32[32,256]{1,0:T(8,128)S(1)}, u32[]{:S(2)}, u32[]{:S(2)}) %collective-permute-start.1) | collective-permute-done | bytes 32800 | tf_op jit(solution)/shard_map/ppermute | solution.py:226
  9.0 2.5 %collective-permute-start.4 = (f32[32,256]{1,0:T(8,128)S(1)}, f32[32,256]{1,0:T(8,128)S(1)}, u32[]{:S(2)}, u32[]{:S(2)}) collective-permute-start(f32[32,256]{1,0:T(8,128)S(1)} %add.19), channel_id=1, source_target_pairs={{6,0},{4,2},{2,4},{0,6},{14,8},{12,10},{10,12},{8,14},{7,1},{5,3},... | collective-permute-start | bytes 98312 | tf_op jit(solution)/shard_map/ppermute | solution.py:226
  11.5 0.4 %collective-permute-start.3 = (f32[32,256]{1,0:T(8,128)S(1)}, f32[32,256]{1,0:T(8,128)S(1)}, u32[]{:S(2)}, u32[]{:S(2)}) collective-permute-start(f32[32,256]{1,0:T(8,128)S(1)} %add.19), channel_id=1, source_target_pairs={{4,0},{6,2},{0,4},{2,6},{12,8},{14,10},{8,12},{10,14},{5,1},{7,3},... | collective-permute-start | bytes 98312 | tf_op jit(solution)/shard_map/ppermute | solution.py:226
  12.0 0.5 %collective-permute-start.2 = (f32[32,256]{1,0:T(8,128)S(1)}, f32[32,256]{1,0:T(8,128)S(1)}, u32[]{:S(2)}, u32[]{:S(2)}) collective-permute-start(f32[32,256]{1,0:T(8,128)S(1)} %add.19), channel_id=1, source_target_pairs={{2,0},{0,2},{6,4},{4,6},{10,8},{8,10},{14,12},{12,14},{3,1},{1,3},... | collective-permute-start | bytes 98312 | tf_op jit(solution)/shard_map/ppermute | solution.py:226
  12.5 1.3 %collective-permute-done.4 = f32[32,256]{1,0:T(8,128)S(1)} collective-permute-done((f32[32,256]{1,0:T(8,128)S(1)}, f32[32,256]{1,0:T(8,128)S(1)}, u32[]{:S(2)}, u32[]{:S(2)}) %collective-permute-start.4) | collective-permute-done | bytes 32800 | tf_op jit(solution)/shard_map/ppermute | solution.py:226
  13.8 1.6 %collective-permute-done.3 = f32[32,256]{1,0:T(8,128)S(1)} collective-permute-done((f32[32,256]{1,0:T(8,128)S(1)}, f32[32,256]{1,0:T(8,128)S(1)}, u32[]{:S(2)}, u32[]{:S(2)}) %collective-permute-start.3) | collective-permute-done | bytes 32800 | tf_op jit(solution)/shard_map/ppermute | solution.py:226
  15.4 0.4 %collective-permute-done.2 = f32[32,256]{1,0:T(8,128)S(1)} collective-permute-done((f32[32,256]{1,0:T(8,128)S(1)}, f32[32,256]{1,0:T(8,128)S(1)}, u32[]{:S(2)}, u32[]{:S(2)}) %collective-permute-start.2) | collective-permute-done | bytes 32800 | tf_op jit(solution)/shard_map/ppermute | solution.py:226
  15.9 2.7 %collective-permute-start.5 = (f32[32,256]{1,0:T(8,128)S(1)}, f32[32,256]{1,0:T(8,128)S(1)}, u32[]{:S(2)}, u32[]{:S(2)}) collective-permute-start(f32[32,256]{1,0:T(8,128)S(1)} %add_add_fusion), channel_id=1, source_target_pairs={{8,0},{10,2},{12,4},{14,6},{0,8},{2,10},{4,12},{6,14},{9,1},{11,3}... | collective-permute-start | bytes 98312 | tf_op jit(solution)/shard_map/ppermute | solution.py:226
  18.5 2.2 %collective-permute-done.5 = f32[32,256]{1,0:T(8,128)S(1)} collective-permute-done((f32[32,256]{1,0:T(8,128)S(1)}, f32[32,256]{1,0:T(8,128)S(1)}, u32[]{:S(2)}, u32[]{:S(2)}) %collective-permute-start.5) | collective-permute-done | bytes 32800 | tf_op jit(solution)/shard_map/ppermute | solution.py:226
  20.8 0.5 %collective-permute-start.7 = (bf16[32,256]{1,0:T(8,128)(2,1)S(1)}, bf16[32,256]{1,0:T(8,128)(2,1)S(1)}, u32[]{:S(2)}, u32[]{:S(2)}) collective-permute-start(bf16[32,256]{1,0:T(8,128)(2,1)S(1)} %add_convert_fusion.refs_2_), channel_id=1, source_target_pairs={{16,0},{17,1},{0,16},{1,17},{18,2},{19,3},{2,18},{3,19},{20,4},{21... | collective-permute-start | bytes 49160 | tf_op jit(solution)/shard_map/ppermute | solution.py:236
  21.3 0.0 collective-permute-start.6
  21.3 1.5 %collective-permute-start.9 = (bf16[64,1536]{1,0:T(8,128)(2,1)S(1)}, bf16[64,1536]{1,0:T(8,128)(2,1)S(1)}, u32[]{:S(2)}, u32[]{:S(2)}) collective-permute-start(bf16[64,1536]{1,0:T(8,128)(2,1)S(1)} %get-tuple-element.16.refs_0_), channel_id=1, source_target_pairs={{16,0},{17,1},{0,16},{1,17},{18,2},{19,3},{2,18},{3,19},{20,4},{21... | collective-permute-start | bytes 589832 | tf_op jit(solution)/shard_map/ppermute | solution.py:236
  22.8 1.8 %collective-permute-done.7.refs_4_ = bf16[32,256]{1,0:T(8,128)(2,1)S(1)} collective-permute-done((bf16[32,256]{1,0:T(8,128)(2,1)S(1)}, bf16[32,256]{1,0:T(8,128)(2,1)S(1)}, u32[]{:S(2)}, u32[]{:S(2)}) %collective-permute-start.7) | collective-permute-done | bytes 16416 | tf_op jit(solution)/shard_map/ppermute | solution.py:236
  24.6 0.0 collective-permute-start.8
  24.6 0.0 copy-done
  24.6 0.1 copy.8
  24.7 0.0 collective-permute-done.6.refs_3_
  24.7 1.0 %collective-permute-done.8.refs_5_ = bf16[32,256]{1,0:T(8,128)(2,1)S(1)} collective-permute-done((bf16[32,256]{1,0:T(8,128)(2,1)S(1)}, bf16[32,256]{1,0:T(8,128)(2,1)S(1)}, u32[]{:S(2)}, u32[]{:S(2)}) %collective-permute-start.8) | collective-permute-done | bytes 16416 | tf_op jit(solution)/shard_map/ppermute | solution.py:236
  25.8 0.0 collective-permute-done.refs_1_
  25.8 0.0 copy-done.1
  25.8 2.6 %rebuild_first.1 = (f32[256,256]{1,0:T(8,128)}, bf16[256,8192]{1,0:T(8,128)(2,1)}, bf16[256,128]{1,0:T(8,128)(2,1)S(1)}) custom-call(f32[1,256]{1,0:T(1,128)S(1)} %bitcast.4, bf16[256,256]{1,0:T(8,128)(2,1)S(1)} %bitcast.3, bf16[64,6656]{1,0:T(8,128)(2,1)S(1)} %cut.1.early.refs_0_, bf16[64,6656]{1,0:T(8,128)(2,1)S(1)} %collective-permute-done.refs_1_, ...), custom_call_target="tpu_custom_call" | custom-call | flops 2000000000 | tf_op jit(solution)/shard_map/rebuild_first/pallas_call | solution.py:185
  28.4 0.4 %collective-permute-done.9.refs_1_ = bf16[64,1536]{1,0:T(8,128)(2,1)S(1)} collective-permute-done((bf16[64,1536]{1,0:T(8,128)(2,1)S(1)}, bf16[64,1536]{1,0:T(8,128)(2,1)S(1)}, u32[]{:S(2)}, u32[]{:S(2)}) %collective-permute-start.9) | collective-permute-done | bytes 196640 | tf_op jit(solution)/shard_map/ppermute | solution.py:236
  28.7 1.1 %rebuild_last.1 = bf16[256,8192]{1,0:T(8,128)(2,1)} custom-call(bf16[256,128]{1,0:T(8,128)(2,1)S(1)} %get-tuple-element.15.weights, bf16[64,1536]{1,0:T(8,128)(2,1)S(1)} %get-tuple-element.16.refs_0_, bf16[64,1536]{1,0:T(8,128)(2,1)S(1)} %collective-permute-done.9.refs_1_, bf16[256,8192]{1,0:T(8,128)(2,1)} %get-tuple-element.17.refs_2_), custom_call_target="tpu_custom_call", output_to_operand_aliasing={{}: (3, {})} | custom-call | tf_op jit(solution)/shard_map/rebuild_last/pallas_call | solution.py:208
  (4 shorter events, 0.0 us)
Async XLA Ops:
  0.6 24.0 %copy-start = (bf16[256,512]{1,0:T(8,128)(2,1)S(1)}, bf16[256,512]{1,0:T(8,128)(2,1)}, u32[]{:S(2)}) copy-start(bf16[256,512]{1,0:T(8,128)(2,1)} %param.7) | copy-start | bytes 786436
  0.6 25.1 %copy-start.1 = (f32[256]{0:T(256)S(1)}, f32[256]{0:T(256)}, u32[]{:S(2)}) copy-start(f32[256]{0:T(256)} %param.6) | copy-start | bytes 3076
  1.9 23.9 %collective-permute-start = (bf16[64,6656]{1,0:T(8,128)(2,1)S(1)}, bf16[64,6656]{1,0:T(8,128)(2,1)S(1)}, u32[]{:S(2)}, u32[]{:S(2)}) collective-permute-start(bf16[64,6656]{1,0:T(8,128)(2,1)S(1)} %cut.1.early.refs_0_), channel_id=1, source_target_pairs={{16,0},{17,1},{0,16},{1,17},{18,2},{19,3},{2,18},{3,19},{20,4},{21... | collective-permute-start | bytes 2555912 | tf_op jit(solution)/shard_map/ppermute | solution.py:236
  7.7 1.3 %collective-permute-start.1 = (f32[32,256]{1,0:T(8,128)S(1)}, f32[32,256]{1,0:T(8,128)S(1)}, u32[]{:S(2)}, u32[]{:S(2)}) collective-permute-start(f32[32,256]{1,0:T(8,128)S(1)} %get-tuple-element.11), channel_id=1, source_target_pairs={{1,0},{0,1},{3,2},{2,3},{5,4},{4,5},{7,6},{6,7},{9,8},{8,9},{11,10... | collective-permute-start | bytes 98312 | tf_op jit(solution)/shard_map/ppermute | solution.py:226
  9.0 4.8 %collective-permute-start.4 = (f32[32,256]{1,0:T(8,128)S(1)}, f32[32,256]{1,0:T(8,128)S(1)}, u32[]{:S(2)}, u32[]{:S(2)}) collective-permute-start(f32[32,256]{1,0:T(8,128)S(1)} %add.19), channel_id=1, source_target_pairs={{6,0},{4,2},{2,4},{0,6},{14,8},{12,10},{10,12},{8,14},{7,1},{5,3},... | collective-permute-start | bytes 98312 | tf_op jit(solution)/shard_map/ppermute | solution.py:226
  11.5 3.9 %collective-permute-start.3 = (f32[32,256]{1,0:T(8,128)S(1)}, f32[32,256]{1,0:T(8,128)S(1)}, u32[]{:S(2)}, u32[]{:S(2)}) collective-permute-start(f32[32,256]{1,0:T(8,128)S(1)} %add.19), channel_id=1, source_target_pairs={{4,0},{6,2},{0,4},{2,6},{12,8},{14,10},{8,12},{10,14},{5,1},{7,3},... | collective-permute-start | bytes 98312 | tf_op jit(solution)/shard_map/ppermute | solution.py:226
  12.0 3.9 %collective-permute-start.2 = (f32[32,256]{1,0:T(8,128)S(1)}, f32[32,256]{1,0:T(8,128)S(1)}, u32[]{:S(2)}, u32[]{:S(2)}) collective-permute-start(f32[32,256]{1,0:T(8,128)S(1)} %add.19), channel_id=1, source_target_pairs={{2,0},{0,2},{6,4},{4,6},{10,8},{8,10},{14,12},{12,14},{3,1},{1,3},... | collective-permute-start | bytes 98312 | tf_op jit(solution)/shard_map/ppermute | solution.py:226
  15.9 4.9 %collective-permute-start.5 = (f32[32,256]{1,0:T(8,128)S(1)}, f32[32,256]{1,0:T(8,128)S(1)}, u32[]{:S(2)}, u32[]{:S(2)}) collective-permute-start(f32[32,256]{1,0:T(8,128)S(1)} %add_add_fusion), channel_id=1, source_target_pairs={{8,0},{10,2},{12,4},{14,6},{0,8},{2,10},{4,12},{6,14},{9,1},{11,3}... | collective-permute-start | bytes 98312 | tf_op jit(solution)/shard_map/ppermute | solution.py:226
  20.8 3.8 %collective-permute-start.7 = (bf16[32,256]{1,0:T(8,128)(2,1)S(1)}, bf16[32,256]{1,0:T(8,128)(2,1)S(1)}, u32[]{:S(2)}, u32[]{:S(2)}) collective-permute-start(bf16[32,256]{1,0:T(8,128)(2,1)S(1)} %add_convert_fusion.refs_2_), channel_id=1, source_target_pairs={{16,0},{17,1},{0,16},{1,17},{18,2},{19,3},{2,18},{3,19},{20,4},{21... | collective-permute-start | bytes 49160 | tf_op jit(solution)/shard_map/ppermute | solution.py:236
  21.3 3.4 %collective-permute-start.6 = (bf16[32,256]{1,0:T(8,128)(2,1)S(1)}, bf16[32,256]{1,0:T(8,128)(2,1)S(1)}, u32[]{:S(2)}, u32[]{:S(2)}) collective-permute-start(bf16[32,256]{1,0:T(8,128)(2,1)S(1)} %add_convert_fusion.refs_2_), channel_id=1, source_target_pairs={{1,0},{0,1},{17,16},{16,17},{3,2},{2,3},{19,18},{18,19},{5,4},{4,5... | collective-permute-start | bytes 49160 | tf_op jit(solution)/shard_map/ppermute | solution.py:236
  21.3 7.4 %collective-permute-start.9 = (bf16[64,1536]{1,0:T(8,128)(2,1)S(1)}, bf16[64,1536]{1,0:T(8,128)(2,1)S(1)}, u32[]{:S(2)}, u32[]{:S(2)}) collective-permute-start(bf16[64,1536]{1,0:T(8,128)(2,1)S(1)} %get-tuple-element.16.refs_0_), channel_id=1, source_target_pairs={{16,0},{17,1},{0,16},{1,17},{18,2},{19,3},{2,18},{3,19},{20,4},{21... | collective-permute-start | bytes 589832 | tf_op jit(solution)/shard_map/ppermute | solution.py:236
  24.6 1.2 %collective-permute-start.8 = (bf16[32,256]{1,0:T(8,128)(2,1)S(1)}, bf16[32,256]{1,0:T(8,128)(2,1)S(1)}, u32[]{:S(2)}, u32[]{:S(2)}) collective-permute-start(bf16[32,256]{1,0:T(8,128)(2,1)S(1)} %collective-permute-done.7.refs_4_), channel_id=1, source_target_pairs={{1,0},{0,1},{17,16},{16,17},{3,2},{2,3},{19,18},{18,19},{5,4},{4,5... | collective-permute-start | bytes 49160 | tf_op jit(solution)/shard_map/ppermute | solution.py:236

commit v24 on v23

--- a/solution.py
+++ b/solution.py
@@ -166,8 +166,8 @@
     weights[...] = value
 
     def operate():
-        high, low = in_parts(scaled[...])
-        square[...] = product(every, high, FIRST) + product(every, low, FIRST)
+        lagged = lagged_and_scaled(known[...], 1.0).astype(jnp.bfloat16)
+        square[...] = product(every, lagged, FIRST) * energy[...]
         return started([pltpu.make_async_copy(square, operator, sent.at[tiles])])
 
     waited(rebuilt(value, [(b, 0) for b in held], made, modes, 0, tiles, sent, operate))

time: 30 us -> 30 us (level)
  no operation moved by 1% of the time
where the time goes in v24:
time: 30 us; the launch traced here: 29.8 us
  starting transfers between devices  11.2 us (37%)
  waiting for transfers between devices  10.1 us (34%)
  Pallas kernels  7.64 us (25%)
  between operations  0.71 us (2%)
    ppermute x5, waiting for transfers between devices, swapped(): return lax.ppermute(value, axis, route)  6.82 us
    ppermute x5, starting transfers between devices, swapped(): return lax.ppermute(value, axis, route)  6.21 us
    ppermute x5, starting transfers between devices, moved(): return lax.ppermute(value, ('tm', 'inner'), route)  5.03 us
    ppermute x5, waiting for transfers between devices, moved(): return lax.ppermute(value, ('tm', 'inner'), route)  3.28 us
    pallas_call x1, Pallas kernels, project(): pl.pallas_call(functools.partial(project_kernel, tiles), out_shape=(half,...  2.82 us
    pallas_call x1, Pallas kernels, rebuild_first(): pl.pallas_call(functools.partial(first_kernel, tiles), out_shape=(jax.Sha...  2.5 us
    pallas_call x1, Pallas kernels, cut(): pl.pallas_call(cut_kernel, out_shape=jax.ShapeDtypeStruct((fields.shape[0...  1.2 us
    pallas_call x1, Pallas kernels, rebuild_last(): pl.pallas_call(functools.partial(last_kernel, begin, tiles), out_shape=ja...  1.12 us
  transfers between devices with their start and end apart: 10, of which 8 were waited for; matrix products, arithmetic and copies ran while one was open for 0% of the time, Pallas kernels for 18%

profile of v24, /device:TPU:0, one launch (start us, length us, event | category | flops | bytes accessed | tf_op | source)
XLA Modules:
  0.0 29.8 jit_solution(9856352851396799979)
XLA Ops:
  0.6 0.0 copy-start
  0.6 0.0 copy-start.1
  0.7 1.2 %cut.1.early.refs_0_ = bf16[64,6656]{1,0:T(8,128)(2,1)S(1)} custom-call(bf16[64,8192]{1,0:T(8,128)(2,1)} %bitcast.5), custom_call_target="tpu_custom_call" | custom-call | tf_op jit(solution)/shard_map/cut/pallas_call | solution.py:54
  1.9 3.0 %collective-permute-start = (bf16[64,6656]{1,0:T(8,128)(2,1)S(1)}, bf16[64,6656]{1,0:T(8,128)(2,1)S(1)}, u32[]{:S(2)}, u32[]{:S(2)}) collective-permute-start(bf16[64,6656]{1,0:T(8,128)(2,1)S(1)} %cut.1.early.refs_0_), channel_id=1, source_target_pairs={{16,0},{17,1},{0,16},{1,17},{18,2},{19,3},{2,18},{3,19},{20,4},{21... | collective-permute-start | bytes 2555912 | tf_op jit(solution)/shard_map/ppermute | solution.py:236
  4.9 2.8 %project.1 = (f32[32,256]{1,0:T(8,128)S(1)}, f32[32,256]{1,0:T(8,128)S(1)}, bf16[64,1536]{1,0:T(8,128)(2,1)S(1)}) custom-call(bf16[64,6656]{1,0:T(8,128)(2,1)S(1)} %cut.1.early.refs_0_, bf16[64,8192]{1,0:T(8,128)(2,1)} %bitcast.6, bf16[8192,256]{1,0:T(8,128)(2,1)} %basis.1), custom_call_target="tpu_custom_call" | custom-call | tf_op jit(solution)/shard_map/project/pallas_call | solution.py:100
  7.7 0.1 collective-permute-start.1
  7.8 1.2 %collective-permute-done.1 = f32[32,256]{1,0:T(8,128)S(1)} collective-permute-done((f32[32,256]{1,0:T(8,128)S(1)}, f32[32,256]{1,0:T(8,128)S(1)}, u32[]{:S(2)}, u32[]{:S(2)}) %collective-permute-start.1) | collective-permute-done | bytes 32800 | tf_op jit(solution)/shard_map/ppermute | solution.py:226
  9.0 2.5 %collective-permute-start.4 = (f32[32,256]{1,0:T(8,128)S(1)}, f32[32,256]{1,0:T(8,128)S(1)}, u32[]{:S(2)}, u32[]{:S(2)}) collective-permute-start(f32[32,256]{1,0:T(8,128)S(1)} %add.19), channel_id=1, source_target_pairs={{6,0},{4,2},{2,4},{0,6},{14,8},{12,10},{10,12},{8,14},{7,1},{5,3},... | collective-permute-start | bytes 98312 | tf_op jit(solution)/shard_map/ppermute | solution.py:226
  11.5 0.4 %collective-permute-start.3 = (f32[32,256]{1,0:T(8,128)S(1)}, f32[32,256]{1,0:T(8,128)S(1)}, u32[]{:S(2)}, u32[]{:S(2)}) collective-permute-start(f32[32,256]{1,0:T(8,128)S(1)} %add.19), channel_id=1, source_target_pairs={{4,0},{6,2},{0,4},{2,6},{12,8},{14,10},{8,12},{10,14},{5,1},{7,3},... | collective-permute-start | bytes 98312 | tf_op jit(solution)/shard_map/ppermute | solution.py:226
  12.0 0.5 %collective-permute-start.2 = (f32[32,256]{1,0:T(8,128)S(1)}, f32[32,256]{1,0:T(8,128)S(1)}, u32[]{:S(2)}, u32[]{:S(2)}) collective-permute-start(f32[32,256]{1,0:T(8,128)S(1)} %add.19), channel_id=1, source_target_pairs={{2,0},{0,2},{6,4},{4,6},{10,8},{8,10},{14,12},{12,14},{3,1},{1,3},... | collective-permute-start | bytes 98312 | tf_op jit(solution)/shard_map/ppermute | solution.py:226
  12.5 1.3 %collective-permute-done.4 = f32[32,256]{1,0:T(8,128)S(1)} collective-permute-done((f32[32,256]{1,0:T(8,128)S(1)}, f32[32,256]{1,0:T(8,128)S(1)}, u32[]{:S(2)}, u32[]{:S(2)}) %collective-permute-start.4) | collective-permute-done | bytes 32800 | tf_op jit(solution)/shard_map/ppermute | solution.py:226
  13.8 1.6 %collective-permute-done.3 = f32[32,256]{1,0:T(8,128)S(1)} collective-permute-done((f32[32,256]{1,0:T(8,128)S(1)}, f32[32,256]{1,0:T(8,128)S(1)}, u32[]{:S(2)}, u32[]{:S(2)}) %collective-permute-start.3) | collective-permute-done | bytes 32800 | tf_op jit(solution)/shard_map/ppermute | solution.py:226
  15.4 0.4 %collective-permute-done.2 = f32[32,256]{1,0:T(8,128)S(1)} collective-permute-done((f32[32,256]{1,0:T(8,128)S(1)}, f32[32,256]{1,0:T(8,128)S(1)}, u32[]{:S(2)}, u32[]{:S(2)}) %collective-permute-start.2) | collective-permute-done | bytes 32800 | tf_op jit(solution)/shard_map/ppermute | solution.py:226
  15.9 2.7 %collective-permute-start.5 = (f32[32,256]{1,0:T(8,128)S(1)}, f32[32,256]{1,0:T(8,128)S(1)}, u32[]{:S(2)}, u32[]{:S(2)}) collective-permute-start(f32[32,256]{1,0:T(8,128)S(1)} %add_add_fusion), channel_id=1, source_target_pairs={{8,0},{10,2},{12,4},{14,6},{0,8},{2,10},{4,12},{6,14},{9,1},{11,3}... | collective-permute-start | bytes 98312 | tf_op jit(solution)/shard_map/ppermute | solution.py:226
  18.5 2.2 %collective-permute-done.5 = f32[32,256]{1,0:T(8,128)S(1)} collective-permute-done((f32[32,256]{1,0:T(8,128)S(1)}, f32[32,256]{1,0:T(8,128)S(1)}, u32[]{:S(2)}, u32[]{:S(2)}) %collective-permute-start.5) | collective-permute-done | bytes 32800 | tf_op jit(solution)/shard_map/ppermute | solution.py:226
  20.8 0.5 %collective-permute-start.7 = (bf16[32,256]{1,0:T(8,128)(2,1)S(1)}, bf16[32,256]{1,0:T(8,128)(2,1)S(1)}, u32[]{:S(2)}, u32[]{:S(2)}) collective-permute-start(bf16[32,256]{1,0:T(8,128)(2,1)S(1)} %add_convert_fusion.refs_2_), channel_id=1, source_target_pairs={{16,0},{17,1},{0,16},{1,17},{18,2},{19,3},{2,18},{3,19},{20,4},{21... | collective-permute-start | bytes 49160 | tf_op jit(solution)/shard_map/ppermute | solution.py:236
  21.3 0.0 collective-permute-start.6
  21.3 1.5 %collective-permute-start.9 = (bf16[64,1536]{1,0:T(8,128)(2,1)S(1)}, bf16[64,1536]{1,0:T(8,128)(2,1)S(1)}, u32[]{:S(2)}, u32[]{:S(2)}) collective-permute-start(bf16[64,1536]{1,0:T(8,128)(2,1)S(1)} %get-tuple-element.16.refs_0_), channel_id=1, source_target_pairs={{16,0},{17,1},{0,16},{1,17},{18,2},{19,3},{2,18},{3,19},{20,4},{21... | collective-permute-start | bytes 589832 | tf_op jit(solution)/shard_map/ppermute | solution.py:236
  22.8 1.8 %collective-permute-done.7.refs_4_ = bf16[32,256]{1,0:T(8,128)(2,1)S(1)} collective-permute-done((bf16[32,256]{1,0:T(8,128)(2,1)S(1)}, bf16[32,256]{1,0:T(8,128)(2,1)S(1)}, u32[]{:S(2)}, u32[]{:S(2)}) %collective-permute-start.7) | collective-permute-done | bytes 16416 | tf_op jit(solution)/shard_map/ppermute | solution.py:236
  24.6 0.0 collective-permute-start.8
  24.6 0.0 copy-done
  24.6 0.1 copy.8
  24.7 0.0 collective-permute-done.6.refs_3_
  24.7 1.0 %collective-permute-done.8.refs_5_ = bf16[32,256]{1,0:T(8,128)(2,1)S(1)} collective-permute-done((bf16[32,256]{1,0:T(8,128)(2,1)S(1)}, bf16[32,256]{1,0:T(8,128)(2,1)S(1)}, u32[]{:S(2)}, u32[]{:S(2)}) %collective-permute-start.8) | collective-permute-done | bytes 16416 | tf_op jit(solution)/shard_map/ppermute | solution.py:236
  25.8 0.0 collective-permute-done.refs_1_
  25.8 0.0 copy-done.1
  25.8 2.5 %rebuild_first.1 = (f32[256,256]{1,0:T(8,128)}, bf16[256,8192]{1,0:T(8,128)(2,1)}, bf16[256,128]{1,0:T(8,128)(2,1)S(1)}) custom-call(f32[1,256]{1,0:T(1,128)S(1)} %bitcast.4, bf16[256,256]{1,0:T(8,128)(2,1)S(1)} %bitcast.3, bf16[64,6656]{1,0:T(8,128)(2,1)S(1)} %cut.1.early.refs_0_, bf16[64,6656]{1,0:T(8,128)(2,1)S(1)} %collective-permute-done.refs_1_, ...), custom_call_target="tpu_custom_call" | custom-call | flops 2000000000 | tf_op jit(solution)/shard_map/rebuild_first/pallas_call | solution.py:185
  28.3 0.4 %collective-permute-done.9.refs_1_ = bf16[64,1536]{1,0:T(8,128)(2,1)S(1)} collective-permute-done((bf16[64,1536]{1,0:T(8,128)(2,1)S(1)}, bf16[64,1536]{1,0:T(8,128)(2,1)S(1)}, u32[]{:S(2)}, u32[]{:S(2)}) %collective-permute-start.9) | collective-permute-done | bytes 196640 | tf_op jit(solution)/shard_map/ppermute | solution.py:236
  28.7 1.1 %rebuild_last.1 = bf16[256,8192]{1,0:T(8,128)(2,1)} custom-call(bf16[256,128]{1,0:T(8,128)(2,1)S(1)} %get-tuple-element.15.weights, bf16[64,1536]{1,0:T(8,128)(2,1)S(1)} %get-tuple-element.16.refs_0_, bf16[64,1536]{1,0:T(8,128)(2,1)S(1)} %collective-permute-done.9.refs_1_, bf16[256,8192]{1,0:T(8,128)(2,1)} %get-tuple-element.17.refs_2_), custom_call_target="tpu_custom_call", output_to_operand_aliasing={{}: (3, {})} | custom-call | tf_op jit(solution)/shard_map/rebuild_last/pallas_call | solution.py:208
  (4 shorter events, 0.0 us)
Async XLA Ops:
  0.6 24.0 %copy-start = (bf16[256,512]{1,0:T(8,128)(2,1)S(1)}, bf16[256,512]{1,0:T(8,128)(2,1)}, u32[]{:S(2)}) copy-start(bf16[256,512]{1,0:T(8,128)(2,1)} %param.7) | copy-start | bytes 786436
  0.6 25.1 %copy-start.1 = (f32[256]{0:T(256)S(1)}, f32[256]{0:T(256)}, u32[]{:S(2)}) copy-start(f32[256]{0:T(256)} %param.6) | copy-start | bytes 3076
  1.9 23.9 %collective-permute-start = (bf16[64,6656]{1,0:T(8,128)(2,1)S(1)}, bf16[64,6656]{1,0:T(8,128)(2,1)S(1)}, u32[]{:S(2)}, u32[]{:S(2)}) collective-permute-start(bf16[64,6656]{1,0:T(8,128)(2,1)S(1)} %cut.1.early.refs_0_), channel_id=1, source_target_pairs={{16,0},{17,1},{0,16},{1,17},{18,2},{19,3},{2,18},{3,19},{20,4},{21... | collective-permute-start | bytes 2555912 | tf_op jit(solution)/shard_map/ppermute | solution.py:236
  7.7 1.3 %collective-permute-start.1 = (f32[32,256]{1,0:T(8,128)S(1)}, f32[32,256]{1,0:T(8,128)S(1)}, u32[]{:S(2)}, u32[]{:S(2)}) collective-permute-start(f32[32,256]{1,0:T(8,128)S(1)} %get-tuple-element.11), channel_id=1, source_target_pairs={{1,0},{0,1},{3,2},{2,3},{5,4},{4,5},{7,6},{6,7},{9,8},{8,9},{11,10... | collective-permute-start | bytes 98312 | tf_op jit(solution)/shard_map/ppermute | solution.py:226
  9.0 4.8 %collective-permute-start.4 = (f32[32,256]{1,0:T(8,128)S(1)}, f32[32,256]{1,0:T(8,128)S(1)}, u32[]{:S(2)}, u32[]{:S(2)}) collective-permute-start(f32[32,256]{1,0:T(8,128)S(1)} %add.19), channel_id=1, source_target_pairs={{6,0},{4,2},{2,4},{0,6},{14,8},{12,10},{10,12},{8,14},{7,1},{5,3},... | collective-permute-start | bytes 98312 | tf_op jit(solution)/shard_map/ppermute | solution.py:226
  11.5 3.9 %collective-permute-start.3 = (f32[32,256]{1,0:T(8,128)S(1)}, f32[32,256]{1,0:T(8,128)S(1)}, u32[]{:S(2)}, u32[]{:S(2)}) collective-permute-start(f32[32,256]{1,0:T(8,128)S(1)} %add.19), channel_id=1, source_target_pairs={{4,0},{6,2},{0,4},{2,6},{12,8},{14,10},{8,12},{10,14},{5,1},{7,3},... | collective-permute-start | bytes 98312 | tf_op jit(solution)/shard_map/ppermute | solution.py:226
  12.0 3.9 %collective-permute-start.2 = (f32[32,256]{1,0:T(8,128)S(1)}, f32[32,256]{1,0:T(8,128)S(1)}, u32[]{:S(2)}, u32[]{:S(2)}) collective-permute-start(f32[32,256]{1,0:T(8,128)S(1)} %add.19), channel_id=1, source_target_pairs={{2,0},{0,2},{6,4},{4,6},{10,8},{8,10},{14,12},{12,14},{3,1},{1,3},... | collective-permute-start | bytes 98312 | tf_op jit(solution)/shard_map/ppermute | solution.py:226
  15.9 4.9 %collective-permute-start.5 = (f32[32,256]{1,0:T(8,128)S(1)}, f32[32,256]{1,0:T(8,128)S(1)}, u32[]{:S(2)}, u32[]{:S(2)}) collective-permute-start(f32[32,256]{1,0:T(8,128)S(1)} %add_add_fusion), channel_id=1, source_target_pairs={{8,0},{10,2},{12,4},{14,6},{0,8},{2,10},{4,12},{6,14},{9,1},{11,3}... | collective-permute-start | bytes 98312 | tf_op jit(solution)/shard_map/ppermute | solution.py:226
  20.8 3.8 %collective-permute-start.7 = (bf16[32,256]{1,0:T(8,128)(2,1)S(1)}, bf16[32,256]{1,0:T(8,128)(2,1)S(1)}, u32[]{:S(2)}, u32[]{:S(2)}) collective-permute-start(bf16[32,256]{1,0:T(8,128)(2,1)S(1)} %add_convert_fusion.refs_2_), channel_id=1, source_target_pairs={{16,0},{17,1},{0,16},{1,17},{18,2},{19,3},{2,18},{3,19},{20,4},{21... | collective-permute-start | bytes 49160 | tf_op jit(solution)/shard_map/ppermute | solution.py:236
  21.3 3.4 %collective-permute-start.6 = (bf16[32,256]{1,0:T(8,128)(2,1)S(1)}, bf16[32,256]{1,0:T(8,128)(2,1)S(1)}, u32[]{:S(2)}, u32[]{:S(2)}) collective-permute-start(bf16[32,256]{1,0:T(8,128)(2,1)S(1)} %add_convert_fusion.refs_2_), channel_id=1, source_target_pairs={{1,0},{0,1},{17,16},{16,17},{3,2},{2,3},{19,18},{18,19},{5,4},{4,5... | collective-permute-start | bytes 49160 | tf_op jit(solution)/shard_map/ppermute | solution.py:236
  21.3 7.4 %collective-permute-start.9 = (bf16[64,1536]{1,0:T(8,128)(2,1)S(1)}, bf16[64,1536]{1,0:T(8,128)(2,1)S(1)}, u32[]{:S(2)}, u32[]{:S(2)}) collective-permute-start(bf16[64,1536]{1,0:T(8,128)(2,1)S(1)} %get-tuple-element.16.refs_0_), channel_id=1, source_target_pairs={{16,0},{17,1},{0,16},{1,17},{18,2},{19,3},{2,18},{3,19},{20,4},{21... | collective-permute-start | bytes 589832 | tf_op jit(solution)/shard_map/ppermute | solution.py:236
  24.6 1.2 %collective-permute-start.8 = (bf16[32,256]{1,0:T(8,128)(2,1)S(1)}, bf16[32,256]{1,0:T(8,128)(2,1)S(1)}, u32[]{:S(2)}, u32[]{:S(2)}) collective-permute-start(bf16[32,256]{1,0:T(8,128)(2,1)S(1)} %collective-permute-done.7.refs_4_), channel_id=1, source_target_pairs={{1,0},{0,1},{17,16},{16,17},{3,2},{2,3},{19,18},{18,19},{5,4},{4,5... | collective-permute-start | bytes 49160 | tf_op jit(solution)/shard_map/ppermute | solution.py:236

commit v25 on v24

--- a/solution.py
+++ b/solution.py
@@ -269,7 +269,7 @@
     rows = eigen_vectors.shape[1] // tm
     vectors = lax.dynamic_slice_in_dim(eigen_vectors, me * rows, rows, 1)
     operator, modes, weights = rebuild_first(
-        inverse_energy[None, :], vectors.T, first, coeffs, cells, 6
+        inverse_energy[None, :], vectors.T, first, coeffs, cells, 13
     )
     return operator, rebuild_last(weights, last, modes, begin, 3)
 

time: 30 us -> 30 us (level)
  no operation moved by 1% of the time
where the time goes in v25:
time: 30 us; the launch traced here: 29.8 us
  starting transfers between devices  11.2 us (37%)
  waiting for transfers between devices  10.1 us (34%)
  Pallas kernels  7.62 us (25%)
  between operations  0.71 us (2%)
    ppermute x5, waiting for transfers between devices, swapped(): return lax.ppermute(value, axis, route)  6.82 us
    ppermute x5, starting transfers between devices, swapped(): return lax.ppermute(value, axis, route)  6.21 us
    ppermute x5, starting transfers between devices, moved(): return lax.ppermute(value, ('tm', 'inner'), route)  5.03 us
    ppermute x5, waiting for transfers between devices, moved(): return lax.ppermute(value, ('tm', 'inner'), route)  3.29 us
    pallas_call x1, Pallas kernels, project(): pl.pallas_call(functools.partial(project_kernel, tiles), out_shape=(half,...  2.82 us
    pallas_call x1, Pallas kernels, rebuild_first(): pl.pallas_call(functools.partial(first_kernel, tiles), out_shape=(jax.Sha...  2.49 us
    pallas_call x1, Pallas kernels, cut(): pl.pallas_call(cut_kernel, out_shape=jax.ShapeDtypeStruct((fields.shape[0...  1.2 us
    pallas_call x1, Pallas kernels, rebuild_last(): pl.pallas_call(functools.partial(last_kernel, begin, tiles), out_shape=ja...  1.12 us
  transfers between devices with their start and end apart: 10, of which 8 were waited for; matrix products, arithmetic and copies ran while one was open for 0% of the time, Pallas kernels for 18%

profile of v25, /device:TPU:0, one launch (start us, length us, event | category | flops | bytes accessed | tf_op | source)
XLA Modules:
  0.0 29.8 jit_solution(1385500083396831710)
XLA Ops:
  0.6 0.0 copy-start
  0.6 0.0 copy-start.1
  0.7 1.2 %cut.1.early.refs_0_ = bf16[64,6656]{1,0:T(8,128)(2,1)S(1)} custom-call(bf16[64,8192]{1,0:T(8,128)(2,1)} %bitcast.5), custom_call_target="tpu_custom_call" | custom-call | tf_op jit(solution)/shard_map/cut/pallas_call | solution.py:54
  1.9 3.0 %collective-permute-start = (bf16[64,6656]{1,0:T(8,128)(2,1)S(1)}, bf16[64,6656]{1,0:T(8,128)(2,1)S(1)}, u32[]{:S(2)}, u32[]{:S(2)}) collective-permute-start(bf16[64,6656]{1,0:T(8,128)(2,1)S(1)} %cut.1.early.refs_0_), channel_id=1, source_target_pairs={{16,0},{17,1},{0,16},{1,17},{18,2},{19,3},{2,18},{3,19},{20,4},{21... | collective-permute-start | bytes 2555912 | tf_op jit(solution)/shard_map/ppermute | solution.py:236
  4.9 2.8 %project.1 = (f32[32,256]{1,0:T(8,128)S(1)}, f32[32,256]{1,0:T(8,128)S(1)}, bf16[64,1536]{1,0:T(8,128)(2,1)S(1)}) custom-call(bf16[64,6656]{1,0:T(8,128)(2,1)S(1)} %cut.1.early.refs_0_, bf16[64,8192]{1,0:T(8,128)(2,1)} %bitcast.6, bf16[8192,256]{1,0:T(8,128)(2,1)} %basis.1), custom_call_target="tpu_custom_call" | custom-call | tf_op jit(solution)/shard_map/project/pallas_call | solution.py:100
  7.7 0.1 collective-permute-start.1
  7.8 1.2 %collective-permute-done.1 = f32[32,256]{1,0:T(8,128)S(1)} collective-permute-done((f32[32,256]{1,0:T(8,128)S(1)}, f32[32,256]{1,0:T(8,128)S(1)}, u32[]{:S(2)}, u32[]{:S(2)}) %collective-permute-start.1) | collective-permute-done | bytes 32800 | tf_op jit(solution)/shard_map/ppermute | solution.py:226
  9.0 2.5 %collective-permute-start.4 = (f32[32,256]{1,0:T(8,128)S(1)}, f32[32,256]{1,0:T(8,128)S(1)}, u32[]{:S(2)}, u32[]{:S(2)}) collective-permute-start(f32[32,256]{1,0:T(8,128)S(1)} %add.19), channel_id=1, source_target_pairs={{6,0},{4,2},{2,4},{0,6},{14,8},{12,10},{10,12},{8,14},{7,1},{5,3},... | collective-permute-start | bytes 98312 | tf_op jit(solution)/shard_map/ppermute | solution.py:226
  11.5 0.4 %collective-permute-start.3 = (f32[32,256]{1,0:T(8,128)S(1)}, f32[32,256]{1,0:T(8,128)S(1)}, u32[]{:S(2)}, u32[]{:S(2)}) collective-permute-start(f32[32,256]{1,0:T(8,128)S(1)} %add.19), channel_id=1, source_target_pairs={{4,0},{6,2},{0,4},{2,6},{12,8},{14,10},{8,12},{10,14},{5,1},{7,3},... | collective-permute-start | bytes 98312 | tf_op jit(solution)/shard_map/ppermute | solution.py:226
  12.0 0.5 %collective-permute-start.2 = (f32[32,256]{1,0:T(8,128)S(1)}, f32[32,256]{1,0:T(8,128)S(1)}, u32[]{:S(2)}, u32[]{:S(2)}) collective-permute-start(f32[32,256]{1,0:T(8,128)S(1)} %add.19), channel_id=1, source_target_pairs={{2,0},{0,2},{6,4},{4,6},{10,8},{8,10},{14,12},{12,14},{3,1},{1,3},... | collective-permute-start | bytes 98312 | tf_op jit(solution)/shard_map/ppermute | solution.py:226
  12.5 1.3 %collective-permute-done.4 = f32[32,256]{1,0:T(8,128)S(1)} collective-permute-done((f32[32,256]{1,0:T(8,128)S(1)}, f32[32,256]{1,0:T(8,128)S(1)}, u32[]{:S(2)}, u32[]{:S(2)}) %collective-permute-start.4) | collective-permute-done | bytes 32800 | tf_op jit(solution)/shard_map/ppermute | solution.py:226
  13.8 1.6 %collective-permute-done.3 = f32[32,256]{1,0:T(8,128)S(1)} collective-permute-done((f32[32,256]{1,0:T(8,128)S(1)}, f32[32,256]{1,0:T(8,128)S(1)}, u32[]{:S(2)}, u32[]{:S(2)}) %collective-permute-start.3) | collective-permute-done | bytes 32800 | tf_op jit(solution)/shard_map/ppermute | solution.py:226
  15.4 0.4 %collective-permute-done.2 = f32[32,256]{1,0:T(8,128)S(1)} collective-permute-done((f32[32,256]{1,0:T(8,128)S(1)}, f32[32,256]{1,0:T(8,128)S(1)}, u32[]{:S(2)}, u32[]{:S(2)}) %collective-permute-start.2) | collective-permute-done | bytes 32800 | tf_op jit(solution)/shard_map/ppermute | solution.py:226
  15.9 2.7 %collective-permute-start.5 = (f32[32,256]{1,0:T(8,128)S(1)}, f32[32,256]{1,0:T(8,128)S(1)}, u32[]{:S(2)}, u32[]{:S(2)}) collective-permute-start(f32[32,256]{1,0:T(8,128)S(1)} %add_add_fusion), channel_id=1, source_target_pairs={{8,0},{10,2},{12,4},{14,6},{0,8},{2,10},{4,12},{6,14},{9,1},{11,3}... | collective-permute-start | bytes 98312 | tf_op jit(solution)/shard_map/ppermute | solution.py:226
  18.5 2.2 %collective-permute-done.5 = f32[32,256]{1,0:T(8,128)S(1)} collective-permute-done((f32[32,256]{1,0:T(8,128)S(1)}, f32[32,256]{1,0:T(8,128)S(1)}, u32[]{:S(2)}, u32[]{:S(2)}) %collective-permute-start.5) | collective-permute-done | bytes 32800 | tf_op jit(solution)/shard_map/ppermute | solution.py:226
  20.8 0.5 %collective-permute-start.7 = (bf16[32,256]{1,0:T(8,128)(2,1)S(1)}, bf16[32,256]{1,0:T(8,128)(2,1)S(1)}, u32[]{:S(2)}, u32[]{:S(2)}) collective-permute-start(bf16[32,256]{1,0:T(8,128)(2,1)S(1)} %add_convert_fusion.refs_2_), channel_id=1, source_target_pairs={{16,0},{17,1},{0,16},{1,17},{18,2},{19,3},{2,18},{3,19},{20,4},{21... | collective-permute-start | bytes 49160 | tf_op jit(solution)/shard_map/ppermute | solution.py:236
  21.3 0.0 collective-permute-start.6
  21.3 1.5 %collective-permute-start.9 = (bf16[64,1536]{1,0:T(8,128)(2,1)S(1)}, bf16[64,1536]{1,0:T(8,128)(2,1)S(1)}, u32[]{:S(2)}, u32[]{:S(2)}) collective-permute-start(bf16[64,1536]{1,0:T(8,128)(2,1)S(1)} %get-tuple-element.16.refs_0_), channel_id=1, source_target_pairs={{16,0},{17,1},{0,16},{1,17},{18,2},{19,3},{2,18},{3,19},{20,4},{21... | collective-permute-start | bytes 589832 | tf_op jit(solution)/shard_map/ppermute | solution.py:236
  22.8 1.8 %collective-permute-done.7.refs_4_ = bf16[32,256]{1,0:T(8,128)(2,1)S(1)} collective-permute-done((bf16[32,256]{1,0:T(8,128)(2,1)S(1)}, bf16[32,256]{1,0:T(8,128)(2,1)S(1)}, u32[]{:S(2)}, u32[]{:S(2)}) %collective-permute-start.7) | collective-permute-done | bytes 16416 | tf_op jit(solution)/shard_map/ppermute | solution.py:236
  24.6 0.0 collective-permute-start.8
  24.6 0.0 copy-done
  24.6 0.1 copy.8
  24.7 0.0 collective-permute-done.6.refs_3_
  24.7 1.0 %collective-permute-done.8.refs_5_ = bf16[32,256]{1,0:T(8,128)(2,1)S(1)} collective-permute-done((bf16[32,256]{1,0:T(8,128)(2,1)S(1)}, bf16[32,256]{1,0:T(8,128)(2,1)S(1)}, u32[]{:S(2)}, u32[]{:S(2)}) %collective-permute-start.8) | collective-permute-done | bytes 16416 | tf_op jit(solution)/shard_map/ppermute | solution.py:236
  25.8 0.0 collective-permute-done.refs_1_
  25.8 0.0 copy-done.1
  25.8 2.5 %rebuild_first.1 = (f32[256,256]{1,0:T(8,128)}, bf16[256,8192]{1,0:T(8,128)(2,1)}, bf16[256,128]{1,0:T(8,128)(2,1)S(1)}) custom-call(f32[1,256]{1,0:T(1,128)S(1)} %bitcast.4, bf16[256,256]{1,0:T(8,128)(2,1)S(1)} %bitcast.3, bf16[64,6656]{1,0:T(8,128)(2,1)S(1)} %cut.1.early.refs_0_, bf16[64,6656]{1,0:T(8,128)(2,1)S(1)} %collective-permute-done.refs_1_, ...), custom_call_target="tpu_custom_call" | custom-call | flops 2000000000 | tf_op jit(solution)/shard_map/rebuild_first/pallas_call | solution.py:185
  28.3 0.4 %collective-permute-done.9.refs_1_ = bf16[64,1536]{1,0:T(8,128)(2,1)S(1)} collective-permute-done((bf16[64,1536]{1,0:T(8,128)(2,1)S(1)}, bf16[64,1536]{1,0:T(8,128)(2,1)S(1)}, u32[]{:S(2)}, u32[]{:S(2)}) %collective-permute-start.9) | collective-permute-done | bytes 196640 | tf_op jit(solution)/shard_map/ppermute | solution.py:236
  28.7 1.1 %rebuild_last.1 = bf16[256,8192]{1,0:T(8,128)(2,1)} custom-call(bf16[256,128]{1,0:T(8,128)(2,1)S(1)} %get-tuple-element.15.weights, bf16[64,1536]{1,0:T(8,128)(2,1)S(1)} %get-tuple-element.16.refs_0_, bf16[64,1536]{1,0:T(8,128)(2,1)S(1)} %collective-permute-done.9.refs_1_, bf16[256,8192]{1,0:T(8,128)(2,1)} %get-tuple-element.17.refs_2_), custom_call_target="tpu_custom_call", output_to_operand_aliasing={{}: (3, {})} | custom-call | tf_op jit(solution)/shard_map/rebuild_last/pallas_call | solution.py:208
  (4 shorter events, 0.0 us)
Async XLA Ops:
  0.6 24.0 %copy-start = (bf16[256,512]{1,0:T(8,128)(2,1)S(1)}, bf16[256,512]{1,0:T(8,128)(2,1)}, u32[]{:S(2)}) copy-start(bf16[256,512]{1,0:T(8,128)(2,1)} %param.7) | copy-start | bytes 786436
  0.6 25.1 %copy-start.1 = (f32[256]{0:T(256)S(1)}, f32[256]{0:T(256)}, u32[]{:S(2)}) copy-start(f32[256]{0:T(256)} %param.6) | copy-start | bytes 3076
  1.9 23.9 %collective-permute-start = (bf16[64,6656]{1,0:T(8,128)(2,1)S(1)}, bf16[64,6656]{1,0:T(8,128)(2,1)S(1)}, u32[]{:S(2)}, u32[]{:S(2)}) collective-permute-start(bf16[64,6656]{1,0:T(8,128)(2,1)S(1)} %cut.1.early.refs_0_), channel_id=1, source_target_pairs={{16,0},{17,1},{0,16},{1,17},{18,2},{19,3},{2,18},{3,19},{20,4},{21... | collective-permute-start | bytes 2555912 | tf_op jit(solution)/shard_map/ppermute | solution.py:236
  7.7 1.3 %collective-permute-start.1 = (f32[32,256]{1,0:T(8,128)S(1)}, f32[32,256]{1,0:T(8,128)S(1)}, u32[]{:S(2)}, u32[]{:S(2)}) collective-permute-start(f32[32,256]{1,0:T(8,128)S(1)} %get-tuple-element.11), channel_id=1, source_target_pairs={{1,0},{0,1},{3,2},{2,3},{5,4},{4,5},{7,6},{6,7},{9,8},{8,9},{11,10... | collective-permute-start | bytes 98312 | tf_op jit(solution)/shard_map/ppermute | solution.py:226
  9.0 4.8 %collective-permute-start.4 = (f32[32,256]{1,0:T(8,128)S(1)}, f32[32,256]{1,0:T(8,128)S(1)}, u32[]{:S(2)}, u32[]{:S(2)}) collective-permute-start(f32[32,256]{1,0:T(8,128)S(1)} %add.19), channel_id=1, source_target_pairs={{6,0},{4,2},{2,4},{0,6},{14,8},{12,10},{10,12},{8,14},{7,1},{5,3},... | collective-permute-start | bytes 98312 | tf_op jit(solution)/shard_map/ppermute | solution.py:226
  11.5 3.9 %collective-permute-start.3 = (f32[32,256]{1,0:T(8,128)S(1)}, f32[32,256]{1,0:T(8,128)S(1)}, u32[]{:S(2)}, u32[]{:S(2)}) collective-permute-start(f32[32,256]{1,0:T(8,128)S(1)} %add.19), channel_id=1, source_target_pairs={{4,0},{6,2},{0,4},{2,6},{12,8},{14,10},{8,12},{10,14},{5,1},{7,3},... | collective-permute-start | bytes 98312 | tf_op jit(solution)/shard_map/ppermute | solution.py:226
  12.0 3.9 %collective-permute-start.2 = (f32[32,256]{1,0:T(8,128)S(1)}, f32[32,256]{1,0:T(8,128)S(1)}, u32[]{:S(2)}, u32[]{:S(2)}) collective-permute-start(f32[32,256]{1,0:T(8,128)S(1)} %add.19), channel_id=1, source_target_pairs={{2,0},{0,2},{6,4},{4,6},{10,8},{8,10},{14,12},{12,14},{3,1},{1,3},... | collective-permute-start | bytes 98312 | tf_op jit(solution)/shard_map/ppermute | solution.py:226
  15.9 4.9 %collective-permute-start.5 = (f32[32,256]{1,0:T(8,128)S(1)}, f32[32,256]{1,0:T(8,128)S(1)}, u32[]{:S(2)}, u32[]{:S(2)}) collective-permute-start(f32[32,256]{1,0:T(8,128)S(1)} %add_add_fusion), channel_id=1, source_target_pairs={{8,0},{10,2},{12,4},{14,6},{0,8},{2,10},{4,12},{6,14},{9,1},{11,3}... | collective-permute-start | bytes 98312 | tf_op jit(solution)/shard_map/ppermute | solution.py:226
  20.8 3.8 %collective-permute-start.7 = (bf16[32,256]{1,0:T(8,128)(2,1)S(1)}, bf16[32,256]{1,0:T(8,128)(2,1)S(1)}, u32[]{:S(2)}, u32[]{:S(2)}) collective-permute-start(bf16[32,256]{1,0:T(8,128)(2,1)S(1)} %add_convert_fusion.refs_2_), channel_id=1, source_target_pairs={{16,0},{17,1},{0,16},{1,17},{18,2},{19,3},{2,18},{3,19},{20,4},{21... | collective-permute-start | bytes 49160 | tf_op jit(solution)/shard_map/ppermute | solution.py:236
  21.3 3.4 %collective-permute-start.6 = (bf16[32,256]{1,0:T(8,128)(2,1)S(1)}, bf16[32,256]{1,0:T(8,128)(2,1)S(1)}, u32[]{:S(2)}, u32[]{:S(2)}) collective-permute-start(bf16[32,256]{1,0:T(8,128)(2,1)S(1)} %add_convert_fusion.refs_2_), channel_id=1, source_target_pairs={{1,0},{0,1},{17,16},{16,17},{3,2},{2,3},{19,18},{18,19},{5,4},{4,5... | collective-permute-start | bytes 49160 | tf_op jit(solution)/shard_map/ppermute | solution.py:236
  21.3 7.4 %collective-permute-start.9 = (bf16[64,1536]{1,0:T(8,128)(2,1)S(1)}, bf16[64,1536]{1,0:T(8,128)(2,1)S(1)}, u32[]{:S(2)}, u32[]{:S(2)}) collective-permute-start(bf16[64,1536]{1,0:T(8,128)(2,1)S(1)} %get-tuple-element.16.refs_0_), channel_id=1, source_target_pairs={{16,0},{17,1},{0,16},{1,17},{18,2},{19,3},{2,18},{3,19},{20,4},{21... | collective-permute-start | bytes 589832 | tf_op jit(solution)/shard_map/ppermute | solution.py:236
  24.6 1.2 %collective-permute-start.8 = (bf16[32,256]{1,0:T(8,128)(2,1)S(1)}, bf16[32,256]{1,0:T(8,128)(2,1)S(1)}, u32[]{:S(2)}, u32[]{:S(2)}) collective-permute-start(bf16[32,256]{1,0:T(8,128)(2,1)S(1)} %collective-permute-done.7.refs_4_), channel_id=1, source_target_pairs={{1,0},{0,1},{17,16},{16,17},{3,2},{2,3},{19,18},{18,19},{5,4},{4,5... | collective-permute-start | bytes 49160 | tf_op jit(solution)/shard_map/ppermute | solution.py:236
